TPU v7x, 32 devices: a whole 2x2x4 slice. The times are simulated.
32 devices in a mesh: dp: 2 (over y), seq: 2 (over core), tensor: 8 (over z, x).
Axes of the slice: x: 2, y: 2, z: 4, core: 2. Of those that a mesh axis runs over, the one named last changes fastest.
Arguments:
- tokens: bfloat16 [2, 2048, 2048], P('dp', 'seq'), may hold values from -6 to 6
- cotangent: bfloat16 [2, 2048, 2048], P('dp', 'seq'), may hold values from -6 to 6
- query_weight: float32 [2048, 2048], P(('dp', 'seq'), 'tensor'), may hold values from -0.125 to 0.125
- output_weight: float32 [2048, 2048], P(('dp', 'seq'), 'tensor'), may hold values from -4 to 4
- kv_weight: float32 [2048, 1024], P(('dp', 'seq'), 'tensor'), may hold values from -0.125 to 0.125
- gate_up_weight: float32 [2048, 2, 8192], P(('dp', 'seq'), None, 'tensor'), may hold values from -0.125 to 0.125
- down_weight: float32 [2048, 8192], P(('dp', 'seq'), 'tensor'), may hold values from -0.0625 to 0.0625
- norm_gains: float32 [2048, 2], P(('dp', 'seq')), may hold values from 0.5 to 1.5
- query_first: float32 [2048, 2048], P(('dp', 'seq'), 'tensor'), may hold values from -64 to 64
- output_first: float32 [2048, 2048], P(('dp', 'seq'), 'tensor'), may hold values from -2 to 2
- kv_first: float32 [2048, 1024], P(('dp', 'seq'), 'tensor'), may hold values from -128 to 128
- gate_up_first: float32 [2048, 2, 8192], P(('dp', 'seq'), None, 'tensor'), may hold values from -12 to 12
- down_first: float32 [2048, 8192], P(('dp', 'seq'), 'tensor'), may hold values from -24 to 24
- gains_first: float32 [2048, 2], P(('dp', 'seq')), may hold values from -80 to 80
- query_second: float32 [2048, 2048], P(('dp', 'seq'), 'tensor'), may hold values from 546.816 to 2191.36
- output_second: float32 [2048, 2048], P(('dp', 'seq'), 'tensor'), may hold values from 0.534 to 2.14
- kv_second: float32 [2048, 1024], P(('dp', 'seq'), 'tensor'), may hold values from 2191.36 to 8744.96
- gate_up_second: float32 [2048, 2, 8192], P(('dp', 'seq'), None, 'tensor'), may hold values from 19.3536 to 77.6192
- down_second: float32 [2048, 8192], P(('dp', 'seq'), 'tensor'), may hold values from 77.4144 to 310.4768
- gains_second: float32 [2048, 2], P(('dp', 'seq')), may hold values from 155.2384 to 4915.2
Outputs:
- block_out: bfloat16 [2, 2048, 2048], P('dp', 'seq')
- tokens_grad: float32 [2, 2048, 2048], P('dp', 'seq')
- query_updated: float32 [2048, 2048], P(('dp', 'seq'), 'tensor')
- output_updated: float32 [2048, 2048], P(('dp', 'seq'), 'tensor')
- kv_updated: float32 [2048, 1024], P(('dp', 'seq'), 'tensor')
- gate_up_updated: float32 [2048, 2, 8192], P(('dp', 'seq'), None, 'tensor')
- down_updated: float32 [2048, 8192], P(('dp', 'seq'), 'tensor')
- gains_updated: float32 [2048, 2], P(('dp', 'seq'))
- query_first_out: float32 [2048, 2048], P(('dp', 'seq'), 'tensor')
- output_first_out: float32 [2048, 2048], P(('dp', 'seq'), 'tensor')
- kv_first_out: float32 [2048, 1024], P(('dp', 'seq'), 'tensor')
- gate_up_first_out: float32 [2048, 2, 8192], P(('dp', 'seq'), None, 'tensor')
- down_first_out: float32 [2048, 8192], P(('dp', 'seq'), 'tensor')
- gains_first_out: float32 [2048, 2], P(('dp', 'seq'))
- query_second_out: float32 [2048, 2048], P(('dp', 'seq'), 'tensor')
- output_second_out: float32 [2048, 2048], P(('dp', 'seq'), 'tensor')
- kv_second_out: float32 [2048, 1024], P(('dp', 'seq'), 'tensor')
- gate_up_second_out: float32 [2048, 2, 8192], P(('dp', 'seq'), None, 'tensor')
- down_second_out: float32 [2048, 8192], P(('dp', 'seq'), 'tensor')
- gains_second_out: float32 [2048, 2], P(('dp', 'seq'))
All inputs are finite; a program needn't handle non-finite values.
Results may differ from a plain program's by a relative error of at most 0.023.
Values may be sent and summed in bfloat16 or wider, within the bound.
No kernel may reach another device: no remote copies, remote signals or barrier semaphores. Data moves between devices by JAX's collectives and lax.ppermute only.
A program may use at most 256 MiB of HBM per device.

v0:
```python
import math

import jax
import jax.numpy as jnp
from jax import lax
from jax.sharding import PartitionSpec as P

D = 2048
FF = 8192
HEADS = 32
KV_HEADS = 8
HEAD_DIM = 64
STEP = 10
FAN_OUT = 2


EPS_NORM = 1e-05
ROPE_BASE = 500000.0
BETA_ONE = 0.9
BETA_TWO = 0.95
ADAM_EPS = 1e-08
DECAY = 0.1
RATE_FACTOR = 3.0
GAIN_RATE = 1.0
MASKED = -1e30


def rope_tables(positions):
    half_dim = HEAD_DIM // 2
    exponent = jnp.arange(half_dim, dtype=jnp.float32) * (2.0 / HEAD_DIM)
    inverse = jnp.power(jnp.float32(ROPE_BASE), -exponent)
    angles = positions.astype(jnp.float32)[:, None] * inverse[None, :]
    return (jnp.cos(angles), jnp.sin(angles))


def rotate(values, cosine, sine_table):
    half_dim = values.shape[-1] // 2
    first_half = values[..., :half_dim]
    second_half = values[..., half_dim:]
    cos_rows = cosine[:, None, :]
    sin_rows = sine_table[:, None, :]
    return jnp.concatenate(
        [
            first_half * cos_rows - second_half * sin_rows,
            second_half * cos_rows + first_half * sin_rows,
        ],
        axis=-1,
    )


def unrotate(values, cosine, sine_table):
    half_dim = values.shape[-1] // 2
    first_half = values[..., :half_dim]
    second_half = values[..., half_dim:]
    cos_rows = cosine[:, None, :]
    sin_rows = sine_table[:, None, :]
    return jnp.concatenate(
        [
            first_half * cos_rows + second_half * sin_rows,
            second_half * cos_rows - first_half * sin_rows,
        ],
        axis=-1,
    )


def normalize_keep(values, gain):
    inverse = lax.rsqrt(jnp.mean(values * values, axis=-1, keepdims=True) + EPS_NORM)
    return (values * inverse * gain, inverse)


def norm_back(values, inverse, gain, incoming):
    scaled = incoming * gain
    gain_grad = jnp.sum(incoming * values * inverse, axis=0)
    inner = jnp.mean(scaled * values, axis=-1, keepdims=True)
    return (inverse * scaled - values * inverse * inverse * inverse * inner, gain_grad)


def adam_step(weight, grad_sum, moment_one, moment_two, step_rate, decay_rate):
    first_new = BETA_ONE * moment_one + (1.0 - BETA_ONE) * grad_sum
    second_new = BETA_TWO * moment_two + (1.0 - BETA_TWO) * grad_sum * grad_sum
    first_hat = first_new / (1.0 - BETA_ONE**STEP)
    second_hat = second_new / (1.0 - BETA_TWO**STEP)
    updated = weight - step_rate * (
        first_hat / (jnp.sqrt(second_hat) + ADAM_EPS) + decay_rate * weight
    )
    return (updated, first_new, second_new)


def body(
    tokens,
    cotangent,
    query_weight,
    output_weight,
    kv_weight,
    gate_up_weight,
    down_weight,
    norm_gains,
    query_first,
    output_first,
    kv_first,
    gate_up_first,
    down_first,
    gains_first,
    query_second,
    output_second,
    kv_second,
    gate_up_second,
    down_second,
    gains_second,
):
    seq_count, span_len, model_width = tokens.shape
    row_count = seq_count * span_len
    query_low = query_weight.astype(jnp.bfloat16)
    output_low = output_weight.astype(jnp.bfloat16)
    kv_low = kv_weight.astype(jnp.bfloat16)
    gate_up_low = gate_up_weight.astype(jnp.bfloat16)
    down_low = down_weight.astype(jnp.bfloat16)
    gains_low = norm_gains.astype(jnp.bfloat16)
    full_query, full_output, full_kv, full_gate_up, full_down, full_gains = (
        lax.all_gather(query_low, ("dp", "seq"), axis=0, tiled=True),
        lax.all_gather(output_low, ("dp", "seq"), axis=0, tiled=True),
        lax.all_gather(kv_low, ("dp", "seq"), axis=0, tiled=True),
        lax.all_gather(gate_up_low, ("dp", "seq"), axis=0, tiled=True),
        lax.all_gather(down_low, ("dp", "seq"), axis=0, tiled=True),
        lax.all_gather(gains_low, ("dp", "seq"), axis=0, tiled=True),
    )
    gain_one = full_gains[:, 0].astype(jnp.float32)
    gain_two = full_gains[:, 1].astype(jnp.float32)
    token_rows = tokens.reshape(row_count, model_width).astype(jnp.float32)
    cot_rows = cotangent.reshape(row_count, model_width)
    normed_one, inverse_one = normalize_keep(token_rows, gain_one)
    normed_one = normed_one.astype(jnp.bfloat16)
    query_raw = jnp.dot(normed_one, full_query, preferred_element_type=jnp.float32)
    kv_raw = jnp.dot(normed_one, full_kv, preferred_element_type=jnp.float32)
    local_heads = full_query.shape[1] // HEAD_DIM
    kv_local = full_kv.shape[1] // (2 * HEAD_DIM)
    group_size = HEADS // KV_HEADS
    head_rows = group_size * span_len
    positions = lax.axis_index("seq") * span_len + jnp.arange(span_len, dtype=jnp.int32)
    cosine, sine_table = rope_tables(positions)
    cos_rows = jnp.tile(cosine, (seq_count, 1))
    sin_rows = jnp.tile(sine_table, (seq_count, 1))
    queries = rotate(
        query_raw.reshape(row_count, local_heads, HEAD_DIM), cos_rows, sin_rows
    ).astype(jnp.bfloat16)
    kv_split = kv_raw.reshape(row_count, kv_local, 2, HEAD_DIM)
    key_part = rotate(kv_split[:, :, 0], cos_rows, sin_rows)
    kv_sent = (
        jnp.stack([key_part, kv_split[:, :, 1]], axis=2)
        .astype(jnp.bfloat16)
        .reshape(seq_count, span_len, kv_local * 2 * HEAD_DIM)
    )
    kv_every = lax.all_gather(kv_sent, "seq", axis=1, tiled=True)
    length = kv_every.shape[1]
    block_len = math.gcd(length, 512)
    block_count = length // block_len
    score_scale = HEAD_DIM ** (-0.5)
    row_places = jnp.tile(positions, group_size)
    block_ids = jnp.arange(block_count, dtype=jnp.int32)
    query_blocks = (
        queries.reshape(seq_count, span_len, kv_local, group_size, HEAD_DIM)
        .transpose(0, 2, 3, 1, 4)
        .reshape(seq_count, kv_local, head_rows, HEAD_DIM)
    )
    kv_blocks = kv_every.reshape(
        seq_count, block_count, block_len, kv_local, 2, HEAD_DIM
    ).transpose(0, 4, 1, 3, 2, 5)
    key_blocks = kv_blocks[:, 0]
    value_blocks = kv_blocks[:, 1]

    def block_scores(query_part, key_block, block_index):
        scores = (
            jnp.einsum("hrd,hkd->hrk", query_part, key_block, preferred_element_type=jnp.float32)
            * score_scale
        )
        key_places = block_index * block_len + jnp.arange(block_len, dtype=jnp.int32)
        visible = row_places[:, None] >= key_places[None, :]
        return (scores, visible)

    def forward_sequence(operands):
        query_part, key_all, value_all = operands

        def stats_step(state_pair, block_items):
            highest, running = state_pair
            key_block, block_index = block_items
            scores, visible = block_scores(query_part, key_block, block_index)
            masked_scores = jnp.where(visible[None], scores, MASKED)
            new_high = jnp.maximum(highest, jnp.max(masked_scores, axis=-1))
            fresh = jnp.where(visible[None], jnp.exp(masked_scores - new_high[..., None]), 0.0)
            running = running * jnp.exp(highest - new_high) + jnp.sum(fresh, axis=-1)
            return ((new_high, running), None)

        start_high = jnp.full(query_part.shape[:2], MASKED, jnp.float32)
        start_sum = jnp.zeros(query_part.shape[:2], jnp.float32)
        (highest, running), unused = lax.scan(
            stats_step, (start_high, start_sum), (key_all, block_ids)
        )
        log_total = highest + jnp.log(running)

        def value_step(accumulated, block_items):
            key_block, value_block, block_index = block_items
            scores, visible = block_scores(query_part, key_block, block_index)
            chances = jnp.where(visible[None], jnp.exp(scores - log_total[..., None]), 0.0).astype(
                jnp.bfloat16
            )
            return (
                accumulated
                + jnp.einsum(
                    "hrk,hkd->hrd", chances, value_block, preferred_element_type=jnp.float32
                ),
                None,
            )

        start_acc = jnp.zeros(query_part.shape, jnp.float32)
        attended_part, unused_two = lax.scan(value_step, start_acc, (key_all, value_all, block_ids))
        return (attended_part, log_total)

    attended, log_totals = lax.map(forward_sequence, (query_blocks, key_blocks, value_blocks))
    attended_low = (
        attended.reshape(seq_count, kv_local, group_size, span_len, HEAD_DIM)
        .transpose(0, 3, 1, 2, 4)
        .reshape(row_count, local_heads * HEAD_DIM)
        .astype(jnp.bfloat16)
    )
    attn_part = jnp.einsum(
        "nc,dc->nd", attended_low, full_output, preferred_element_type=jnp.float32
    )
    attn_out = lax.psum(attn_part.astype(jnp.bfloat16), "tensor").astype(jnp.float32)
    resid_one = token_rows + attn_out
    normed_two, inverse_two = normalize_keep(resid_one, gain_two)
    normed_two = normed_two.astype(jnp.bfloat16)
    gate_up = jnp.einsum(
        "nd,dkf->nkf", normed_two, full_gate_up, preferred_element_type=jnp.float32
    )
    gate_part = gate_up[:, 0]
    up_part = gate_up[:, 1]
    sigmoid_gate = jax.nn.sigmoid(gate_part)
    silu_gate = gate_part * sigmoid_gate
    hidden = (silu_gate * up_part).astype(jnp.bfloat16)
    mlp_part = jnp.einsum("nf,df->nd", hidden, full_down, preferred_element_type=jnp.float32)
    mlp_out = lax.psum(mlp_part.astype(jnp.bfloat16), "tensor").astype(jnp.float32)
    block_out = (resid_one + mlp_out).astype(jnp.bfloat16).reshape(seq_count, span_len, model_width)
    full_query, full_output, full_kv, full_gate_up, full_down, full_gains = (
        lax.all_gather(query_low, ("dp", "seq"), axis=0, tiled=True),
        lax.all_gather(output_low, ("dp", "seq"), axis=0, tiled=True),
        lax.all_gather(kv_low, ("dp", "seq"), axis=0, tiled=True),
        lax.all_gather(gate_up_low, ("dp", "seq"), axis=0, tiled=True),
        lax.all_gather(down_low, ("dp", "seq"), axis=0, tiled=True),
        lax.all_gather(gains_low, ("dp", "seq"), axis=0, tiled=True),
    )
    gain_one = full_gains[:, 0].astype(jnp.float32)
    gain_two = full_gains[:, 1].astype(jnp.float32)
    down_grad = jnp.einsum("nd,nf->df", cot_rows, hidden, preferred_element_type=jnp.float32)
    hidden_grad = jnp.einsum("nd,df->nf", cot_rows, full_down, preferred_element_type=jnp.float32)
    gate_grad = hidden_grad * up_part * (sigmoid_gate * (1.0 + gate_part * (1.0 - sigmoid_gate)))
    up_grad = hidden_grad * silu_gate
    gate_up_grad_low = jnp.stack([gate_grad, up_grad], axis=1).astype(jnp.bfloat16)
    gate_up_grad = jnp.einsum(
        "nd,nkf->dkf", normed_two, gate_up_grad_low, preferred_element_type=jnp.float32
    )
    two_part = jnp.einsum(
        "nkf,dkf->nd", gate_up_grad_low, full_gate_up, preferred_element_type=jnp.float32
    )
    normed_two_grad = lax.psum(two_part.astype(jnp.bfloat16), "tensor").astype(jnp.float32)
    resid_back, gain_two_grad = norm_back(resid_one, inverse_two, gain_two, normed_two_grad)
    resid_grad = cot_rows.astype(jnp.float32) + resid_back
    resid_low = resid_grad.astype(jnp.bfloat16)
    output_grad = jnp.einsum(
        "nd,nc->dc", resid_low, attended_low, preferred_element_type=jnp.float32
    )
    attended_grad = jnp.einsum(
        "nd,dc->nc", resid_low, full_output, preferred_element_type=jnp.float32
    ).astype(jnp.bfloat16)
    grad_blocks = (
        attended_grad.reshape(seq_count, span_len, kv_local, group_size, HEAD_DIM)
        .transpose(0, 2, 3, 1, 4)
        .reshape(seq_count, kv_local, head_rows, HEAD_DIM)
    )
    row_delta = jnp.sum(grad_blocks.astype(jnp.float32) * attended, axis=-1)

    def backward_sequence(operands):
        query_part, key_all, value_all, log_total, grad_part, delta_part = operands

        def grad_step(query_grad, block_items):
            key_block, value_block, block_index = block_items
            scores, visible = block_scores(query_part, key_block, block_index)
            chances = jnp.where(visible[None], jnp.exp(scores - log_total[..., None]), 0.0)
            chances_low = chances.astype(jnp.bfloat16)
            chance_grad = jnp.einsum(
                "hrd,hkd->hrk", grad_part, value_block, preferred_element_type=jnp.float32
            )
            score_grad = (chances * (chance_grad - delta_part[..., None])).astype(jnp.bfloat16)
            query_grad = query_grad + jnp.einsum(
                "hrk,hkd->hrd", score_grad, key_block, preferred_element_type=jnp.float32
            )
            key_grad = (
                jnp.einsum(
                    "hrk,hrd->hkd", score_grad, query_part, preferred_element_type=jnp.float32
                )
                * score_scale
            )
            value_grad = jnp.einsum(
                "hrk,hrd->hkd", chances_low, grad_part, preferred_element_type=jnp.float32
            )
            return (query_grad, (key_grad, value_grad))

        start_grad = jnp.zeros(query_part.shape, jnp.float32)
        query_grad, (key_grads, value_grads) = lax.scan(
            grad_step, start_grad, (key_all, value_all, block_ids)
        )
        return (query_grad * score_scale, key_grads, value_grads)

    query_grads, key_grads, value_grads = lax.map(
        backward_sequence,
        (query_blocks, key_blocks, value_blocks, log_totals, grad_blocks, row_delta),
    )
    kv_grad_full = (
        jnp.stack([key_grads, value_grads], axis=4)
        .transpose(0, 1, 3, 2, 4, 5)
        .reshape(seq_count, length, kv_local * 2 * HEAD_DIM)
    )
    kv_grad_local = lax.psum_scatter(
        kv_grad_full.astype(jnp.bfloat16), "seq", scatter_dimension=1, tiled=True
    ).astype(jnp.float32)
    kv_local_split = kv_grad_local.reshape(row_count, kv_local, 2, HEAD_DIM)
    key_back = unrotate(kv_local_split[:, :, 0], cos_rows, sin_rows)
    kv_raw_grad = (
        jnp.stack([key_back, kv_local_split[:, :, 1]], axis=2)
        .reshape(row_count, kv_local * 2 * HEAD_DIM)
        .astype(jnp.bfloat16)
    )
    query_rows_grad = (
        query_grads.reshape(seq_count, kv_local, group_size, span_len, HEAD_DIM)
        .transpose(0, 3, 1, 2, 4)
        .reshape(row_count, local_heads, HEAD_DIM)
    )
    query_raw_grad = (
        unrotate(query_rows_grad, cos_rows, sin_rows)
        .reshape(row_count, local_heads * HEAD_DIM)
        .astype(jnp.bfloat16)
    )
    query_weight_grad = jnp.einsum(
        "nd,nc->dc", normed_one, query_raw_grad, preferred_element_type=jnp.float32
    )
    kv_weight_grad = jnp.einsum(
        "nd,nc->dc", normed_one, kv_raw_grad, preferred_element_type=jnp.float32
    )
    one_part = jnp.einsum(
        "nc,dc->nd", query_raw_grad, full_query, preferred_element_type=jnp.float32
    ) + jnp.einsum("nc,dc->nd", kv_raw_grad, full_kv, preferred_element_type=jnp.float32)
    normed_one_grad = lax.psum(one_part.astype(jnp.bfloat16), "tensor").astype(jnp.float32)
    token_back, gain_one_grad = norm_back(token_rows, inverse_one, gain_one, normed_one_grad)
    tokens_grad = (resid_grad + token_back).reshape(seq_count, span_len, model_width)
    gains_grad = jnp.stack([gain_one_grad, gain_two_grad], axis=1)
    grad_shards = (
        lax.psum_scatter(
            query_weight_grad.astype(jnp.bfloat16), ("dp", "seq"), scatter_dimension=0, tiled=True
        ).astype(jnp.float32),
        lax.psum_scatter(
            output_grad.astype(jnp.bfloat16), ("dp", "seq"), scatter_dimension=0, tiled=True
        ).astype(jnp.float32),
        lax.psum_scatter(
            kv_weight_grad.astype(jnp.bfloat16), ("dp", "seq"), scatter_dimension=0, tiled=True
        ).astype(jnp.float32),
        lax.psum_scatter(
            gate_up_grad.astype(jnp.bfloat16), ("dp", "seq"), scatter_dimension=0, tiled=True
        ).astype(jnp.float32),
        lax.psum_scatter(
            down_grad.astype(jnp.bfloat16), ("dp", "seq"), scatter_dimension=0, tiled=True
        ).astype(jnp.float32),
        lax.psum_scatter(
            gains_grad.astype(jnp.bfloat16), ("dp", "seq"), scatter_dimension=0, tiled=True
        ).astype(jnp.float32),
    )
    masters = (query_weight, output_weight, kv_weight, gate_up_weight, down_weight, norm_gains)
    first_moments = (query_first, output_first, kv_first, gate_up_first, down_first, gains_first)
    second_moments = (
        query_second,
        output_second,
        kv_second,
        gate_up_second,
        down_second,
        gains_second,
    )
    rate_list = (
        RATE_FACTOR * D ** (-0.5),
        RATE_FACTOR * FAN_OUT ** (-0.5),
        RATE_FACTOR * D ** (-0.5),
        RATE_FACTOR * D ** (-0.5),
        RATE_FACTOR * FF ** (-0.5),
        GAIN_RATE,
    )
    decay_list = (DECAY, DECAY, DECAY, DECAY, DECAY, 0.0)
    results = [
        adam_step(master, shard_grad, moment_one, moment_two, step_rate, decay_rate)
        for master, shard_grad, moment_one, moment_two, step_rate, decay_rate in zip(
            masters, grad_shards, first_moments, second_moments, rate_list, decay_list
        )
    ]
    new_weights = tuple((result_set[0] for result_set in results))
    new_firsts = tuple((result_set[1] for result_set in results))
    new_seconds = tuple((result_set[2] for result_set in results))
    return (block_out, tokens_grad) + new_weights + new_firsts + new_seconds


def solution(mesh):
    placed = (
        P("dp", "seq", None),
        P("dp", "seq", None),
        P(("dp", "seq"), "tensor"),
        P(("dp", "seq"), "tensor"),
        P(("dp", "seq"), "tensor"),
        P(("dp", "seq"), None, "tensor"),
        P(("dp", "seq"), "tensor"),
        P(("dp", "seq"), None),
        P(("dp", "seq"), "tensor"),
        P(("dp", "seq"), "tensor"),
        P(("dp", "seq"), "tensor"),
        P(("dp", "seq"), None, "tensor"),
        P(("dp", "seq"), "tensor"),
        P(("dp", "seq"), None),
        P(("dp", "seq"), "tensor"),
        P(("dp", "seq"), "tensor"),
        P(("dp", "seq"), "tensor"),
        P(("dp", "seq"), None, "tensor"),
        P(("dp", "seq"), "tensor"),
        P(("dp", "seq"), None),
    )
    return jax.shard_map(
        body,
        mesh=mesh,
        in_specs=placed,
        out_specs=(
            P("dp", "seq", None),
            P("dp", "seq", None),
            P(("dp", "seq"), "tensor"),
            P(("dp", "seq"), "tensor"),
            P(("dp", "seq"), "tensor"),
            P(("dp", "seq"), None, "tensor"),
            P(("dp", "seq"), "tensor"),
            P(("dp", "seq"), None),
            P(("dp", "seq"), "tensor"),
            P(("dp", "seq"), "tensor"),
            P(("dp", "seq"), "tensor"),
            P(("dp", "seq"), None, "tensor"),
            P(("dp", "seq"), "tensor"),
            P(("dp", "seq"), None),
            P(("dp", "seq"), "tensor"),
            P(("dp", "seq"), "tensor"),
            P(("dp", "seq"), "tensor"),
            P(("dp", "seq"), None, "tensor"),
            P(("dp", "seq"), "tensor"),
            P(("dp", "seq"), None),
        ),
        check_vma=False,
    )
```

profile of v0, /device:TPU:0, one launch (start us, length us, event | category | flops | bytes accessed | tf_op | source)
XLA Modules:
  0.0 1143.0 jit_solution(15163933326049446242)
XLA Ops:
  11.7 3.1 fusion.71
  14.8 6.1 all_gather.27
  21.0 10.7 all_gather.28
  31.9 3.8 fusion.124
  37.0 2.4 all_gather.29
  42.1 3.6 fusion.96
  48.2 20.7 %while.62 = (s32[]{:T(128)}, f32[1,4096]{1,0:T(1,128)S(1)}, f32[1,4096]{1,0:T(1,128)S(1)}, s32[4]{0:T(128)S(1)}, bf16[4,1,512,64]{3,2,1,0:T(8,128)(2,1)S(1)}, /*...) while((s32[]{:T(128)}, f32[1,4096]{1,0:T(1,128)S(1)}, ...), condition=%wide.region_4.5_spmd.clone, body=%wide.region_1.4_spmd.clone.sunk | while | flops 289427968 | bytes 18262168 | solution.py:195
  50.9 2.5 fusion.221
  56.0 2.5 fusion.221
  61.2 2.5 fusion.221
  66.4 2.5 fusion.221
  69.0 14.9 %while.63 = (s32[]{:T(128)}, f32[1,4096,64]{1,2,0:T(8,128)S(1)}, s32[4]{0:T(128)S(1)}, bf16[4,1,512,64]{3,2,1,0:T(8,128)(2,1)S(1)}, bf16[1,4096,64]{2,1,0:T(8,12...) while((s32[]{:T(128)}, f32[1,4096,64]{1,2,0:T(8,128)S(1)}, ...), condition=%wide.region_6.7_spmd.clone, body=%wide.region_5.6_spmd.clone.sunk | while | flops 547881472 | bytes 3499674 | solution.py:215
  70.3 2.4 fusion.226
  74.0 2.4 fusion.226
  77.7 2.4 fusion.226
  81.5 2.4 fusion.226
  84.9 2.2 convert_element_type.268
  88.4 4.7 convolution_convert_fusion.1
  93.2 4.8 copy.180
  99.7 150.2 %all-reduce.5.cloned.1.call-done = bf16[1024,2048]{1,0:T(8,128)(2,1)} async-done(((bf16[1024,2048]{1,0:T(8,128)(2,1)}), bf16[1024,2048]{1,0:T(8,128)(2,1)}) %all-reduce.5.cloned.1.call-update) | async-done | bytes 4194320 | tf_op jit(solution)/shard_map/psum | solution.py:228
  249.9 4.9 multiply_reduce_fusion
  254.8 54.4 %all-gather.9.cloned.1.call-done = bf16[2048,2,1024]{2,0,1:T(8,128)(2,1)} async-done(((bf16[512,2,1024]{2,0,1:T(8,128)(2,1)}), bf16[2048,2,1024]{2,0,1:T(8,128)(2,1)}) %all-gather.9.cloned.1.call-update) | async-done | bytes 8388624 | tf_op jit(solution)/shard_map/all_gather | solution.py:123
  309.2 15.9 %fusion.158 = f32[1024,2,1024]{2,0,1:T(8,128)} fusion(bf16[2048,2,1024]{2,0,1:T(8,128)(2,1)} %all-gather.9.cloned.1.call-done, bf16[1024,2048]{1,0:T(8,128)(2,1)} %all-reduce.5.cloned.1.call-done, bf16[1,1024,2048]{2,1,0:T(8,128)(2,1)} %param.26, f32[2048]{0:T(1024)S(1)} %bitcast.415, f32[1024]{0:T(1024)S(1)} %add_rsqrt_fusion), kind=kOutput, calls=%fused_computation.233 | convolution fusion | flops 8602517504 | bytes 25178112 | tf_op jit(solution)/shard_map/nd,dkf->nkf/dot_general | solution.py:232
  325.1 20.6 %all-gather.11.cloned.1.call-done = bf16[2048,1024]{1,0:T(8,128)(2,1)} async-done(((bf16[512,1024]{1,0:T(8,128)(2,1)}), bf16[2048,1024]{1,0:T(8,128)(2,1)}) %all-gather.11.cloned.1.call-update) | async-done | bytes 4194320 | tf_op jit(solution)/shard_map/all_gather | solution.py:124
  345.7 11.8 %fusion.120 = (bf16[1024,1,1024]{2,0,1:T(8,128)(2,1)S(1)}, bf16[1024,1,1024]{2,0,1:T(8,128)(2,1)S(1)}) fusion(f32[1024,2,1024]{2,0,1:T(8,128)} %fusion.158, bf16[2048,1024]{1,0:T(8,128)(2,1)} %all-gather.11.cloned.1.call-done, bf16[1,1024,2048]{2,1,0:T(8,128)(2,1)} %param.27), kind=kOutput, calls=%fused_computation.154 | convolution fusion | flops 4308598784 | bytes 20971520 | tf_op jit(solution)/shard_map/nd,df->nf/dot_general | solution.py:254
  359.6 10.5 bitcast_convert_fusion
  373.2 12.2 %convolution_convert_fusion.2 = bf16[1024,2048]{1,0:T(8,128)(2,1)} fusion(bf16[2048,1024]{1,0:T(8,128)(2,1)} %all-gather.11.cloned.1.call-done, f32[1024,2,1024]{2,0,1:T(8,128)} %fusion.158), kind=kOutput, calls=%fused_computation.139 | convolution fusion | flops 4303355904 | bytes 16777216 | tf_op jit(solution)/shard_map/nf,df->nd/dot_general | solution.py:240
  385.4 141.1 %all-reduce.7.cloned.1.call-done = bf16[1024,2048]{1,0:T(8,128)(2,1)} async-done(((bf16[1024,2048]{1,0:T(8,128)(2,1)}), bf16[1024,2048]{1,0:T(8,128)(2,1)}) %all-reduce.7.cloned.1.call-update) | async-done | bytes 4194320 | tf_op jit(solution)/shard_map/psum | solution.py:264
  526.6 8.1 fusion.70
  534.9 6.5 fusion.67
  541.4 2.7 fusion.121
  548.7 46.2 %while.64 = (s32[]{:T(128)}, f32[1,4096,64]{1,2,0:T(8,128)S(1)}, bf16[4,1,512,64]{2,3,1,0:T(8,128)(2,1)}, bf16[4,1,512,64]{2,3,1,0:T(8,128)(2,1)}, s32[4]{0:T(12...) while((s32[]{:T(128)}, f32[1,4096,64]{1,2,0:T(8,128)S(1)}, ...), condition=%wide.region_14.15_spmd.clone, body=%wide.region_13.14_spmd.clone.sunk | while | flops 1359512064 | bytes 47948092 | solution.py:308
  550.0 2.9 bitcast_select_fusion.3
  554.4 2.3 fusion.237
  561.5 2.9 bitcast_select_fusion.3
  565.8 2.3 fusion.237
  572.9 2.9 bitcast_select_fusion.3
  577.3 2.3 fusion.237
  584.4 2.9 bitcast_select_fusion.3
  588.8 2.3 fusion.237
  600.2 5.4 reduce-scatter.10.cloned.1.call-done
  609.5 3.4 add_convert_fusion
  613.5 4.8 fusion.106
  618.4 6.7 convolution_convert_fusion.3
  625.1 4.6 fusion.109
  630.2 11.4 %convert_bitcast_fusion.1 = bf16[2048,1024]{0,1:T(8,128)(2,1)} fusion(bf16[1,1024,2048]{2,1,0:T(8,128)(2,1)} %param.27, f32[1024,2,1024]{2,0,1:T(8,128)} %fusion.158), kind=kOutput, calls=%fused_computation.133 | convolution fusion | flops 4303355904 | bytes 16777216 | tf_op jit(solution)/shard_map/nd,nf->df/dot_general | solution.py:253
  641.8 243.5 %all-reduce.9.cloned.1.call-done = (bf16[1024,2048]{1,0:T(8,128)(2,1)}, bf16[1024,2048]{1,0:T(8,128)(2,1)}) async-done(((bf16[1024,2048]{1,0:T(8,128)(2,1)}, bf16[1024,2048]{1,0:T(8,128)(2,1)}), (bf16[1024,2048]{1,0:T(8,128)(2,1)}, bf16[1024,2048]{1,0:T(8,128)(2,1)})) %all-reduce.9.cloned.1.call-update) | async-done | bytes 8388624 | tf_op jit(solution)/shard_map/psum | solution.py:241
  885.3 5.8 fusion.77
  892.4 14.9 %convolution_convert_fusion = bf16[2048,2,1024]{2,0,1:T(8,128)(2,1)} fusion(bf16[1024,1,1024]{2,0,1:T(8,128)(2,1)} %copy-done.45, bf16[1024,1,1024]{2,0,1:T(8,128)(2,1)S(1)} %copy-done.44, bf16[1024,2048]{1,0:T(8,128)(2,1)} %all-reduce.5.cloned.1.call-done, bf16[1,1024,2048]{2,1,0:T(8,128)(2,1)} %param.26, f32[2048]{0:T(1024)S(1)} %bitcast.418, ...), kind=kOutput, calls=%fused_computation.99 | convolution fusion | flops 8615100416 | bytes 20983808 | tf_op jit(solution)/shard_map/nd,nkf->dkf/dot_general | solution.py:258
  910.7 3.0 copy.149
  915.6 2.8 multiply_subtract_fusion.3
  918.4 21.3 %reduce-scatter.14.cloned.1.call-done = bf16[512,256]{1,0:T(8,128)(2,1)} async-done(((bf16[2048,256]{1,0:T(8,128)(2,1)}), bf16[512,256]{1,0:T(8,128)(2,1)}) %reduce-scatter.14.cloned.1.call-update) | async-done | bytes 262160 | tf_op jit(solution)/shard_map/reduce_scatter | solution.py:359
  939.7 2.7 multiply_subtract_fusion.2
  942.4 21.7 %reduce-scatter.16.cloned.1.call-done = bf16[512,128]{1,0:T(8,128)(2,1)} async-done(((bf16[2048,128]{1,0:T(8,128)(2,1)}), bf16[512,128]{1,0:T(8,128)(2,1)}) %reduce-scatter.16.cloned.1.call-update) | async-done | bytes 131088 | tf_op jit(solution)/shard_map/reduce_scatter | solution.py:362
  966.1 45.4 %reduce-scatter.20.cloned.1.call-done = bf16[512,1024]{0,1:T(8,128)(2,1)} async-done(((bf16[2048,1024]{0,1:T(8,128)(2,1)}), bf16[512,1024]{0,1:T(8,128)(2,1)}) %reduce-scatter.20.cloned.1.call-update) | async-done | bytes 1048592 | tf_op jit(solution)/shard_map/reduce_scatter | solution.py:368
  1011.6 6.4 multiply_subtract_fusion.1
  1017.9 3.0 copy.154
  1021.0 2.9 copy.156
  1025.7 14.1 %fusion.65 = (f32[1,1024,2048]{2,1,0:T(8,128)}, bf16[1,1024,2048]{2,1,0:T(8,128)(2,1)}) fusion(f32[1024,2048]{1,0:T(8,128)} %copy-done, bf16[1024,2048]{1,0:T(8,128)(2,1)} %get-tuple-element.549, bf16[1,1024,2048]{2,1,0:T(8,128)(2,1)} %param.26, f32[1024]{0:T(1024)S(1)} %broadcast_multiply_fusion.1, f32[2048]{0:T(1024)S(1)} %bitcast.424, ...), kind=kLoop, calls=%fused_computation.78 | loop fusion | flops 31457280 | bytes 37765120 | tf_op jit(solution)/shard_map/reshape | solution.py:353
  1041.5 68.6 %reduce-scatter.18.cloned.1.call-done = bf16[512,2,1024]{2,0,1:T(8,128)(2,1)} async-done(((bf16[2048,2,1024]{2,0,1:T(8,128)(2,1)}), bf16[512,2,1024]{2,0,1:T(8,128)(2,1)}) %reduce-scatter.18.cloned.1.call-update) | async-done | bytes 2097168 | tf_op jit(solution)/shard_map/reduce_scatter | solution.py:365
  1110.1 10.4 multiply_subtract_fusion
  1120.5 5.2 copy.153
  1125.8 5.2 copy.155
  1131.0 5.2 copy.157
  (292 shorter events, 79.6 us)
Async XLA Ops:
  7.2 13.8 %copy-start.25 = (f32[512,128]{1,0:T(8,128)S(1)}, f32[512,128]{1,0:T(8,128)}, u32[]{:S(2)}) copy-start(f32[512,128]{1,0:T(8,128)} %param.30) | copy-start | bytes 786436
  7.2 33.4 %all-gather.5.cloned.1.call-start = ((), (), s32[]{:S(2)}) async-start(), calls=%async_computation.7 | async-start | bytes 1310720 | tf_op jit(solution)/shard_map/all_gather | solution.py:120
  9.1 79.3 %all-gather.7.cloned.1.call-start = ((), (), s32[]{:S(2)}) async-start(), calls=%async_computation.8 | async-start | bytes 1310720 | tf_op jit(solution)/shard_map/all_gather | solution.py:121
  10.9 239.0 %all-reduce.5.cloned.1.call-start = ((), (), s32[]{:S(2)}) async-start(), calls=%async_computation.9 | async-start | bytes 8388608 | tf_op jit(solution)/shard_map/psum | solution.py:228
  11.0 25.4 %copy-start.38 = (f32[32]{0:T(128)}, f32[32]{0:T(128)S(1)}, u32[]{:S(2)}) copy-start(f32[32]{0:T(128)S(1)} %negate_power_fusion) | copy-start | bytes 388
  14.8 27.3 %copy-start.35 = (f32[1024]{0:T(1024)}, f32[1024]{0:T(1024)S(1)}, u32[]{:S(2)}) copy-start(f32[1024]{0:T(1024)S(1)} %add_rsqrt_fusion.1) | copy-start | bytes 12292
  21.0 21.1 %copy-start.31 = (f32[2048,1]{0,1:T(1,128)}, f32[2048,1]{0,1:T(1,128)S(1)}, u32[]{:S(2)}) copy-start(f32[2048,1]{0,1:T(1,128)S(1)} %get-tuple-element.585) | copy-start | bytes 24580
  31.7 4.0 copy-start.10
  36.4 9.3 copy-start.21
  36.4 9.3 copy-start.23
  83.9 3.2 copy-start.14
  83.9 9.2 copy-start.16
  83.9 9.1 copy-start.17
  88.3 4.8 copy-start.8
  93.1 4.9 copy-start.4
  93.1 216.1 %all-gather.9.cloned.1.call-start = ((), (), s32[]{:S(2)}) async-start(), calls=%async_computation.10 | async-start | bytes 10485760 | tf_op jit(solution)/shard_map/all_gather | solution.py:123
  98.0 247.7 %all-gather.11.cloned.1.call-start = ((), (), s32[]{:S(2)}) async-start(), calls=%async_computation.11 | async-start | bytes 5242880 | tf_op jit(solution)/shard_map/all_gather | solution.py:124
  99.2 427.4 %all-reduce.7.cloned.1.call-start = ((), (), s32[]{:S(2)}) async-start(), calls=%async_computation.12 | async-start | bytes 8388608 | tf_op jit(solution)/shard_map/psum | solution.py:264
  345.7 13.9 %copy-start.42 = (bf16[2048,2,1024]{2,0,1:T(8,128)(2,1)S(1)}, bf16[2048,2,1024]{2,0,1:T(8,128)(2,1)}, u32[]{:S(2)}) copy-start(bf16[2048,2,1024]{2,0,1:T(8,128)(2,1)} %all-gather.9.cloned.1.call-done) | copy-start | bytes 25165828
  370.1 235.5 %reduce-scatter.10.cloned.1.call-start = ((), (), s32[]{:S(2)}) async-start(), calls=%async_computation.13 | async-start | bytes 786432 | tf_op jit(solution)/shard_map/reduce_scatter | solution.py:322
  526.6 8.1 copy-start.1
  526.6 8.1 copy-start.2
  526.6 8.3 copy-start.3
  534.9 6.5 copy-start.12
  541.4 3.5 copy-start
  550.0 2.9 copy-start.29
  554.3 2.4 copy-start.30
  554.3 2.4 copy-start.27
  558.1 2.0 copy-start.28
  561.5 2.9 copy-start.29
  565.8 2.4 copy-start.30
  565.8 2.4 copy-start.27
  569.6 2.0 copy-start.28
  572.9 2.9 copy-start.29
  577.3 2.4 copy-start.30
  577.3 2.4 copy-start.27
  581.1 2.0 copy-start.28
  584.4 2.9 copy-start.29
  588.8 2.4 copy-start.30
  588.8 2.4 copy-start.27
  592.6 2.0 copy-start.28
  597.2 2.7 copy-start.22
  597.2 2.7 copy-start.24
  598.5 286.8 %all-reduce.9.cloned.1.call-start = ((), (), s32[]{:S(2)}) async-start(), calls=%async_computation.20 | async-start | bytes 16777216 | tf_op jit(solution)/shard_map/psum | solution.py:241
  598.6 8.9 copy-start.34
  598.6 8.9 copy-start.39
  599.3 8.8 copy-start.11
  612.9 5.5 copy-start.9
  612.9 302.7 %reduce-scatter.12.cloned.1.call-start = ((), (), s32[]{:S(2)}) async-start(), calls=%async_computation.14 | async-start | bytes 1310720 | tf_op jit(solution)/shard_map/reduce_scatter | solution.py:356
  618.3 321.4 %reduce-scatter.14.cloned.1.call-start = ((), (), s32[]{:S(2)}) async-start(), calls=%async_computation.15 | async-start | bytes 1310720 | tf_op jit(solution)/shard_map/reduce_scatter | solution.py:359
  625.1 339.0 %reduce-scatter.16.cloned.1.call-start = ((), (), s32[]{:S(2)}) async-start(), calls=%async_computation.16 | async-start | bytes 655360 | tf_op jit(solution)/shard_map/reduce_scatter | solution.py:362
  629.8 381.8 %reduce-scatter.20.cloned.1.call-start = ((), (), s32[]{:S(2)}) async-start(), calls=%async_computation.18 | async-start | bytes 5242880 | tf_op jit(solution)/shard_map/reduce_scatter | solution.py:368
  641.7 398.2 %reduce-scatter.22.cloned.1.call-start = ((), (), s32[]{:S(2)}) async-start(), calls=%async_computation.19 | async-start | bytes 655360
  885.3 7.1 copy-start.44
  892.2 217.9 %reduce-scatter.18.cloned.1.call-start = ((), (), s32[]{:S(2)}) async-start(), calls=%async_computation.17 | async-start | bytes 10485760 | tf_op jit(solution)/shard_map/reduce_scatter | solution.py:365
  910.7 3.0 copy-start.18
  910.7 4.9 copy-start.19
  913.8 25.9 %copy-start.20 = (f32[512,256]{1,0:T(8,128)S(1)}, f32[512,256]{1,0:T(8,128)}, u32[]{:S(2)}) copy-start(f32[512,256]{1,0:T(8,128)} %param.29) | copy-start | bytes 1572868
  915.6 48.5 %copy-start.26 = (f32[512,128]{1,0:T(8,128)S(1)}, f32[512,128]{1,0:T(8,128)}, u32[]{:S(2)}) copy-start(f32[512,128]{1,0:T(8,128)} %param.30) | copy-start | bytes 786436
  915.6 96.0 %copy-start.6 = (f32[512,1024]{0,1:T(8,128)S(1)}, f32[512,1024]{0,1:T(8,128)}, u32[]{:S(2)}) copy-start(f32[512,1024]{0,1:T(8,128)} %copy.152) | copy-start | bytes 6291460
  1017.9 6.0 copy-start.7
  1025.7 15.1 %copy-start.37 = (f32[512,2]{0,1:T(2,128)S(1)}, f32[512,2]{0,1:T(2,128)}, u32[]{:S(2)}) copy-start(f32[512,2]{0,1:T(2,128)} %param.33) | copy-start | bytes 12292
  1025.7 15.1 %copy-start.40 = (f32[512,2]{0,1:T(2,128)S(1)}, f32[512,2]{0,1:T(2,128)}, u32[]{:S(2)}) copy-start(f32[512,2]{0,1:T(2,128)} %param.39) | copy-start | bytes 12292
  1025.7 15.2 %copy-start.41 = (f32[512,2]{0,1:T(2,128)S(1)}, f32[512,2]{0,1:T(2,128)}, u32[]{:S(2)}) copy-start(f32[512,2]{0,1:T(2,128)} %param.45) | copy-start | bytes 12292
  (8 other events, 10.0 us)
Sparse Core Ops, SparseCore 0:
  10.2 22.2 all-gather.4
  34.6 16.6 all-gather.6
  93.2 156.5 all-reduce.4
  251.9 57.2 all-gather.8
  311.2 34.4 all-gather.10
  370.2 156.2 all-reduce.6
  598.6 6.9 reduce-scatter.9
  613.0 272.2 all-reduce.8
  888.5 23.8 reduce-scatter.11
  914.8 24.8 reduce-scatter.13
  942.4 21.6 reduce-scatter.15
  967.0 44.5 reduce-scatter.19
  1014.2 21.6 reduce-scatter.21
  1038.3 71.7 reduce-scatter.17
where the time goes:
time: 1150 us; the launch traced here: 1140 us
  waiting for transfers between devices  773 us (67%)
  matrix products  168 us (15%)
  other arithmetic  91.3 us (8%)
  local copies, waits for them, and re-layouts  66.7 us (6%)
  blocking collectives  19.2 us (2%)
  between operations  15 us (1%)
    psum x1, waiting for transfers between devices, body(): lax.psum(mlp_part.astype(jnp.bfloat16), 'tensor').astype(jnp.float32)  244 us
    psum x1, waiting for transfers between devices, body(): lax.psum(attn_part.astype(jnp.bfloat16), 'tensor').astype(jnp.float32)  150 us
    psum x1, waiting for transfers between devices, body(): lax.psum(two_part.astype(jnp.bfloat16), 'tensor').astype(jnp.float32)  141 us
    reduce_scatter x1, waiting for transfers between devices, body(): lax.psum_scatter(gate_up_grad.astype(jnp.bfloat16), ('dp', 'seq'), scatte...  68.6 us
    all_gather x1, waiting for transfers between devices, body(): lax.all_gather(gate_up_low, ('dp', 'seq'), axis=0, tiled=True)  54.4 us
    unnamed x99, local copies, waits for them, and re-layouts  45.5 us
    reduce_scatter x1, waiting for transfers between devices, body(): lax.psum_scatter(down_grad.astype(jnp.bfloat16), ('dp', 'seq'), scatter_d...  45.4 us
    sub x6, other arithmetic, adam_step(): weight - step_rate * (first_hat / (jnp.sqrt(second_hat) + ADAM_EPS) + dec...  24.9 us
  transfers between devices with their start and end apart: 14, of which 10 were waited for; matrix products, arithmetic and copies ran while one was open for 17% of the time, Pallas kernels for 0%

commit v1 on v0

v1 whole, which is shorter than its diff:
```python
import functools

import jax
import jax.numpy as jnp
from jax import lax
from jax.experimental import pallas as pl
from jax.experimental.pallas import tpu as pltpu
from jax.sharding import PartitionSpec as P

D = 2048
FF = 8192
HEADS = 32
KV_HEADS = 8
HEAD_DIM = 64
STEP = 10
FAN_OUT = 2

EPS_NORM = 1e-05
ROPE_BASE = 500000.0
BETA_ONE = 0.9
BETA_TWO = 0.95
ADAM_EPS = 1e-08
DECAY = 0.1
RATE_FACTOR = 3.0
GAIN_RATE = 1.0
MASKED = -1e30

F32 = jnp.float32
BF16 = jnp.bfloat16
GROUP = HEADS // KV_HEADS
QUARTER = D // 4
ORDER = (0, 2, 4, 6, 1, 3, 5, 7)
WIDTH_ORDER = (0, 2, 1, 3)
HIGH_GROUPS = [[0, 2, 4, 6], [1, 3, 5, 7]]
AT_TENSOR, AT_OFFSET, AT_SEQ, AT_LOW, AT_HIGH = 4, 5, 6, 7, 8


def vmem(mib):
    return pltpu.CompilerParams(vmem_limit_bytes=mib * 1024 * 1024)


COST_SCALE = 0.5


def cost(us):
    return pl.CostEstimate(flops=0, bytes_accessed=int(COST_SCALE * us * 3.69e6), transcendentals=0)


def dot(a, b):
    return lax.dot_general(a, b, (((1,), (0,)), ((), ())), preferred_element_type=F32)


def dot_nt(a, b):
    return lax.dot_general(a, b, (((1,), (1,)), ((), ())), preferred_element_type=F32)


def swap_halves(values):
    lane = lax.broadcasted_iota(jnp.int32, values.shape, 1)
    half = HEAD_DIM // 2
    return jnp.where(
        lane % HEAD_DIM < half,
        pltpu.roll(values, 128 - half, 1),
        pltpu.roll(values, half, 1),
    )


def width_block(info, place):
    return pl.ds(pl.multiple_of(info[place] * QUARTER, QUARTER), QUARTER)


def project_kernel(info, tok, w0, w1, w2, w3, cosine, sine, normed, q_out, kv_out, gains, gain_rows):
    pieces = (w0, w1, w2, w3)

    @pl.when(pl.program_id(0) == 0)
    def _():
        for place, piece in enumerate(pieces):
            turned = piece[:, 384:512].astype(F32).T
            gain_rows[:, place * QUARTER : (place + 1) * QUARTER] = turned[0:8]
        natural_store(info, gains, gain_rows[...])

    parts = [tok[:, width_block(info, place)].astype(F32) for place in range(4)]
    square = sum(jnp.sum(part * part, axis=1, keepdims=True) for part in parts)
    inverse = lax.rsqrt(square * (1.0 / D) + EPS_NORM)
    total = None
    for place, (part, piece) in enumerate(zip(parts, pieces)):
        cols = slice(place * QUARTER, (place + 1) * QUARTER)
        low = (part * inverse * gain_rows[0:1, cols]).astype(BF16)
        normed[:, cols] = low
        term = dot(low, piece[:, 0:384])
        total = term if total is None else total + term
    cos, sin = cosine[...], sine[...]
    for c in (0, 128):
        raw = total[:, c : c + 128]
        q_out[:, c : c + 128] = (raw * cos + swap_halves(raw) * sin).astype(BF16)
    raw = total[:, 256:384]
    turned = raw * cos + swap_halves(raw) * sin
    lane = lax.broadcasted_iota(jnp.int32, raw.shape, 1)
    kv_out[...] = jnp.where(lane < HEAD_DIM, turned, raw).astype(BF16)


def heads_wide(turned):
    return jnp.concatenate(
        [turned[h * HEAD_DIM : (h + 1) * HEAD_DIM] for h in range(GROUP)], axis=1
    )


def heads_tall(wide, rows):
    return jnp.concatenate([wide[:, h * rows : (h + 1) * rows] for h in range(GROUP)], axis=0)


def diagonal_mask(rows, keys, shift):
    key = lax.broadcasted_iota(jnp.int32, (keys, GROUP * rows), 0)
    query = lax.broadcasted_iota(jnp.int32, (keys, GROUP * rows), 1) % rows
    return key <= query + shift


def diagonal_block(rows, keys, step, info):
    start = info[AT_OFFSET] + step
    ratio = keys // rows
    diagonal = lax.div(start, jnp.int32(ratio))
    return diagonal, (start - diagonal * ratio) * rows


def attend_kernel(
    rows, keys, info, q, kv, out, log_out, piece0, piece1, piece2, piece3, kv_turned, acc, high
):
    step = pl.program_id(0)

    @pl.when(step == 0)
    def _():
        turned = kv[...].T
        row = lax.broadcasted_iota(jnp.int32, turned.shape, 0)
        kv_turned[...] = jnp.where(row < HEAD_DIM, jnp.ones_like(turned), turned)

    wide = heads_wide((q[...] * (HEAD_DIM**-0.5)).astype(F32).T).astype(BF16)
    wide = jnp.concatenate([wide, jnp.zeros_like(wide)], axis=0)
    diagonal, shift = diagonal_block(rows, keys, step, info)

    def scores_of(j):
        return dot(kv[pl.ds(pl.multiple_of(j * keys, keys), keys), :], wide)

    def values_of(j):
        return kv_turned[:, pl.ds(pl.multiple_of(j * keys, keys), keys)]

    scores = jnp.where(diagonal_mask(rows, keys, shift), scores_of(diagonal), MASKED)
    top = jnp.max(scores, axis=0, keepdims=True)
    high[...] = top
    acc[...] = dot(values_of(diagonal), jnp.exp(scores - top).astype(BF16))

    def body(j, carry):
        scores = scores_of(j)
        old = high[...]
        top = jnp.maximum(old, jnp.max(scores, axis=0, keepdims=True))
        high[...] = top
        chances = jnp.exp(scores - top).astype(BF16)
        acc[...] = acc[...] * jnp.exp(old - top) + dot(values_of(j), chances)
        return carry

    lax.fori_loop(0, diagonal, body, 0)
    total = acc[0:1, :]
    log_out[0] = high[...] + jnp.log(total)
    result = acc[HEAD_DIM:, :] * (1.0 / total)
    out[...] = heads_tall(result, rows).T.astype(BF16)
    for k, piece in enumerate((piece0, piece1, piece2, piece3)):

        @pl.when(lax.bitwise_xor(step, info[AT_HIGH]) == k)
        def _():
            piece[...] = out[...]


def attend_back_kernel(
    rows, keys, spans, info, q, grad0, grad1, grad2, grad3, att, log_in, kv, cosine, sine,
    dq_out, piece0, piece1, piece2, piece3, dkv_out, kv_turned, dkv, dq_acc, grad,
):
    step = pl.program_id(0)

    @pl.when(step == 0)
    def _():
        kv_turned[...] = kv[...].T[0:HEAD_DIM]
        dkv[...] = jnp.zeros_like(dkv)

    for k, piece in enumerate((grad0, grad1, grad2, grad3)):

        @pl.when(lax.bitwise_xor(step, info[AT_HIGH]) == k)
        def _():
            grad[...] = piece[...]

    scaled = q[...] * (HEAD_DIM**-0.5)
    grads = grad[...]
    zero_tall = jnp.zeros((GROUP * rows, HEAD_DIM), BF16)
    q_tall = jnp.concatenate(
        [scaled[:, h * HEAD_DIM : (h + 1) * HEAD_DIM] for h in range(GROUP)], axis=0
    ).astype(BF16)
    g_tall = jnp.concatenate(
        [grads[:, h * HEAD_DIM : (h + 1) * HEAD_DIM] for h in range(GROUP)], axis=0
    )
    q_tall = jnp.concatenate([q_tall, zero_tall], axis=1)
    g_tall = jnp.concatenate([zero_tall, g_tall], axis=1)
    q_wide = heads_wide(scaled.astype(F32).T).astype(BF16)
    g_turned = grads.astype(F32).T
    g_wide = heads_wide(g_turned).astype(BF16)
    zero_wide = jnp.zeros_like(g_wide)
    product = heads_wide(g_turned * att[...].astype(F32).T)
    delta = jnp.sum(product, axis=0, keepdims=True)
    q_wide = jnp.concatenate([q_wide, zero_wide], axis=0)
    g_wide = jnp.concatenate([zero_wide, g_wide], axis=0)
    logs = log_in[0]
    diagonal, shift = diagonal_block(rows, keys, step, info)

    def one_block(j, mask):
        place = pl.ds(pl.multiple_of(j * keys, keys), keys)
        block = kv[place, :]
        chances = jnp.exp(dot(block, q_wide) - logs)
        if mask is not None:
            chances = jnp.where(mask, chances, 0.0)
        chance_grad = dot(block, g_wide)
        score_grad = (chances * (chance_grad - delta)).astype(BF16)
        dkv[place, :] += dot(score_grad, q_tall) + dot(chances.astype(BF16), g_tall)
        return dot(kv_turned[:, place], score_grad)

    dq_acc[...] = one_block(diagonal, diagonal_mask(rows, keys, shift))

    def body(j, carry):
        dq_acc[...] += one_block(j, None)
        return carry

    lax.fori_loop(0, diagonal, body, 0)
    dq = heads_tall(dq_acc[...] * (HEAD_DIM**-0.5), rows).T
    cos, sin = cosine[...], sine[...]
    for c in (0, 128):
        raw = dq[:, c : c + 128]
        dq_out[:, c : c + 128] = (raw * cos - swap_halves(raw) * sin).astype(BF16)
    for k, piece in enumerate((piece0, piece1, piece2, piece3)):

        @pl.when(lax.bitwise_xor(step, info[AT_HIGH]) == k)
        def _():
            piece[...] = dq_out[...]

    @pl.when(step == pl.num_programs(0) - 1)
    def _():
        span = dkv_out.shape[1]
        for r in range(spans):
            at = lax.bitwise_xor(info[AT_SEQ], jnp.int32(r)) * span
            dkv_out[r] = dkv[pl.ds(pl.multiple_of(at, span), span), :].astype(BF16)


def out_kernel(info, a0, a1, a2, a3, w0, w1, w2, w3, keep, send, total):
    half = keep.shape[0]
    low = info[AT_LOW]
    for place, w in enumerate((w0, w1, w2, w3)):
        cols = width_block(info, place)
        total[...] = sum(
            dot_nt(a[...], w[lax.bitwise_xor(info[AT_HIGH], jnp.int32(k))])
            for k, a in enumerate((a0, a1, a2, a3))
        )
        keep[:, cols] = total[pl.ds(pl.multiple_of(low * half, half), half), :]
        send[:, cols] = total[pl.ds(pl.multiple_of((1 - low) * half, half), half), :].astype(BF16)


def norm_kernel(info, keep, got, tok, gains, resid_out, low_a, low_b):
    resid = tok[...].astype(F32) + keep[...] + got[...].astype(F32)
    resid_out[...] = resid
    inverse = lax.rsqrt(jnp.mean(resid * resid, axis=1, keepdims=True) + EPS_NORM)
    low = (resid * inverse * gains[1:2, :]).astype(BF16)
    half = low.shape[0] // 2
    low_a[...] = low[:half]
    low_b[...] = low[half:]


def mlp_kernel(
    info, near, far, dy, gate_up_all, down_all, *rest,
):
    mlp_keep, mlp_send, two_keep, two_send, hidden_out, grad_out, x, gate_up, down, sems = rest[-10:]
    step = pl.program_id(0)
    wide = FF // 8
    n = x.shape[0]

    def copies(group):
        cols = pl.ds(group * 256, 256)
        up_cols = pl.ds(wide + group * 256, 256)
        for k, (src, dst, c) in enumerate(
            ((gate_up_all, gate_up, cols), (gate_up_all, gate_up, up_cols), (down_all, down, cols))
        ):
            yield pltpu.make_async_copy(src.at[:, c], dst.at[:, c], sems.at[group, k])

    @pl.when(step == 0)
    def _():
        for group in range(4):
            for copy in copies(group):
                copy.start()
        x[: n // 2] = near[...]
        x[n // 2 :] = far[...]

    for group in range(4):

        @pl.when(step == group)
        def _():
            for copy in copies(group):
                copy.wait()
            cols = slice(group * 256, (group + 1) * 256)
            up_cols = slice(wide + group * 256, wide + (group + 1) * 256)
            gate = dot(x[...], gate_up[:, cols])
            up = dot(x[...], gate_up[:, up_cols])
            hidden_grad = dot(dy[0], down[:, cols])
            sigmoid = 1.0 / (1.0 + jnp.exp(-gate))
            silu = gate * sigmoid
            hidden_out[:, cols] = (silu * up).astype(BF16)
            grad_out[:, cols] = (
                hidden_grad * up * (sigmoid * (1.0 + gate * (1.0 - sigmoid)))
            ).astype(BF16)
            grad_out[:, up_cols] = (hidden_grad * silu).astype(BF16)

    @pl.when(step >= 4)
    def _():
        rows = pl.ds(pl.multiple_of((step - 4) * QUARTER, QUARTER), QUARTER)
        two = dot_nt(grad_out[...], gate_up[rows, :]).astype(BF16)
        two_keep[...] = two[: n // 2]
        two_send[...] = two[n // 2 :]
        mlp = dot_nt(hidden_out[...], down[rows, :]).astype(BF16)
        size = n // 8
        for i in range(4):
            owner = lax.bitwise_xor(info[AT_HIGH], jnp.int32(i))
            mlp_keep[owner] = mlp[i * size : (i + 1) * size]
            mlp_send[owner] = mlp[n // 2 + i * size : n // 2 + (i + 1) * size]


def norm_back(values, incoming, gain):
    inverse = lax.rsqrt(jnp.mean(values * values, axis=1, keepdims=True) + EPS_NORM)
    scaled = incoming * gain
    gain_grad = jnp.sum(incoming * values * inverse, axis=0, keepdims=True)
    inner = jnp.mean(scaled * values, axis=1, keepdims=True)
    return inverse * scaled - values * (inverse * inverse * inverse * inner), gain_grad


def summed(parts):
    return sum(part[...].astype(F32) for part in parts)


def norm_back_kernel(info, *refs):
    parts_a, parts_b = refs[0:4], refs[4:8]
    resid, dy, gains, resid_grad, resid_low, gain_grad = refs[8:]
    half = dy.shape[1]
    sums = []
    for i, parts in enumerate((parts_a, parts_b)):
        rows = slice(i * half, (i + 1) * half)
        back, gain_part = norm_back(resid[rows], summed(parts), gains[1:2, :])
        full = dy[i].astype(F32) + back
        resid_grad[rows] = full
        resid_low[rows] = full.astype(BF16)
        sums.append(gain_part)
    gain_grad[...] = sums[0] + sums[1]


def out_back_kernel(info, own, other, w0, w1, w2, w3, both, g0, g1, g2, g3):
    half = own.shape[0]
    low = info[AT_LOW]
    for place in range(4):
        cols = slice(place * QUARTER, (place + 1) * QUARTER)
        natural = width_block(info, place)
        both[pl.ds(pl.multiple_of(low * half, half), half), cols] = own[:, natural]
        both[pl.ds(pl.multiple_of((1 - low) * half, half), half), cols] = other[:, natural]
    for k, out in enumerate((g0, g1, g2, g3)):
        high = lax.bitwise_xor(info[AT_HIGH], jnp.int32(k))
        out[...] = sum(
            dot(both[:, place * QUARTER : (place + 1) * QUARTER], w[high])
            for place, w in enumerate((w0, w1, w2, w3))
        ).astype(BF16)


def natural_store(info, out, value):
    for place in range(4):
        out[:, width_block(info, place)] = value[:, place * QUARTER : (place + 1) * QUARTER]


def kv_back_kernel(info, dkv, dkv_more, cosine, sine, out, p0, p1, p2, p3):
    raw = dkv[...].astype(F32) + dkv_more[...].astype(F32)
    turned = raw * cosine[...] - swap_halves(raw) * sine[...]
    lane = lax.broadcasted_iota(jnp.int32, raw.shape, 1)
    out[...] = jnp.where(lane < HEAD_DIM, turned, raw).astype(BF16)
    rows = p0.shape[0]
    for k, piece in enumerate((p0, p1, p2, p3)):
        at = lax.bitwise_xor(info[AT_HIGH], jnp.int32(k)) * rows
        piece[...] = out[pl.ds(pl.multiple_of(at, rows), rows), :]


def one_kernel(info, q0, q1, q2, q3, k0, k1, k2, k3, w, keep, send, total):
    half = keep.shape[0]
    low = info[AT_LOW]
    both = [
        jnp.concatenate([q[...], k[...]], axis=1)
        for q, k in zip((q0, q1, q2, q3), (k0, k1, k2, k3))
    ]
    for place in range(4):
        cols = width_block(info, place)
        total[...] = sum(
            dot_nt(part, w[k, info[place]])
            for k, part in enumerate(both)
        )
        keep[:, cols] = total[pl.ds(pl.multiple_of(low * half, half), half), :]
        send[:, cols] = total[pl.ds(pl.multiple_of((1 - low) * half, half), half), :].astype(BF16)


def tokens_back_kernel(info, keep, got, tok, resid_grad, gains, low):
    back, unused = norm_back(
        tok[...].astype(F32), keep[...] + got[...].astype(F32), gains[0:1, :]
    )
    low[...] = (resid_grad[...] + back).astype(BF16)


def block_out_kernel(parts_a, parts_b, resid, low):
    half = parts_a.shape[1]
    for i, parts in enumerate((parts_a, parts_b)):
        rows = slice(i * half, (i + 1) * half)
        low[rows] = (sum(parts[k].astype(F32) for k in range(4)) + resid[rows]).astype(BF16)


def reorder_kernel(info, src, out):
    half = out.shape[1]
    out[0] = src[:half]
    out[1] = src[half:]


def place_kernel(info, near, far, out):
    size = near.shape[1]
    at = info[AT_LOW] * size
    out[pl.ds(pl.multiple_of(at, size), size), :] = near[0].astype(out.dtype)
    out[pl.ds(pl.multiple_of(size - at, size), size), :] = far[0].astype(out.dtype)


def weight_grad_kernel(a, b, *outs):
    result = lax.dot_general(
        a[...], b[...], (((0,), (0,)), ((), ())), preferred_element_type=F32
    ).astype(BF16)
    if len(outs) == 1:
        outs[0][...] = result
        return

    @pl.when(pl.program_id(0) < 2)
    def _():
        outs[0][...] = result

    @pl.when(pl.program_id(0) >= 2)
    def _():
        outs[1][...] = result


def pair_sum_kernel(a, b, out):
    out[...] = (a[...].astype(F32) + b[...].astype(F32)).astype(BF16)


def adam_kernel(rate, decay, weight, one, two, *refs):
    outs = refs[-3:]
    if len(weight.shape) == 2:
        grad = summed(refs[:-3])
        results = adam_step(weight[...], grad, one[...], two[...], rate, decay)
        for out, result in zip(outs, results):
            out[...] = result
        return
    wide = weight.shape[2]
    for k in range(2):
        cols = slice(k * wide, (k + 1) * wide)
        grad = sum(ref[:, cols].astype(F32) for ref in refs[:-3])
        results = adam_step(weight[:, k, :], grad, one[:, k, :], two[:, k, :], rate, decay)
        for out, result in zip(outs, results):
            out[:, k, :] = result


def step_owner(step):
    return lax.rem(step, 4) * 2 + lax.div(step, 4)


def tensor_block(step, info):
    return lax.bitwise_xor(info[AT_TENSOR], step_owner(step))


def adam_step(weight, grad_sum, moment_one, moment_two, step_rate, decay_rate):
    first_new = BETA_ONE * moment_one + (1.0 - BETA_ONE) * grad_sum
    second_new = BETA_TWO * moment_two + (1.0 - BETA_TWO) * grad_sum * grad_sum
    first_hat = first_new / (1.0 - BETA_ONE**STEP)
    second_hat = second_new / (1.0 - BETA_TWO**STEP)
    updated = weight - step_rate * (
        first_hat / (jnp.sqrt(second_hat) + ADAM_EPS) + decay_rate * weight
    )
    return (updated, first_new, second_new)


def rope_tables(positions):
    half_dim = HEAD_DIM // 2
    exponent = jnp.arange(half_dim, dtype=F32) * (2.0 / HEAD_DIM)
    inverse = jnp.power(F32(ROPE_BASE), -exponent)
    angles = positions.astype(F32)[:, None] * inverse[None, :]
    cosine, sine = jnp.cos(angles), jnp.sin(angles)
    return (
        jnp.concatenate([cosine] * 4, axis=1),
        jnp.concatenate([-sine, sine, -sine, sine], axis=1),
    )


def whole(shape, dims=None):
    zeros = (0,) * len(shape)
    return pl.BlockSpec(shape, lambda *unused: zeros)


def body(
    tokens, cotangent, query_weight, output_weight, kv_weight, gate_up_weight, down_weight, norm_gains,
    query_first, output_first, kv_first, gate_up_first, down_first, gains_first,
    query_second, output_second, kv_second, gate_up_second, down_second, gains_second,
    *, dp_size, seq_size,
):
    fast = dp_size == 2 and seq_size == 2
    span = tokens.shape[1]
    length = span * seq_size
    rows = span // 4
    keys = max(rows, 128)
    block = span // 8
    half_block = block // 2
    tensor_id = lax.axis_index("tensor").astype(jnp.int32)
    seq_id = lax.axis_index("seq").astype(jnp.int32)
    dp_id = lax.axis_index("dp").astype(jnp.int32)
    own_width = dp_id * 2 + seq_id if fast else jnp.int32(0)
    order = WIDTH_ORDER if fast else (0, 1, 2, 3)
    info = jnp.stack(
        [lax.bitwise_xor(own_width, jnp.int32(o)) for o in order]
        + [tensor_id, seq_id * 4, seq_id if fast else jnp.int32(0), tensor_id % 2, tensor_id // 2]
    )

    def after(value, point):
        return lax.optimization_barrier((value, point))[0]

    def swap_tensor(value, mask):
        return lax.ppermute(value, "tensor", [(i, i ^ mask) for i in range(8)])

    def swap_dp(value):
        return lax.ppermute(value, "dp", [(0, 1), (1, 0)])

    def swap_seq(value):
        return lax.ppermute(value, "seq", [(0, 1), (1, 0)])

    def gather_width(shard, point=None, last=None):
        if fast:
            other = swap_dp(shard)
            own = shard
            if last is not None:
                own, other = after(own, point), after(other, last)
            return [shard, other, swap_seq(own), swap_seq(other)]
        axis = shard.ndim - 2
        full = lax.all_gather(shard, ("dp", "seq"), axis=axis, tiled=True)
        return [lax.slice_in_dim(full, i * QUARTER, (i + 1) * QUARTER, axis=axis) for i in range(4)]

    def gather_all(shard):
        return lax.all_gather(shard, ("dp", "seq"), axis=0, tiled=True)

    def scatter_all(full):
        return lax.psum_scatter(full, ("dp", "seq"), scatter_dimension=0, tiled=True)

    def weight_full(a, b, halves=False):
        n, width = b.shape
        if halves:
            specs = [
                pl.BlockSpec((QUARTER, width), lambda i: (jnp.minimum(i, 1), 0)),
                pl.BlockSpec((QUARTER, width), lambda i: (jnp.maximum(i - 2, 0), 0)),
            ]
        else:
            specs = [pl.BlockSpec((QUARTER, width), lambda i: (i, 0))]
        outs = pl.pallas_call(
            weight_grad_kernel,
            grid=(4,),
            in_specs=[pl.BlockSpec((n, QUARTER), lambda i: (0, i)), whole((n, width))],
            out_specs=specs,
            out_shape=[jax.ShapeDtypeStruct((D // len(specs), width), BF16)] * len(specs),
            compiler_params=vmem(56),
            cost_estimate=cost(n * width / 160000),
            name="weight_grad",
        )(a, b)
        return tuple(outs) if halves else outs[0]

    def weight_halves(a, b):
        return weight_full(a, b, True)

    def pair_sum(a, b, place):
        part = pl.BlockSpec((QUARTER, a.shape[1]), lambda i: (place, 0))
        return pl.pallas_call(
            pair_sum_kernel,
            grid=(1,),
            in_specs=[part, part],
            out_specs=whole((QUARTER, a.shape[1])),
            out_shape=jax.ShapeDtypeStruct((QUARTER, a.shape[1]), BF16),
            compiler_params=vmem(48),
            cost_estimate=cost(1.5),
            name="pair_sum",
        )(a, b)

    def scatter_near(halves, point):
        keep, send = halves
        if not fast:
            return keep, send, None
        got = after(swap_seq(send), point)
        return keep, got, pair_sum(keep, got, 1)

    def send_far(near):
        return swap_dp(near[2]) if fast else None

    def scatter_far(near, far):
        keep, got, low = near
        if fast:
            return [keep, got, far]
        full = jnp.concatenate([keep, got], axis=0)
        return [lax.psum_scatter(full, ("dp", "seq"), scatter_dimension=0, tiled=True)]

    def swap_high(pieces):
        return [pieces[0]] + [swap_tensor(pieces[k], 2 * k) for k in (1, 2, 3)]

    def scatter_parts(total):
        n = total.shape[0] // 4
        return [total[:n]] + [
            swap_tensor(total[i * n : (i + 1) * n].astype(BF16), mask)
            for i, mask in ((1, 2), (2, 4), (3, 6))
        ]

    def gather_near(own):
        return jnp.concatenate([own] + [swap_tensor(own, mask) for mask in (2, 4, 6)], axis=0)

    attn_low = jnp.concatenate(
        [query_weight, kv_weight, jnp.pad(norm_gains, ((0, 0), (0, 126)))], axis=1
    ).astype(BF16)
    back_low = jnp.concatenate([query_weight, kv_weight], axis=1).astype(BF16)
    output_low = after(output_weight.astype(BF16), attn_low)
    output_near = lax.all_gather(output_low, "tensor", axis=0, axis_index_groups=HIGH_GROUPS)
    token_rows = tokens.reshape(span, D)
    cot_rows = cotangent.reshape(span, D)
    positions = seq_id * span + jnp.arange(span, dtype=jnp.int32)
    cosine, sine = rope_tables(positions)
    attn_w = gather_width(attn_low, attn_low, (cosine, sine))
    back_parts = [swap_tensor(after(back_low, attn_w[1]), mask) for mask in (2, 4, 6)]
    gate_up_late, down_late = after((gate_up_weight, down_weight), attn_w[1])
    gate_up_low = jnp.concatenate(
        [gate_up_late[:, 0, :], gate_up_late[:, 1, :]], axis=1
    ).astype(BF16)
    down_low = down_late.astype(BF16)

    half_span = span // 2
    dy = pl.pallas_call(
        reorder_kernel,
        grid_spec=pltpu.PrefetchScalarGridSpec(
            num_scalar_prefetch=1,
            grid=(8,),
            in_specs=[pl.BlockSpec((block, D), lambda i, info: (tensor_block(i, info), 0))],
            out_specs=pl.BlockSpec((2, half_block, D), lambda i, info: (0, i, 0)),
        ),
        out_shape=jax.ShapeDtypeStruct((2, half_span, D), BF16),
        cost_estimate=cost(7.5),
        name="reorder",
    )(info, cot_rows)

    normed_one, queries, kv_own, gains = pl.pallas_call(
        project_kernel,
        grid_spec=pltpu.PrefetchScalarGridSpec(
            num_scalar_prefetch=1,
            grid=(span // rows,),
            in_specs=[pl.BlockSpec((rows, D), lambda i, info: (i, 0))]
            + [whole((QUARTER, 512))] * 4
            + [pl.BlockSpec((rows, 128), lambda i, info: (i, 0))] * 2,
            out_specs=[
                pl.BlockSpec((rows, D), lambda i, info: (i, 0)),
                pl.BlockSpec((rows, 256), lambda i, info: (i, 0)),
                pl.BlockSpec((rows, 128), lambda i, info: (i, 0)),
                whole((8, D)),
            ],
            scratch_shapes=[pltpu.VMEM((8, D), F32)],
        ),
        out_shape=[
            jax.ShapeDtypeStruct((span, D), BF16),
            jax.ShapeDtypeStruct((span, 256), BF16),
            jax.ShapeDtypeStruct((span, 128), BF16),
            jax.ShapeDtypeStruct((8, D), F32),
        ],
        compiler_params=vmem(48),
        cost_estimate=cost(7),
        name="project",
    )(info, token_rows, *attn_w, cosine, sine)

    if fast:
        kv_other = swap_seq(kv_own)
        kv_all = jnp.where(
            seq_id == 0,
            jnp.concatenate([kv_own, kv_other], axis=0),
            jnp.concatenate([kv_other, kv_own], axis=0),
        )
    else:
        kv_all = lax.all_gather(kv_own, "seq", axis=0, tiled=True)

    steps = 4
    attended, logs, *att_pieces = pl.pallas_call(
        functools.partial(attend_kernel, rows, keys),
        grid_spec=pltpu.PrefetchScalarGridSpec(
            num_scalar_prefetch=1,
            grid=(steps,),
            in_specs=[
                pl.BlockSpec((rows, 256), lambda i, info: (i, 0)),
                whole((length, 128)),
            ],
            out_specs=[
                pl.BlockSpec((rows, 256), lambda i, info: (i, 0)),
                pl.BlockSpec((1, 1, GROUP * rows), lambda i, info: (i, 0, 0)),
            ]
            + [whole((rows, 256))] * 4,
            scratch_shapes=[
                pltpu.VMEM((128, length), BF16),
                pltpu.VMEM((128, GROUP * rows), F32),
                pltpu.VMEM((1, GROUP * rows), F32),
            ],
        ),
        out_shape=[
            jax.ShapeDtypeStruct((span, 256), BF16),
            jax.ShapeDtypeStruct((steps, 1, GROUP * rows), F32),
        ]
        + [jax.ShapeDtypeStruct((rows, 256), BF16)] * 4,
        compiler_params=vmem(48),
        cost_estimate=cost(18),
        name="attend",
    )(info, queries, kv_all)

    gate_up_w = gather_all(gate_up_low)
    down_w = gather_all(down_low)
    output_w = gather_width(after(output_near, queries), attended, attended)

    back_near = jnp.stack(after([back_low] + back_parts, output_w[1]), axis=0)
    back_w = lax.all_gather(back_near, ("dp", "seq"), axis=1, tiled=True)
    back_w = back_w.reshape(4, 4, QUARTER, 384)

    att_parts = after(swap_high(att_pieces), dy)
    out_keep, out_send = pl.pallas_call(
        out_kernel,
        grid_spec=pltpu.PrefetchScalarGridSpec(
            num_scalar_prefetch=1,
            grid=(1,),
            in_specs=[whole((rows, 256))] * 4 + [whole((4, QUARTER, 256))] * 4,
            out_specs=[whole((block, D))] * 2,
            scratch_shapes=[pltpu.VMEM((rows, QUARTER), F32)],
        ),
        out_shape=[jax.ShapeDtypeStruct((block, D), F32), jax.ShapeDtypeStruct((block, D), BF16)],
        compiler_params=vmem(48),
        cost_estimate=cost(3.8),
        name="attention_out",
    )(info, *att_parts, *output_w)
    out_got = swap_tensor(out_send, 1)
    own_rows = pl.BlockSpec((block, D), lambda i, info: (info[AT_TENSOR], 0))
    resid_one, low_a, low_b = pl.pallas_call(
        norm_kernel,
        grid_spec=pltpu.PrefetchScalarGridSpec(
            num_scalar_prefetch=1,
            grid=(1,),
            in_specs=[whole((block, D))] * 2 + [own_rows, whole((8, D))],
            out_specs=[whole((block, D)), whole((half_block, D)), whole((half_block, D))],
        ),
        out_shape=[
            jax.ShapeDtypeStruct((block, D), F32),
            jax.ShapeDtypeStruct((half_block, D), BF16),
            jax.ShapeDtypeStruct((half_block, D), BF16),
        ],
        cost_estimate=cost(3.5),
        name="second_norm",
    )(info, out_keep, out_got, token_rows, gains)

    def mlp(chunk, near, far, before):
        n = half_span
        anywhere = pl.BlockSpec(memory_space=pl.ANY)
        late_columns = pl.BlockSpec(
            (4, half_block, QUARTER), lambda i, info: (0, 0, jnp.maximum(i - 4, 0))
        )
        late_half = pl.BlockSpec((n // 2, QUARTER), lambda i, info: (0, jnp.maximum(i - 4, 0)))
        return pl.pallas_call(
            mlp_kernel,
            grid_spec=pltpu.PrefetchScalarGridSpec(
                num_scalar_prefetch=1,
                grid=(8,),
                in_specs=[whole((n // 2, D))] * 2
                + [pl.BlockSpec((1, n, D), lambda i, info: (chunk, 0, 0))]
                + [anywhere] * (2 + len(before)),
                out_specs=[
                    late_columns,
                    late_columns,
                    late_half,
                    late_half,
                    pl.BlockSpec((n, 1024), lambda i, info: (chunk, 0)),
                    pl.BlockSpec((n, 2048), lambda i, info: (chunk, 0)),
                    pl.BlockSpec((n, D), lambda i, info: (chunk, 0)),
                ],
                scratch_shapes=[
                    pltpu.VMEM((D, 2048), BF16),
                    pltpu.VMEM((D, 1024), BF16),
                    pltpu.SemaphoreType.DMA((4, 3)),
                ],
            ),
            out_shape=[
                jax.ShapeDtypeStruct((4, half_block, D), BF16),
                jax.ShapeDtypeStruct((4, half_block, D), BF16),
                jax.ShapeDtypeStruct((n // 2, D), BF16),
                jax.ShapeDtypeStruct((n // 2, D), BF16),
                jax.ShapeDtypeStruct((span, 1024), BF16),
                jax.ShapeDtypeStruct((span, 2048), BF16),
                jax.ShapeDtypeStruct((span, D), BF16),
            ],
            input_output_aliases={6: 4, 7: 5, 8: 6} if before else {},
            compiler_params=vmem(56),
            cost_estimate=cost(22.5),
            name="mlp",
        )(info, near, far, dy, gate_up_w, down_w, *before)

    near_a = gather_near(low_a)
    near_b = gather_near(low_b)
    far_a = after(swap_tensor(near_a, 1), near_b)
    far_b = swap_tensor(near_b, 1)
    mlp_keep_a, mlp_send_a, two_keep_a, two_send_a, hidden, gate_up_back, x = mlp(
        0, near_a, far_a, ()
    )
    two_got_a = swap_tensor(two_send_a, 1)
    mlp_keep_b, mlp_send_b, two_keep_b, two_send_b, hidden, gate_up_back, x = mlp(
        1, near_b, far_b, (hidden, gate_up_back, x)
    )
    two_got_b = swap_tensor(two_send_b, 1)
    total_a = two_keep_a.astype(F32) + after(two_got_a, two_send_b).astype(F32)
    two_a = scatter_parts(total_a)
    hidden, gate_up_back = after((hidden, gate_up_back), total_a)
    down_full = weight_full(dy.reshape(span, D), hidden)
    gate_up_full = weight_full(x, gate_up_back)
    total_b = two_keep_b.astype(F32) + after(
        two_got_b, (down_full, gate_up_full, two_a)
    ).astype(F32)
    two_b = scatter_parts(total_b)
    down_grad, gate_up_grad = (scatter_all(full) for full in after((down_full, gate_up_full), total_b))
    mlp_got_a = swap_tensor(after(mlp_send_a, total_b), 1)

    resid_grad, resid_low, gain_two_grad = pl.pallas_call(
        norm_back_kernel,
        grid_spec=pltpu.PrefetchScalarGridSpec(
            num_scalar_prefetch=1,
            grid=(1,),
            in_specs=[whole((half_block, D))] * 8
            + [
                whole((block, D)),
                pl.BlockSpec((2, half_block, D), lambda i, info: (0, 0, 0)),
                whole((8, D)),
            ],
            out_specs=[whole((block, D)), whole((block, D)), whole((1, D))],
        ),
        out_shape=[
            jax.ShapeDtypeStruct((block, D), F32),
            jax.ShapeDtypeStruct((block, D), BF16),
            jax.ShapeDtypeStruct((1, D), F32),
        ],
        cost_estimate=cost(4.7),
        name="second_norm_back",
    )(info, *two_a, *two_b, resid_one, dy, gains)
    resid_other = swap_tensor(resid_low, 1)
    mlp_total_a = (mlp_keep_a.astype(F32) + after(mlp_got_a, resid_low).astype(F32)).astype(BF16)
    mlp_parts_a = lax.all_to_all(mlp_total_a, "tensor", 0, 0, axis_index_groups=HIGH_GROUPS)
    resid_other = after(resid_other, mlp_total_a)
    mlp_got_b = swap_tensor(after(mlp_send_b, resid_other), 1)
    resid_both, *grad_pieces = pl.pallas_call(
        out_back_kernel,
        grid_spec=pltpu.PrefetchScalarGridSpec(
            num_scalar_prefetch=1,
            grid=(1,),
            in_specs=[whole((block, D))] * 2 + [whole((4, QUARTER, 256))] * 4,
            out_specs=[whole((rows, D))] + [whole((rows, 256))] * 4,
        ),
        out_shape=[jax.ShapeDtypeStruct((rows, D), BF16)]
        + [jax.ShapeDtypeStruct((rows, 256), BF16)] * 4,
        compiler_params=vmem(48),
        cost_estimate=cost(3.9),
        name="attention_out_back",
    )(info, resid_low, resid_other, *output_w)
    grad_parts = swap_high(grad_pieces)
    mlp_total_b = (mlp_keep_b.astype(F32) + after(mlp_got_b, grad_parts).astype(F32)).astype(BF16)
    mlp_parts_b = lax.all_to_all(mlp_total_b, "tensor", 0, 0, axis_index_groups=HIGH_GROUPS)
    grad_parts = after(grad_parts, (mlp_total_b, down_grad, back_w))

    spans = seq_size if fast else length // span
    dq, *dq_pieces, dkv = pl.pallas_call(
        functools.partial(attend_back_kernel, rows, keys, spans),
        grid_spec=pltpu.PrefetchScalarGridSpec(
            num_scalar_prefetch=1,
            grid=(steps,),
            in_specs=[pl.BlockSpec((rows, 256), lambda i, info: (i, 0))]
            + [whole((rows, 256))] * 4
            + [
                pl.BlockSpec((rows, 256), lambda i, info: (i, 0)),
                pl.BlockSpec((1, 1, GROUP * rows), lambda i, info: (i, 0, 0)),
                whole((length, 128)),
                pl.BlockSpec((rows, 128), lambda i, info: (i, 0)),
                pl.BlockSpec((rows, 128), lambda i, info: (i, 0)),
            ],
            out_specs=[pl.BlockSpec((rows, 256), lambda i, info: (i, 0))]
            + [whole((rows, 256))] * 4
            + [whole((spans, span, 128))],
            scratch_shapes=[
                pltpu.VMEM((HEAD_DIM, length), BF16),
                pltpu.VMEM((length, 128), F32),
                pltpu.VMEM((HEAD_DIM, GROUP * rows), F32),
                pltpu.VMEM((rows, 256), BF16),
            ],
        ),
        out_shape=[jax.ShapeDtypeStruct((span, 256), BF16)]
        + [jax.ShapeDtypeStruct((rows, 256), BF16)] * 4
        + [jax.ShapeDtypeStruct((spans, span, 128), BF16)],
        compiler_params=vmem(48),
        cost_estimate=cost(23),
        name="attend_back",
    )(info, queries, *grad_parts, attended, logs, kv_all, cosine, sine)

    if fast:
        dkv_own, dkv_more = dkv[0], swap_seq(dkv[1])
    else:
        dkv_own = lax.psum_scatter(dkv.reshape(length, 128), "seq", scatter_dimension=0, tiled=True)
        dkv_more = jnp.zeros_like(dkv_own)
    dq_parts = swap_high(dq_pieces)
    dkv_more = after(dkv_more, dq_parts)
    dkv_low, *dkv_pieces = pl.pallas_call(
        kv_back_kernel,
        grid_spec=pltpu.PrefetchScalarGridSpec(
            num_scalar_prefetch=1,
            grid=(1,),
            in_specs=[whole((span, 128))] * 4,
            out_specs=[whole((span, 128))] + [whole((rows, 128))] * 4,
        ),
        out_shape=[jax.ShapeDtypeStruct((span, 128), BF16)]
        + [jax.ShapeDtypeStruct((rows, 128), BF16)] * 4,
        cost_estimate=cost(3.2),
        name="kv_back",
    )(info, dkv_own, dkv_more, cosine, sine)

    dkv_parts = swap_high(dkv_pieces)
    block_low = pl.pallas_call(
        block_out_kernel,
        out_shape=jax.ShapeDtypeStruct((block, D), BF16),
        cost_estimate=cost(3),
        name="block_out",
    )(*after((mlp_parts_a, mlp_parts_b), dkv_low), resid_one)
    dkv_parts = after(dkv_parts, (gate_up_grad, block_low))
    one_keep, one_send = pl.pallas_call(
        one_kernel,
        grid_spec=pltpu.PrefetchScalarGridSpec(
            num_scalar_prefetch=1,
            grid=(1,),
            in_specs=[whole((rows, 256))] * 4
            + [whole((rows, 128))] * 4
            + [whole((4, 4, QUARTER, 384))],
            out_specs=[whole((block, D))] * 2,
            scratch_shapes=[pltpu.VMEM((rows, QUARTER), F32)],
        ),
        out_shape=[jax.ShapeDtypeStruct((block, D), F32), jax.ShapeDtypeStruct((block, D), BF16)],
        compiler_params=vmem(48),
        cost_estimate=cost(5.8),
        name="attention_in_back",
    )(info, *dq_parts, *dkv_parts, back_w)
    one_got = swap_tensor(one_send, 1)
    dqkv = after(jnp.concatenate([dq, dkv_low], axis=1), one_send)
    attn_halves = weight_halves(normed_one, dqkv)
    out_halves = weight_halves(
        after(resid_both, one_send), jnp.concatenate(att_parts, axis=1)
    )

    block_near = lax.all_gather(block_low, "tensor", axis=0, axis_index_groups=HIGH_GROUPS)
    one_got = after(one_got, (attn_halves, out_halves))
    out_near = scatter_near(out_halves, one_got)
    out_far = send_far(out_near)

    tokens_low = pl.pallas_call(
        tokens_back_kernel,
        grid_spec=pltpu.PrefetchScalarGridSpec(
            num_scalar_prefetch=1,
            grid=(1,),
            in_specs=[whole((block, D))] * 2 + [own_rows, whole((block, D)), whole((8, D))],
            out_specs=whole((block, D)),
        ),
        out_shape=jax.ShapeDtypeStruct((block, D), BF16),
        cost_estimate=cost(4.3),
        name="first_norm_back",
    )(info, one_keep, one_got, token_rows, resid_grad, gains)
    tokens_near = lax.all_gather(tokens_low, "tensor", axis=0, axis_index_groups=HIGH_GROUPS)

    attn_near = scatter_near(attn_halves, one_send)
    attn_far = send_far(attn_near)

    def adam(weight, one, two, terms, rate, decay):
        size = weight.shape[0] // 4
        if weight.ndim == 3:
            mine = pl.BlockSpec((size, 2, weight.shape[2]), lambda i: (i, 0, 0))
            wide = 2 * weight.shape[2]
        else:
            mine = pl.BlockSpec((size, weight.shape[1]), lambda i: (i, 0))
            wide = weight.shape[1]
        return pl.pallas_call(
            functools.partial(adam_kernel, rate, decay),
            grid=(4,),
            in_specs=[mine] * 3
            + [
                pl.BlockSpec((size, wide), lambda i, column=column: (i, column))
                for term, column in terms
            ],
            out_specs=[mine] * 3,
            out_shape=[jax.ShapeDtypeStruct(weight.shape, F32)] * 3,
            compiler_params=vmem(56),
            cost_estimate=cost(weight.size / 75000),
            name="adam",
        )(weight, one, two, *[term for term, column in terms])

    fan_in = RATE_FACTOR * D ** (-0.5)
    gate_up_grad, down_grad = after((gate_up_grad, down_grad), tokens_low)
    gate_up_new = adam(
        gate_up_weight, gate_up_first, gate_up_second, [(gate_up_grad, 0)], fan_in, DECAY
    )
    down_new = adam(
        down_weight, down_first, down_second, [(down_grad, 0)], RATE_FACTOR * FF ** (-0.5), DECAY
    )

    products = jnp.concatenate(
        [
            jnp.sum(
                attn_halves[i // 2][(i % 2) * QUARTER : (i % 2 + 1) * QUARTER].astype(F32)
                * w[:, :384].astype(F32),
                axis=1,
            )
            / w[:, 384].astype(F32)
            for i, w in enumerate(attn_w)
        ]
    )
    gain_grads = jnp.stack(
        [
            products,
            jnp.concatenate(
                [lax.dynamic_slice(gain_two_grad[0], (info[i] * QUARTER,), (QUARTER,)) for i in range(4)]
            ),
        ]
    )
    if fast:
        gain_grads = gain_grads[:, : 2 * QUARTER] + swap_seq(gain_grads[:, 2 * QUARTER :])
        gains_grad = gain_grads[:, :QUARTER] + swap_dp(gain_grads[:, QUARTER:])
    else:
        shard = norm_gains.shape[0]
        gains_grad = lax.dynamic_slice(
            lax.psum(gain_grads, ("dp", "seq")),
            (0, (dp_id * seq_size + seq_id) * shard),
            (2, shard),
        )
    gains_grad = gains_grad + swap_tensor(gains_grad, 1)
    block_far = swap_tensor(after(block_near, gains_grad), 1)
    tokens_near = after(tokens_near, (gate_up_new, down_new, block_far, gains_grad))
    tokens_far = swap_tensor(tokens_near, 1)

    attn_terms = after(scatter_far(attn_near, attn_far), tokens_near)
    query_new = adam(
        query_weight, query_first, query_second, [(term, 0) for term in attn_terms], fan_in, DECAY
    )
    kv_new = adam(kv_weight, kv_first, kv_second, [(term, 2) for term in attn_terms], fan_in, DECAY)

    out_terms = scatter_far(out_near, out_far)
    out_rows = sum(term[: out_terms[-1].shape[0]].astype(F32) for term in after(out_terms, tokens_near))
    output_terms = swap_high([out_rows[:, k * 256 : (k + 1) * 256].astype(BF16) for k in range(4)])
    output_new = adam(
        output_weight,
        output_first,
        output_second,
        [(term, 0) for term in output_terms],
        RATE_FACTOR * FAN_OUT ** (-0.5),
        DECAY,
    )

    gains_grad = after(gains_grad, tokens_near)
    for mask in (2, 4):
        gains_grad = gains_grad + swap_tensor(gains_grad, mask)
    gains_grad = gains_grad.T
    gains_new = adam_step(norm_gains, gains_grad, gains_first, gains_second, GAIN_RATE, 0.0)


    def place(parts, dtype, name):
        return pl.pallas_call(
            place_kernel,
            grid_spec=pltpu.PrefetchScalarGridSpec(
                num_scalar_prefetch=1,
                grid=(4,),
                in_specs=[pl.BlockSpec((1, block, D), lambda i, info: (i, 0, 0))] * 2,
                out_specs=pl.BlockSpec((rows, D), lambda i, info: (i, 0)),
            ),
            out_shape=jax.ShapeDtypeStruct((span, D), dtype),
            compiler_params=vmem(48),
            cost_estimate=cost(5),
            name=name,
        )(info, *parts).reshape(tokens.shape)

    tokens_grad = place((tokens_near, tokens_far), F32, "tokens_grad")
    block_out = place((block_near, block_far), BF16, "block_out_rows")

    results = (query_new, output_new, kv_new, gate_up_new, down_new, gains_new)
    return (block_out, tokens_grad) + tuple(r[i] for i in range(3) for r in results)


def solution(mesh):
    wide = P(("dp", "seq"), "tensor")
    weights = (wide, wide, wide, P(("dp", "seq"), None, "tensor"), wide, P(("dp", "seq"), None))
    rows = P("dp", "seq", None)
    return jax.shard_map(
        functools.partial(body, dp_size=mesh.shape["dp"], seq_size=mesh.shape["seq"]),
        mesh=mesh,
        in_specs=(rows, rows) + weights * 3,
        out_specs=(rows, rows) + weights * 3,
        check_vma=False,
    )
```

time: 1150 us -> 572 us (0.50)
  waiting for transfers between devices: 773 us -> 199 us
  Pallas kernels: 0 us -> 184 us
  matrix products: 168 us -> 0 us
  starting transfers between devices: 1.74 us -> 91.5 us
  other arithmetic: 91.3 us -> 34.1 us
  local copies, waits for them, and re-layouts: 66.7 us -> 40.1 us
  blocking collectives: 19.2 us -> 0 us
    psum x3 -> x0, waiting for transfers between devices: 535 us -> none  [the longest x1 244 us: body(): lax.psum(mlp_part.astype(jnp.bfloat16), 'tensor').astype(jnp.float32)]
    ppermute x0 -> x58, waiting for transfers between devices: none -> 199 us  [the longest x44 136 us: swap_tensor(): return lax.ppermute(value, 'tensor', [(i, i ^ mask) for i in range(8)])]
    pallas_call x0 -> x27, Pallas kernels: none -> 184 us  [the longest x2 46 us: mlp(): pl.pallas_call(mlp_kernel, grid_spec=pltpu.PrefetchScalarGridSpec(num_sca...]
    dot_general x43 -> x0, matrix products: 168 us -> none  [the longest x8 16.9 us: block_scores(): jnp.einsum('hrd,hkd->hrk', query_part, key_block, preferred_element_type=...]
    reduce_scatter x6 -> x2, waiting for transfers between devices: 162 us -> 0.02 us  [scatter_all(): lax.psum_scatter(full, ('dp', 'seq'), scatter_dimension=0, tiled=True)]
    ppermute x0 -> x58, starting transfers between devices: none -> 81.8 us  [the longest x44 63.7 us: swap_tensor(): return lax.ppermute(value, 'tensor', [(i, i ^ mask) for i in range(8)])]
    all_gather x4 -> x6, waiting for transfers between devices: 75.1 us -> 0.03 us  [the longest x1 0.02 us: body(): back_w = lax.all_gather(back_near, ('dp', 'seq'), axis=1, tiled=True)]
    reduce_sum x9 -> x2, other arithmetic: 33.9 us -> 0.56 us  [body(): jnp.sum(attn_halves[i // 2][i % 2 * QUARTER:(i % 2 + 1) * QUARTER].astype...]
  transfers between devices with their start and end apart: 14 -> 68, of which waited for: 10 -> 25; matrix products, arithmetic and copies ran while one was open for 17% -> 8% of each run, Pallas kernels for 0% -> 32%
where the time goes in v1:
time: 572 us; the launch traced here: 564 us
  waiting for transfers between devices  199 us (35%)
  Pallas kernels  184 us (32%)
  starting transfers between devices  91.5 us (16%)
  local copies, waits for them, and re-layouts  40.1 us (7%)
  other arithmetic  34.1 us (6%)
  between operations  15.5 us (3%)
    ppermute x44, waiting for transfers between devices, swap_tensor(): return lax.ppermute(value, 'tensor', [(i, i ^ mask) for i in range(8)])  136 us
    ppermute x44, starting transfers between devices, swap_tensor(): return lax.ppermute(value, 'tensor', [(i, i ^ mask) for i in range(8)])  63.7 us
    ppermute x5, waiting for transfers between devices, swap_dp(): return lax.ppermute(value, 'dp', [(0, 1), (1, 0)])  57.2 us
    pallas_call x2, Pallas kernels, mlp(): pl.pallas_call(mlp_kernel, grid_spec=pltpu.PrefetchScalarGridSpec(num_sca...  46 us
    pallas_call x4, Pallas kernels, weight_full(): pl.pallas_call(weight_grad_kernel, grid=(4,), in_specs=[pl.BlockSpec((n,...  33.5 us
    pallas_call x5, Pallas kernels, adam(): pl.pallas_call(functools.partial(adam_kernel, rate, decay), grid=(4,), in...  31.5 us
    unnamed x169, local copies, waits for them, and re-layouts  29.3 us
  transfers between devices with their start and end apart: 68, of which 25 were waited for; matrix products, arithmetic and copies ran while one was open for 8% of the time, Pallas kernels for 32%

profile of v1, /device:TPU:0, one launch (start us, length us, event | category | flops | bytes accessed | tf_op | source)
XLA Modules:
  0.0 564.5 jit_solution(14782446849715824478)
XLA Ops:
  12.3 3.0 collective-permute-start
  18.2 9.1 %collective-permute-done.w1 = bf16[512,512]{1,0:T(8,128)(2,1)S(1)} collective-permute-done((bf16[512,512]{1,0:T(8,128)(2,1)S(1)}, bf16[512,512]{1,0:T(8,128)(2,1)S(1)}, u32[]{:S(2)}, u32[]{:S(2)}) %collective-permute-start) | collective-permute-done | bytes 524320 | tf_op jit(solution)/shard_map/ppermute | solution.py:534
  28.4 3.4 copy.51
  37.5 7.1 %project.1 = (bf16[1024,2048]{1,0:T(8,128)(2,1)}, bf16[1024,256]{1,0:T(8,128)(2,1)S(1)}, bf16[1024,128]{1,0:T(8,128)(2,1)S(1)}, f32[8,2048]{1,0:T(8,128)S(1)}) custom-call(s32[9]{0:T(128)S(1)} %stack.63.info, bf16[1024,2048]{1,0:T(8,128)(2,1)} %bitcast.52, bf16[512,512]{1,0:T(8,128)(2,1)S(1)} %copy-done.20, bf16[512,512]{1,0:T(8,128)(2,1)S(1)} %collective-permute-done.w1, ...), custom_call_target="tpu_custom_call" | custom-call | bytes 12915000 | tf_op jit(solution)/shard_map/project/pallas_call | solution.py:655
  50.3 2.6 collective-permute-start.34
  54.5 7.7 %attend.1 = (bf16[1024,256]{1,0:T(8,128)(2,1)S(1)}, f32[4,1,1024]{2,1,0:T(1,128)S(1)}, bf16[256,256]{1,0:T(8,128)(2,1)S(1)}, bf16[256,256]{1,0:T(8,128)(2,1)S(1)...) custom-call(s32[9]{0:T(128)S(1)} %stack.63.info, bf16[1024,256]{1,0:T(8,128)(2,1)S(1)} %get-tuple-element.147.q, ...), custom_call_target="tpu_custom_call" | custom-call | bytes 33210000 | tf_op jit(solution)/shard_map/attend/pallas_call | solution.py:693
  64.3 23.4 %collective-permute-done.7.w1 = bf16[4,512,256]{2,1,0:T(8,128)(2,1)S(1)} collective-permute-done((bf16[4,512,256]{2,1,0:T(8,128)(2,1)}, bf16[4,512,256]{2,1,0:T(8,128)(2,1)S(1)}, u32[]{:S(2)}, u32[]{:S(2)}) %collective-permute-start.7) | collective-permute-done | bytes 1048608 | tf_op jit(solution)/shard_map/ppermute | solution.py:534
  88.7 2.8 pad_maximum_fusion.1
  94.1 2.8 collective-permute-start.5
  97.0 7.4 %reorder.1.dy.refs_9_ = bf16[2,512,2048]{2,1,0:T(8,128)(2,1)} custom-call(s32[9]{0:T(128)} %copy-done.36, bf16[1024,2048]{1,0:T(8,128)(2,1)} %bitcast.57), custom_call_target="tpu_custom_call" | custom-call | bytes 13837500 | tf_op jit(solution)/shard_map/reorder/pallas_call | solution.py:642
  104.4 2.8 collective-permute-done.5.a2
  108.6 3.8 attention_out.1
  114.8 10.3 %collective-permute-done.10.got = bf16[128,2048]{1,0:T(8,128)(2,1)S(1)} collective-permute-done((bf16[128,2048]{1,0:T(8,128)(2,1)S(1)}, bf16[128,2048]{1,0:T(8,128)(2,1)S(1)}, u32[]{:S(2)}, u32[]{:S(2)}) %collective-permute-start.10) | collective-permute-done | bytes 524320 | tf_op jit(solution)/shard_map/ppermute | solution.py:531
  126.0 3.5 second_norm.1
  129.5 3.6 collective-permute-start.11
  136.5 5.4 collective-permute-done.11
  141.9 12.4 %collective-permute-done.12 = bf16[64,2048]{1,0:T(8,128)(2,1)S(1)} collective-permute-done((bf16[64,2048]{1,0:T(8,128)(2,1)}, bf16[64,2048]{1,0:T(8,128)(2,1)S(1)}, u32[]{:S(2)}, u32[]{:S(2)}) %collective-permute-start.12) | collective-permute-done | bytes 262176 | tf_op jit(solution)/shard_map/ppermute | solution.py:531
  156.9 3.5 collective-permute-start.15
  163.5 4.2 collective-permute-done.15
  168.4 12.2 %collective-permute-done.16 = bf16[64,2048]{1,0:T(8,128)(2,1)S(1)} collective-permute-done((bf16[64,2048]{1,0:T(8,128)(2,1)S(1)}, bf16[64,2048]{1,0:T(8,128)(2,1)S(1)}, u32[]{:S(2)}, u32[]{:S(2)}) %collective-permute-start.16) | collective-permute-done | bytes 262176 | tf_op jit(solution)/shard_map/ppermute | solution.py:531
  182.6 22.8 %mlp.2 = (bf16[4,64,2048]{2,1,0:T(8,128)(2,1)}, bf16[4,64,2048]{2,1,0:T(8,128)(2,1)}, bf16[256,2048]{1,0:T(8,128)(2,1)}, bf16[256,2048]{1,0:T(8,128)(2,1)}, bf16...) custom-call(s32[9]{0:T(128)} %copy-done.36, bf16[256,2048]{1,0:T(8,128)(2,1)} %copy-done.58, ...), custom_call_target="tpu_custom_call" | custom-call | bytes 41512500 | tf_op jit(solution)/shard_map/mlp/pallas_call | solution.py:772
  207.0 23.1 %mlp.3 = (bf16[4,64,2048]{2,1,0:T(8,128)(2,1)}, bf16[4,64,2048]{2,1,0:T(8,128)(2,1)}, bf16[256,2048]{1,0:T(8,128)(2,1)}, bf16[256,2048]{1,0:T(8,128)(2,1)}, bf16...) custom-call(s32[9]{0:T(128)} %copy-done.36, ...), custom_call_target="tpu_custom_call", output_to_operand_aliasing={{4}: (6, {}), {5}: (7, {}), {6}: (8, {})} | custom-call | bytes 41512500 | tf_op jit(solution)/shard_map/mlp/pallas_call | solution.py:772
  232.0 2.8 collective-permute-start.21
  238.0 8.5 %weight_grad.4 = bf16[2048,1024]{1,0:T(8,128)(2,1)} custom-call(bf16[1024,2048]{1,0:T(8,128)(2,1)} %bitcast.51, bf16[1024,1024]{1,0:T(8,128)(2,1)} %get-tuple-element.182.b), custom_call_target="tpu_custom_call" | custom-call | bytes 12091392 | tf_op jit(solution)/shard_map/weight_grad/pallas_call | solution.py:565
  246.5 13.3 %weight_grad.5 = bf16[2048,2048]{1,0:T(8,128)(2,1)} custom-call(bf16[1024,2048]{1,0:T(8,128)(2,1)} %get-tuple-element.183.a, bf16[1024,2048]{1,0:T(8,128)(2,1)} %get-tuple-element.184.b), custom_call_target="tpu_custom_call" | custom-call | bytes 24182784 | tf_op jit(solution)/shard_map/weight_grad/pallas_call | solution.py:565
  259.9 3.7 fusion.8
  273.3 4.1 collective-permute-done.25.refs_5_
  277.5 9.1 %collective-permute-done.26.refs_6_ = bf16[64,2048]{1,0:T(8,128)(2,1)} collective-permute-done((bf16[64,2048]{1,0:T(8,128)(2,1)S(1)}, bf16[64,2048]{1,0:T(8,128)(2,1)}, u32[]{:S(2)}, u32[]{:S(2)}) %collective-permute-start.26) | collective-permute-done | bytes 262176 | tf_op jit(solution)/shard_map/ppermute | solution.py:531
  286.6 4.7 second_norm_back.1
  291.9 2.9 add_convert_fusion.2
  294.8 11.1 %collective-permute-done.28.other = bf16[128,2048]{1,0:T(8,128)(2,1)S(1)} collective-permute-done((bf16[128,2048]{1,0:T(8,128)(2,1)}, bf16[128,2048]{1,0:T(8,128)(2,1)S(1)}, u32[]{:S(2)}, u32[]{:S(2)}) %collective-permute-start.28) | collective-permute-done | bytes 524320 | tf_op jit(solution)/shard_map/ppermute | solution.py:531
  306.7 4.3 all-to-all-start
  314.3 3.4 attention_out_back.1
  321.3 2.4 collective-permute-start.31
  323.8 6.5 %collective-permute-done.30.grad1 = bf16[256,256]{1,0:T(8,128)(2,1)S(1)} collective-permute-done((bf16[256,256]{1,0:T(8,128)(2,1)S(1)}, bf16[256,256]{1,0:T(8,128)(2,1)S(1)}, u32[]{:S(2)}, u32[]{:S(2)}) %collective-permute-start.30) | collective-permute-done | bytes 131104 | tf_op jit(solution)/shard_map/ppermute | solution.py:531
  330.2 13.5 %collective-permute-done.31.grad2 = bf16[256,256]{1,0:T(8,128)(2,1)S(1)} collective-permute-done((bf16[256,256]{1,0:T(8,128)(2,1)S(1)}, bf16[256,256]{1,0:T(8,128)(2,1)S(1)}, u32[]{:S(2)}, u32[]{:S(2)}) %collective-permute-start.31) | collective-permute-done | bytes 131104 | tf_op jit(solution)/shard_map/ppermute | solution.py:531
  343.8 2.7 add_convert_fusion.1
  346.5 4.2 all-to-all-start.1
  351.6 10.6 %attend_back.1 = (bf16[1024,256]{1,0:T(8,128)(2,1)S(1)}, bf16[256,256]{1,0:T(8,128)(2,1)S(1)}, bf16[256,256]{1,0:T(8,128)(2,1)S(1)}, bf16[256,256]{1,0:T(8,128)(...) custom-call(s32[9]{0:T(128)S(1)} %copy-done.38, bf16[1024,256]{1,0:T(8,128)(2,1)S(1)} %get-tuple-element.147.q, ...), custom_call_target="tpu_custom_call" | custom-call | bytes 42435000 | tf_op jit(solution)/shard_map/attend_back/pallas_call | solution.py:880
  363.7 9.5 %collective-permute-start.36 = (bf16[1024,128]{1,0:T(8,128)(2,1)S(1)}, bf16[1024,128]{1,0:T(8,128)(2,1)S(1)}, u32[]{:S(2)}, u32[]{:S(2)}) collective-permute-start(bf16[1024,128]{1,0:T(8,128)(2,1)S(1)} %get-tuple-element.293), channel_id=1, source_target_pairs={{0,8},{8,0},{1,9},{9,1},{2,10},{10,2},{3,11},{11,3},{4,12},{12,4},... | collective-permute-start | bytes 786440 | tf_op jit(solution)/shard_map/ppermute | solution.py:537
  373.2 3.3 collective-permute-start.37
  380.6 8.1 %collective-permute-done.38.q2 = bf16[256,256]{1,0:T(8,128)(2,1)S(1)} collective-permute-done((bf16[256,256]{1,0:T(8,128)(2,1)S(1)}, bf16[256,256]{1,0:T(8,128)(2,1)S(1)}, u32[]{:S(2)}, u32[]{:S(2)}) %collective-permute-start.38) | collective-permute-done | bytes 131104 | tf_op jit(solution)/shard_map/ppermute | solution.py:531
  389.4 3.1 kv_back.1
  392.7 3.0 block_out.1
  396.3 2.8 collective-permute-start.40
  399.1 2.4 collective-permute-start.42
  402.9 3.6 collective-permute-done.41.k2
  411.1 5.8 %attention_in_back.1 = (f32[128,2048]{1,0:T(8,128)S(1)}, bf16[128,2048]{1,0:T(8,128)(2,1)S(1)}) custom-call(s32[9]{0:T(128)S(1)} %copy-done.39, bf16[256,256]{1,0:T(8,128)(2,1)S(1)} %copy-done.33, bf16[256,256]{1,0:T(8,128)(2,1)S(1)} %collective-permute-done.37.q1, bf16[256,256]{1,0:T(8,128)(2,1)S(1)} %collective-permute-done.38.q2, ...), custom_call_target="tpu_custom_call" | custom-call | bytes 10701000 | tf_op jit(solution)/shard_map/attention_in_back/pallas_call | solution.py:941
  422.0 6.1 %weight_grad.6 = (bf16[1024,384]{1,0:T(8,128)(2,1)}, bf16[1024,384]{1,0:T(8,128)(2,1)}) custom-call(bf16[1024,2048]{1,0:T(8,128)(2,1)} %get-tuple-element.219.a, bf16[1024,384]{1,0:T(8,128)(2,1)} %pad_maximum_fusion.2.b), custom_call_target="tpu_custom_call" | custom-call | bytes 4534272 | tf_op jit(solution)/shard_map/weight_grad/pallas_call | solution.py:565
  428.1 5.6 weight_grad.7
  434.5 4.1 first_norm_back.1
  442.4 3.2 collective-permute-done.44
  446.0 3.2 collective-permute-done.45
  449.6 13.4 %adam.5 = (f32[512,2,1024]{2,1,0:T(2,128)}, f32[512,2,1024]{2,1,0:T(2,128)}, f32[512,2,1024]{2,1,0:T(2,128)}) custom-call(f32[512,2,1024]{2,1,0:T(2,128)} %weight.5, f32[512,2,1024]{2,1,0:T(2,128)} %one.5, f32[512,2,1024]{2,1,0:T(2,128)} %two.5, bf16[512,2048]{1,0:T(8,128)(2,1)} %reduce-scatter.5.cloned.1.call-done.refs_0_), custom_call_target="tpu_custom_call" | custom-call | bytes 25794968 | tf_op jit(solution)/shard_map/adam/pallas_call | solution.py:994
  463.0 6.9 %adam.6 = (f32[512,1024]{1,0:T(8,128)}, f32[512,1024]{1,0:T(8,128)}, f32[512,1024]{1,0:T(8,128)}) custom-call(f32[512,1024]{1,0:T(8,128)} %weight.6, f32[512,1024]{1,0:T(8,128)} %one.6, f32[512,1024]{1,0:T(8,128)} %two.6, bf16[512,1024]{1,0:T(8,128)(2,1)} %reduce-scatter.3.cloned.1.call-done.refs_0_), custom_call_target="tpu_custom_call" | custom-call | bytes 12897484 | tf_op jit(solution)/shard_map/adam/pallas_call | solution.py:994
  469.8 25.0 %collective-permute-done.46.far = bf16[4,128,2048]{2,1,0:T(8,128)(2,1)S(1)} collective-permute-done((bf16[4,128,2048]{2,1,0:T(8,128)(2,1)}, bf16[4,128,2048]{2,1,0:T(8,128)(2,1)S(1)}, u32[]{:S(2)}, u32[]{:S(2)}) %collective-permute-start.46) | collective-permute-done | bytes 2097184 | tf_op jit(solution)/shard_map/ppermute | solution.py:531
  502.6 21.5 %collective-permute-done.52 = bf16[512,1024]{1,0:T(8,128)(2,1)S(1)} collective-permute-done((bf16[512,1024]{1,0:T(8,128)(2,1)S(1)}, bf16[512,1024]{1,0:T(8,128)(2,1)S(1)}, u32[]{:S(2)}, u32[]{:S(2)}) %collective-permute-start.52) | collective-permute-done | bytes 1048608 | tf_op jit(solution)/shard_map/ppermute | solution.py:534
  524.1 2.8 collective-permute-start.56
  534.3 3.0 block_out_rows.1
  537.3 3.8 adam.7
  541.2 3.5 adam.9
  544.6 3.0 collective-permute-done.57
  549.1 3.9 adam.8
  553.0 4.2 tokens_grad.1
  (327 shorter events, 109.6 us)
Async XLA Ops:
  7.2 38.0 %all-gather.16.cloned.1.call-start = ((), (), s32[]{:S(2)}) async-start(), calls=%async_computation.9 | async-start | bytes 1310720 | tf_op jit(solution)/shard_map/all_gather | solution.py:628
  12.2 170.3 %all-gather.12.cloned.1.call-start = ((), (), s32[]{:S(2)}) async-start(), calls=%async_computation.5 | async-start | bytes 5242880 | tf_op jit(solution)/shard_map/all_gather | solution.py:551
  12.3 15.0 %collective-permute-start = (bf16[512,512]{1,0:T(8,128)(2,1)S(1)}, bf16[512,512]{1,0:T(8,128)(2,1)S(1)}, u32[]{:S(2)}, u32[]{:S(2)}) collective-permute-start(bf16[512,512]{1,0:T(8,128)(2,1)S(1)} %fusion.1.w0), channel_id=1, source_target_pairs={{0,16},{16,0},{1,17},{17,1},{2,18},{18,2},{3,19},{19,3},{4,20},{20... | collective-permute-start | bytes 1572872 | tf_op jit(solution)/shard_map/ppermute | solution.py:534
  28.4 154.2 %all-gather.10.cloned.1.call-start = ((), (), s32[]{:S(2)}) async-start(), calls=%async_computation.4 | async-start | bytes 10485760 | tf_op jit(solution)/shard_map/all_gather | solution.py:551
  33.5 317.3 %all-gather.14.cloned.1.call-start = ((), (), s32[]{:S(2)}) async-start(), calls=%async_computation.7 | async-start | bytes 7864320 | tf_op jit(solution)/shard_map/all_gather | solution.py:728
  45.2 42.5 %collective-permute-start.7 = (bf16[4,512,256]{2,1,0:T(8,128)(2,1)}, bf16[4,512,256]{2,1,0:T(8,128)(2,1)S(1)}, u32[]{:S(2)}, u32[]{:S(2)}) collective-permute-start(bf16[4,512,256]{2,1,0:T(8,128)(2,1)} %bitcast.43), channel_id=1, source_target_pairs={{0,16},{16,0},{1,17},{17,1},{2,18},{18,2},{3,19},{19,3},{4,20},{20... | collective-permute-start | bytes 3145736 | tf_op jit(solution)/shard_map/ppermute | solution.py:534
  47.0 6.1 %collective-permute-start.3 = (bf16[1024,128]{1,0:T(8,128)(2,1)S(1)}, bf16[1024,128]{1,0:T(8,128)(2,1)}, u32[]{:S(2)}, u32[]{:S(2)}) collective-permute-start(bf16[1024,128]{1,0:T(8,128)(2,1)S(1)} %get-tuple-element.148), channel_id=1, source_target_pairs={{0,8},{8,0},{1,9},{9,1},{2,10},{10,2},{3,11},{11,3},{4,12},{12,4},... | collective-permute-start | bytes 786440 | tf_op jit(solution)/shard_map/ppermute | solution.py:537
  48.7 39.0 %collective-permute-start.33 = (bf16[512,384]{1,0:T(8,128)(2,1)}, bf16[512,384]{1,0:T(8,128)(2,1)}, u32[]{:S(2)}, u32[]{:S(2)}) collective-permute-start(bf16[512,384]{1,0:T(8,128)(2,1)} %pad_maximum_fusion.6), channel_id=1, source_target_pairs={{0,2},{1,3},{2,0},{3,1},{4,6},{5,7},{6,4},{7,5},{8,10},{9,11},{10,... | collective-permute-start | bytes 1179656 | tf_op jit(solution)/shard_map/ppermute | solution.py:531
  50.3 37.4 %collective-permute-start.34 = (bf16[512,384]{1,0:T(8,128)(2,1)}, bf16[512,384]{1,0:T(8,128)(2,1)}, u32[]{:S(2)}, u32[]{:S(2)}) collective-permute-start(bf16[512,384]{1,0:T(8,128)(2,1)} %pad_maximum_fusion.6), channel_id=1, source_target_pairs={{0,4},{1,5},{2,6},{3,7},{4,0},{5,1},{6,2},{7,3},{8,12},{9,13},{10,... | collective-permute-start | bytes 1179656 | tf_op jit(solution)/shard_map/ppermute | solution.py:531
  52.9 34.8 %collective-permute-start.35 = (bf16[512,384]{1,0:T(8,128)(2,1)}, bf16[512,384]{1,0:T(8,128)(2,1)}, u32[]{:S(2)}, u32[]{:S(2)}) collective-permute-start(bf16[512,384]{1,0:T(8,128)(2,1)} %pad_maximum_fusion.6), channel_id=1, source_target_pairs={{0,6},{1,7},{2,4},{3,5},{4,2},{5,3},{6,0},{7,1},{8,14},{9,15},{10,... | collective-permute-start | bytes 1179656 | tf_op jit(solution)/shard_map/ppermute | solution.py:531
  91.5 259.3 %reduce-scatter.3.cloned.1.call-start = ((), (), s32[]{:S(2)}) async-start(), calls=%async_computation.6 | async-start | bytes 5242880 | tf_op jit(solution)/shard_map/reduce_scatter | solution.py:554
  92.0 15.1 %collective-permute-start.8 = (bf16[4,512,256]{2,1,0:T(8,128)(2,1)S(1)}, bf16[4,512,256]{2,1,0:T(8,128)(2,1)}, u32[]{:S(2)}, u32[]{:S(2)}) collective-permute-start(bf16[4,512,256]{2,1,0:T(8,128)(2,1)S(1)} %bitcast.44), channel_id=1, source_target_pairs={{0,8},{8,0},{1,9},{9,1},{2,10},{10,2},{3,11},{11,3},{4,12},{12,4},... | collective-permute-start | bytes 3145736 | tf_op jit(solution)/shard_map/ppermute | solution.py:537
  92.1 15.1 %collective-permute-start.9 = (bf16[4,512,256]{2,1,0:T(8,128)(2,1)}, bf16[4,512,256]{2,1,0:T(8,128)(2,1)}, u32[]{:S(2)}, u32[]{:S(2)}) collective-permute-start(bf16[4,512,256]{2,1,0:T(8,128)(2,1)} %copy-done.6), channel_id=1, source_target_pairs={{0,8},{8,0},{1,9},{9,1},{2,10},{10,2},{3,11},{11,3},{4,12},{12,4},... | collective-permute-start | bytes 3145736 | tf_op jit(solution)/shard_map/ppermute | solution.py:537
  92.6 11.8 %collective-permute-start.4 = (bf16[256,256]{1,0:T(8,128)(2,1)}, bf16[256,256]{1,0:T(8,128)(2,1)S(1)}, u32[]{:S(2)}, u32[]{:S(2)}) collective-permute-start(bf16[256,256]{1,0:T(8,128)(2,1)} %copy-done.52), channel_id=1, source_target_pairs={{0,2},{1,3},{2,0},{3,1},{4,6},{5,7},{6,4},{7,5},{8,10},{9,11},{10,... | collective-permute-start | bytes 393224 | tf_op jit(solution)/shard_map/ppermute | solution.py:531
  94.1 13.1 %collective-permute-start.5 = (bf16[256,256]{1,0:T(8,128)(2,1)}, bf16[256,256]{1,0:T(8,128)(2,1)S(1)}, u32[]{:S(2)}, u32[]{:S(2)}) collective-permute-start(bf16[256,256]{1,0:T(8,128)(2,1)} %copy-done.51), channel_id=1, source_target_pairs={{0,4},{1,5},{2,6},{3,7},{4,0},{5,1},{6,2},{7,3},{8,12},{9,13},{10,... | collective-permute-start | bytes 393224 | tf_op jit(solution)/shard_map/ppermute | solution.py:531
  96.8 10.3 %collective-permute-start.6 = (bf16[256,256]{1,0:T(8,128)(2,1)}, bf16[256,256]{1,0:T(8,128)(2,1)}, u32[]{:S(2)}, u32[]{:S(2)}) collective-permute-start(bf16[256,256]{1,0:T(8,128)(2,1)} %copy-done.50), channel_id=1, source_target_pairs={{0,6},{1,7},{2,4},{3,5},{4,2},{5,3},{6,0},{7,1},{8,14},{9,15},{10,... | collective-permute-start | bytes 393224 | tf_op jit(solution)/shard_map/ppermute | solution.py:531
  113.3 11.9 %collective-permute-start.10 = (bf16[128,2048]{1,0:T(8,128)(2,1)S(1)}, bf16[128,2048]{1,0:T(8,128)(2,1)S(1)}, u32[]{:S(2)}, u32[]{:S(2)}) collective-permute-start(bf16[128,2048]{1,0:T(8,128)(2,1)S(1)} %get-tuple-element.163), channel_id=1, source_target_pairs={{0,1},{1,0},{2,3},{3,2},{4,5},{5,4},{6,7},{7,6},{8,9},{9,8},{10,11... | collective-permute-start | bytes 1572872 | tf_op jit(solution)/shard_map/ppermute | solution.py:531
  129.5 12.4 %collective-permute-start.11 = (bf16[64,2048]{1,0:T(8,128)(2,1)}, bf16[64,2048]{1,0:T(8,128)(2,1)S(1)}, u32[]{:S(2)}, u32[]{:S(2)}) collective-permute-start(bf16[64,2048]{1,0:T(8,128)(2,1)} %get-tuple-element.165), channel_id=1, source_target_pairs={{0,2},{1,3},{2,0},{3,1},{4,6},{5,7},{6,4},{7,5},{8,10},{9,11},{10,... | collective-permute-start | bytes 786440 | tf_op jit(solution)/shard_map/ppermute | solution.py:531
  133.1 21.3 %collective-permute-start.12 = (bf16[64,2048]{1,0:T(8,128)(2,1)}, bf16[64,2048]{1,0:T(8,128)(2,1)S(1)}, u32[]{:S(2)}, u32[]{:S(2)}) collective-permute-start(bf16[64,2048]{1,0:T(8,128)(2,1)} %get-tuple-element.165), channel_id=1, source_target_pairs={{0,4},{1,5},{2,6},{3,7},{4,0},{5,1},{6,2},{7,3},{8,12},{9,13},{10,... | collective-permute-start | bytes 786440 | tf_op jit(solution)/shard_map/ppermute | solution.py:531
  134.9 19.4 %collective-permute-start.13 = (bf16[64,2048]{1,0:T(8,128)(2,1)}, bf16[64,2048]{1,0:T(8,128)(2,1)S(1)}, u32[]{:S(2)}, u32[]{:S(2)}) collective-permute-start(bf16[64,2048]{1,0:T(8,128)(2,1)} %get-tuple-element.165), channel_id=1, source_target_pairs={{0,6},{1,7},{2,4},{3,5},{4,2},{5,3},{6,0},{7,1},{8,14},{9,15},{10,... | collective-permute-start | bytes 786440 | tf_op jit(solution)/shard_map/ppermute | solution.py:531
  155.3 27.2 %collective-permute-start.14 = (bf16[256,2048]{1,0:T(8,128)(2,1)S(1)}, bf16[256,2048]{1,0:T(8,128)(2,1)}, u32[]{:S(2)}, u32[]{:S(2)}) collective-permute-start(bf16[256,2048]{1,0:T(8,128)(2,1)S(1)} %constant_dynamic-update-slice_fusion.near), channel_id=1, source_target_pairs={{0,1},{1,0},{2,3},{3,2},{4,5},{5,4},{6,7},{7,6},{8,9},{9,8},{10,11... | collective-permute-start | bytes 3145736 | tf_op jit(solution)/shard_map/ppermute | solution.py:531
  156.9 10.8 %collective-permute-start.15 = (bf16[64,2048]{1,0:T(8,128)(2,1)S(1)}, bf16[64,2048]{1,0:T(8,128)(2,1)S(1)}, u32[]{:S(2)}, u32[]{:S(2)}) collective-permute-start(bf16[64,2048]{1,0:T(8,128)(2,1)S(1)} %copy-done.71), channel_id=1, source_target_pairs={{0,2},{1,3},{2,0},{3,1},{4,6},{5,7},{6,4},{7,5},{8,10},{9,11},{10,... | collective-permute-start | bytes 786440 | tf_op jit(solution)/shard_map/ppermute | solution.py:531
  160.4 20.2 %collective-permute-start.16 = (bf16[64,2048]{1,0:T(8,128)(2,1)S(1)}, bf16[64,2048]{1,0:T(8,128)(2,1)S(1)}, u32[]{:S(2)}, u32[]{:S(2)}) collective-permute-start(bf16[64,2048]{1,0:T(8,128)(2,1)S(1)} %copy-done.71), channel_id=1, source_target_pairs={{0,4},{1,5},{2,6},{3,7},{4,0},{5,1},{6,2},{7,3},{8,12},{9,13},{10,... | collective-permute-start | bytes 786440 | tf_op jit(solution)/shard_map/ppermute | solution.py:531
  161.8 19.5 %collective-permute-start.17 = (bf16[64,2048]{1,0:T(8,128)(2,1)S(1)}, bf16[64,2048]{1,0:T(8,128)(2,1)S(1)}, u32[]{:S(2)}, u32[]{:S(2)}) collective-permute-start(bf16[64,2048]{1,0:T(8,128)(2,1)S(1)} %copy-done.71), channel_id=1, source_target_pairs={{0,6},{1,7},{2,4},{3,5},{4,2},{5,3},{6,0},{7,1},{8,14},{9,15},{10,... | collective-permute-start | bytes 786440 | tf_op jit(solution)/shard_map/ppermute | solution.py:531
  182.0 24.9 %collective-permute-start.18 = (bf16[256,2048]{1,0:T(8,128)(2,1)}, bf16[256,2048]{1,0:T(8,128)(2,1)}, u32[]{:S(2)}, u32[]{:S(2)}) collective-permute-start(bf16[256,2048]{1,0:T(8,128)(2,1)} %constant_dynamic-update-slice_fusion.4.near), channel_id=1, source_target_pairs={{0,1},{1,0},{2,3},{3,2},{4,5},{5,4},{6,7},{7,6},{8,9},{9,8},{10,11... | collective-permute-start | bytes 3145736 | tf_op jit(solution)/shard_map/ppermute | solution.py:531
  205.4 25.3 %collective-permute-start.20 = (bf16[256,2048]{1,0:T(8,128)(2,1)}, bf16[256,2048]{1,0:T(8,128)(2,1)S(1)}, u32[]{:S(2)}, u32[]{:S(2)}) collective-permute-start(bf16[256,2048]{1,0:T(8,128)(2,1)} %get-tuple-element.180), channel_id=1, source_target_pairs={{0,1},{1,0},{2,3},{3,2},{4,5},{5,4},{6,7},{7,6},{8,9},{9,8},{10,11... | collective-permute-start | bytes 3145736 | tf_op jit(solution)/shard_map/ppermute | solution.py:531
  230.1 29.7 %collective-permute-start.19 = (bf16[256,2048]{1,0:T(8,128)(2,1)}, bf16[256,2048]{1,0:T(8,128)(2,1)}, u32[]{:S(2)}, u32[]{:S(2)}) collective-permute-start(bf16[256,2048]{1,0:T(8,128)(2,1)} %get-tuple-element.176), channel_id=1, source_target_pairs={{0,1},{1,0},{2,3},{3,2},{4,5},{5,4},{6,7},{7,6},{8,9},{9,8},{10,11... | collective-permute-start | bytes 3145736 | tf_op jit(solution)/shard_map/ppermute | solution.py:531
  232.0 27.8 %collective-permute-start.21 = (bf16[64,2048]{1,0:T(8,128)(2,1)}, bf16[64,2048]{1,0:T(8,128)(2,1)}, u32[]{:S(2)}, u32[]{:S(2)}) collective-permute-start(bf16[64,2048]{1,0:T(8,128)(2,1)} %get-tuple-element.292), channel_id=1, source_target_pairs={{0,2},{1,3},{2,0},{3,1},{4,6},{5,7},{6,4},{7,5},{8,10},{9,11},{10,... | collective-permute-start | bytes 786440 | tf_op jit(solution)/shard_map/ppermute | solution.py:531
  234.8 25.0 %collective-permute-start.22 = (bf16[64,2048]{1,0:T(8,128)(2,1)}, bf16[64,2048]{1,0:T(8,128)(2,1)}, u32[]{:S(2)}, u32[]{:S(2)}) collective-permute-start(bf16[64,2048]{1,0:T(8,128)(2,1)} %get-tuple-element.291), channel_id=1, source_target_pairs={{0,4},{1,5},{2,6},{3,7},{4,0},{5,1},{6,2},{7,3},{8,12},{9,13},{10,... | collective-permute-start | bytes 786440 | tf_op jit(solution)/shard_map/ppermute | solution.py:531
  235.6 24.3 %collective-permute-start.23 = (bf16[64,2048]{1,0:T(8,128)(2,1)}, bf16[64,2048]{1,0:T(8,128)(2,1)}, u32[]{:S(2)}, u32[]{:S(2)}) collective-permute-start(bf16[64,2048]{1,0:T(8,128)(2,1)} %get-tuple-element.290), channel_id=1, source_target_pairs={{0,6},{1,7},{2,4},{3,5},{4,2},{5,3},{6,0},{7,1},{8,14},{9,15},{10,... | collective-permute-start | bytes 786440 | tf_op jit(solution)/shard_map/ppermute | solution.py:531
  263.5 144.2 %reduce-scatter.5.cloned.1.call-start = ((), (), s32[]{:S(2)}) async-start(), calls=%async_computation.8 | async-start | bytes 10485760 | tf_op jit(solution)/shard_map/reduce_scatter | solution.py:554
  264.1 27.8 %collective-permute-start.24 = (bf16[4,64,2048]{2,1,0:T(8,128)(2,1)}, bf16[4,64,2048]{2,1,0:T(8,128)(2,1)}, u32[]{:S(2)}, u32[]{:S(2)}) collective-permute-start(bf16[4,64,2048]{2,1,0:T(8,128)(2,1)} %get-tuple-element.186), channel_id=1, source_target_pairs={{0,1},{1,0},{2,3},{3,2},{4,5},{5,4},{6,7},{7,6},{8,9},{9,8},{10,11... | collective-permute-start | bytes 3145736 | tf_op jit(solution)/shard_map/ppermute | solution.py:531
  266.9 10.6 %collective-permute-start.25 = (bf16[64,2048]{1,0:T(8,128)(2,1)S(1)}, bf16[64,2048]{1,0:T(8,128)(2,1)}, u32[]{:S(2)}, u32[]{:S(2)}) collective-permute-start(bf16[64,2048]{1,0:T(8,128)(2,1)S(1)} %get-tuple-element.289), channel_id=1, source_target_pairs={{0,2},{1,3},{2,0},{3,1},{4,6},{5,7},{6,4},{7,5},{8,10},{9,11},{10,... | collective-permute-start | bytes 786440 | tf_op jit(solution)/shard_map/ppermute | solution.py:531
  268.1 18.5 %collective-permute-start.26 = (bf16[64,2048]{1,0:T(8,128)(2,1)S(1)}, bf16[64,2048]{1,0:T(8,128)(2,1)}, u32[]{:S(2)}, u32[]{:S(2)}) collective-permute-start(bf16[64,2048]{1,0:T(8,128)(2,1)S(1)} %get-tuple-element.288), channel_id=1, source_target_pairs={{0,4},{1,5},{2,6},{3,7},{4,0},{5,1},{6,2},{7,3},{8,12},{9,13},{10,... | collective-permute-start | bytes 786440 | tf_op jit(solution)/shard_map/ppermute | solution.py:531
  269.7 16.9 %collective-permute-start.27 = (bf16[64,2048]{1,0:T(8,128)(2,1)S(1)}, bf16[64,2048]{1,0:T(8,128)(2,1)}, u32[]{:S(2)}, u32[]{:S(2)}) collective-permute-start(bf16[64,2048]{1,0:T(8,128)(2,1)S(1)} %get-tuple-element.287), channel_id=1, source_target_pairs={{0,6},{1,7},{2,4},{3,5},{4,2},{5,3},{6,0},{7,1},{8,14},{9,15},{10,... | collective-permute-start | bytes 786440 | tf_op jit(solution)/shard_map/ppermute | solution.py:531
  291.3 14.7 %collective-permute-start.28 = (bf16[128,2048]{1,0:T(8,128)(2,1)}, bf16[128,2048]{1,0:T(8,128)(2,1)S(1)}, u32[]{:S(2)}, u32[]{:S(2)}) collective-permute-start(bf16[128,2048]{1,0:T(8,128)(2,1)} %get-tuple-element.188.own), channel_id=1, source_target_pairs={{0,1},{1,0},{2,3},{3,2},{4,5},{5,4},{6,7},{7,6},{8,9},{9,8},{10,11... | collective-permute-start | bytes 1572872 | tf_op jit(solution)/shard_map/ppermute | solution.py:531
  306.7 37.0 %collective-permute-start.29 = (bf16[4,64,2048]{2,1,0:T(8,128)(2,1)}, bf16[4,64,2048]{2,1,0:T(8,128)(2,1)}, u32[]{:S(2)}, u32[]{:S(2)}) collective-permute-start(bf16[4,64,2048]{2,1,0:T(8,128)(2,1)} %get-tuple-element.193), channel_id=1, source_target_pairs={{0,1},{1,0},{2,3},{3,2},{4,5},{5,4},{6,7},{7,6},{8,9},{9,8},{10,11... | collective-permute-start | bytes 3145736 | tf_op jit(solution)/shard_map/ppermute | solution.py:531
  306.7 39.8 %all-to-all-start = ((bf16[4,64,2048]{2,1,0:T(8,128)(2,1)}), bf16[4,64,2048]{2,1,0:T(8,128)(2,1)}, u32[]{:S(2)}, u32[]{:S(2)}) async-start(bf16[4,64,2048]{2,1,0:T(8,128)(2,1)} %add_convert_fusion.2), calls=%async_computation | async-start | bytes 2097152 | tf_op jit(solution)/shard_map/all_to_all | solution.py:857
  319.4 10.9 %collective-permute-start.30 = (bf16[256,256]{1,0:T(8,128)(2,1)S(1)}, bf16[256,256]{1,0:T(8,128)(2,1)S(1)}, u32[]{:S(2)}, u32[]{:S(2)}) collective-permute-start(bf16[256,256]{1,0:T(8,128)(2,1)S(1)} %get-tuple-element.195), channel_id=1, source_target_pairs={{0,2},{1,3},{2,0},{3,1},{4,6},{5,7},{6,4},{7,5},{8,10},{9,11},{10,... | collective-permute-start | bytes 393224 | tf_op jit(solution)/shard_map/ppermute | solution.py:531
  321.3 22.4 %collective-permute-start.31 = (bf16[256,256]{1,0:T(8,128)(2,1)S(1)}, bf16[256,256]{1,0:T(8,128)(2,1)S(1)}, u32[]{:S(2)}, u32[]{:S(2)}) collective-permute-start(bf16[256,256]{1,0:T(8,128)(2,1)S(1)} %get-tuple-element.196), channel_id=1, source_target_pairs={{0,4},{1,5},{2,6},{3,7},{4,0},{5,1},{6,2},{7,3},{8,12},{9,13},{10,... | collective-permute-start | bytes 393224 | tf_op jit(solution)/shard_map/ppermute | solution.py:531
  323.7 20.0 %collective-permute-start.32 = (bf16[256,256]{1,0:T(8,128)(2,1)S(1)}, bf16[256,256]{1,0:T(8,128)(2,1)S(1)}, u32[]{:S(2)}, u32[]{:S(2)}) collective-permute-start(bf16[256,256]{1,0:T(8,128)(2,1)S(1)} %get-tuple-element.197), channel_id=1, source_target_pairs={{0,6},{1,7},{2,4},{3,5},{4,2},{5,3},{6,0},{7,1},{8,14},{9,15},{10,... | collective-permute-start | bytes 393224 | tf_op jit(solution)/shard_map/ppermute | solution.py:531
  346.5 46.1 %all-to-all-start.1 = ((bf16[4,64,2048]{2,1,0:T(8,128)(2,1)}), bf16[4,64,2048]{2,1,0:T(8,128)(2,1)}, u32[]{:S(2)}, u32[]{:S(2)}) async-start(bf16[4,64,2048]{2,1,0:T(8,128)(2,1)} %add_convert_fusion.1), calls=%async_computation.1 | async-start | bytes 2097152 | tf_op jit(solution)/shard_map/all_to_all | solution.py:876
  350.7 98.4 %all-gather.18.cloned.1.call-start = ((), (), s32[]{:S(2)}) async-start(), calls=%async_computation.10 | async-start | bytes 2621440 | tf_op jit(solution)/shard_map/all_gather | solution.py:964
  363.7 25.0 %collective-permute-start.36 = (bf16[1024,128]{1,0:T(8,128)(2,1)S(1)}, bf16[1024,128]{1,0:T(8,128)(2,1)S(1)}, u32[]{:S(2)}, u32[]{:S(2)}) collective-permute-start(bf16[1024,128]{1,0:T(8,128)(2,1)S(1)} %get-tuple-element.293), channel_id=1, source_target_pairs={{0,8},{8,0},{1,9},{9,1},{2,10},{10,2},{3,11},{11,3},{4,12},{12,4},... | collective-permute-start | bytes 786440 | tf_op jit(solution)/shard_map/ppermute | solution.py:537
  373.2 7.4 %collective-permute-start.37 = (bf16[256,256]{1,0:T(8,128)(2,1)S(1)}, bf16[256,256]{1,0:T(8,128)(2,1)S(1)}, u32[]{:S(2)}, u32[]{:S(2)}) collective-permute-start(bf16[256,256]{1,0:T(8,128)(2,1)S(1)} %get-tuple-element.212), channel_id=1, source_target_pairs={{0,2},{1,3},{2,0},{3,1},{4,6},{5,7},{6,4},{7,5},{8,10},{9,11},{10,... | collective-permute-start | bytes 393224 | tf_op jit(solution)/shard_map/ppermute | solution.py:531
  376.5 12.2 %collective-permute-start.38 = (bf16[256,256]{1,0:T(8,128)(2,1)S(1)}, bf16[256,256]{1,0:T(8,128)(2,1)S(1)}, u32[]{:S(2)}, u32[]{:S(2)}) collective-permute-start(bf16[256,256]{1,0:T(8,128)(2,1)S(1)} %get-tuple-element.213), channel_id=1, source_target_pairs={{0,4},{1,5},{2,6},{3,7},{4,0},{5,1},{6,2},{7,3},{8,12},{9,13},{10,... | collective-permute-start | bytes 393224 | tf_op jit(solution)/shard_map/ppermute | solution.py:531
  377.3 11.5 %collective-permute-start.39 = (bf16[256,256]{1,0:T(8,128)(2,1)S(1)}, bf16[256,256]{1,0:T(8,128)(2,1)S(1)}, u32[]{:S(2)}, u32[]{:S(2)}) collective-permute-start(bf16[256,256]{1,0:T(8,128)(2,1)S(1)} %get-tuple-element.214), channel_id=1, source_target_pairs={{0,6},{1,7},{2,4},{3,5},{4,2},{5,3},{6,0},{7,1},{8,14},{9,15},{10,... | collective-permute-start | bytes 393224 | tf_op jit(solution)/shard_map/ppermute | solution.py:531
  395.7 100.4 %all-gather.20.cloned.1.call-start = ((), (), s32[]{:S(2)}) async-start(), calls=%async_computation.11 | async-start | bytes 2621440 | tf_op jit(solution)/shard_map/all_gather | solution.py:981
  396.3 5.9 %collective-permute-start.40 = (bf16[256,128]{1,0:T(8,128)(2,1)S(1)}, bf16[256,128]{1,0:T(8,128)(2,1)S(1)}, u32[]{:S(2)}, u32[]{:S(2)}) collective-permute-start(bf16[256,128]{1,0:T(8,128)(2,1)S(1)} %copy-done.80), channel_id=1, source_target_pairs={{0,2},{1,3},{2,0},{3,1},{4,6},{5,7},{6,4},{7,5},{8,10},{9,11},{10,... | collective-permute-start | bytes 196616 | tf_op jit(solution)/shard_map/ppermute | solution.py:531
  399.1 7.4 %collective-permute-start.41 = (bf16[256,128]{1,0:T(8,128)(2,1)S(1)}, bf16[256,128]{1,0:T(8,128)(2,1)S(1)}, u32[]{:S(2)}, u32[]{:S(2)}) collective-permute-start(bf16[256,128]{1,0:T(8,128)(2,1)S(1)} %copy-done.79), channel_id=1, source_target_pairs={{0,4},{1,5},{2,6},{3,7},{4,0},{5,1},{6,2},{7,3},{8,12},{9,13},{10,... | collective-permute-start | bytes 196616 | tf_op jit(solution)/shard_map/ppermute | solution.py:531
  399.1 8.0 %collective-permute-start.42 = (bf16[256,128]{1,0:T(8,128)(2,1)S(1)}, bf16[256,128]{1,0:T(8,128)(2,1)S(1)}, u32[]{:S(2)}, u32[]{:S(2)}) collective-permute-start(bf16[256,128]{1,0:T(8,128)(2,1)S(1)} %copy-done.78), channel_id=1, source_target_pairs={{0,6},{1,7},{2,4},{3,5},{4,2},{5,3},{6,0},{7,1},{8,14},{9,15},{10,... | collective-permute-start | bytes 196616 | tf_op jit(solution)/shard_map/ppermute | solution.py:531
  416.9 16.8 %collective-permute-start.47 = (bf16[128,2048]{1,0:T(8,128)(2,1)S(1)}, bf16[128,2048]{1,0:T(8,128)(2,1)S(1)}, u32[]{:S(2)}, u32[]{:S(2)}) collective-permute-start(bf16[128,2048]{1,0:T(8,128)(2,1)S(1)} %get-tuple-element.230), channel_id=1, source_target_pairs={{0,1},{1,0},{2,3},{3,2},{4,5},{5,4},{6,7},{7,6},{8,9},{9,8},{10,11... | collective-permute-start | bytes 1572872 | tf_op jit(solution)/shard_map/ppermute | solution.py:531
  441.9 3.7 collective-permute-start.44
  445.6 3.6 collective-permute-start.45
  449.2 45.6 %collective-permute-start.46 = (bf16[4,128,2048]{2,1,0:T(8,128)(2,1)}, bf16[4,128,2048]{2,1,0:T(8,128)(2,1)S(1)}, u32[]{:S(2)}, u32[]{:S(2)}) collective-permute-start(bf16[4,128,2048]{2,1,0:T(8,128)(2,1)} %bitcast.49), channel_id=1, source_target_pairs={{0,1},{1,0},{2,3},{3,2},{4,5},{5,4},{6,7},{7,6},{8,9},{9,8},{10,11... | collective-permute-start | bytes 6291464 | tf_op jit(solution)/shard_map/ppermute | solution.py:531
  449.6 46.9 %collective-permute-start.51 = (bf16[1024,1024]{1,0:T(8,128)(2,1)}, bf16[1024,1024]{1,0:T(8,128)(2,1)}, u32[]{:S(2)}, u32[]{:S(2)}) collective-permute-start(bf16[1024,1024]{1,0:T(8,128)(2,1)} %get-tuple-element.240), channel_id=1, source_target_pairs={{0,8},{8,0},{1,9},{9,1},{2,10},{10,2},{3,11},{11,3},{4,12},{12,4},... | collective-permute-start | bytes 6291464 | tf_op jit(solution)/shard_map/ppermute | solution.py:537
  496.1 56.9 %collective-permute-start.48 = (bf16[4,128,2048]{2,1,0:T(8,128)(2,1)}, bf16[4,128,2048]{2,1,0:T(8,128)(2,1)S(1)}, u32[]{:S(2)}, u32[]{:S(2)}) collective-permute-start(bf16[4,128,2048]{2,1,0:T(8,128)(2,1)} %bitcast.47), channel_id=1, source_target_pairs={{0,1},{1,0},{2,3},{3,2},{4,5},{5,4},{6,7},{7,6},{8,9},{9,8},{10,11... | collective-permute-start | bytes 6291464 | tf_op jit(solution)/shard_map/ppermute | solution.py:531
  498.0 26.1 %collective-permute-start.52 = (bf16[512,1024]{1,0:T(8,128)(2,1)S(1)}, bf16[512,1024]{1,0:T(8,128)(2,1)S(1)}, u32[]{:S(2)}, u32[]{:S(2)}) collective-permute-start(bf16[512,1024]{1,0:T(8,128)(2,1)S(1)} %pair_sum.3), channel_id=1, source_target_pairs={{0,16},{16,0},{1,17},{17,1},{2,18},{18,2},{3,19},{19,3},{4,20},{20... | collective-permute-start | bytes 3145736 | tf_op jit(solution)/shard_map/ppermute | solution.py:534
  502.2 31.9 %collective-permute-start.50 = (bf16[512,384]{1,0:T(8,128)(2,1)S(1)}, bf16[512,384]{1,0:T(8,128)(2,1)S(1)}, u32[]{:S(2)}, u32[]{:S(2)}) collective-permute-start(bf16[512,384]{1,0:T(8,128)(2,1)S(1)} %pair_sum.2), channel_id=1, source_target_pairs={{0,16},{16,0},{1,17},{17,1},{2,18},{18,2},{3,19},{19,3},{4,20},{20... | collective-permute-start | bytes 1179656 | tf_op jit(solution)/shard_map/ppermute | solution.py:534
  524.1 8.0 %collective-permute-start.56 = (f32[2,512]{1,0:T(2,128)S(1)}, f32[2,512]{1,0:T(2,128)S(1)}, u32[]{:S(2)}, u32[]{:S(2)}) collective-permute-start(f32[2,512]{1,0:T(2,128)S(1)} %add.98), channel_id=1, source_target_pairs={{0,2},{1,3},{2,0},{3,1},{4,6},{5,7},{6,4},{7,5},{8,10},{9,11},{10,... | collective-permute-start | bytes 12296 | tf_op jit(solution)/shard_map/ppermute | solution.py:531
  529.8 18.5 %collective-permute-start.53 = (bf16[512,256]{1,0:T(8,128)(2,1)S(1)}, bf16[512,256]{1,0:T(8,128)(2,1)S(1)}, u32[]{:S(2)}, u32[]{:S(2)}) collective-permute-start(bf16[512,256]{1,0:T(8,128)(2,1)S(1)} %get-tuple-element.285), channel_id=1, source_target_pairs={{0,2},{1,3},{2,0},{3,1},{4,6},{5,7},{6,4},{7,5},{8,10},{9,11},{10,... | collective-permute-start | bytes 786440 | tf_op jit(solution)/shard_map/ppermute | solution.py:531
  529.8 18.5 %collective-permute-start.54 = (bf16[512,256]{1,0:T(8,128)(2,1)S(1)}, bf16[512,256]{1,0:T(8,128)(2,1)S(1)}, u32[]{:S(2)}, u32[]{:S(2)}) collective-permute-start(bf16[512,256]{1,0:T(8,128)(2,1)S(1)} %get-tuple-element.284), channel_id=1, source_target_pairs={{0,4},{1,5},{2,6},{3,7},{4,0},{5,1},{6,2},{7,3},{8,12},{9,13},{10,... | collective-permute-start | bytes 786440 | tf_op jit(solution)/shard_map/ppermute | solution.py:531
  532.1 16.2 %collective-permute-start.55 = (bf16[512,256]{1,0:T(8,128)(2,1)S(1)}, bf16[512,256]{1,0:T(8,128)(2,1)S(1)}, u32[]{:S(2)}, u32[]{:S(2)}) collective-permute-start(bf16[512,256]{1,0:T(8,128)(2,1)S(1)} %get-tuple-element.283), channel_id=1, source_target_pairs={{0,6},{1,7},{2,4},{3,5},{4,2},{5,3},{6,0},{7,1},{8,14},{9,15},{10,... | collective-permute-start | bytes 786440 | tf_op jit(solution)/shard_map/ppermute | solution.py:531
  534.2 13.4 %collective-permute-start.57 = (f32[2,512]{1,0:T(2,128)S(1)}, f32[2,512]{1,0:T(2,128)S(1)}, u32[]{:S(2)}, u32[]{:S(2)}) collective-permute-start(f32[2,512]{1,0:T(2,128)S(1)} %add.101), channel_id=1, source_target_pairs={{0,4},{1,5},{2,6},{3,7},{4,0},{5,1},{6,2},{7,3},{8,12},{9,13},{10,... | collective-permute-start | bytes 12296 | tf_op jit(solution)/shard_map/ppermute | solution.py:531
  (85 other events, 1252.1 us)
Sparse Core Ops, SparseCore 0:
  12.3 30.6 all-gather.15
  45.1 50.7 all-gather.11
  98.1 60.4 all-gather.9
  160.6 46.4 all-gather.13
  263.7 44.6 reduce-scatter.2
  311.5 71.7 reduce-scatter.4
  395.9 45.7 all-gather.17
  443.8 44.5 all-gather.19

commit v2 on v1

--- a/solution.py
+++ b/solution.py
@@ -122,7 +122,7 @@
 
 
 def attend_kernel(
-    rows, keys, info, q, kv, out, log_out, piece0, piece1, piece2, piece3, kv_turned, acc, high
+    rows, keys, info, q, kv, out, log_out, kv_turned, acc, high
 ):
     step = pl.program_id(0)
 
@@ -161,11 +161,6 @@
     log_out[0] = high[...] + jnp.log(total)
     result = acc[HEAD_DIM:, :] * (1.0 / total)
     out[...] = heads_tall(result, rows).T.astype(BF16)
-    for k, piece in enumerate((piece0, piece1, piece2, piece3)):
-
-        @pl.when(lax.bitwise_xor(step, info[AT_HIGH]) == k)
-        def _():
-            piece[...] = out[...]
 
 
 def attend_back_kernel(
@@ -244,15 +239,12 @@
             dkv_out[r] = dkv[pl.ds(pl.multiple_of(at, span), span), :].astype(BF16)
 
 
-def out_kernel(info, a0, a1, a2, a3, w0, w1, w2, w3, keep, send, total):
+def out_kernel(info, att, w0, w1, w2, w3, keep, send, total):
     half = keep.shape[0]
     low = info[AT_LOW]
     for place, w in enumerate((w0, w1, w2, w3)):
         cols = width_block(info, place)
-        total[...] = sum(
-            dot_nt(a[...], w[lax.bitwise_xor(info[AT_HIGH], jnp.int32(k))])
-            for k, a in enumerate((a0, a1, a2, a3))
-        )
+        total[...] = sum(dot_nt(att[k], w[k]) for k in range(4))
         keep[:, cols] = total[pl.ds(pl.multiple_of(low * half, half), half), :]
         send[:, cols] = total[pl.ds(pl.multiple_of((1 - low) * half, half), half), :].astype(BF16)
 
@@ -383,18 +375,17 @@
         piece[...] = out[pl.ds(pl.multiple_of(at, rows), rows), :]
 
 
-def one_kernel(info, q0, q1, q2, q3, k0, k1, k2, k3, w, keep, send, total):
+def one_kernel(info, q0, q1, q2, q3, k0, k1, k2, k3, w0, w1, w2, w3, keep, send, total):
     half = keep.shape[0]
     low = info[AT_LOW]
     both = [
         jnp.concatenate([q[...], k[...]], axis=1)
         for q, k in zip((q0, q1, q2, q3), (k0, k1, k2, k3))
     ]
-    for place in range(4):
+    for place, w in enumerate((w0, w1, w2, w3)):
         cols = width_block(info, place)
         total[...] = sum(
-            dot_nt(part, w[k, info[place]])
-            for k, part in enumerate(both)
+            dot_nt(part, w[k]) for k, part in enumerate(both)
         )
         keep[:, cols] = total[pl.ds(pl.multiple_of(low * half, half), half), :]
         send[:, cols] = total[pl.ds(pl.multiple_of((1 - low) * half, half), half), :].astype(BF16)
@@ -425,6 +416,21 @@
     at = info[AT_LOW] * size
     out[pl.ds(pl.multiple_of(at, size), size), :] = near[0].astype(out.dtype)
     out[pl.ds(pl.multiple_of(size - at, size), size), :] = far[0].astype(out.dtype)
+
+
+def place_own_kernel(info, near, own, far, out):
+    size = near.shape[1]
+    at = info[AT_LOW] * size
+    out[pl.ds(pl.multiple_of(at, size), size), :] = near[0].astype(out.dtype)
+    other = pl.ds(pl.multiple_of(size - at, size), size)
+
+    @pl.when(pl.program_id(0) == 0)
+    def _():
+        out[other, :] = own[...].astype(out.dtype)
+
+    @pl.when(pl.program_id(0) > 0)
+    def _():
+        out[other, :] = far[0].astype(out.dtype)
 
 
 def weight_grad_kernel(a, b, *outs):
@@ -524,6 +530,17 @@
         + [tensor_id, seq_id * 4, seq_id if fast else jnp.int32(0), tensor_id % 2, tensor_id // 2]
     )
 
+    def by_xor(parts):
+        return [
+            lax.dynamic_index_in_dim(
+                parts, lax.bitwise_xor(info[AT_HIGH], jnp.int32(k)), 0, keepdims=False
+            )
+            for k in range(4)
+        ]
+
+    def others(near):
+        return jnp.stack(by_xor(near)[1:], axis=0)
+
     def after(value, point):
         return lax.optimization_barrier((value, point))[0]
 
@@ -631,13 +648,6 @@
     positions = seq_id * span + jnp.arange(span, dtype=jnp.int32)
     cosine, sine = rope_tables(positions)
     attn_w = gather_width(attn_low, attn_low, (cosine, sine))
-    back_parts = [swap_tensor(after(back_low, attn_w[1]), mask) for mask in (2, 4, 6)]
-    gate_up_late, down_late = after((gate_up_weight, down_weight), attn_w[1])
-    gate_up_low = jnp.concatenate(
-        [gate_up_late[:, 0, :], gate_up_late[:, 1, :]], axis=1
-    ).astype(BF16)
-    down_low = down_late.astype(BF16)
-
     half_span = span // 2
     dy = pl.pallas_call(
         reorder_kernel,
@@ -679,6 +689,12 @@
         name="project",
     )(info, token_rows, *attn_w, cosine, sine)
 
+    gate_up_late, down_late = after((gate_up_weight, down_weight), queries)
+    gate_up_low = jnp.concatenate(
+        [gate_up_late[:, 0, :], gate_up_late[:, 1, :]], axis=1
+    ).astype(BF16)
+    down_low = down_late.astype(BF16)
+
     if fast:
         kv_other = swap_seq(kv_own)
         kv_all = jnp.where(
@@ -690,8 +706,8 @@
         kv_all = lax.all_gather(kv_own, "seq", axis=0, tiled=True)
 
     steps = 4
-    attended, logs, *att_pieces = pl.pallas_call(
-        functools.partial(attend_kernel, rows, keys),
+    attended, logs = pl.pallas_call(
+        functools.partial(attend_kernel, rows, max(keys, 2 * rows)),
         grid_spec=pltpu.PrefetchScalarGridSpec(
             num_scalar_prefetch=1,
             grid=(steps,),
@@ -702,8 +718,7 @@
             out_specs=[
                 pl.BlockSpec((rows, 256), lambda i, info: (i, 0)),
                 pl.BlockSpec((1, 1, GROUP * rows), lambda i, info: (i, 0, 0)),
-            ]
-            + [whole((rows, 256))] * 4,
+            ],
             scratch_shapes=[
                 pltpu.VMEM((128, length), BF16),
                 pltpu.VMEM((128, GROUP * rows), F32),
@@ -713,8 +728,7 @@
         out_shape=[
             jax.ShapeDtypeStruct((span, 256), BF16),
             jax.ShapeDtypeStruct((steps, 1, GROUP * rows), F32),
-        ]
-        + [jax.ShapeDtypeStruct((rows, 256), BF16)] * 4,
+        ],
         compiler_params=vmem(48),
         cost_estimate=cost(18),
         name="attend",
@@ -722,19 +736,18 @@
 
     gate_up_w = gather_all(gate_up_low)
     down_w = gather_all(down_low)
-    output_w = gather_width(after(output_near, queries), attended, attended)
-
-    back_near = jnp.stack(after([back_low] + back_parts, output_w[1]), axis=0)
-    back_w = lax.all_gather(back_near, ("dp", "seq"), axis=1, tiled=True)
-    back_w = back_w.reshape(4, 4, QUARTER, 384)
-
-    att_parts = after(swap_high(att_pieces), dy)
+    att_parts = lax.all_to_all(
+        attended.reshape(4, rows, 256), "tensor", 0, 0, axis_index_groups=HIGH_GROUPS
+    )
+    att_parts = after(att_parts, dy)
+    output_w = gather_width(after(output_near, queries), att_parts, att_parts)
+
     out_keep, out_send = pl.pallas_call(
         out_kernel,
         grid_spec=pltpu.PrefetchScalarGridSpec(
             num_scalar_prefetch=1,
             grid=(1,),
-            in_specs=[whole((rows, 256))] * 4 + [whole((4, QUARTER, 256))] * 4,
+            in_specs=[whole((4, rows, 256))] + [whole((4, QUARTER, 256))] * 4,
             out_specs=[whole((block, D))] * 2,
             scratch_shapes=[pltpu.VMEM((rows, QUARTER), F32)],
         ),
@@ -742,7 +755,7 @@
         compiler_params=vmem(48),
         cost_estimate=cost(3.8),
         name="attention_out",
-    )(info, *att_parts, *output_w)
+    )(info, att_parts, *output_w)
     out_got = swap_tensor(out_send, 1)
     own_rows = pl.BlockSpec((block, D), lambda i, info: (info[AT_TENSOR], 0))
     resid_one, low_a, low_b = pl.pallas_call(
@@ -815,13 +828,16 @@
         0, near_a, far_a, ()
     )
     two_got_a = swap_tensor(two_send_a, 1)
+    back_low = after(back_low, near_b)
+    back_parts = [swap_tensor(back_low, mask) for mask in (2, 4, 6)]
     mlp_keep_b, mlp_send_b, two_keep_b, two_send_b, hidden, gate_up_back, x = mlp(
         1, near_b, far_b, (hidden, gate_up_back, x)
     )
     two_got_b = swap_tensor(two_send_b, 1)
     total_a = two_keep_a.astype(F32) + after(two_got_a, two_send_b).astype(F32)
     two_a = scatter_parts(total_a)
-    hidden, gate_up_back = after((hidden, gate_up_back), total_a)
+    back_near = jnp.stack(after([back_low] + back_parts, two_send_b), axis=0)
+    hidden, gate_up_back = after((hidden, gate_up_back), (total_a, back_near))
     down_full = weight_full(dy.reshape(span, D), hidden)
     gate_up_full = weight_full(x, gate_up_back)
     total_b = two_keep_b.astype(F32) + after(
@@ -874,6 +890,7 @@
     grad_parts = swap_high(grad_pieces)
     mlp_total_b = (mlp_keep_b.astype(F32) + after(mlp_got_b, grad_parts).astype(F32)).astype(BF16)
     mlp_parts_b = lax.all_to_all(mlp_total_b, "tensor", 0, 0, axis_index_groups=HIGH_GROUPS)
+    back_w = gather_width(back_near, resid_low, resid_low)
     grad_parts = after(grad_parts, (mlp_total_b, down_grad, back_w))
 
     spans = seq_size if fast else length // span
@@ -945,7 +962,7 @@
             grid=(1,),
             in_specs=[whole((rows, 256))] * 4
             + [whole((rows, 128))] * 4
-            + [whole((4, 4, QUARTER, 384))],
+            + [whole((4, QUARTER, 384))] * 4,
             out_specs=[whole((block, D))] * 2,
             scratch_shapes=[pltpu.VMEM((rows, QUARTER), F32)],
         ),
@@ -953,12 +970,12 @@
         compiler_params=vmem(48),
         cost_estimate=cost(5.8),
         name="attention_in_back",
-    )(info, *dq_parts, *dkv_parts, back_w)
+    )(info, *dq_parts, *dkv_parts, *back_w)
     one_got = swap_tensor(one_send, 1)
     dqkv = after(jnp.concatenate([dq, dkv_low], axis=1), one_send)
     attn_halves = weight_halves(normed_one, dqkv)
     out_halves = weight_halves(
-        after(resid_both, one_send), jnp.concatenate(att_parts, axis=1)
+        after(resid_both, one_send), jnp.concatenate(by_xor(att_parts), axis=1)
     )
 
     block_near = lax.all_gather(block_low, "tensor", axis=0, axis_index_groups=HIGH_GROUPS)
@@ -978,6 +995,7 @@
         cost_estimate=cost(4.3),
         name="first_norm_back",
     )(info, one_keep, one_got, token_rows, resid_grad, gains)
+    tokens_own = swap_tensor(tokens_low, 1)
     tokens_near = lax.all_gather(tokens_low, "tensor", axis=0, axis_index_groups=HIGH_GROUPS)
 
     attn_near = scatter_near(attn_halves, one_send)
@@ -1036,7 +1054,7 @@
     )
     if fast:
         gain_grads = gain_grads[:, : 2 * QUARTER] + swap_seq(gain_grads[:, 2 * QUARTER :])
-        gains_grad = gain_grads[:, :QUARTER] + swap_dp(gain_grads[:, QUARTER:])
+        gain_grads = gain_grads + swap_tensor(gain_grads, 1)
     else:
         shard = norm_gains.shape[0]
         gains_grad = lax.dynamic_slice(
@@ -1044,10 +1062,15 @@
             (0, (dp_id * seq_size + seq_id) * shard),
             (2, shard),
         )
-    gains_grad = gains_grad + swap_tensor(gains_grad, 1)
-    block_far = swap_tensor(after(block_near, gains_grad), 1)
-    tokens_near = after(tokens_near, (gate_up_new, down_new, block_far, gains_grad))
-    tokens_far = swap_tensor(tokens_near, 1)
+        gain_grads = gains_grad + swap_tensor(gains_grad, 1)
+    block_far = swap_tensor(after(block_near, (gain_grads, tokens_own)), 1)
+    if fast:
+        gains_grad = gain_grads[:, :QUARTER] + swap_dp(gain_grads[:, QUARTER:])
+    else:
+        gains_grad = gain_grads
+    early = (gate_up_new, down_new, gains_grad) + ((out_far, attn_far) if fast else ())
+    tokens_near = after(tokens_near, early)
+    tokens_far = swap_tensor(others(tokens_near), 1)
 
     attn_terms = after(scatter_far(attn_near, attn_far), tokens_near)
     query_new = adam(
@@ -1089,7 +1112,30 @@
             name=name,
         )(info, *parts).reshape(tokens.shape)
 
-    tokens_grad = place((tokens_near, tokens_far), F32, "tokens_grad")
+    def place_own(parts, dtype, name):
+        return pl.pallas_call(
+            place_own_kernel,
+            grid_spec=pltpu.PrefetchScalarGridSpec(
+                num_scalar_prefetch=1,
+                grid=(4,),
+                in_specs=[
+                    pl.BlockSpec(
+                        (1, block, D), lambda i, info: (lax.bitwise_xor(info[AT_HIGH], i), 0, 0)
+                    ),
+                    whole((block, D)),
+                    pl.BlockSpec((1, block, D), lambda i, info: (jnp.maximum(i - 1, 0), 0, 0)),
+                ],
+                out_specs=pl.BlockSpec(
+                    (rows, D), lambda i, info: (lax.bitwise_xor(info[AT_HIGH], i), 0)
+                ),
+            ),
+            out_shape=jax.ShapeDtypeStruct((span, D), dtype),
+            compiler_params=vmem(48),
+            cost_estimate=cost(5),
+            name=name,
+        )(info, *parts).reshape(tokens.shape)
+
+    tokens_grad = place_own((tokens_near, tokens_own, tokens_far), F32, "tokens_grad")
     block_out = place((block_near, block_far), BF16, "block_out_rows")
 
     results = (query_new, output_new, kv_new, gate_up_new, down_new, gains_new)

time: 572 us -> 549 us (0.960)
  waiting for transfers between devices: 199 us -> 153 us
  starting transfers between devices: 91.5 us -> 122 us
  other arithmetic: 34.1 us -> 25.5 us
    ppermute x44 -> x42, waiting for transfers between devices: 136 us -> 103 us  [swap_tensor(): return lax.ppermute(value, 'tensor', [(i, i ^ mask) for i in range(8)])]
    ppermute x5 -> x6, waiting for transfers between devices: 57.2 us -> 34.8 us  [swap_dp(): return lax.ppermute(value, 'dp', [(0, 1), (1, 0)])]
    ppermute x44 -> x42, starting transfers between devices: 63.7 us -> 76.4 us  [swap_tensor(): return lax.ppermute(value, 'tensor', [(i, i ^ mask) for i in range(8)])]
    all_gather x1, waiting for transfers between devices: 0.01 us -> 6.43 us  [body(): lax.all_gather(tokens_low, 'tensor', axis=0, axis_index_groups=HIGH_GROUPS)]
    ppermute x9 -> x11, starting transfers between devices: 10.7 us -> 16.7 us  [swap_seq(): return lax.ppermute(value, 'seq', [(0, 1), (1, 0)])]
    pallas_call x1 -> x2, Pallas kernels: 7.75 us -> 12.3 us  [the longest x1 8.13 us: body(): pl.pallas_call(functools.partial(attend_kernel, rows, max(keys, 2 * rows)...]
    unnamed x169 -> x163, local copies, waits for them, and re-layouts: 29.3 us -> 24.9 us
  transfers between devices with their start and end apart: 68 -> 69, of which waited for: 25 -> 23; matrix products, arithmetic and copies ran while one was open for 8% -> 6% of each run, Pallas kernels for 32% -> 34%
where the time goes in v2:
time: 549 us; the launch traced here: 541 us
  Pallas kernels  188 us (34%)
  waiting for transfers between devices  153 us (28%)
  starting transfers between devices  122 us (22%)
  local copies, waits for them, and re-layouts  36.4 us (7%)
  other arithmetic  25.5 us (5%)
  between operations  15.6 us (3%)
    ppermute x42, waiting for transfers between devices, swap_tensor(): return lax.ppermute(value, 'tensor', [(i, i ^ mask) for i in range(8)])  103 us
    ppermute x42, starting transfers between devices, swap_tensor(): return lax.ppermute(value, 'tensor', [(i, i ^ mask) for i in range(8)])  76.4 us
    pallas_call x2, Pallas kernels, mlp(): pl.pallas_call(mlp_kernel, grid_spec=pltpu.PrefetchScalarGridSpec(num_sca...  45.9 us
    ppermute x6, waiting for transfers between devices, swap_dp(): return lax.ppermute(value, 'dp', [(0, 1), (1, 0)])  34.8 us
    pallas_call x4, Pallas kernels, weight_full(): pl.pallas_call(weight_grad_kernel, grid=(4,), in_specs=[pl.BlockSpec((n,...  33.4 us
    pallas_call x5, Pallas kernels, adam(): pl.pallas_call(functools.partial(adam_kernel, rate, decay), grid=(4,), in...  31 us
    unnamed x163, local copies, waits for them, and re-layouts  24.9 us
    ppermute x11, starting transfers between devices, swap_seq(): return lax.ppermute(value, 'seq', [(0, 1), (1, 0)])  16.7 us
  transfers between devices with their start and end apart: 69, of which 23 were waited for; matrix products, arithmetic and copies ran while one was open for 6% of the time, Pallas kernels for 34%

profile of v2, /device:TPU:0, one launch (start us, length us, event | category | flops | bytes accessed | tf_op | source)
XLA Modules:
  0.0 540.7 jit_solution(10182448996334565347)
XLA Ops:
  12.2 3.0 collective-permute-start
  18.1 9.1 %collective-permute-done.w1 = bf16[512,512]{1,0:T(8,128)(2,1)S(1)} collective-permute-done((bf16[512,512]{1,0:T(8,128)(2,1)S(1)}, bf16[512,512]{1,0:T(8,128)(2,1)S(1)}, u32[]{:S(2)}, u32[]{:S(2)}) %collective-permute-start) | collective-permute-done | bytes 524320 | tf_op jit(solution)/shard_map/ppermute | solution.py:551
  30.4 7.1 %project.1 = (bf16[1024,2048]{1,0:T(8,128)(2,1)}, bf16[1024,256]{1,0:T(8,128)(2,1)S(1)}, bf16[1024,128]{1,0:T(8,128)(2,1)S(1)}, f32[8,2048]{1,0:T(8,128)S(1)}) custom-call(s32[9]{0:T(128)S(1)} %stack.69.info, bf16[1024,2048]{1,0:T(8,128)(2,1)} %bitcast.60, bf16[512,512]{1,0:T(8,128)(2,1)S(1)} %copy-done.23, bf16[512,512]{1,0:T(8,128)(2,1)S(1)} %collective-permute-done.w1, ...), custom_call_target="tpu_custom_call" | custom-call | bytes 12915000 | tf_op jit(solution)/shard_map/project/pallas_call | solution.py:665
  39.3 3.3 copy.51
  46.5 8.1 %attend.1 = (bf16[1024,256]{1,0:T(8,128)(2,1)}, f32[4,1,1024]{2,1,0:T(1,128)S(1)}) custom-call(s32[9]{0:T(128)S(1)} %stack.69.info, bf16[1024,256]{1,0:T(8,128)(2,1)S(1)} %get-tuple-element.142.q, bf16[2048,128]{1,0:T(8,128)(2,1)S(1)} %maximum_select_fusion.kv), custom_call_target="tpu_custom_call" | custom-call | bytes 33210000 | tf_op jit(solution)/shard_map/attend/pallas_call | solution.py:709
  55.4 4.9 all-to-all-start
  60.8 7.4 %reorder.1.dy.refs_9_ = bf16[2,512,2048]{2,1,0:T(8,128)(2,1)} custom-call(s32[9]{0:T(128)} %copy-done.37, bf16[1024,2048]{1,0:T(8,128)(2,1)} %bitcast.64), custom_call_target="tpu_custom_call" | custom-call | bytes 13837500 | tf_op jit(solution)/shard_map/reorder/pallas_call | solution.py:652
  68.2 2.4 all-to-all-done.att
  70.6 6.6 %collective-permute-start.5 = (bf16[4,512,256]{2,1,0:T(8,128)(2,1)S(1)}, bf16[4,512,256]{2,1,0:T(8,128)(2,1)S(1)}, u32[]{:S(2)}, u32[]{:S(2)}) collective-permute-start(bf16[4,512,256]{2,1,0:T(8,128)(2,1)S(1)} %bitcast.54), channel_id=1, source_target_pairs={{0,8},{8,0},{1,9},{9,1},{2,10},{10,2},{3,11},{11,3},{4,12},{12,4},... | collective-permute-start | bytes 3145736 | tf_op jit(solution)/shard_map/ppermute | solution.py:554
  77.2 9.5 %collective-permute-done.4.w1 = bf16[4,512,256]{2,1,0:T(8,128)(2,1)} collective-permute-done((bf16[4,512,256]{2,1,0:T(8,128)(2,1)}, bf16[4,512,256]{2,1,0:T(8,128)(2,1)}, u32[]{:S(2)}, u32[]{:S(2)}) %collective-permute-start.4) | collective-permute-done | bytes 1048608 | tf_op jit(solution)/shard_map/ppermute | solution.py:551
  86.7 2.9 collective-permute-done.6.w3
  90.5 3.4 attention_out.1
  96.2 12.7 %collective-permute-done.7.got = bf16[128,2048]{1,0:T(8,128)(2,1)S(1)} collective-permute-done((bf16[128,2048]{1,0:T(8,128)(2,1)S(1)}, bf16[128,2048]{1,0:T(8,128)(2,1)S(1)}, u32[]{:S(2)}, u32[]{:S(2)}) %collective-permute-start.7) | collective-permute-done | bytes 524320 | tf_op jit(solution)/shard_map/ppermute | solution.py:548
  109.7 3.6 second_norm.1
  114.8 2.7 collective-permute-start.9
  118.8 7.0 %collective-permute-done.8 = bf16[64,2048]{1,0:T(8,128)(2,1)S(1)} collective-permute-done((bf16[64,2048]{1,0:T(8,128)(2,1)}, bf16[64,2048]{1,0:T(8,128)(2,1)S(1)}, u32[]{:S(2)}, u32[]{:S(2)}) %collective-permute-start.8) | collective-permute-done | bytes 262176 | tf_op jit(solution)/shard_map/ppermute | solution.py:548
  125.8 10.6 %collective-permute-done.9 = bf16[64,2048]{1,0:T(8,128)(2,1)S(1)} collective-permute-done((bf16[64,2048]{1,0:T(8,128)(2,1)}, bf16[64,2048]{1,0:T(8,128)(2,1)S(1)}, u32[]{:S(2)}, u32[]{:S(2)}) %collective-permute-start.9) | collective-permute-done | bytes 262176 | tf_op jit(solution)/shard_map/ppermute | solution.py:548
  138.1 4.3 collective-permute-start.12
  144.9 5.8 %collective-permute-done.12 = bf16[64,2048]{1,0:T(8,128)(2,1)S(1)} collective-permute-done((bf16[64,2048]{1,0:T(8,128)(2,1)S(1)}, bf16[64,2048]{1,0:T(8,128)(2,1)S(1)}, u32[]{:S(2)}, u32[]{:S(2)}) %collective-permute-start.12) | collective-permute-done | bytes 262176 | tf_op jit(solution)/shard_map/ppermute | solution.py:548
  150.8 12.6 %collective-permute-done.13 = bf16[64,2048]{1,0:T(8,128)(2,1)S(1)} collective-permute-done((bf16[64,2048]{1,0:T(8,128)(2,1)S(1)}, bf16[64,2048]{1,0:T(8,128)(2,1)S(1)}, u32[]{:S(2)}, u32[]{:S(2)}) %collective-permute-start.13) | collective-permute-done | bytes 262176 | tf_op jit(solution)/shard_map/ppermute | solution.py:548
  164.0 22.8 %mlp.2 = (bf16[4,64,2048]{2,1,0:T(8,128)(2,1)}, bf16[4,64,2048]{2,1,0:T(8,128)(2,1)}, bf16[256,2048]{1,0:T(8,128)(2,1)}, bf16[256,2048]{1,0:T(8,128)(2,1)}, bf16...) custom-call(s32[9]{0:T(128)} %copy-done.37, bf16[256,2048]{1,0:T(8,128)(2,1)} %copy-done.54, ...), custom_call_target="tpu_custom_call" | custom-call | bytes 41512500 | tf_op jit(solution)/shard_map/mlp/pallas_call | solution.py:785
  188.5 3.5 collective-permute-start.18
  194.5 23.1 %mlp.3 = (bf16[4,64,2048]{2,1,0:T(8,128)(2,1)}, bf16[4,64,2048]{2,1,0:T(8,128)(2,1)}, bf16[256,2048]{1,0:T(8,128)(2,1)}, bf16[256,2048]{1,0:T(8,128)(2,1)}, bf16...) custom-call(s32[9]{0:T(128)} %copy-done.37, ...), custom_call_target="tpu_custom_call", output_to_operand_aliasing={{4}: (6, {}), {5}: (7, {}), {6}: (8, {})} | custom-call | bytes 41512500 | tf_op jit(solution)/shard_map/mlp/pallas_call | solution.py:785
  225.0 13.3 %weight_grad.5 = bf16[2048,2048]{1,0:T(8,128)(2,1)} custom-call(bf16[1024,2048]{1,0:T(8,128)(2,1)} %get-tuple-element.176.a, bf16[1024,2048]{1,0:T(8,128)(2,1)} %get-tuple-element.177.b), custom_call_target="tpu_custom_call" | custom-call | bytes 24182784 | tf_op jit(solution)/shard_map/weight_grad/pallas_call | solution.py:582
  238.4 8.4 %weight_grad.4 = bf16[2048,1024]{1,0:T(8,128)(2,1)} custom-call(bf16[1024,2048]{1,0:T(8,128)(2,1)} %bitcast.59, bf16[1024,1024]{1,0:T(8,128)(2,1)} %get-tuple-element.175.b), custom_call_target="tpu_custom_call" | custom-call | bytes 12091392 | tf_op jit(solution)/shard_map/weight_grad/pallas_call | solution.py:582
  246.8 3.7 fusion.8
  253.9 17.2 %collective-permute-start.25 = (bf16[64,2048]{1,0:T(8,128)(2,1)S(1)}, bf16[64,2048]{1,0:T(8,128)(2,1)S(1)}, u32[]{:S(2)}, u32[]{:S(2)}) collective-permute-start(bf16[64,2048]{1,0:T(8,128)(2,1)S(1)} %get-tuple-element.282), channel_id=1, source_target_pairs={{0,2},{1,3},{2,0},{3,1},{4,6},{5,7},{6,4},{7,5},{8,10},{9,11},{10,... | collective-permute-start | bytes 786440 | tf_op jit(solution)/shard_map/ppermute | solution.py:548
  273.6 2.6 collective-permute-start.33
  278.1 6.1 %collective-permute-done.26.refs_6_ = bf16[64,2048]{1,0:T(8,128)(2,1)} collective-permute-done((bf16[64,2048]{1,0:T(8,128)(2,1)S(1)}, bf16[64,2048]{1,0:T(8,128)(2,1)}, u32[]{:S(2)}, u32[]{:S(2)}) %collective-permute-start.26) | collective-permute-done | bytes 262176 | tf_op jit(solution)/shard_map/ppermute | solution.py:548
  284.2 5.3 second_norm_back.1
  291.1 2.9 add_convert_fusion.2
  294.0 6.7 %collective-permute-done.28.other = bf16[128,2048]{1,0:T(8,128)(2,1)S(1)} collective-permute-done((bf16[128,2048]{1,0:T(8,128)(2,1)}, bf16[128,2048]{1,0:T(8,128)(2,1)S(1)}, u32[]{:S(2)}, u32[]{:S(2)}) %collective-permute-start.28) | collective-permute-done | bytes 524320 | tf_op jit(solution)/shard_map/ppermute | solution.py:548
  303.2 8.1 %all-to-all-start.1 = ((bf16[4,64,2048]{2,1,0:T(8,128)(2,1)}), bf16[4,64,2048]{2,1,0:T(8,128)(2,1)}, u32[]{:S(2)}, u32[]{:S(2)}) async-start(bf16[4,64,2048]{2,1,0:T(8,128)(2,1)} %add_convert_fusion.2), calls=%async_computation.1 | async-start | bytes 2097152 | tf_op jit(solution)/shard_map/all_to_all | solution.py:873
  315.9 3.4 attention_out_back.1
  320.3 2.5 collective-permute-start.30
  325.2 2.9 collective-permute-done.30.grad1
  332.2 2.7 add_convert_fusion.1
  334.9 4.3 all-to-all-start.2
  344.0 11.5 %attend_back.1 = (bf16[1024,256]{1,0:T(8,128)(2,1)S(1)}, bf16[256,256]{1,0:T(8,128)(2,1)S(1)}, bf16[256,256]{1,0:T(8,128)(2,1)S(1)}, bf16[256,256]{1,0:T(8,128)(...) custom-call(s32[9]{0:T(128)S(1)} %copy-done.39, bf16[1024,256]{1,0:T(8,128)(2,1)S(1)} %copy-done.15, ...), custom_call_target="tpu_custom_call" | custom-call | bytes 42435000 | tf_op jit(solution)/shard_map/attend_back/pallas_call | solution.py:897
  357.0 9.2 %collective-permute-start.36 = (bf16[1024,128]{1,0:T(8,128)(2,1)S(1)}, bf16[1024,128]{1,0:T(8,128)(2,1)S(1)}, u32[]{:S(2)}, u32[]{:S(2)}) collective-permute-start(bf16[1024,128]{1,0:T(8,128)(2,1)S(1)} %get-tuple-element.290), channel_id=1, source_target_pairs={{0,8},{8,0},{1,9},{9,1},{2,10},{10,2},{3,11},{11,3},{4,12},{12,4},... | collective-permute-start | bytes 786440 | tf_op jit(solution)/shard_map/ppermute | solution.py:554
  368.2 2.3 collective-permute-start.38
  370.7 2.8 collective-permute-done.37.q1
  373.4 7.6 %collective-permute-done.38.q2 = bf16[256,256]{1,0:T(8,128)(2,1)S(1)} collective-permute-done((bf16[256,256]{1,0:T(8,128)(2,1)S(1)}, bf16[256,256]{1,0:T(8,128)(2,1)S(1)}, u32[]{:S(2)}, u32[]{:S(2)}) %collective-permute-start.38) | collective-permute-done | bytes 131104 | tf_op jit(solution)/shard_map/ppermute | solution.py:548
  381.8 3.1 kv_back.1
  385.0 3.0 block_out.1
  388.3 2.2 collective-permute-start.40
  393.0 4.6 collective-permute-done.41.k2
  397.7 6.1 %attention_in_back.1 = (f32[128,2048]{1,0:T(8,128)S(1)}, bf16[128,2048]{1,0:T(8,128)(2,1)}) custom-call(s32[9]{0:T(128)S(1)} %copy-done.40, bf16[256,256]{1,0:T(8,128)(2,1)S(1)} %get-tuple-element.201.q0, bf16[256,256]{1,0:T(8,128)(2,1)S(1)} %collective-permute-done.37.q1, bf16[256,256]{1,0:T(8,128)(2,1)S(1)} %collective-permute-done.38.q2, ...), custom_call_target="tpu_custom_call" | custom-call | bytes 10701000 | tf_op jit(solution)/shard_map/attention_in_back/pallas_call | solution.py:958
  406.1 5.5 %weight_grad.7 = (bf16[1024,1024]{1,0:T(8,128)(2,1)}, bf16[1024,1024]{1,0:T(8,128)(2,1)}) custom-call(bf16[256,2048]{1,0:T(8,128)(2,1)} %copy-done.24, bf16[256,1024]{1,0:T(8,128)(2,1)} %pad_maximum_fusion.6.b), custom_call_target="tpu_custom_call" | custom-call | bytes 3022848 | tf_op jit(solution)/shard_map/weight_grad/pallas_call | solution.py:582
  412.6 6.1 %weight_grad.6 = (bf16[1024,384]{1,0:T(8,128)(2,1)}, bf16[1024,384]{1,0:T(8,128)(2,1)}) custom-call(bf16[1024,2048]{1,0:T(8,128)(2,1)} %get-tuple-element.209.a, bf16[1024,384]{1,0:T(8,128)(2,1)} %pad_maximum_fusion.3.b), custom_call_target="tpu_custom_call" | custom-call | bytes 4534272 | tf_op jit(solution)/shard_map/weight_grad/pallas_call | solution.py:582
  419.5 4.1 first_norm_back.1
  426.8 2.5 pair_sum.2
  429.3 2.5 collective-permute-start.50
  435.8 10.3 %collective-permute-done.44 = f32[2,1024]{1,0:T(2,128)S(1)} collective-permute-done((f32[2,1024]{1,0:T(2,128)S(1)}, f32[2,1024]{1,0:T(2,128)S(1)}, u32[]{:S(2)}, u32[]{:S(2)}) %collective-permute-start.44) | collective-permute-done | bytes 8224 | tf_op jit(solution)/shard_map/ppermute | solution.py:548
  447.8 16.2 %collective-permute-done.48 = f32[2,512]{1,0:T(2,128)S(1)} collective-permute-done((f32[2,512]{1,0:T(2,128)S(1)}, f32[2,512]{1,0:T(2,128)S(1)}, u32[]{:S(2)}, u32[]{:S(2)}) %collective-permute-start.48) | collective-permute-done | bytes 4128 | tf_op jit(solution)/shard_map/ppermute | solution.py:551
  464.0 13.2 %adam.5 = (f32[512,2,1024]{2,1,0:T(2,128)}, f32[512,2,1024]{2,1,0:T(2,128)}, f32[512,2,1024]{2,1,0:T(2,128)}) custom-call(f32[512,2,1024]{2,1,0:T(2,128)} %weight.5, f32[512,2,1024]{2,1,0:T(2,128)} %one.5, f32[512,2,1024]{2,1,0:T(2,128)} %two.5, bf16[512,2048]{1,0:T(8,128)(2,1)} %reduce-scatter.5.cloned.1.call-done.refs_0_), custom_call_target="tpu_custom_call" | custom-call | bytes 25794968 | tf_op jit(solution)/shard_map/adam/pallas_call | solution.py:1012
  477.2 6.7 %adam.6 = (f32[512,1024]{1,0:T(8,128)}, f32[512,1024]{1,0:T(8,128)}, f32[512,1024]{1,0:T(8,128)}) custom-call(f32[512,1024]{1,0:T(8,128)} %weight.6, f32[512,1024]{1,0:T(8,128)} %one.6, f32[512,1024]{1,0:T(8,128)} %two.6, bf16[512,1024]{1,0:T(8,128)(2,1)} %reduce-scatter.3.cloned.1.call-done.refs_0_), custom_call_target="tpu_custom_call" | custom-call | bytes 12897484 | tf_op jit(solution)/shard_map/adam/pallas_call | solution.py:1012
  483.9 6.4 %all-gather.17.cloned.1.call-done = bf16[512,2048]{1,0:T(8,128)(2,1)} async-done(((bf16[128,2048]{1,0:T(8,128)(2,1)}), bf16[512,2048]{1,0:T(8,128)(2,1)}) %all-gather.17.cloned.1.call-update) | async-done | bytes 2097168 | tf_op jit(solution)/shard_map/all_gather | solution.py:999
  501.8 4.7 block_out_rows.1
  506.6 3.3 adam.9
  509.9 3.9 adam.7
  513.8 10.0 %collective-permute-done.58 = f32[2,512]{1,0:T(2,128)S(1)} collective-permute-done((f32[2,512]{1,0:T(2,128)S(1)}, f32[2,512]{1,0:T(2,128)S(1)}, u32[]{:S(2)}, u32[]{:S(2)}) %collective-permute-start.58) | collective-permute-done | bytes 4128 | tf_op jit(solution)/shard_map/ppermute | solution.py:548
  525.3 3.9 adam.8
  529.2 4.2 tokens_grad.1
  (325 shorter events, 102.2 us)
Async XLA Ops:
  7.2 37.4 %all-gather.13.cloned.1.call-start = ((), (), s32[]{:S(2)}) async-start(), calls=%async_computation.9 | async-start | bytes 1310720 | tf_op jit(solution)/shard_map/all_gather | solution.py:645
  12.2 151.8 %all-gather.11.cloned.1.call-start = ((), (), s32[]{:S(2)}) async-start(), calls=%async_computation.6 | async-start | bytes 5242880 | tf_op jit(solution)/shard_map/all_gather | solution.py:568
  12.2 15.0 %collective-permute-start = (bf16[512,512]{1,0:T(8,128)(2,1)S(1)}, bf16[512,512]{1,0:T(8,128)(2,1)S(1)}, u32[]{:S(2)}, u32[]{:S(2)}) collective-permute-start(bf16[512,512]{1,0:T(8,128)(2,1)S(1)} %fusion.1.w0), channel_id=1, source_target_pairs={{0,16},{16,0},{1,17},{17,1},{2,18},{18,2},{3,19},{19,3},{4,20},{20... | collective-permute-start | bytes 1572872 | tf_op jit(solution)/shard_map/ppermute | solution.py:551
  15.3 12.0 %collective-permute-start.1 = (bf16[512,512]{1,0:T(8,128)(2,1)S(1)}, bf16[512,512]{1,0:T(8,128)(2,1)S(1)}, u32[]{:S(2)}, u32[]{:S(2)}) collective-permute-start(bf16[512,512]{1,0:T(8,128)(2,1)S(1)} %fusion.1.w0), channel_id=1, source_target_pairs={{0,8},{8,0},{1,9},{9,1},{2,10},{10,2},{3,11},{11,3},{4,12},{12,4},... | collective-permute-start | bytes 1572872 | tf_op jit(solution)/shard_map/ppermute | solution.py:554
  39.3 124.8 %all-gather.9.cloned.1.call-start = ((), (), s32[]{:S(2)}) async-start(), calls=%async_computation.5 | async-start | bytes 10485760 | tf_op jit(solution)/shard_map/all_gather | solution.py:568
  44.6 42.1 %collective-permute-start.4 = (bf16[4,512,256]{2,1,0:T(8,128)(2,1)}, bf16[4,512,256]{2,1,0:T(8,128)(2,1)}, u32[]{:S(2)}, u32[]{:S(2)}) collective-permute-start(bf16[4,512,256]{2,1,0:T(8,128)(2,1)} %bitcast.53), channel_id=1, source_target_pairs={{0,16},{16,0},{1,17},{17,1},{2,18},{18,2},{3,19},{19,3},{4,20},{20... | collective-permute-start | bytes 3145736 | tf_op jit(solution)/shard_map/ppermute | solution.py:551
  55.4 15.2 %all-to-all-start = ((bf16[4,256,256]{2,1,0:T(8,128)(2,1)}), bf16[4,256,256]{2,1,0:T(8,128)(2,1)S(1)}, u32[]{:S(2)}, u32[]{:S(2)}) async-start(bf16[4,256,256]{2,1,0:T(8,128)(2,1)} %bitcast.10), calls=%async_computation | async-start | bytes 1048576 | tf_op jit(solution)/shard_map/all_to_all | solution.py:739
  60.3 279.0 %reduce-scatter.3.cloned.1.call-start = ((), (), s32[]{:S(2)}) async-start(), calls=%async_computation.7 | async-start | bytes 5242880 | tf_op jit(solution)/shard_map/reduce_scatter | solution.py:571
  70.6 16.1 %collective-permute-start.5 = (bf16[4,512,256]{2,1,0:T(8,128)(2,1)S(1)}, bf16[4,512,256]{2,1,0:T(8,128)(2,1)S(1)}, u32[]{:S(2)}, u32[]{:S(2)}) collective-permute-start(bf16[4,512,256]{2,1,0:T(8,128)(2,1)S(1)} %bitcast.54), channel_id=1, source_target_pairs={{0,8},{8,0},{1,9},{9,1},{2,10},{10,2},{3,11},{11,3},{4,12},{12,4},... | collective-permute-start | bytes 3145736 | tf_op jit(solution)/shard_map/ppermute | solution.py:554
  94.9 14.0 %collective-permute-start.7 = (bf16[128,2048]{1,0:T(8,128)(2,1)S(1)}, bf16[128,2048]{1,0:T(8,128)(2,1)S(1)}, u32[]{:S(2)}, u32[]{:S(2)}) collective-permute-start(bf16[128,2048]{1,0:T(8,128)(2,1)S(1)} %get-tuple-element.151), channel_id=1, source_target_pairs={{0,1},{1,0},{2,3},{3,2},{4,5},{5,4},{6,7},{7,6},{8,9},{9,8},{10,11... | collective-permute-start | bytes 1572872 | tf_op jit(solution)/shard_map/ppermute | solution.py:548
  113.3 12.5 %collective-permute-start.8 = (bf16[64,2048]{1,0:T(8,128)(2,1)}, bf16[64,2048]{1,0:T(8,128)(2,1)S(1)}, u32[]{:S(2)}, u32[]{:S(2)}) collective-permute-start(bf16[64,2048]{1,0:T(8,128)(2,1)} %get-tuple-element.153), channel_id=1, source_target_pairs={{0,2},{1,3},{2,0},{3,1},{4,6},{5,7},{6,4},{7,5},{8,10},{9,11},{10,... | collective-permute-start | bytes 786440 | tf_op jit(solution)/shard_map/ppermute | solution.py:548
  114.8 21.6 %collective-permute-start.9 = (bf16[64,2048]{1,0:T(8,128)(2,1)}, bf16[64,2048]{1,0:T(8,128)(2,1)S(1)}, u32[]{:S(2)}, u32[]{:S(2)}) collective-permute-start(bf16[64,2048]{1,0:T(8,128)(2,1)} %get-tuple-element.153), channel_id=1, source_target_pairs={{0,4},{1,5},{2,6},{3,7},{4,0},{5,1},{6,2},{7,3},{8,12},{9,13},{10,... | collective-permute-start | bytes 786440 | tf_op jit(solution)/shard_map/ppermute | solution.py:548
  118.5 17.9 %collective-permute-start.10 = (bf16[64,2048]{1,0:T(8,128)(2,1)}, bf16[64,2048]{1,0:T(8,128)(2,1)S(1)}, u32[]{:S(2)}, u32[]{:S(2)}) collective-permute-start(bf16[64,2048]{1,0:T(8,128)(2,1)} %get-tuple-element.153), channel_id=1, source_target_pairs={{0,6},{1,7},{2,4},{3,5},{4,2},{5,3},{6,0},{7,1},{8,14},{9,15},{10,... | collective-permute-start | bytes 786440 | tf_op jit(solution)/shard_map/ppermute | solution.py:548
  136.5 27.5 %collective-permute-start.11 = (bf16[256,2048]{1,0:T(8,128)(2,1)S(1)}, bf16[256,2048]{1,0:T(8,128)(2,1)}, u32[]{:S(2)}, u32[]{:S(2)}) collective-permute-start(bf16[256,2048]{1,0:T(8,128)(2,1)S(1)} %constant_dynamic-update-slice_fusion.near), channel_id=1, source_target_pairs={{0,1},{1,0},{2,3},{3,2},{4,5},{5,4},{6,7},{7,6},{8,9},{9,8},{10,11... | collective-permute-start | bytes 3145736 | tf_op jit(solution)/shard_map/ppermute | solution.py:548
  138.1 12.7 %collective-permute-start.12 = (bf16[64,2048]{1,0:T(8,128)(2,1)S(1)}, bf16[64,2048]{1,0:T(8,128)(2,1)S(1)}, u32[]{:S(2)}, u32[]{:S(2)}) collective-permute-start(bf16[64,2048]{1,0:T(8,128)(2,1)S(1)} %copy-done.68), channel_id=1, source_target_pairs={{0,2},{1,3},{2,0},{3,1},{4,6},{5,7},{6,4},{7,5},{8,10},{9,11},{10,... | collective-permute-start | bytes 786440 | tf_op jit(solution)/shard_map/ppermute | solution.py:548
  142.4 21.0 %collective-permute-start.13 = (bf16[64,2048]{1,0:T(8,128)(2,1)S(1)}, bf16[64,2048]{1,0:T(8,128)(2,1)S(1)}, u32[]{:S(2)}, u32[]{:S(2)}) collective-permute-start(bf16[64,2048]{1,0:T(8,128)(2,1)S(1)} %copy-done.68), channel_id=1, source_target_pairs={{0,4},{1,5},{2,6},{3,7},{4,0},{5,1},{6,2},{7,3},{8,12},{9,13},{10,... | collective-permute-start | bytes 786440 | tf_op jit(solution)/shard_map/ppermute | solution.py:548
  143.4 20.0 %collective-permute-start.14 = (bf16[64,2048]{1,0:T(8,128)(2,1)S(1)}, bf16[64,2048]{1,0:T(8,128)(2,1)S(1)}, u32[]{:S(2)}, u32[]{:S(2)}) collective-permute-start(bf16[64,2048]{1,0:T(8,128)(2,1)S(1)} %copy-done.68), channel_id=1, source_target_pairs={{0,6},{1,7},{2,4},{3,5},{4,2},{5,3},{6,0},{7,1},{8,14},{9,15},{10,... | collective-permute-start | bytes 786440 | tf_op jit(solution)/shard_map/ppermute | solution.py:548
  163.5 31.0 %collective-permute-start.15 = (bf16[256,2048]{1,0:T(8,128)(2,1)S(1)}, bf16[256,2048]{1,0:T(8,128)(2,1)}, u32[]{:S(2)}, u32[]{:S(2)}) collective-permute-start(bf16[256,2048]{1,0:T(8,128)(2,1)S(1)} %constant_dynamic-update-slice_fusion.4.near), channel_id=1, source_target_pairs={{0,1},{1,0},{2,3},{3,2},{4,5},{5,4},{6,7},{7,6},{8,9},{9,8},{10,11... | collective-permute-start | bytes 3145736 | tf_op jit(solution)/shard_map/ppermute | solution.py:548
  186.9 31.3 %collective-permute-start.17 = (bf16[256,2048]{1,0:T(8,128)(2,1)}, bf16[256,2048]{1,0:T(8,128)(2,1)S(1)}, u32[]{:S(2)}, u32[]{:S(2)}) collective-permute-start(bf16[256,2048]{1,0:T(8,128)(2,1)} %get-tuple-element.168), channel_id=1, source_target_pairs={{0,1},{1,0},{2,3},{3,2},{4,5},{5,4},{6,7},{7,6},{8,9},{9,8},{10,11... | collective-permute-start | bytes 3145736 | tf_op jit(solution)/shard_map/ppermute | solution.py:548
  188.5 32.1 %collective-permute-start.18 = (bf16[512,384]{1,0:T(8,128)(2,1)S(1)}, bf16[512,384]{1,0:T(8,128)(2,1)S(1)}, u32[]{:S(2)}, u32[]{:S(2)}) collective-permute-start(bf16[512,384]{1,0:T(8,128)(2,1)S(1)} %pad_maximum_fusion.7), channel_id=1, source_target_pairs={{0,2},{1,3},{2,0},{3,1},{4,6},{5,7},{6,4},{7,5},{8,10},{9,11},{10,... | collective-permute-start | bytes 1179656 | tf_op jit(solution)/shard_map/ppermute | solution.py:548
  192.0 30.4 %collective-permute-start.19 = (bf16[512,384]{1,0:T(8,128)(2,1)S(1)}, bf16[512,384]{1,0:T(8,128)(2,1)S(1)}, u32[]{:S(2)}, u32[]{:S(2)}) collective-permute-start(bf16[512,384]{1,0:T(8,128)(2,1)S(1)} %pad_maximum_fusion.7), channel_id=1, source_target_pairs={{0,4},{1,5},{2,6},{3,7},{4,0},{5,1},{6,2},{7,3},{8,12},{9,13},{10,... | collective-permute-start | bytes 1179656 | tf_op jit(solution)/shard_map/ppermute | solution.py:548
  193.0 31.0 %collective-permute-start.20 = (bf16[512,384]{1,0:T(8,128)(2,1)S(1)}, bf16[512,384]{1,0:T(8,128)(2,1)S(1)}, u32[]{:S(2)}, u32[]{:S(2)}) collective-permute-start(bf16[512,384]{1,0:T(8,128)(2,1)S(1)} %pad_maximum_fusion.7), channel_id=1, source_target_pairs={{0,6},{1,7},{2,4},{3,5},{4,2},{5,3},{6,0},{7,1},{8,14},{9,15},{10,... | collective-permute-start | bytes 1179656 | tf_op jit(solution)/shard_map/ppermute | solution.py:548
  217.6 29.2 %collective-permute-start.16 = (bf16[256,2048]{1,0:T(8,128)(2,1)}, bf16[256,2048]{1,0:T(8,128)(2,1)}, u32[]{:S(2)}, u32[]{:S(2)}) collective-permute-start(bf16[256,2048]{1,0:T(8,128)(2,1)} %get-tuple-element.164), channel_id=1, source_target_pairs={{0,1},{1,0},{2,3},{3,2},{4,5},{5,4},{6,7},{7,6},{8,9},{9,8},{10,11... | collective-permute-start | bytes 3145736 | tf_op jit(solution)/shard_map/ppermute | solution.py:548
  219.5 27.3 %collective-permute-start.21 = (bf16[64,2048]{1,0:T(8,128)(2,1)}, bf16[64,2048]{1,0:T(8,128)(2,1)S(1)}, u32[]{:S(2)}, u32[]{:S(2)}) collective-permute-start(bf16[64,2048]{1,0:T(8,128)(2,1)} %get-tuple-element.285), channel_id=1, source_target_pairs={{0,2},{1,3},{2,0},{3,1},{4,6},{5,7},{6,4},{7,5},{8,10},{9,11},{10,... | collective-permute-start | bytes 786440 | tf_op jit(solution)/shard_map/ppermute | solution.py:548
  220.6 26.2 %collective-permute-start.22 = (bf16[64,2048]{1,0:T(8,128)(2,1)}, bf16[64,2048]{1,0:T(8,128)(2,1)}, u32[]{:S(2)}, u32[]{:S(2)}) collective-permute-start(bf16[64,2048]{1,0:T(8,128)(2,1)} %get-tuple-element.284), channel_id=1, source_target_pairs={{0,4},{1,5},{2,6},{3,7},{4,0},{5,1},{6,2},{7,3},{8,12},{9,13},{10,... | collective-permute-start | bytes 786440 | tf_op jit(solution)/shard_map/ppermute | solution.py:548
  222.4 24.4 %collective-permute-start.23 = (bf16[64,2048]{1,0:T(8,128)(2,1)}, bf16[64,2048]{1,0:T(8,128)(2,1)}, u32[]{:S(2)}, u32[]{:S(2)}) collective-permute-start(bf16[64,2048]{1,0:T(8,128)(2,1)} %get-tuple-element.283), channel_id=1, source_target_pairs={{0,6},{1,7},{2,4},{3,5},{4,2},{5,3},{6,0},{7,1},{8,14},{9,15},{10,... | collective-permute-start | bytes 786440 | tf_op jit(solution)/shard_map/ppermute | solution.py:548
  250.6 147.1 %reduce-scatter.5.cloned.1.call-start = ((), (), s32[]{:S(2)}) async-start(), calls=%async_computation.8 | async-start | bytes 10485760 | tf_op jit(solution)/shard_map/reduce_scatter | solution.py:571
  251.2 39.9 %collective-permute-start.24 = (bf16[4,64,2048]{2,1,0:T(8,128)(2,1)}, bf16[4,64,2048]{2,1,0:T(8,128)(2,1)}, u32[]{:S(2)}, u32[]{:S(2)}) collective-permute-start(bf16[4,64,2048]{2,1,0:T(8,128)(2,1)} %get-tuple-element.179), channel_id=1, source_target_pairs={{0,1},{1,0},{2,3},{3,2},{4,5},{5,4},{6,7},{7,6},{8,9},{9,8},{10,11... | collective-permute-start | bytes 3145736 | tf_op jit(solution)/shard_map/ppermute | solution.py:548
  253.9 24.2 %collective-permute-start.25 = (bf16[64,2048]{1,0:T(8,128)(2,1)S(1)}, bf16[64,2048]{1,0:T(8,128)(2,1)S(1)}, u32[]{:S(2)}, u32[]{:S(2)}) collective-permute-start(bf16[64,2048]{1,0:T(8,128)(2,1)S(1)} %get-tuple-element.282), channel_id=1, source_target_pairs={{0,2},{1,3},{2,0},{3,1},{4,6},{5,7},{6,4},{7,5},{8,10},{9,11},{10,... | collective-permute-start | bytes 786440 | tf_op jit(solution)/shard_map/ppermute | solution.py:548
  271.1 13.0 %collective-permute-start.26 = (bf16[64,2048]{1,0:T(8,128)(2,1)S(1)}, bf16[64,2048]{1,0:T(8,128)(2,1)}, u32[]{:S(2)}, u32[]{:S(2)}) collective-permute-start(bf16[64,2048]{1,0:T(8,128)(2,1)S(1)} %get-tuple-element.281), channel_id=1, source_target_pairs={{0,4},{1,5},{2,6},{3,7},{4,0},{5,1},{6,2},{7,3},{8,12},{9,13},{10,... | collective-permute-start | bytes 786440 | tf_op jit(solution)/shard_map/ppermute | solution.py:548
  271.5 12.7 %collective-permute-start.27 = (bf16[64,2048]{1,0:T(8,128)(2,1)S(1)}, bf16[64,2048]{1,0:T(8,128)(2,1)}, u32[]{:S(2)}, u32[]{:S(2)}) collective-permute-start(bf16[64,2048]{1,0:T(8,128)(2,1)S(1)} %get-tuple-element.280), channel_id=1, source_target_pairs={{0,6},{1,7},{2,4},{3,5},{4,2},{5,3},{6,0},{7,1},{8,14},{9,15},{10,... | collective-permute-start | bytes 786440 | tf_op jit(solution)/shard_map/ppermute | solution.py:548
  273.6 51.6 %collective-permute-start.33 = (bf16[4,512,384]{2,1,0:T(8,128)(2,1)S(1)}, bf16[4,512,384]{2,1,0:T(8,128)(2,1)}, u32[]{:S(2)}, u32[]{:S(2)}) collective-permute-start(bf16[4,512,384]{2,1,0:T(8,128)(2,1)S(1)} %pad_maximum_fusion.1.w0), channel_id=1, source_target_pairs={{0,16},{16,0},{1,17},{17,1},{2,18},{18,2},{3,19},{19,3},{4,20},{20... | collective-permute-start | bytes 4718600 | tf_op jit(solution)/shard_map/ppermute | solution.py:551
  289.5 11.2 %collective-permute-start.28 = (bf16[128,2048]{1,0:T(8,128)(2,1)}, bf16[128,2048]{1,0:T(8,128)(2,1)S(1)}, u32[]{:S(2)}, u32[]{:S(2)}) collective-permute-start(bf16[128,2048]{1,0:T(8,128)(2,1)} %get-tuple-element.181.own), channel_id=1, source_target_pairs={{0,1},{1,0},{2,3},{3,2},{4,5},{5,4},{6,7},{7,6},{8,9},{9,8},{10,11... | collective-permute-start | bytes 1572872 | tf_op jit(solution)/shard_map/ppermute | solution.py:548
  301.5 30.8 %collective-permute-start.29 = (bf16[4,64,2048]{2,1,0:T(8,128)(2,1)}, bf16[4,64,2048]{2,1,0:T(8,128)(2,1)}, u32[]{:S(2)}, u32[]{:S(2)}) collective-permute-start(bf16[4,64,2048]{2,1,0:T(8,128)(2,1)} %get-tuple-element.186), channel_id=1, source_target_pairs={{0,1},{1,0},{2,3},{3,2},{4,5},{5,4},{6,7},{7,6},{8,9},{9,8},{10,11... | collective-permute-start | bytes 3145736 | tf_op jit(solution)/shard_map/ppermute | solution.py:548
  303.2 31.7 %all-to-all-start.1 = ((bf16[4,64,2048]{2,1,0:T(8,128)(2,1)}), bf16[4,64,2048]{2,1,0:T(8,128)(2,1)}, u32[]{:S(2)}, u32[]{:S(2)}) async-start(bf16[4,64,2048]{2,1,0:T(8,128)(2,1)} %add_convert_fusion.2), calls=%async_computation.1 | async-start | bytes 2097152 | tf_op jit(solution)/shard_map/all_to_all | solution.py:873
  320.3 7.8 %collective-permute-start.30 = (bf16[256,256]{1,0:T(8,128)(2,1)S(1)}, bf16[256,256]{1,0:T(8,128)(2,1)S(1)}, u32[]{:S(2)}, u32[]{:S(2)}) collective-permute-start(bf16[256,256]{1,0:T(8,128)(2,1)S(1)} %get-tuple-element.188), channel_id=1, source_target_pairs={{0,2},{1,3},{2,0},{3,1},{4,6},{5,7},{6,4},{7,5},{8,10},{9,11},{10,... | collective-permute-start | bytes 393224 | tf_op jit(solution)/shard_map/ppermute | solution.py:548
  322.8 7.3 %collective-permute-start.31 = (bf16[256,256]{1,0:T(8,128)(2,1)S(1)}, bf16[256,256]{1,0:T(8,128)(2,1)S(1)}, u32[]{:S(2)}, u32[]{:S(2)}) collective-permute-start(bf16[256,256]{1,0:T(8,128)(2,1)S(1)} %get-tuple-element.189), channel_id=1, source_target_pairs={{0,4},{1,5},{2,6},{3,7},{4,0},{5,1},{6,2},{7,3},{8,12},{9,13},{10,... | collective-permute-start | bytes 393224 | tf_op jit(solution)/shard_map/ppermute | solution.py:548
  324.7 6.9 %collective-permute-start.32 = (bf16[256,256]{1,0:T(8,128)(2,1)S(1)}, bf16[256,256]{1,0:T(8,128)(2,1)S(1)}, u32[]{:S(2)}, u32[]{:S(2)}) collective-permute-start(bf16[256,256]{1,0:T(8,128)(2,1)S(1)} %get-tuple-element.190), channel_id=1, source_target_pairs={{0,6},{1,7},{2,4},{3,5},{4,2},{5,3},{6,0},{7,1},{8,14},{9,15},{10,... | collective-permute-start | bytes 393224 | tf_op jit(solution)/shard_map/ppermute | solution.py:548
  325.2 14.1 %collective-permute-start.34 = (bf16[4,512,384]{2,1,0:T(8,128)(2,1)S(1)}, bf16[4,512,384]{2,1,0:T(8,128)(2,1)}, u32[]{:S(2)}, u32[]{:S(2)}) collective-permute-start(bf16[4,512,384]{2,1,0:T(8,128)(2,1)S(1)} %pad_maximum_fusion.1.w0), channel_id=1, source_target_pairs={{0,8},{8,0},{1,9},{9,1},{2,10},{10,2},{3,11},{11,3},{4,12},{12,4},... | collective-permute-start | bytes 4718600 | tf_op jit(solution)/shard_map/ppermute | solution.py:554
  328.1 11.2 %collective-permute-start.35 = (bf16[4,512,384]{2,1,0:T(8,128)(2,1)}, bf16[4,512,384]{2,1,0:T(8,128)(2,1)}, u32[]{:S(2)}, u32[]{:S(2)}) collective-permute-start(bf16[4,512,384]{2,1,0:T(8,128)(2,1)} %collective-permute-done.33.w1), channel_id=1, source_target_pairs={{0,8},{8,0},{1,9},{9,1},{2,10},{10,2},{3,11},{11,3},{4,12},{12,4},... | collective-permute-start | bytes 4718600 | tf_op jit(solution)/shard_map/ppermute | solution.py:554
  334.9 50.0 %all-to-all-start.2 = ((bf16[4,64,2048]{2,1,0:T(8,128)(2,1)}), bf16[4,64,2048]{2,1,0:T(8,128)(2,1)}, u32[]{:S(2)}, u32[]{:S(2)}) async-start(bf16[4,64,2048]{2,1,0:T(8,128)(2,1)} %add_convert_fusion.1), calls=%async_computation.2 | async-start | bytes 2097152 | tf_op jit(solution)/shard_map/all_to_all | solution.py:892
  339.2 107.2 %all-gather.15.cloned.1.call-start = ((), (), s32[]{:S(2)}) async-start(), calls=%async_computation.10 | async-start | bytes 2621440 | tf_op jit(solution)/shard_map/all_gather | solution.py:981
  357.0 24.0 %collective-permute-start.36 = (bf16[1024,128]{1,0:T(8,128)(2,1)S(1)}, bf16[1024,128]{1,0:T(8,128)(2,1)S(1)}, u32[]{:S(2)}, u32[]{:S(2)}) collective-permute-start(bf16[1024,128]{1,0:T(8,128)(2,1)S(1)} %get-tuple-element.290), channel_id=1, source_target_pairs={{0,8},{8,0},{1,9},{9,1},{2,10},{10,2},{3,11},{11,3},{4,12},{12,4},... | collective-permute-start | bytes 786440 | tf_op jit(solution)/shard_map/ppermute | solution.py:554
  366.3 7.2 %collective-permute-start.37 = (bf16[256,256]{1,0:T(8,128)(2,1)S(1)}, bf16[256,256]{1,0:T(8,128)(2,1)S(1)}, u32[]{:S(2)}, u32[]{:S(2)}) collective-permute-start(bf16[256,256]{1,0:T(8,128)(2,1)S(1)} %get-tuple-element.202), channel_id=1, source_target_pairs={{0,2},{1,3},{2,0},{3,1},{4,6},{5,7},{6,4},{7,5},{8,10},{9,11},{10,... | collective-permute-start | bytes 393224 | tf_op jit(solution)/shard_map/ppermute | solution.py:548
  368.2 12.9 %collective-permute-start.38 = (bf16[256,256]{1,0:T(8,128)(2,1)S(1)}, bf16[256,256]{1,0:T(8,128)(2,1)S(1)}, u32[]{:S(2)}, u32[]{:S(2)}) collective-permute-start(bf16[256,256]{1,0:T(8,128)(2,1)S(1)} %get-tuple-element.203), channel_id=1, source_target_pairs={{0,4},{1,5},{2,6},{3,7},{4,0},{5,1},{6,2},{7,3},{8,12},{9,13},{10,... | collective-permute-start | bytes 393224 | tf_op jit(solution)/shard_map/ppermute | solution.py:548
  370.4 10.7 %collective-permute-start.39 = (bf16[256,256]{1,0:T(8,128)(2,1)S(1)}, bf16[256,256]{1,0:T(8,128)(2,1)S(1)}, u32[]{:S(2)}, u32[]{:S(2)}) collective-permute-start(bf16[256,256]{1,0:T(8,128)(2,1)S(1)} %get-tuple-element.204), channel_id=1, source_target_pairs={{0,6},{1,7},{2,4},{3,5},{4,2},{5,3},{6,0},{7,1},{8,14},{9,15},{10,... | collective-permute-start | bytes 393224 | tf_op jit(solution)/shard_map/ppermute | solution.py:548
  388.0 102.3 %all-gather.17.cloned.1.call-start = ((), (), s32[]{:S(2)}) async-start(), calls=%async_computation.11 | async-start | bytes 2621440 | tf_op jit(solution)/shard_map/all_gather | solution.py:999
  390.5 7.1 %collective-permute-start.41 = (bf16[256,128]{1,0:T(8,128)(2,1)S(1)}, bf16[256,128]{1,0:T(8,128)(2,1)S(1)}, u32[]{:S(2)}, u32[]{:S(2)}) collective-permute-start(bf16[256,128]{1,0:T(8,128)(2,1)S(1)} %copy-done.76), channel_id=1, source_target_pairs={{0,4},{1,5},{2,6},{3,7},{4,0},{5,1},{6,2},{7,3},{8,12},{9,13},{10,... | collective-permute-start | bytes 196616 | tf_op jit(solution)/shard_map/ppermute | solution.py:548
  391.3 6.3 %collective-permute-start.42 = (bf16[256,128]{1,0:T(8,128)(2,1)S(1)}, bf16[256,128]{1,0:T(8,128)(2,1)S(1)}, u32[]{:S(2)}, u32[]{:S(2)}) collective-permute-start(bf16[256,128]{1,0:T(8,128)(2,1)S(1)} %copy-done.75), channel_id=1, source_target_pairs={{0,6},{1,7},{2,4},{3,5},{4,2},{5,3},{6,0},{7,1},{8,14},{9,15},{10,... | collective-permute-start | bytes 196616 | tf_op jit(solution)/shard_map/ppermute | solution.py:548
  404.7 13.9 %collective-permute-start.45 = (bf16[128,2048]{1,0:T(8,128)(2,1)}, bf16[128,2048]{1,0:T(8,128)(2,1)S(1)}, u32[]{:S(2)}, u32[]{:S(2)}) collective-permute-start(bf16[128,2048]{1,0:T(8,128)(2,1)} %get-tuple-element.220), channel_id=1, source_target_pairs={{0,1},{1,0},{2,3},{3,2},{4,5},{5,4},{6,7},{7,6},{8,9},{9,8},{10,11... | collective-permute-start | bytes 1572872 | tf_op jit(solution)/shard_map/ppermute | solution.py:548
  411.6 13.6 %collective-permute-start.49 = (bf16[1024,1024]{1,0:T(8,128)(2,1)}, bf16[1024,1024]{1,0:T(8,128)(2,1)}, u32[]{:S(2)}, u32[]{:S(2)}) collective-permute-start(bf16[1024,1024]{1,0:T(8,128)(2,1)} %get-tuple-element.229), channel_id=1, source_target_pairs={{0,8},{8,0},{1,9},{9,1},{2,10},{10,2},{3,11},{11,3},{4,12},{12,4},... | collective-permute-start | bytes 6291464 | tf_op jit(solution)/shard_map/ppermute | solution.py:554
  424.3 11.4 %collective-permute-start.51 = (bf16[1024,384]{1,0:T(8,128)(2,1)}, bf16[1024,384]{1,0:T(8,128)(2,1)S(1)}, u32[]{:S(2)}, u32[]{:S(2)}) collective-permute-start(bf16[1024,384]{1,0:T(8,128)(2,1)} %get-tuple-element.223), channel_id=1, source_target_pairs={{0,8},{8,0},{1,9},{9,1},{2,10},{10,2},{3,11},{11,3},{4,12},{12,4},... | collective-permute-start | bytes 2359304 | tf_op jit(solution)/shard_map/ppermute | solution.py:554
  429.3 54.6 %collective-permute-start.50 = (bf16[512,1024]{1,0:T(8,128)(2,1)}, bf16[512,1024]{1,0:T(8,128)(2,1)}, u32[]{:S(2)}, u32[]{:S(2)}) collective-permute-start(bf16[512,1024]{1,0:T(8,128)(2,1)} %pair_sum.2), channel_id=1, source_target_pairs={{0,16},{16,0},{1,17},{17,1},{2,18},{18,2},{3,19},{19,3},{4,20},{20... | collective-permute-start | bytes 3145736 | tf_op jit(solution)/shard_map/ppermute | solution.py:551
  432.2 14.3 %collective-permute-start.46 = (bf16[128,2048]{1,0:T(8,128)(2,1)S(1)}, bf16[128,2048]{1,0:T(8,128)(2,1)S(1)}, u32[]{:S(2)}, u32[]{:S(2)}) collective-permute-start(bf16[128,2048]{1,0:T(8,128)(2,1)S(1)} %copy-done.50), channel_id=1, source_target_pairs={{0,1},{1,0},{2,3},{3,2},{4,5},{5,4},{6,7},{7,6},{8,9},{9,8},{10,11... | collective-permute-start | bytes 1572872 | tf_op jit(solution)/shard_map/ppermute | solution.py:548
  434.9 11.2 %collective-permute-start.44 = (f32[2,1024]{1,0:T(2,128)S(1)}, f32[2,1024]{1,0:T(2,128)S(1)}, u32[]{:S(2)}, u32[]{:S(2)}) collective-permute-start(f32[2,1024]{1,0:T(2,128)S(1)} %fusion.4), channel_id=1, source_target_pairs={{0,1},{1,0},{2,3},{3,2},{4,5},{5,4},{6,7},{7,6},{8,9},{9,8},{10,11... | collective-permute-start | bytes 24584 | tf_op jit(solution)/shard_map/ppermute | solution.py:548
  435.7 48.1 %collective-permute-start.52 = (bf16[512,384]{1,0:T(8,128)(2,1)S(1)}, bf16[512,384]{1,0:T(8,128)(2,1)S(1)}, u32[]{:S(2)}, u32[]{:S(2)}) collective-permute-start(bf16[512,384]{1,0:T(8,128)(2,1)S(1)} %pair_sum.3), channel_id=1, source_target_pairs={{0,16},{16,0},{1,17},{17,1},{2,18},{18,2},{3,19},{19,3},{4,20},{20... | collective-permute-start | bytes 1179656 | tf_op jit(solution)/shard_map/ppermute | solution.py:551
  446.1 17.9 %collective-permute-start.48 = (f32[2,512]{1,0:T(2,128)S(1)}, f32[2,512]{1,0:T(2,128)S(1)}, u32[]{:S(2)}, u32[]{:S(2)}) collective-permute-start(f32[2,512]{1,0:T(2,128)S(1)} %slice.166), channel_id=1, source_target_pairs={{0,16},{16,0},{1,17},{17,1},{2,18},{18,2},{3,19},{19,3},{4,20},{20... | collective-permute-start | bytes 12296 | tf_op jit(solution)/shard_map/ppermute | solution.py:551
  446.4 54.5 %collective-permute-start.47 = (bf16[4,128,2048]{2,1,0:T(8,128)(2,1)}, bf16[4,128,2048]{2,1,0:T(8,128)(2,1)}, u32[]{:S(2)}, u32[]{:S(2)}) collective-permute-start(bf16[4,128,2048]{2,1,0:T(8,128)(2,1)} %bitcast.57), channel_id=1, source_target_pairs={{0,1},{1,0},{2,3},{3,2},{4,5},{5,4},{6,7},{7,6},{8,9},{9,8},{10,11... | collective-permute-start | bytes 6291464 | tf_op jit(solution)/shard_map/ppermute | solution.py:548
  492.1 37.1 %collective-permute-start.53 = (bf16[3,128,2048]{2,1,0:T(8,128)(2,1)S(1)}, bf16[3,128,2048]{2,1,0:T(8,128)(2,1)S(1)}, u32[]{:S(2)}, u32[]{:S(2)}) collective-permute-start(bf16[3,128,2048]{2,1,0:T(8,128)(2,1)S(1)} %pad_maximum_fusion.2), channel_id=1, source_target_pairs={{0,1},{1,0},{2,3},{3,2},{4,5},{5,4},{6,7},{7,6},{8,9},{9,8},{10,11... | collective-permute-start | bytes 4718600 | tf_op jit(solution)/shard_map/ppermute | solution.py:548
  493.6 6.0 %collective-permute-start.57 = (f32[2,512]{1,0:T(2,128)S(1)}, f32[2,512]{1,0:T(2,128)S(1)}, u32[]{:S(2)}, u32[]{:S(2)}) collective-permute-start(f32[2,512]{1,0:T(2,128)S(1)} %slice_add_fusion), channel_id=1, source_target_pairs={{0,2},{1,3},{2,0},{3,1},{4,6},{5,7},{6,4},{7,5},{8,10},{9,11},{10,... | collective-permute-start | bytes 12296 | tf_op jit(solution)/shard_map/ppermute | solution.py:548
  496.6 27.8 %collective-permute-start.54 = (bf16[512,256]{1,0:T(8,128)(2,1)S(1)}, bf16[512,256]{1,0:T(8,128)(2,1)S(1)}, u32[]{:S(2)}, u32[]{:S(2)}) collective-permute-start(bf16[512,256]{1,0:T(8,128)(2,1)S(1)} %get-tuple-element.278), channel_id=1, source_target_pairs={{0,2},{1,3},{2,0},{3,1},{4,6},{5,7},{6,4},{7,5},{8,10},{9,11},{10,... | collective-permute-start | bytes 786440 | tf_op jit(solution)/shard_map/ppermute | solution.py:548
  498.6 25.8 %collective-permute-start.55 = (bf16[512,256]{1,0:T(8,128)(2,1)S(1)}, bf16[512,256]{1,0:T(8,128)(2,1)S(1)}, u32[]{:S(2)}, u32[]{:S(2)}) collective-permute-start(bf16[512,256]{1,0:T(8,128)(2,1)S(1)} %get-tuple-element.277), channel_id=1, source_target_pairs={{0,4},{1,5},{2,6},{3,7},{4,0},{5,1},{6,2},{7,3},{8,12},{9,13},{10,... | collective-permute-start | bytes 786440 | tf_op jit(solution)/shard_map/ppermute | solution.py:548
  499.6 24.8 %collective-permute-start.56 = (bf16[512,256]{1,0:T(8,128)(2,1)S(1)}, bf16[512,256]{1,0:T(8,128)(2,1)S(1)}, u32[]{:S(2)}, u32[]{:S(2)}) collective-permute-start(bf16[512,256]{1,0:T(8,128)(2,1)S(1)} %get-tuple-element.276), channel_id=1, source_target_pairs={{0,6},{1,7},{2,4},{3,5},{4,2},{5,3},{6,0},{7,1},{8,14},{9,15},{10,... | collective-permute-start | bytes 786440 | tf_op jit(solution)/shard_map/ppermute | solution.py:548
  501.0 22.8 %collective-permute-start.58 = (f32[2,512]{1,0:T(2,128)S(1)}, f32[2,512]{1,0:T(2,128)S(1)}, u32[]{:S(2)}, u32[]{:S(2)}) collective-permute-start(f32[2,512]{1,0:T(2,128)S(1)} %add.122), channel_id=1, source_target_pairs={{0,4},{1,5},{2,6},{3,7},{4,0},{5,1},{6,2},{7,3},{8,12},{9,13},{10,... | collective-permute-start | bytes 12296 | tf_op jit(solution)/shard_map/ppermute | solution.py:548
  (83 other events, 1395.6 us)
Sparse Core Ops, SparseCore 0:
  12.3 30.6 all-gather.12
  45.1 49.1 all-gather.10
  96.5 59.7 all-gather.8
  250.7 67.8 reduce-scatter.2
  321.8 73.6 reduce-scatter.4
  397.5 45.9 all-gather.14
  445.6 44.6 all-gather.16

commit v3 on v2

--- a/solution.py
+++ b/solution.py
@@ -448,6 +448,16 @@
     @pl.when(pl.program_id(0) >= 2)
     def _():
         outs[1][...] = result
+
+
+def mlp_grad_kernel(x, gate_up_back, dy, hidden, out):
+    for a, b, cols in (
+        (x, gate_up_back, slice(0, gate_up_back.shape[1])),
+        (dy, hidden, slice(gate_up_back.shape[1], out.shape[1])),
+    ):
+        out[:, cols] = lax.dot_general(
+            a[...], b[...], (((0,), (0,)), ((), ())), preferred_element_type=F32
+        ).astype(BF16)
 
 
 def pair_sum_kernel(a, b, out):
@@ -838,13 +848,22 @@
     two_a = scatter_parts(total_a)
     back_near = jnp.stack(after([back_low] + back_parts, two_send_b), axis=0)
     hidden, gate_up_back = after((hidden, gate_up_back), (total_a, back_near))
-    down_full = weight_full(dy.reshape(span, D), hidden)
-    gate_up_full = weight_full(x, gate_up_back)
+    narrow = pl.BlockSpec((span, QUARTER), lambda i: (0, i))
+    mlp_full = pl.pallas_call(
+        mlp_grad_kernel,
+        grid=(4,),
+        in_specs=[narrow, whole((span, 2048)), narrow, whole((span, 1024))],
+        out_specs=pl.BlockSpec((QUARTER, 3072), lambda i: (i, 0)),
+        out_shape=jax.ShapeDtypeStruct((D, 3072), BF16),
+        compiler_params=vmem(56),
+        cost_estimate=cost(22),
+        name="mlp_grad",
+    )(x, gate_up_back, dy.reshape(span, D), hidden)
     total_b = two_keep_b.astype(F32) + after(
-        two_got_b, (down_full, gate_up_full, two_a)
+        two_got_b, (mlp_full, two_a)
     ).astype(F32)
     two_b = scatter_parts(total_b)
-    down_grad, gate_up_grad = (scatter_all(full) for full in after((down_full, gate_up_full), total_b))
+    mlp_grad = scatter_all(after(mlp_full, total_b))
     mlp_got_a = swap_tensor(after(mlp_send_a, total_b), 1)
 
     resid_grad, resid_low, gain_two_grad = pl.pallas_call(
@@ -891,7 +910,7 @@
     mlp_total_b = (mlp_keep_b.astype(F32) + after(mlp_got_b, grad_parts).astype(F32)).astype(BF16)
     mlp_parts_b = lax.all_to_all(mlp_total_b, "tensor", 0, 0, axis_index_groups=HIGH_GROUPS)
     back_w = gather_width(back_near, resid_low, resid_low)
-    grad_parts = after(grad_parts, (mlp_total_b, down_grad, back_w))
+    grad_parts = after(grad_parts, (mlp_total_b, back_w))
 
     spans = seq_size if fast else length // span
     dq, *dq_pieces, dkv = pl.pallas_call(
@@ -954,7 +973,7 @@
         cost_estimate=cost(3),
         name="block_out",
     )(*after((mlp_parts_a, mlp_parts_b), dkv_low), resid_one)
-    dkv_parts = after(dkv_parts, (gate_up_grad, block_low))
+    dkv_parts = after(dkv_parts, (mlp_grad, block_low))
     one_keep, one_send = pl.pallas_call(
         one_kernel,
         grid_spec=pltpu.PrefetchScalarGridSpec(
@@ -1025,12 +1044,12 @@
         )(weight, one, two, *[term for term, column in terms])
 
     fan_in = RATE_FACTOR * D ** (-0.5)
-    gate_up_grad, down_grad = after((gate_up_grad, down_grad), tokens_low)
+    mlp_grad = after(mlp_grad, tokens_low)
     gate_up_new = adam(
-        gate_up_weight, gate_up_first, gate_up_second, [(gate_up_grad, 0)], fan_in, DECAY
+        gate_up_weight, gate_up_first, gate_up_second, [(mlp_grad, 0)], fan_in, DECAY
     )
     down_new = adam(
-        down_weight, down_first, down_second, [(down_grad, 0)], RATE_FACTOR * FF ** (-0.5), DECAY
+        down_weight, down_first, down_second, [(mlp_grad, 2)], RATE_FACTOR * FF ** (-0.5), DECAY
     )
 
     products = jnp.concatenate(
@@ -1054,7 +1073,7 @@
     )
     if fast:
         gain_grads = gain_grads[:, : 2 * QUARTER] + swap_seq(gain_grads[:, 2 * QUARTER :])
-        gain_grads = gain_grads + swap_tensor(gain_grads, 1)
+        gain_got = swap_tensor(gain_grads, 1)
     else:
         shard = norm_gains.shape[0]
         gains_grad = lax.dynamic_slice(
@@ -1062,13 +1081,11 @@
             (0, (dp_id * seq_size + seq_id) * shard),
             (2, shard),
         )
-        gain_grads = gains_grad + swap_tensor(gains_grad, 1)
-    block_far = swap_tensor(after(block_near, (gain_grads, tokens_own)), 1)
-    if fast:
-        gains_grad = gain_grads[:, :QUARTER] + swap_dp(gain_grads[:, QUARTER:])
-    else:
-        gains_grad = gain_grads
-    early = (gate_up_new, down_new, gains_grad) + ((out_far, attn_far) if fast else ())
+        gain_grads = gains_grad
+        gain_got = swap_tensor(gains_grad, 1)
+    block_far = swap_tensor(after(block_near, tokens_own), 1)
+    gain_grads = gain_grads + gain_got
+    early = (gate_up_new, down_new, gain_grads) + ((out_far, attn_far) if fast else ())
     tokens_near = after(tokens_near, early)
     tokens_far = swap_tensor(others(tokens_near), 1)
 
@@ -1090,7 +1107,11 @@
         DECAY,
     )
 
-    gains_grad = after(gains_grad, tokens_near)
+    gain_grads = after(gain_grads, tokens_near)
+    if fast:
+        gains_grad = gain_grads[:, :QUARTER] + swap_dp(gain_grads[:, QUARTER:])
+    else:
+        gains_grad = gain_grads
     for mask in (2, 4):
         gains_grad = gains_grad + swap_tensor(gains_grad, mask)
     gains_grad = gains_grad.T

time: 549 us -> 543 us (0.989)
    pallas_call x4 -> x2, Pallas kernels: 33.4 us -> 11.9 us  [weight_full(): pl.pallas_call(weight_grad_kernel, grid=(4,), in_specs=[pl.BlockSpec((n,...]
    pallas_call x0 -> x1, Pallas kernels: none -> 19.2 us  [body(): pl.pallas_call(mlp_grad_kernel, grid=(4,), in_specs=[narrow, whole((span,...]
    ppermute x6, waiting for transfers between devices: 34.8 us -> 18 us  [swap_dp(): return lax.ppermute(value, 'dp', [(0, 1), (1, 0)])]
    all_gather x1, waiting for transfers between devices: 6.43 us -> 14.2 us  [body(): lax.all_gather(tokens_low, 'tensor', axis=0, axis_index_groups=HIGH_GROUPS)]
    unnamed x163 -> x157, local copies, waits for them, and re-layouts: 24.9 us -> 25.5 us
  transfers between devices with their start and end apart: 69 -> 68, of which waited for: 23 -> 24; matrix products, arithmetic and copies ran while one was open for 6% -> 6% of each run, Pallas kernels for 34% -> 34%
where the time goes in v3:
time: 543 us; the launch traced here: 534 us
  Pallas kernels  184 us (34%)
  waiting for transfers between devices  148 us (27%)
  starting transfers between devices  123 us (23%)
  local copies, waits for them, and re-layouts  37 us (7%)
  other arithmetic  27.7 us (5%)
  between operations  15.5 us (3%)
    ppermute x42, waiting for transfers between devices, swap_tensor(): return lax.ppermute(value, 'tensor', [(i, i ^ mask) for i in range(8)])  108 us
    ppermute x42, starting transfers between devices, swap_tensor(): return lax.ppermute(value, 'tensor', [(i, i ^ mask) for i in range(8)])  76.9 us
    pallas_call x2, Pallas kernels, mlp(): pl.pallas_call(mlp_kernel, grid_spec=pltpu.PrefetchScalarGridSpec(num_sca...  46 us
    pallas_call x5, Pallas kernels, adam(): pl.pallas_call(functools.partial(adam_kernel, rate, decay), grid=(4,), in...  30.9 us
    unnamed x157, local copies, waits for them, and re-layouts  25.5 us
    pallas_call x1, Pallas kernels, body(): pl.pallas_call(mlp_grad_kernel, grid=(4,), in_specs=[narrow, whole((span,...  19.2 us
    ppermute x6, waiting for transfers between devices, swap_dp(): return lax.ppermute(value, 'dp', [(0, 1), (1, 0)])  18 us
    ppermute x11, starting transfers between devices, swap_seq(): return lax.ppermute(value, 'seq', [(0, 1), (1, 0)])  16.4 us
  transfers between devices with their start and end apart: 68, of which 24 were waited for; matrix products, arithmetic and copies ran while one was open for 6% of the time, Pallas kernels for 34%

profile of v3, /device:TPU:0, one launch (start us, length us, event | category | flops | bytes accessed | tf_op | source)
XLA Modules:
  0.0 534.4 jit_solution(12798354249007431698)
XLA Ops:
  12.2 3.0 collective-permute-start
  18.1 9.1 %collective-permute-done.w1 = bf16[512,512]{1,0:T(8,128)(2,1)S(1)} collective-permute-done((bf16[512,512]{1,0:T(8,128)(2,1)S(1)}, bf16[512,512]{1,0:T(8,128)(2,1)S(1)}, u32[]{:S(2)}, u32[]{:S(2)}) %collective-permute-start) | collective-permute-done | bytes 524320 | tf_op jit(solution)/shard_map/ppermute | solution.py:561
  30.3 7.1 %project.1 = (bf16[1024,2048]{1,0:T(8,128)(2,1)}, bf16[1024,256]{1,0:T(8,128)(2,1)S(1)}, bf16[1024,128]{1,0:T(8,128)(2,1)S(1)}, f32[8,2048]{1,0:T(8,128)S(1)}) custom-call(s32[9]{0:T(128)S(1)} %stack.69.info, bf16[1024,2048]{1,0:T(8,128)(2,1)} %bitcast.60, bf16[512,512]{1,0:T(8,128)(2,1)S(1)} %copy-done.23, bf16[512,512]{1,0:T(8,128)(2,1)S(1)} %collective-permute-done.w1, ...), custom_call_target="tpu_custom_call" | custom-call | bytes 12915000 | tf_op jit(solution)/shard_map/project/pallas_call | solution.py:675
  39.4 3.3 copy.51
  46.5 8.1 %attend.1 = (bf16[1024,256]{1,0:T(8,128)(2,1)}, f32[4,1,1024]{2,1,0:T(1,128)S(1)}) custom-call(s32[9]{0:T(128)S(1)} %stack.69.info, bf16[1024,256]{1,0:T(8,128)(2,1)S(1)} %get-tuple-element.140.q, bf16[2048,128]{1,0:T(8,128)(2,1)S(1)} %maximum_select_fusion.kv), custom_call_target="tpu_custom_call" | custom-call | bytes 33210000 | tf_op jit(solution)/shard_map/attend/pallas_call | solution.py:719
  56.0 4.9 all-to-all-start
  61.4 7.4 %reorder.1.dy.refs_9_ = bf16[2,512,2048]{2,1,0:T(8,128)(2,1)} custom-call(s32[9]{0:T(128)} %copy-done.37, bf16[1024,2048]{1,0:T(8,128)(2,1)} %bitcast.64), custom_call_target="tpu_custom_call" | custom-call | bytes 13837500 | tf_op jit(solution)/shard_map/reorder/pallas_call | solution.py:662
  68.9 2.4 all-to-all-done.att
  71.2 6.6 %collective-permute-start.5 = (bf16[4,512,256]{2,1,0:T(8,128)(2,1)S(1)}, bf16[4,512,256]{2,1,0:T(8,128)(2,1)S(1)}, u32[]{:S(2)}, u32[]{:S(2)}) collective-permute-start(bf16[4,512,256]{2,1,0:T(8,128)(2,1)S(1)} %bitcast.54), channel_id=1, source_target_pairs={{0,8},{8,0},{1,9},{9,1},{2,10},{10,2},{3,11},{11,3},{4,12},{12,4},... | collective-permute-start | bytes 3145736 | tf_op jit(solution)/shard_map/ppermute | solution.py:564
  77.8 8.9 %collective-permute-done.4.w1 = bf16[4,512,256]{2,1,0:T(8,128)(2,1)} collective-permute-done((bf16[4,512,256]{2,1,0:T(8,128)(2,1)}, bf16[4,512,256]{2,1,0:T(8,128)(2,1)}, u32[]{:S(2)}, u32[]{:S(2)}) %collective-permute-start.4) | collective-permute-done | bytes 1048608 | tf_op jit(solution)/shard_map/ppermute | solution.py:561
  86.7 2.9 collective-permute-done.6.w3
  90.6 3.4 attention_out.1
  96.3 12.7 %collective-permute-done.7.got = bf16[128,2048]{1,0:T(8,128)(2,1)S(1)} collective-permute-done((bf16[128,2048]{1,0:T(8,128)(2,1)S(1)}, bf16[128,2048]{1,0:T(8,128)(2,1)S(1)}, u32[]{:S(2)}, u32[]{:S(2)}) %collective-permute-start.7) | collective-permute-done | bytes 524320 | tf_op jit(solution)/shard_map/ppermute | solution.py:558
  109.7 3.6 second_norm.1
  114.8 2.7 collective-permute-start.9
  118.8 7.0 %collective-permute-done.8 = bf16[64,2048]{1,0:T(8,128)(2,1)S(1)} collective-permute-done((bf16[64,2048]{1,0:T(8,128)(2,1)}, bf16[64,2048]{1,0:T(8,128)(2,1)S(1)}, u32[]{:S(2)}, u32[]{:S(2)}) %collective-permute-start.8) | collective-permute-done | bytes 262176 | tf_op jit(solution)/shard_map/ppermute | solution.py:558
  125.8 10.6 %collective-permute-done.9 = bf16[64,2048]{1,0:T(8,128)(2,1)S(1)} collective-permute-done((bf16[64,2048]{1,0:T(8,128)(2,1)}, bf16[64,2048]{1,0:T(8,128)(2,1)S(1)}, u32[]{:S(2)}, u32[]{:S(2)}) %collective-permute-start.9) | collective-permute-done | bytes 262176 | tf_op jit(solution)/shard_map/ppermute | solution.py:558
  138.1 4.4 collective-permute-start.12
  144.9 5.9 %collective-permute-done.12 = bf16[64,2048]{1,0:T(8,128)(2,1)S(1)} collective-permute-done((bf16[64,2048]{1,0:T(8,128)(2,1)S(1)}, bf16[64,2048]{1,0:T(8,128)(2,1)S(1)}, u32[]{:S(2)}, u32[]{:S(2)}) %collective-permute-start.12) | collective-permute-done | bytes 262176 | tf_op jit(solution)/shard_map/ppermute | solution.py:558
  150.8 12.6 %collective-permute-done.13 = bf16[64,2048]{1,0:T(8,128)(2,1)S(1)} collective-permute-done((bf16[64,2048]{1,0:T(8,128)(2,1)S(1)}, bf16[64,2048]{1,0:T(8,128)(2,1)S(1)}, u32[]{:S(2)}, u32[]{:S(2)}) %collective-permute-start.13) | collective-permute-done | bytes 262176 | tf_op jit(solution)/shard_map/ppermute | solution.py:558
  164.1 22.8 %mlp.2 = (bf16[4,64,2048]{2,1,0:T(8,128)(2,1)}, bf16[4,64,2048]{2,1,0:T(8,128)(2,1)}, bf16[256,2048]{1,0:T(8,128)(2,1)}, bf16[256,2048]{1,0:T(8,128)(2,1)}, bf16...) custom-call(s32[9]{0:T(128)} %copy-done.37, bf16[256,2048]{1,0:T(8,128)(2,1)} %copy-done.53, ...), custom_call_target="tpu_custom_call" | custom-call | bytes 41512500 | tf_op jit(solution)/shard_map/mlp/pallas_call | solution.py:795
  188.6 3.5 collective-permute-start.18
  194.5 23.1 %mlp.3 = (bf16[4,64,2048]{2,1,0:T(8,128)(2,1)}, bf16[4,64,2048]{2,1,0:T(8,128)(2,1)}, bf16[256,2048]{1,0:T(8,128)(2,1)}, bf16[256,2048]{1,0:T(8,128)(2,1)}, bf16...) custom-call(s32[9]{0:T(128)} %copy-done.37, ...), custom_call_target="tpu_custom_call", output_to_operand_aliasing={{4}: (6, {}), {5}: (7, {}), {6}: (8, {})} | custom-call | bytes 41512500 | tf_op jit(solution)/shard_map/mlp/pallas_call | solution.py:795
  225.0 19.2 %mlp_grad.1 = bf16[2048,3072]{1,0:T(8,128)(2,1)} custom-call(bf16[1024,2048]{1,0:T(8,128)(2,1)} %get-tuple-element.163.x, bf16[1024,2048]{1,0:T(8,128)(2,1)} %get-tuple-element.174.gate_up_back, bf16[1024,2048]{1,0:T(8,128)(2,1)} %bitcast.59, bf16[1024,1024]{1,0:T(8,128)(2,1)} %get-tuple-element.175.hidden), custom_call_target="tpu_custom_call" | custom-call | bytes 40590000 | tf_op jit(solution)/shard_map/mlp_grad/pallas_call | solution.py:852
  245.7 3.7 fusion.8
  251.2 16.9 %collective-permute-start.25 = (bf16[64,2048]{1,0:T(8,128)(2,1)S(1)}, bf16[64,2048]{1,0:T(8,128)(2,1)S(1)}, u32[]{:S(2)}, u32[]{:S(2)}) collective-permute-start(bf16[64,2048]{1,0:T(8,128)(2,1)S(1)} %get-tuple-element.278), channel_id=1, source_target_pairs={{0,2},{1,3},{2,0},{3,1},{4,6},{5,7},{6,4},{7,5},{8,10},{9,11},{10,... | collective-permute-start | bytes 786440 | tf_op jit(solution)/shard_map/ppermute | solution.py:558
  270.5 2.6 collective-permute-start.33
  275.1 5.9 %collective-permute-done.26.refs_6_ = bf16[64,2048]{1,0:T(8,128)(2,1)} collective-permute-done((bf16[64,2048]{1,0:T(8,128)(2,1)S(1)}, bf16[64,2048]{1,0:T(8,128)(2,1)}, u32[]{:S(2)}, u32[]{:S(2)}) %collective-permute-start.26) | collective-permute-done | bytes 262176 | tf_op jit(solution)/shard_map/ppermute | solution.py:558
  281.0 5.0 second_norm_back.1
  287.7 2.9 add_convert_fusion.2
  290.6 6.9 %collective-permute-done.28.other = bf16[128,2048]{1,0:T(8,128)(2,1)S(1)} collective-permute-done((bf16[128,2048]{1,0:T(8,128)(2,1)}, bf16[128,2048]{1,0:T(8,128)(2,1)S(1)}, u32[]{:S(2)}, u32[]{:S(2)}) %collective-permute-start.28) | collective-permute-done | bytes 524320 | tf_op jit(solution)/shard_map/ppermute | solution.py:558
  300.0 8.2 %all-to-all-start.1 = ((bf16[4,64,2048]{2,1,0:T(8,128)(2,1)}), bf16[4,64,2048]{2,1,0:T(8,128)(2,1)}, u32[]{:S(2)}, u32[]{:S(2)}) async-start(bf16[4,64,2048]{2,1,0:T(8,128)(2,1)} %add_convert_fusion.2), calls=%async_computation.1 | async-start | bytes 2097152 | tf_op jit(solution)/shard_map/all_to_all | solution.py:892
  312.8 3.4 attention_out_back.1
  317.2 2.7 collective-permute-start.30
  322.3 2.7 collective-permute-done.30.grad1
  325.1 3.6 collective-permute-done.31.grad2
  329.3 2.7 add_convert_fusion.1
  332.1 4.3 all-to-all-start.2
  341.1 11.5 %attend_back.1 = (bf16[1024,256]{1,0:T(8,128)(2,1)S(1)}, bf16[256,256]{1,0:T(8,128)(2,1)S(1)}, bf16[256,256]{1,0:T(8,128)(2,1)S(1)}, bf16[256,256]{1,0:T(8,128)(...) custom-call(s32[9]{0:T(128)S(1)} %copy-done.39, bf16[1024,256]{1,0:T(8,128)(2,1)S(1)} %copy-done.15, ...), custom_call_target="tpu_custom_call" | custom-call | bytes 42435000 | tf_op jit(solution)/shard_map/attend_back/pallas_call | solution.py:916
  354.1 8.9 %collective-permute-start.36 = (bf16[1024,128]{1,0:T(8,128)(2,1)S(1)}, bf16[1024,128]{1,0:T(8,128)(2,1)S(1)}, u32[]{:S(2)}, u32[]{:S(2)}) collective-permute-start(bf16[1024,128]{1,0:T(8,128)(2,1)S(1)} %get-tuple-element.286), channel_id=1, source_target_pairs={{0,8},{8,0},{1,9},{9,1},{2,10},{10,2},{3,11},{11,3},{4,12},{12,4},... | collective-permute-start | bytes 786440 | tf_op jit(solution)/shard_map/ppermute | solution.py:564
  364.7 2.4 collective-permute-start.38
  367.4 2.8 collective-permute-done.37.q1
  370.2 7.5 %collective-permute-done.38.q2 = bf16[256,256]{1,0:T(8,128)(2,1)S(1)} collective-permute-done((bf16[256,256]{1,0:T(8,128)(2,1)S(1)}, bf16[256,256]{1,0:T(8,128)(2,1)S(1)}, u32[]{:S(2)}, u32[]{:S(2)}) %collective-permute-start.38) | collective-permute-done | bytes 131104 | tf_op jit(solution)/shard_map/ppermute | solution.py:558
  378.4 3.1 kv_back.1
  381.5 3.0 block_out.1
  384.6 2.2 collective-permute-start.40
  389.8 4.2 collective-permute-done.41.k2
  394.0 5.3 attention_in_back.1
  401.9 5.8 %weight_grad.3 = (bf16[1024,1024]{1,0:T(8,128)(2,1)}, bf16[1024,1024]{1,0:T(8,128)(2,1)}) custom-call(bf16[256,2048]{1,0:T(8,128)(2,1)} %copy-done.24, bf16[256,1024]{1,0:T(8,128)(2,1)} %pad_maximum_fusion.6.b), custom_call_target="tpu_custom_call" | custom-call | bytes 3022848 | tf_op jit(solution)/shard_map/weight_grad/pallas_call | solution.py:592
  408.6 6.1 %weight_grad.2 = (bf16[1024,384]{1,0:T(8,128)(2,1)}, bf16[1024,384]{1,0:T(8,128)(2,1)}) custom-call(bf16[1024,2048]{1,0:T(8,128)(2,1)} %get-tuple-element.217.a, bf16[1024,384]{1,0:T(8,128)(2,1)} %pad_maximum_fusion.3.b), custom_call_target="tpu_custom_call" | custom-call | bytes 4534272 | tf_op jit(solution)/shard_map/weight_grad/pallas_call | solution.py:592
  415.5 4.1 first_norm_back.1
  422.4 2.5 pair_sum.2
  424.9 2.3 collective-permute-start.49
  432.4 10.2 %collective-permute-done.44.own = bf16[128,2048]{1,0:T(8,128)(2,1)S(1)} collective-permute-done((bf16[128,2048]{1,0:T(8,128)(2,1)}, bf16[128,2048]{1,0:T(8,128)(2,1)S(1)}, u32[]{:S(2)}, u32[]{:S(2)}) %collective-permute-start.44) | collective-permute-done | bytes 524320 | tf_op jit(solution)/shard_map/ppermute | solution.py:558
  444.2 13.2 %adam.5 = (f32[512,2,1024]{2,1,0:T(2,128)}, f32[512,2,1024]{2,1,0:T(2,128)}, f32[512,2,1024]{2,1,0:T(2,128)}) custom-call(f32[512,2,1024]{2,1,0:T(2,128)} %weight.5, f32[512,2,1024]{2,1,0:T(2,128)} %one.5, f32[512,2,1024]{2,1,0:T(2,128)} %two.5, bf16[512,3072]{1,0:T(8,128)(2,1)} %reduce-scatter.2.cloned.1.call-done.refs_0_), custom_call_target="tpu_custom_call" | custom-call | bytes 25794968 | tf_op jit(solution)/shard_map/adam/pallas_call | solution.py:1031
  457.4 6.7 %adam.6 = (f32[512,1024]{1,0:T(8,128)}, f32[512,1024]{1,0:T(8,128)}, f32[512,1024]{1,0:T(8,128)}) custom-call(f32[512,1024]{1,0:T(8,128)} %weight.6, f32[512,1024]{1,0:T(8,128)} %one.6, f32[512,1024]{1,0:T(8,128)} %two.6, bf16[512,3072]{1,0:T(8,128)(2,1)} %reduce-scatter.2.cloned.1.call-done.refs_0_), custom_call_target="tpu_custom_call" | custom-call | bytes 12897484 | tf_op jit(solution)/shard_map/adam/pallas_call | solution.py:1031
  464.0 14.2 %all-gather.17.cloned.1.call-done = bf16[512,2048]{1,0:T(8,128)(2,1)} async-done(((bf16[128,2048]{1,0:T(8,128)(2,1)}), bf16[512,2048]{1,0:T(8,128)(2,1)}) %all-gather.17.cloned.1.call-update) | async-done | bytes 2097168 | tf_op jit(solution)/shard_map/all_gather | solution.py:1018
  493.4 3.0 block_out_rows.1
  496.3 3.3 adam.9
  499.7 3.9 adam.7
  503.6 10.4 %collective-permute-done.58 = f32[2,512]{1,0:T(2,128)S(1)} collective-permute-done((f32[2,512]{1,0:T(2,128)S(1)}, f32[2,512]{1,0:T(2,128)S(1)}, u32[]{:S(2)}, u32[]{:S(2)}) %collective-permute-start.58) | collective-permute-done | bytes 4128 | tf_op jit(solution)/shard_map/ppermute | solution.py:558
  515.5 3.9 adam.8
  519.4 3.6 collective-permute-done.52.far
  522.9 4.2 tokens_grad.1
  (315 shorter events, 104.1 us)
Async XLA Ops:
  7.2 37.4 %all-gather.13.cloned.1.call-start = ((), (), s32[]{:S(2)}) async-start(), calls=%async_computation.7 | async-start | bytes 1310720 | tf_op jit(solution)/shard_map/all_gather | solution.py:655
  12.2 151.9 %all-gather.11.cloned.1.call-start = ((), (), s32[]{:S(2)}) async-start(), calls=%async_computation.5 | async-start | bytes 5242880 | tf_op jit(solution)/shard_map/all_gather | solution.py:578
  12.2 15.0 %collective-permute-start = (bf16[512,512]{1,0:T(8,128)(2,1)S(1)}, bf16[512,512]{1,0:T(8,128)(2,1)S(1)}, u32[]{:S(2)}, u32[]{:S(2)}) collective-permute-start(bf16[512,512]{1,0:T(8,128)(2,1)S(1)} %fusion.1.w0), channel_id=1, source_target_pairs={{0,16},{16,0},{1,17},{17,1},{2,18},{18,2},{3,19},{19,3},{4,20},{20... | collective-permute-start | bytes 1572872 | tf_op jit(solution)/shard_map/ppermute | solution.py:561
  15.3 12.0 %collective-permute-start.1 = (bf16[512,512]{1,0:T(8,128)(2,1)S(1)}, bf16[512,512]{1,0:T(8,128)(2,1)S(1)}, u32[]{:S(2)}, u32[]{:S(2)}) collective-permute-start(bf16[512,512]{1,0:T(8,128)(2,1)S(1)} %fusion.1.w0), channel_id=1, source_target_pairs={{0,8},{8,0},{1,9},{9,1},{2,10},{10,2},{3,11},{11,3},{4,12},{12,4},... | collective-permute-start | bytes 1572872 | tf_op jit(solution)/shard_map/ppermute | solution.py:564
  39.3 124.8 %all-gather.9.cloned.1.call-start = ((), (), s32[]{:S(2)}) async-start(), calls=%async_computation.4 | async-start | bytes 10485760 | tf_op jit(solution)/shard_map/all_gather | solution.py:578
  44.6 42.1 %collective-permute-start.4 = (bf16[4,512,256]{2,1,0:T(8,128)(2,1)}, bf16[4,512,256]{2,1,0:T(8,128)(2,1)}, u32[]{:S(2)}, u32[]{:S(2)}) collective-permute-start(bf16[4,512,256]{2,1,0:T(8,128)(2,1)} %bitcast.53), channel_id=1, source_target_pairs={{0,16},{16,0},{1,17},{17,1},{2,18},{18,2},{3,19},{19,3},{4,20},{20... | collective-permute-start | bytes 3145736 | tf_op jit(solution)/shard_map/ppermute | solution.py:561
  56.0 15.2 %all-to-all-start = ((bf16[4,256,256]{2,1,0:T(8,128)(2,1)}), bf16[4,256,256]{2,1,0:T(8,128)(2,1)S(1)}, u32[]{:S(2)}, u32[]{:S(2)}) async-start(bf16[4,256,256]{2,1,0:T(8,128)(2,1)} %bitcast.10), calls=%async_computation | async-start | bytes 1048576 | tf_op jit(solution)/shard_map/all_to_all | solution.py:749
  60.9 333.0 %reduce-scatter.2.cloned.1.call-start = ((), (), s32[]{:S(2)}) async-start(), calls=%async_computation.6 | async-start | bytes 15728640 | tf_op jit(solution)/shard_map/reduce_scatter | solution.py:581
  71.2 15.5 %collective-permute-start.5 = (bf16[4,512,256]{2,1,0:T(8,128)(2,1)S(1)}, bf16[4,512,256]{2,1,0:T(8,128)(2,1)S(1)}, u32[]{:S(2)}, u32[]{:S(2)}) collective-permute-start(bf16[4,512,256]{2,1,0:T(8,128)(2,1)S(1)} %bitcast.54), channel_id=1, source_target_pairs={{0,8},{8,0},{1,9},{9,1},{2,10},{10,2},{3,11},{11,3},{4,12},{12,4},... | collective-permute-start | bytes 3145736 | tf_op jit(solution)/shard_map/ppermute | solution.py:564
  95.0 14.0 %collective-permute-start.7 = (bf16[128,2048]{1,0:T(8,128)(2,1)S(1)}, bf16[128,2048]{1,0:T(8,128)(2,1)S(1)}, u32[]{:S(2)}, u32[]{:S(2)}) collective-permute-start(bf16[128,2048]{1,0:T(8,128)(2,1)S(1)} %get-tuple-element.149), channel_id=1, source_target_pairs={{0,1},{1,0},{2,3},{3,2},{4,5},{5,4},{6,7},{7,6},{8,9},{9,8},{10,11... | collective-permute-start | bytes 1572872 | tf_op jit(solution)/shard_map/ppermute | solution.py:558
  113.3 12.5 %collective-permute-start.8 = (bf16[64,2048]{1,0:T(8,128)(2,1)}, bf16[64,2048]{1,0:T(8,128)(2,1)S(1)}, u32[]{:S(2)}, u32[]{:S(2)}) collective-permute-start(bf16[64,2048]{1,0:T(8,128)(2,1)} %get-tuple-element.151), channel_id=1, source_target_pairs={{0,2},{1,3},{2,0},{3,1},{4,6},{5,7},{6,4},{7,5},{8,10},{9,11},{10,... | collective-permute-start | bytes 786440 | tf_op jit(solution)/shard_map/ppermute | solution.py:558
  114.8 21.6 %collective-permute-start.9 = (bf16[64,2048]{1,0:T(8,128)(2,1)}, bf16[64,2048]{1,0:T(8,128)(2,1)S(1)}, u32[]{:S(2)}, u32[]{:S(2)}) collective-permute-start(bf16[64,2048]{1,0:T(8,128)(2,1)} %get-tuple-element.151), channel_id=1, source_target_pairs={{0,4},{1,5},{2,6},{3,7},{4,0},{5,1},{6,2},{7,3},{8,12},{9,13},{10,... | collective-permute-start | bytes 786440 | tf_op jit(solution)/shard_map/ppermute | solution.py:558
  118.6 17.9 %collective-permute-start.10 = (bf16[64,2048]{1,0:T(8,128)(2,1)}, bf16[64,2048]{1,0:T(8,128)(2,1)S(1)}, u32[]{:S(2)}, u32[]{:S(2)}) collective-permute-start(bf16[64,2048]{1,0:T(8,128)(2,1)} %get-tuple-element.151), channel_id=1, source_target_pairs={{0,6},{1,7},{2,4},{3,5},{4,2},{5,3},{6,0},{7,1},{8,14},{9,15},{10,... | collective-permute-start | bytes 786440 | tf_op jit(solution)/shard_map/ppermute | solution.py:558
  136.5 27.6 %collective-permute-start.11 = (bf16[256,2048]{1,0:T(8,128)(2,1)S(1)}, bf16[256,2048]{1,0:T(8,128)(2,1)}, u32[]{:S(2)}, u32[]{:S(2)}) collective-permute-start(bf16[256,2048]{1,0:T(8,128)(2,1)S(1)} %constant_dynamic-update-slice_fusion.near), channel_id=1, source_target_pairs={{0,1},{1,0},{2,3},{3,2},{4,5},{5,4},{6,7},{7,6},{8,9},{9,8},{10,11... | collective-permute-start | bytes 3145736 | tf_op jit(solution)/shard_map/ppermute | solution.py:558
  138.1 12.7 %collective-permute-start.12 = (bf16[64,2048]{1,0:T(8,128)(2,1)S(1)}, bf16[64,2048]{1,0:T(8,128)(2,1)S(1)}, u32[]{:S(2)}, u32[]{:S(2)}) collective-permute-start(bf16[64,2048]{1,0:T(8,128)(2,1)S(1)} %copy-done.65), channel_id=1, source_target_pairs={{0,2},{1,3},{2,0},{3,1},{4,6},{5,7},{6,4},{7,5},{8,10},{9,11},{10,... | collective-permute-start | bytes 786440 | tf_op jit(solution)/shard_map/ppermute | solution.py:558
  142.4 21.0 %collective-permute-start.13 = (bf16[64,2048]{1,0:T(8,128)(2,1)S(1)}, bf16[64,2048]{1,0:T(8,128)(2,1)S(1)}, u32[]{:S(2)}, u32[]{:S(2)}) collective-permute-start(bf16[64,2048]{1,0:T(8,128)(2,1)S(1)} %copy-done.65), channel_id=1, source_target_pairs={{0,4},{1,5},{2,6},{3,7},{4,0},{5,1},{6,2},{7,3},{8,12},{9,13},{10,... | collective-permute-start | bytes 786440 | tf_op jit(solution)/shard_map/ppermute | solution.py:558
  143.4 20.0 %collective-permute-start.14 = (bf16[64,2048]{1,0:T(8,128)(2,1)S(1)}, bf16[64,2048]{1,0:T(8,128)(2,1)S(1)}, u32[]{:S(2)}, u32[]{:S(2)}) collective-permute-start(bf16[64,2048]{1,0:T(8,128)(2,1)S(1)} %copy-done.65), channel_id=1, source_target_pairs={{0,6},{1,7},{2,4},{3,5},{4,2},{5,3},{6,0},{7,1},{8,14},{9,15},{10,... | collective-permute-start | bytes 786440 | tf_op jit(solution)/shard_map/ppermute | solution.py:558
  163.5 31.0 %collective-permute-start.15 = (bf16[256,2048]{1,0:T(8,128)(2,1)S(1)}, bf16[256,2048]{1,0:T(8,128)(2,1)}, u32[]{:S(2)}, u32[]{:S(2)}) collective-permute-start(bf16[256,2048]{1,0:T(8,128)(2,1)S(1)} %constant_dynamic-update-slice_fusion.4.near), channel_id=1, source_target_pairs={{0,1},{1,0},{2,3},{3,2},{4,5},{5,4},{6,7},{7,6},{8,9},{9,8},{10,11... | collective-permute-start | bytes 3145736 | tf_op jit(solution)/shard_map/ppermute | solution.py:558
  186.9 31.3 %collective-permute-start.17 = (bf16[256,2048]{1,0:T(8,128)(2,1)}, bf16[256,2048]{1,0:T(8,128)(2,1)S(1)}, u32[]{:S(2)}, u32[]{:S(2)}) collective-permute-start(bf16[256,2048]{1,0:T(8,128)(2,1)} %get-tuple-element.167), channel_id=1, source_target_pairs={{0,1},{1,0},{2,3},{3,2},{4,5},{5,4},{6,7},{7,6},{8,9},{9,8},{10,11... | collective-permute-start | bytes 3145736 | tf_op jit(solution)/shard_map/ppermute | solution.py:558
  188.6 32.1 %collective-permute-start.18 = (bf16[512,384]{1,0:T(8,128)(2,1)S(1)}, bf16[512,384]{1,0:T(8,128)(2,1)S(1)}, u32[]{:S(2)}, u32[]{:S(2)}) collective-permute-start(bf16[512,384]{1,0:T(8,128)(2,1)S(1)} %pad_maximum_fusion.7), channel_id=1, source_target_pairs={{0,2},{1,3},{2,0},{3,1},{4,6},{5,7},{6,4},{7,5},{8,10},{9,11},{10,... | collective-permute-start | bytes 1179656 | tf_op jit(solution)/shard_map/ppermute | solution.py:558
  192.1 30.4 %collective-permute-start.19 = (bf16[512,384]{1,0:T(8,128)(2,1)S(1)}, bf16[512,384]{1,0:T(8,128)(2,1)S(1)}, u32[]{:S(2)}, u32[]{:S(2)}) collective-permute-start(bf16[512,384]{1,0:T(8,128)(2,1)S(1)} %pad_maximum_fusion.7), channel_id=1, source_target_pairs={{0,4},{1,5},{2,6},{3,7},{4,0},{5,1},{6,2},{7,3},{8,12},{9,13},{10,... | collective-permute-start | bytes 1179656 | tf_op jit(solution)/shard_map/ppermute | solution.py:558
  193.0 31.0 %collective-permute-start.20 = (bf16[512,384]{1,0:T(8,128)(2,1)S(1)}, bf16[512,384]{1,0:T(8,128)(2,1)S(1)}, u32[]{:S(2)}, u32[]{:S(2)}) collective-permute-start(bf16[512,384]{1,0:T(8,128)(2,1)S(1)} %pad_maximum_fusion.7), channel_id=1, source_target_pairs={{0,6},{1,7},{2,4},{3,5},{4,2},{5,3},{6,0},{7,1},{8,14},{9,15},{10,... | collective-permute-start | bytes 1179656 | tf_op jit(solution)/shard_map/ppermute | solution.py:558
  217.7 26.6 %collective-permute-start.16 = (bf16[256,2048]{1,0:T(8,128)(2,1)}, bf16[256,2048]{1,0:T(8,128)(2,1)}, u32[]{:S(2)}, u32[]{:S(2)}) collective-permute-start(bf16[256,2048]{1,0:T(8,128)(2,1)} %get-tuple-element.162), channel_id=1, source_target_pairs={{0,1},{1,0},{2,3},{3,2},{4,5},{5,4},{6,7},{7,6},{8,9},{9,8},{10,11... | collective-permute-start | bytes 3145736 | tf_op jit(solution)/shard_map/ppermute | solution.py:558
  219.6 24.7 %collective-permute-start.21 = (bf16[64,2048]{1,0:T(8,128)(2,1)}, bf16[64,2048]{1,0:T(8,128)(2,1)S(1)}, u32[]{:S(2)}, u32[]{:S(2)}) collective-permute-start(bf16[64,2048]{1,0:T(8,128)(2,1)} %get-tuple-element.281), channel_id=1, source_target_pairs={{0,2},{1,3},{2,0},{3,1},{4,6},{5,7},{6,4},{7,5},{8,10},{9,11},{10,... | collective-permute-start | bytes 786440 | tf_op jit(solution)/shard_map/ppermute | solution.py:558
  220.6 25.1 %collective-permute-start.22 = (bf16[64,2048]{1,0:T(8,128)(2,1)}, bf16[64,2048]{1,0:T(8,128)(2,1)}, u32[]{:S(2)}, u32[]{:S(2)}) collective-permute-start(bf16[64,2048]{1,0:T(8,128)(2,1)} %get-tuple-element.280), channel_id=1, source_target_pairs={{0,4},{1,5},{2,6},{3,7},{4,0},{5,1},{6,2},{7,3},{8,12},{9,13},{10,... | collective-permute-start | bytes 786440 | tf_op jit(solution)/shard_map/ppermute | solution.py:558
  222.5 23.3 %collective-permute-start.23 = (bf16[64,2048]{1,0:T(8,128)(2,1)}, bf16[64,2048]{1,0:T(8,128)(2,1)}, u32[]{:S(2)}, u32[]{:S(2)}) collective-permute-start(bf16[64,2048]{1,0:T(8,128)(2,1)} %get-tuple-element.279), channel_id=1, source_target_pairs={{0,6},{1,7},{2,4},{3,5},{4,2},{5,3},{6,0},{7,1},{8,14},{9,15},{10,... | collective-permute-start | bytes 786440 | tf_op jit(solution)/shard_map/ppermute | solution.py:558
  249.4 38.2 %collective-permute-start.24 = (bf16[4,64,2048]{2,1,0:T(8,128)(2,1)}, bf16[4,64,2048]{2,1,0:T(8,128)(2,1)}, u32[]{:S(2)}, u32[]{:S(2)}) collective-permute-start(bf16[4,64,2048]{2,1,0:T(8,128)(2,1)} %get-tuple-element.177), channel_id=1, source_target_pairs={{0,1},{1,0},{2,3},{3,2},{4,5},{5,4},{6,7},{7,6},{8,9},{9,8},{10,11... | collective-permute-start | bytes 3145736 | tf_op jit(solution)/shard_map/ppermute | solution.py:558
  251.2 23.9 %collective-permute-start.25 = (bf16[64,2048]{1,0:T(8,128)(2,1)S(1)}, bf16[64,2048]{1,0:T(8,128)(2,1)S(1)}, u32[]{:S(2)}, u32[]{:S(2)}) collective-permute-start(bf16[64,2048]{1,0:T(8,128)(2,1)S(1)} %get-tuple-element.278), channel_id=1, source_target_pairs={{0,2},{1,3},{2,0},{3,1},{4,6},{5,7},{6,4},{7,5},{8,10},{9,11},{10,... | collective-permute-start | bytes 786440 | tf_op jit(solution)/shard_map/ppermute | solution.py:558
  268.0 13.0 %collective-permute-start.26 = (bf16[64,2048]{1,0:T(8,128)(2,1)S(1)}, bf16[64,2048]{1,0:T(8,128)(2,1)}, u32[]{:S(2)}, u32[]{:S(2)}) collective-permute-start(bf16[64,2048]{1,0:T(8,128)(2,1)S(1)} %get-tuple-element.277), channel_id=1, source_target_pairs={{0,4},{1,5},{2,6},{3,7},{4,0},{5,1},{6,2},{7,3},{8,12},{9,13},{10,... | collective-permute-start | bytes 786440 | tf_op jit(solution)/shard_map/ppermute | solution.py:558
  268.4 12.6 %collective-permute-start.27 = (bf16[64,2048]{1,0:T(8,128)(2,1)S(1)}, bf16[64,2048]{1,0:T(8,128)(2,1)}, u32[]{:S(2)}, u32[]{:S(2)}) collective-permute-start(bf16[64,2048]{1,0:T(8,128)(2,1)S(1)} %get-tuple-element.276), channel_id=1, source_target_pairs={{0,6},{1,7},{2,4},{3,5},{4,2},{5,3},{6,0},{7,1},{8,14},{9,15},{10,... | collective-permute-start | bytes 786440 | tf_op jit(solution)/shard_map/ppermute | solution.py:558
  270.5 51.8 %collective-permute-start.33 = (bf16[4,512,384]{2,1,0:T(8,128)(2,1)S(1)}, bf16[4,512,384]{2,1,0:T(8,128)(2,1)}, u32[]{:S(2)}, u32[]{:S(2)}) collective-permute-start(bf16[4,512,384]{2,1,0:T(8,128)(2,1)S(1)} %pad_maximum_fusion.1.w0), channel_id=1, source_target_pairs={{0,16},{16,0},{1,17},{17,1},{2,18},{18,2},{3,19},{19,3},{4,20},{20... | collective-permute-start | bytes 4718600 | tf_op jit(solution)/shard_map/ppermute | solution.py:561
  286.0 11.5 %collective-permute-start.28 = (bf16[128,2048]{1,0:T(8,128)(2,1)}, bf16[128,2048]{1,0:T(8,128)(2,1)S(1)}, u32[]{:S(2)}, u32[]{:S(2)}) collective-permute-start(bf16[128,2048]{1,0:T(8,128)(2,1)} %get-tuple-element.179.own), channel_id=1, source_target_pairs={{0,1},{1,0},{2,3},{3,2},{4,5},{5,4},{6,7},{7,6},{8,9},{9,8},{10,11... | collective-permute-start | bytes 1572872 | tf_op jit(solution)/shard_map/ppermute | solution.py:558
  298.3 31.0 %collective-permute-start.29 = (bf16[4,64,2048]{2,1,0:T(8,128)(2,1)}, bf16[4,64,2048]{2,1,0:T(8,128)(2,1)}, u32[]{:S(2)}, u32[]{:S(2)}) collective-permute-start(bf16[4,64,2048]{2,1,0:T(8,128)(2,1)} %get-tuple-element.184), channel_id=1, source_target_pairs={{0,1},{1,0},{2,3},{3,2},{4,5},{5,4},{6,7},{7,6},{8,9},{9,8},{10,11... | collective-permute-start | bytes 3145736 | tf_op jit(solution)/shard_map/ppermute | solution.py:558
  300.0 32.0 %all-to-all-start.1 = ((bf16[4,64,2048]{2,1,0:T(8,128)(2,1)}), bf16[4,64,2048]{2,1,0:T(8,128)(2,1)}, u32[]{:S(2)}, u32[]{:S(2)}) async-start(bf16[4,64,2048]{2,1,0:T(8,128)(2,1)} %add_convert_fusion.2), calls=%async_computation.1 | async-start | bytes 2097152 | tf_op jit(solution)/shard_map/all_to_all | solution.py:892
  317.2 7.8 %collective-permute-start.30 = (bf16[256,256]{1,0:T(8,128)(2,1)S(1)}, bf16[256,256]{1,0:T(8,128)(2,1)S(1)}, u32[]{:S(2)}, u32[]{:S(2)}) collective-permute-start(bf16[256,256]{1,0:T(8,128)(2,1)S(1)} %get-tuple-element.186), channel_id=1, source_target_pairs={{0,2},{1,3},{2,0},{3,1},{4,6},{5,7},{6,4},{7,5},{8,10},{9,11},{10,... | collective-permute-start | bytes 393224 | tf_op jit(solution)/shard_map/ppermute | solution.py:558
  320.0 8.7 %collective-permute-start.31 = (bf16[256,256]{1,0:T(8,128)(2,1)S(1)}, bf16[256,256]{1,0:T(8,128)(2,1)S(1)}, u32[]{:S(2)}, u32[]{:S(2)}) collective-permute-start(bf16[256,256]{1,0:T(8,128)(2,1)S(1)} %get-tuple-element.187), channel_id=1, source_target_pairs={{0,4},{1,5},{2,6},{3,7},{4,0},{5,1},{6,2},{7,3},{8,12},{9,13},{10,... | collective-permute-start | bytes 393224 | tf_op jit(solution)/shard_map/ppermute | solution.py:558
  321.7 7.0 %collective-permute-start.32 = (bf16[256,256]{1,0:T(8,128)(2,1)S(1)}, bf16[256,256]{1,0:T(8,128)(2,1)S(1)}, u32[]{:S(2)}, u32[]{:S(2)}) collective-permute-start(bf16[256,256]{1,0:T(8,128)(2,1)S(1)} %get-tuple-element.188), channel_id=1, source_target_pairs={{0,6},{1,7},{2,4},{3,5},{4,2},{5,3},{6,0},{7,1},{8,14},{9,15},{10,... | collective-permute-start | bytes 393224 | tf_op jit(solution)/shard_map/ppermute | solution.py:558
  322.3 14.1 %collective-permute-start.34 = (bf16[4,512,384]{2,1,0:T(8,128)(2,1)S(1)}, bf16[4,512,384]{2,1,0:T(8,128)(2,1)}, u32[]{:S(2)}, u32[]{:S(2)}) collective-permute-start(bf16[4,512,384]{2,1,0:T(8,128)(2,1)S(1)} %pad_maximum_fusion.1.w0), channel_id=1, source_target_pairs={{0,8},{8,0},{1,9},{9,1},{2,10},{10,2},{3,11},{11,3},{4,12},{12,4},... | collective-permute-start | bytes 4718600 | tf_op jit(solution)/shard_map/ppermute | solution.py:564
  325.1 11.3 %collective-permute-start.35 = (bf16[4,512,384]{2,1,0:T(8,128)(2,1)}, bf16[4,512,384]{2,1,0:T(8,128)(2,1)}, u32[]{:S(2)}, u32[]{:S(2)}) collective-permute-start(bf16[4,512,384]{2,1,0:T(8,128)(2,1)} %collective-permute-done.33.w1), channel_id=1, source_target_pairs={{0,8},{8,0},{1,9},{9,1},{2,10},{10,2},{3,11},{11,3},{4,12},{12,4},... | collective-permute-start | bytes 4718600 | tf_op jit(solution)/shard_map/ppermute | solution.py:564
  332.1 49.4 %all-to-all-start.2 = ((bf16[4,64,2048]{2,1,0:T(8,128)(2,1)}), bf16[4,64,2048]{2,1,0:T(8,128)(2,1)}, u32[]{:S(2)}, u32[]{:S(2)}) async-start(bf16[4,64,2048]{2,1,0:T(8,128)(2,1)} %add_convert_fusion.1), calls=%async_computation.2 | async-start | bytes 2097152 | tf_op jit(solution)/shard_map/all_to_all | solution.py:911
  336.3 96.1 %all-gather.15.cloned.1.call-start = ((), (), s32[]{:S(2)}) async-start(), calls=%async_computation.8 | async-start | bytes 2621440 | tf_op jit(solution)/shard_map/all_gather | solution.py:1000
  354.1 23.5 %collective-permute-start.36 = (bf16[1024,128]{1,0:T(8,128)(2,1)S(1)}, bf16[1024,128]{1,0:T(8,128)(2,1)S(1)}, u32[]{:S(2)}, u32[]{:S(2)}) collective-permute-start(bf16[1024,128]{1,0:T(8,128)(2,1)S(1)} %get-tuple-element.286), channel_id=1, source_target_pairs={{0,8},{8,0},{1,9},{9,1},{2,10},{10,2},{3,11},{11,3},{4,12},{12,4},... | collective-permute-start | bytes 786440 | tf_op jit(solution)/shard_map/ppermute | solution.py:564
  363.0 7.1 %collective-permute-start.37 = (bf16[256,256]{1,0:T(8,128)(2,1)S(1)}, bf16[256,256]{1,0:T(8,128)(2,1)S(1)}, u32[]{:S(2)}, u32[]{:S(2)}) collective-permute-start(bf16[256,256]{1,0:T(8,128)(2,1)S(1)} %get-tuple-element.199), channel_id=1, source_target_pairs={{0,2},{1,3},{2,0},{3,1},{4,6},{5,7},{6,4},{7,5},{8,10},{9,11},{10,... | collective-permute-start | bytes 393224 | tf_op jit(solution)/shard_map/ppermute | solution.py:558
  364.7 12.9 %collective-permute-start.38 = (bf16[256,256]{1,0:T(8,128)(2,1)S(1)}, bf16[256,256]{1,0:T(8,128)(2,1)S(1)}, u32[]{:S(2)}, u32[]{:S(2)}) collective-permute-start(bf16[256,256]{1,0:T(8,128)(2,1)S(1)} %get-tuple-element.200), channel_id=1, source_target_pairs={{0,4},{1,5},{2,6},{3,7},{4,0},{5,1},{6,2},{7,3},{8,12},{9,13},{10,... | collective-permute-start | bytes 393224 | tf_op jit(solution)/shard_map/ppermute | solution.py:558
  367.1 10.5 %collective-permute-start.39 = (bf16[256,256]{1,0:T(8,128)(2,1)S(1)}, bf16[256,256]{1,0:T(8,128)(2,1)S(1)}, u32[]{:S(2)}, u32[]{:S(2)}) collective-permute-start(bf16[256,256]{1,0:T(8,128)(2,1)S(1)} %get-tuple-element.201), channel_id=1, source_target_pairs={{0,6},{1,7},{2,4},{3,5},{4,2},{5,3},{6,0},{7,1},{8,14},{9,15},{10,... | collective-permute-start | bytes 393224 | tf_op jit(solution)/shard_map/ppermute | solution.py:558
  384.6 93.6 %all-gather.17.cloned.1.call-start = ((), (), s32[]{:S(2)}) async-start(), calls=%async_computation.9 | async-start | bytes 2621440 | tf_op jit(solution)/shard_map/all_gather | solution.py:1018
  384.6 5.1 collective-permute-start.40
  386.8 7.1 %collective-permute-start.41 = (bf16[256,128]{1,0:T(8,128)(2,1)S(1)}, bf16[256,128]{1,0:T(8,128)(2,1)S(1)}, u32[]{:S(2)}, u32[]{:S(2)}) collective-permute-start(bf16[256,128]{1,0:T(8,128)(2,1)S(1)} %copy-done.73), channel_id=1, source_target_pairs={{0,4},{1,5},{2,6},{3,7},{4,0},{5,1},{6,2},{7,3},{8,12},{9,13},{10,... | collective-permute-start | bytes 196616 | tf_op jit(solution)/shard_map/ppermute | solution.py:558
  387.9 6.1 %collective-permute-start.42 = (bf16[256,128]{1,0:T(8,128)(2,1)S(1)}, bf16[256,128]{1,0:T(8,128)(2,1)S(1)}, u32[]{:S(2)}, u32[]{:S(2)}) collective-permute-start(bf16[256,128]{1,0:T(8,128)(2,1)S(1)} %copy-done.72), channel_id=1, source_target_pairs={{0,6},{1,7},{2,4},{3,5},{4,2},{5,3},{6,0},{7,1},{8,14},{9,15},{10,... | collective-permute-start | bytes 196616 | tf_op jit(solution)/shard_map/ppermute | solution.py:558
  400.3 14.4 %collective-permute-start.43 = (bf16[128,2048]{1,0:T(8,128)(2,1)S(1)}, bf16[128,2048]{1,0:T(8,128)(2,1)S(1)}, u32[]{:S(2)}, u32[]{:S(2)}) collective-permute-start(bf16[128,2048]{1,0:T(8,128)(2,1)S(1)} %get-tuple-element.216), channel_id=1, source_target_pairs={{0,1},{1,0},{2,3},{3,2},{4,5},{5,4},{6,7},{7,6},{8,9},{9,8},{10,11... | collective-permute-start | bytes 1572872 | tf_op jit(solution)/shard_map/ppermute | solution.py:558
  407.6 13.2 %collective-permute-start.48 = (bf16[1024,1024]{1,0:T(8,128)(2,1)}, bf16[1024,1024]{1,0:T(8,128)(2,1)}, u32[]{:S(2)}, u32[]{:S(2)}) collective-permute-start(bf16[1024,1024]{1,0:T(8,128)(2,1)} %get-tuple-element.225), channel_id=1, source_target_pairs={{0,8},{8,0},{1,9},{9,1},{2,10},{10,2},{3,11},{11,3},{4,12},{12,4},... | collective-permute-start | bytes 6291464 | tf_op jit(solution)/shard_map/ppermute | solution.py:564
  420.1 10.6 %collective-permute-start.50 = (bf16[1024,384]{1,0:T(8,128)(2,1)}, bf16[1024,384]{1,0:T(8,128)(2,1)S(1)}, u32[]{:S(2)}, u32[]{:S(2)}) collective-permute-start(bf16[1024,384]{1,0:T(8,128)(2,1)} %get-tuple-element.221), channel_id=1, source_target_pairs={{0,8},{8,0},{1,9},{9,1},{2,10},{10,2},{3,11},{11,3},{4,12},{12,4},... | collective-permute-start | bytes 2359304 | tf_op jit(solution)/shard_map/ppermute | solution.py:564
  424.9 39.1 %collective-permute-start.49 = (bf16[512,1024]{1,0:T(8,128)(2,1)}, bf16[512,1024]{1,0:T(8,128)(2,1)}, u32[]{:S(2)}, u32[]{:S(2)}) collective-permute-start(bf16[512,1024]{1,0:T(8,128)(2,1)} %pair_sum.2), channel_id=1, source_target_pairs={{0,16},{16,0},{1,17},{17,1},{2,18},{18,2},{3,19},{19,3},{4,20},{20... | collective-permute-start | bytes 3145736 | tf_op jit(solution)/shard_map/ppermute | solution.py:561
  428.6 14.0 %collective-permute-start.44 = (bf16[128,2048]{1,0:T(8,128)(2,1)}, bf16[128,2048]{1,0:T(8,128)(2,1)S(1)}, u32[]{:S(2)}, u32[]{:S(2)}) collective-permute-start(bf16[128,2048]{1,0:T(8,128)(2,1)} %first_norm_back.1), channel_id=1, source_target_pairs={{0,1},{1,0},{2,3},{3,2},{4,5},{5,4},{6,7},{7,6},{8,9},{9,8},{10,11... | collective-permute-start | bytes 1572872 | tf_op jit(solution)/shard_map/ppermute | solution.py:558
  431.7 32.3 %collective-permute-start.51 = (bf16[512,384]{1,0:T(8,128)(2,1)}, bf16[512,384]{1,0:T(8,128)(2,1)}, u32[]{:S(2)}, u32[]{:S(2)}) collective-permute-start(bf16[512,384]{1,0:T(8,128)(2,1)} %pair_sum.3), channel_id=1, source_target_pairs={{0,16},{16,0},{1,17},{17,1},{2,18},{18,2},{3,19},{19,3},{4,20},{20... | collective-permute-start | bytes 1179656 | tf_op jit(solution)/shard_map/ppermute | solution.py:561
  431.9 12.3 %collective-permute-start.47 = (f32[2,1024]{1,0:T(2,128)S(1)}, f32[2,1024]{1,0:T(2,128)S(1)}, u32[]{:S(2)}, u32[]{:S(2)}) collective-permute-start(f32[2,1024]{1,0:T(2,128)S(1)} %fusion.4), channel_id=1, source_target_pairs={{0,1},{1,0},{2,3},{3,2},{4,5},{5,4},{6,7},{7,6},{8,9},{9,8},{10,11... | collective-permute-start | bytes 24584 | tf_op jit(solution)/shard_map/ppermute | solution.py:558
  442.6 48.8 %collective-permute-start.45 = (bf16[4,128,2048]{2,1,0:T(8,128)(2,1)}, bf16[4,128,2048]{2,1,0:T(8,128)(2,1)S(1)}, u32[]{:S(2)}, u32[]{:S(2)}) collective-permute-start(bf16[4,128,2048]{2,1,0:T(8,128)(2,1)} %bitcast.57), channel_id=1, source_target_pairs={{0,1},{1,0},{2,3},{3,2},{4,5},{5,4},{6,7},{7,6},{8,9},{9,8},{10,11... | collective-permute-start | bytes 6291464 | tf_op jit(solution)/shard_map/ppermute | solution.py:558
  481.0 41.9 %collective-permute-start.52 = (bf16[3,128,2048]{2,1,0:T(8,128)(2,1)}, bf16[3,128,2048]{2,1,0:T(8,128)(2,1)S(1)}, u32[]{:S(2)}, u32[]{:S(2)}) collective-permute-start(bf16[3,128,2048]{2,1,0:T(8,128)(2,1)} %pad_maximum_fusion.2), channel_id=1, source_target_pairs={{0,1},{1,0},{2,3},{3,2},{4,5},{5,4},{6,7},{7,6},{8,9},{9,8},{10,11... | collective-permute-start | bytes 4718600 | tf_op jit(solution)/shard_map/ppermute | solution.py:558
  482.5 3.7 collective-permute-start.56
  486.1 4.0 collective-permute-start.57
  487.0 27.5 %collective-permute-start.53 = (bf16[512,256]{1,0:T(8,128)(2,1)S(1)}, bf16[512,256]{1,0:T(8,128)(2,1)S(1)}, u32[]{:S(2)}, u32[]{:S(2)}) collective-permute-start(bf16[512,256]{1,0:T(8,128)(2,1)S(1)} %get-tuple-element.274), channel_id=1, source_target_pairs={{0,2},{1,3},{2,0},{3,1},{4,6},{5,7},{6,4},{7,5},{8,10},{9,11},{10,... | collective-permute-start | bytes 786440 | tf_op jit(solution)/shard_map/ppermute | solution.py:558
  489.0 25.5 %collective-permute-start.54 = (bf16[512,256]{1,0:T(8,128)(2,1)S(1)}, bf16[512,256]{1,0:T(8,128)(2,1)S(1)}, u32[]{:S(2)}, u32[]{:S(2)}) collective-permute-start(bf16[512,256]{1,0:T(8,128)(2,1)S(1)} %get-tuple-element.273), channel_id=1, source_target_pairs={{0,4},{1,5},{2,6},{3,7},{4,0},{5,1},{6,2},{7,3},{8,12},{9,13},{10,... | collective-permute-start | bytes 786440 | tf_op jit(solution)/shard_map/ppermute | solution.py:558
  490.1 24.5 %collective-permute-start.55 = (bf16[512,256]{1,0:T(8,128)(2,1)S(1)}, bf16[512,256]{1,0:T(8,128)(2,1)S(1)}, u32[]{:S(2)}, u32[]{:S(2)}) collective-permute-start(bf16[512,256]{1,0:T(8,128)(2,1)S(1)} %get-tuple-element.272), channel_id=1, source_target_pairs={{0,6},{1,7},{2,4},{3,5},{4,2},{5,3},{6,0},{7,1},{8,14},{9,15},{10,... | collective-permute-start | bytes 786440 | tf_op jit(solution)/shard_map/ppermute | solution.py:558
  491.4 22.5 %collective-permute-start.58 = (f32[2,512]{1,0:T(2,128)S(1)}, f32[2,512]{1,0:T(2,128)S(1)}, u32[]{:S(2)}, u32[]{:S(2)}) collective-permute-start(f32[2,512]{1,0:T(2,128)S(1)} %add.120), channel_id=1, source_target_pairs={{0,4},{1,5},{2,6},{3,7},{4,0},{5,1},{6,2},{7,3},{8,12},{9,13},{10,... | collective-permute-start | bytes 12296 | tf_op jit(solution)/shard_map/ppermute | solution.py:558
  (79 other events, 1361.8 us)
Sparse Core Ops, SparseCore 0:
  12.3 30.6 all-gather.12
  45.1 49.2 all-gather.10
  96.5 59.7 all-gather.8
  249.5 113.8 reduce-scatter.1
  384.7 46.7 all-gather.14
  433.5 44.6 all-gather.16

commit v4 on v3

--- a/solution.py
+++ b/solution.py
@@ -260,8 +260,9 @@
 
 
 def mlp_kernel(
-    info, near, far, dy, gate_up_all, down_all, *rest,
+    parts, info, *refs,
 ):
+    sources, (dy, weights, *rest) = refs[: 2 * parts], refs[2 * parts :]
     mlp_keep, mlp_send, two_keep, two_send, hidden_out, grad_out, x, gate_up, down, sems = rest[-10:]
     step = pl.program_id(0)
     wide = FF // 8
@@ -271,17 +272,22 @@
         cols = pl.ds(group * 256, 256)
         up_cols = pl.ds(wide + group * 256, 256)
         for k, (src, dst, c) in enumerate(
-            ((gate_up_all, gate_up, cols), (gate_up_all, gate_up, up_cols), (down_all, down, cols))
+            ((cols, gate_up, cols), (up_cols, gate_up, up_cols), (pl.ds(2 * wide + group * 256, 256), down, cols))
         ):
-            yield pltpu.make_async_copy(src.at[:, c], dst.at[:, c], sems.at[group, k])
+            yield pltpu.make_async_copy(weights.at[:, src], dst.at[:, c], sems.at[group, k])
 
     @pl.when(step == 0)
     def _():
         for group in range(4):
             for copy in copies(group):
                 copy.start()
-        x[: n // 2] = near[...]
-        x[n // 2 :] = far[...]
+        size = n // 8
+        piece = size // parts
+        for i, source in enumerate(sources):
+            half, part = divmod(i, parts)
+            for k in range(4):
+                at = (half * 4 + k) * size + part * piece
+                x[at : at + piece] = source[k * piece : (k + 1) * piece]
 
     for group in range(4):
 
@@ -744,8 +750,7 @@
         name="attend",
     )(info, queries, kv_all)
 
-    gate_up_w = gather_all(gate_up_low)
-    down_w = gather_all(down_low)
+    mlp_w = gather_all(jnp.concatenate([gate_up_low, down_low], axis=1))
     att_parts = lax.all_to_all(
         attended.reshape(4, rows, 256), "tensor", 0, 0, axis_index_groups=HIGH_GROUPS
     )
@@ -785,7 +790,7 @@
         name="second_norm",
     )(info, out_keep, out_got, token_rows, gains)
 
-    def mlp(chunk, near, far, before):
+    def mlp(chunk, nears, fars, before):
         n = half_span
         anywhere = pl.BlockSpec(memory_space=pl.ANY)
         late_columns = pl.BlockSpec(
@@ -793,13 +798,13 @@
         )
         late_half = pl.BlockSpec((n // 2, QUARTER), lambda i, info: (0, jnp.maximum(i - 4, 0)))
         return pl.pallas_call(
-            mlp_kernel,
+            functools.partial(mlp_kernel, len(nears)),
             grid_spec=pltpu.PrefetchScalarGridSpec(
                 num_scalar_prefetch=1,
                 grid=(8,),
-                in_specs=[whole((n // 2, D))] * 2
+                in_specs=[whole((n // 2 // len(nears), D))] * (2 * len(nears))
                 + [pl.BlockSpec((1, n, D), lambda i, info: (chunk, 0, 0))]
-                + [anywhere] * (2 + len(before)),
+                + [anywhere] * (1 + len(before)),
                 out_specs=[
                     late_columns,
                     late_columns,
@@ -824,24 +829,24 @@
                 jax.ShapeDtypeStruct((span, 2048), BF16),
                 jax.ShapeDtypeStruct((span, D), BF16),
             ],
-            input_output_aliases={6: 4, 7: 5, 8: 6} if before else {},
+            input_output_aliases={5: 4, 6: 5, 7: 6} if before else {},
             compiler_params=vmem(56),
             cost_estimate=cost(22.5),
             name="mlp",
-        )(info, near, far, dy, gate_up_w, down_w, *before)
+        )(info, *nears, *fars, dy, mlp_w, *before)
 
     near_a = gather_near(low_a)
     near_b = gather_near(low_b)
     far_a = after(swap_tensor(near_a, 1), near_b)
     far_b = swap_tensor(near_b, 1)
     mlp_keep_a, mlp_send_a, two_keep_a, two_send_a, hidden, gate_up_back, x = mlp(
-        0, near_a, far_a, ()
+        0, (near_a,), (far_a,), ()
     )
     two_got_a = swap_tensor(two_send_a, 1)
     back_low = after(back_low, near_b)
     back_parts = [swap_tensor(back_low, mask) for mask in (2, 4, 6)]
     mlp_keep_b, mlp_send_b, two_keep_b, two_send_b, hidden, gate_up_back, x = mlp(
-        1, near_b, far_b, (hidden, gate_up_back, x)
+        1, (near_b,), (far_b,), (hidden, gate_up_back, x)
     )
     two_got_b = swap_tensor(two_send_b, 1)
     total_a = two_keep_a.astype(F32) + after(two_got_a, two_send_b).astype(F32)

time: 543 us -> 535 us (0.985)
    unnamed x157 -> x161, local copies, waits for them, and re-layouts: 25.5 us -> 25.4 us
  transfers between devices with their start and end apart: 68 -> 67, of which waited for: 24 -> 26; matrix products, arithmetic and copies ran while one was open for 6% -> 6% of each run, Pallas kernels for 34% -> 34%
where the time goes in v4:
time: 535 us; the launch traced here: 526 us
  Pallas kernels  184 us (34%)
  waiting for transfers between devices  145 us (27%)
  starting transfers between devices  121 us (23%)
  local copies, waits for them, and re-layouts  34.8 us (7%)
  other arithmetic  26 us (5%)
  between operations  15.2 us (3%)
    ppermute x42, waiting for transfers between devices, swap_tensor(): return lax.ppermute(value, 'tensor', [(i, i ^ mask) for i in range(8)])  107 us
    ppermute x42, starting transfers between devices, swap_tensor(): return lax.ppermute(value, 'tensor', [(i, i ^ mask) for i in range(8)])  76.3 us
    pallas_call x2, Pallas kernels, mlp(): pl.pallas_call(functools.partial(mlp_kernel, len(nears)), grid_spec=pltpu...  45.9 us
    pallas_call x5, Pallas kernels, adam(): pl.pallas_call(functools.partial(adam_kernel, rate, decay), grid=(4,), in...  30.9 us
    unnamed x161, local copies, waits for them, and re-layouts  25.4 us
    pallas_call x1, Pallas kernels, body(): pl.pallas_call(mlp_grad_kernel, grid=(4,), in_specs=[narrow, whole((span,...  19.2 us
    ppermute x11, starting transfers between devices, swap_seq(): return lax.ppermute(value, 'seq', [(0, 1), (1, 0)])  16 us
    all_gather x1, waiting for transfers between devices, body(): lax.all_gather(tokens_low, 'tensor', axis=0, axis_index_groups=HIGH_GROUPS)  14.2 us
  transfers between devices with their start and end apart: 67, of which 26 were waited for; matrix products, arithmetic and copies ran while one was open for 6% of the time, Pallas kernels for 34%

profile of v4, /device:TPU:0, one launch (start us, length us, event | category | flops | bytes accessed | tf_op | source)
XLA Modules:
  0.0 526.1 jit_solution(2652741752463873382)
XLA Ops:
  10.4 3.0 collective-permute-start
  17.1 8.2 %collective-permute-done.w1 = bf16[512,512]{1,0:T(8,128)(2,1)S(1)} collective-permute-done((bf16[512,512]{1,0:T(8,128)(2,1)S(1)}, bf16[512,512]{1,0:T(8,128)(2,1)S(1)}, u32[]{:S(2)}, u32[]{:S(2)}) %collective-permute-start) | collective-permute-done | bytes 524320 | tf_op jit(solution)/shard_map/ppermute | solution.py:567
  28.5 7.3 %project.1 = (bf16[1024,2048]{1,0:T(8,128)(2,1)}, bf16[1024,256]{1,0:T(8,128)(2,1)S(1)}, bf16[1024,128]{1,0:T(8,128)(2,1)S(1)}, f32[8,2048]{1,0:T(8,128)S(1)}) custom-call(s32[9]{0:T(128)S(1)} %stack.69.info, bf16[1024,2048]{1,0:T(8,128)(2,1)} %bitcast.60, bf16[512,512]{1,0:T(8,128)(2,1)S(1)} %copy-done.23, bf16[512,512]{1,0:T(8,128)(2,1)S(1)} %collective-permute-done.w1, ...), custom_call_target="tpu_custom_call" | custom-call | bytes 12915000 | tf_op jit(solution)/shard_map/project/pallas_call | solution.py:681
  40.1 2.7 all-gather.10.cloned.1.call-done
  44.4 8.1 %attend.1 = (bf16[1024,256]{1,0:T(8,128)(2,1)}, f32[4,1,1024]{2,1,0:T(1,128)S(1)}) custom-call(s32[9]{0:T(128)S(1)} %stack.69.info, bf16[1024,256]{1,0:T(8,128)(2,1)S(1)} %get-tuple-element.140.q, bf16[2048,128]{1,0:T(8,128)(2,1)S(1)} %maximum_select_fusion.kv), custom_call_target="tpu_custom_call" | custom-call | bytes 33210000 | tf_op jit(solution)/shard_map/attend/pallas_call | solution.py:725
  53.9 3.5 all-to-all-start
  57.9 7.5 %reorder.1.refs_2_.refs_9_ = bf16[2,512,2048]{2,1,0:T(8,128)(2,1)} custom-call(s32[9]{0:T(128)} %copy-done.37, bf16[1024,2048]{1,0:T(8,128)(2,1)} %bitcast.64), custom_call_target="tpu_custom_call" | custom-call | bytes 13837500 | tf_op jit(solution)/shard_map/reorder/pallas_call | solution.py:668
  65.4 2.3 all-to-all-done.att
  67.7 6.2 %collective-permute-start.5 = (bf16[4,512,256]{2,1,0:T(8,128)(2,1)S(1)}, bf16[4,512,256]{2,1,0:T(8,128)(2,1)S(1)}, u32[]{:S(2)}, u32[]{:S(2)}) collective-permute-start(bf16[4,512,256]{2,1,0:T(8,128)(2,1)S(1)} %bitcast.54), channel_id=1, source_target_pairs={{0,8},{8,0},{1,9},{9,1},{2,10},{10,2},{3,11},{11,3},{4,12},{12,4},... | collective-permute-start | bytes 3145736 | tf_op jit(solution)/shard_map/ppermute | solution.py:570
  73.8 5.9 %collective-permute-done.4.w1 = bf16[4,512,256]{2,1,0:T(8,128)(2,1)} collective-permute-done((bf16[4,512,256]{2,1,0:T(8,128)(2,1)}, bf16[4,512,256]{2,1,0:T(8,128)(2,1)}, u32[]{:S(2)}, u32[]{:S(2)}) %collective-permute-start.4) | collective-permute-done | bytes 1048608 | tf_op jit(solution)/shard_map/ppermute | solution.py:567
  79.7 2.9 collective-permute-done.6.w3
  83.6 3.4 attention_out.1
  89.3 12.6 %collective-permute-done.7.got = bf16[128,2048]{1,0:T(8,128)(2,1)S(1)} collective-permute-done((bf16[128,2048]{1,0:T(8,128)(2,1)S(1)}, bf16[128,2048]{1,0:T(8,128)(2,1)S(1)}, u32[]{:S(2)}, u32[]{:S(2)}) %collective-permute-start.7) | collective-permute-done | bytes 524320 | tf_op jit(solution)/shard_map/ppermute | solution.py:564
  102.7 3.5 second_norm.1
  108.7 3.1 collective-permute-start.10
  111.7 6.6 %collective-permute-done.8 = bf16[64,2048]{1,0:T(8,128)(2,1)S(1)} collective-permute-done((bf16[64,2048]{1,0:T(8,128)(2,1)}, bf16[64,2048]{1,0:T(8,128)(2,1)S(1)}, u32[]{:S(2)}, u32[]{:S(2)}) %collective-permute-start.8) | collective-permute-done | bytes 262176 | tf_op jit(solution)/shard_map/ppermute | solution.py:564
  118.4 10.6 %collective-permute-done.9 = bf16[64,2048]{1,0:T(8,128)(2,1)S(1)} collective-permute-done((bf16[64,2048]{1,0:T(8,128)(2,1)}, bf16[64,2048]{1,0:T(8,128)(2,1)S(1)}, u32[]{:S(2)}, u32[]{:S(2)}) %collective-permute-start.9) | collective-permute-done | bytes 262176 | tf_op jit(solution)/shard_map/ppermute | solution.py:564
  130.6 4.3 collective-permute-start.12
  135.2 2.1 collective-permute-start.14
  137.4 5.8 %collective-permute-done.12 = bf16[64,2048]{1,0:T(8,128)(2,1)S(1)} collective-permute-done((bf16[64,2048]{1,0:T(8,128)(2,1)S(1)}, bf16[64,2048]{1,0:T(8,128)(2,1)S(1)}, u32[]{:S(2)}, u32[]{:S(2)}) %collective-permute-start.12) | collective-permute-done | bytes 262176 | tf_op jit(solution)/shard_map/ppermute | solution.py:564
  143.2 12.4 %collective-permute-done.13 = bf16[64,2048]{1,0:T(8,128)(2,1)S(1)} collective-permute-done((bf16[64,2048]{1,0:T(8,128)(2,1)S(1)}, bf16[64,2048]{1,0:T(8,128)(2,1)S(1)}, u32[]{:S(2)}, u32[]{:S(2)}) %collective-permute-start.13) | collective-permute-done | bytes 262176 | tf_op jit(solution)/shard_map/ppermute | solution.py:564
  156.4 22.8 %mlp.2 = (bf16[4,64,2048]{2,1,0:T(8,128)(2,1)}, bf16[4,64,2048]{2,1,0:T(8,128)(2,1)}, bf16[256,2048]{1,0:T(8,128)(2,1)}, bf16[256,2048]{1,0:T(8,128)(2,1)}, bf16...) custom-call(s32[9]{0:T(128)} %copy-done.37, bf16[256,2048]{1,0:T(8,128)(2,1)} %copy-done.55, ...), custom_call_target="tpu_custom_call" | custom-call | bytes 41512500 | tf_op jit(solution)/shard_map/mlp/pallas_call | solution.py:800
  180.8 3.7 collective-permute-start.18
  186.9 23.1 %mlp.3 = (bf16[4,64,2048]{2,1,0:T(8,128)(2,1)}, bf16[4,64,2048]{2,1,0:T(8,128)(2,1)}, bf16[256,2048]{1,0:T(8,128)(2,1)}, bf16[256,2048]{1,0:T(8,128)(2,1)}, bf16...) custom-call(s32[9]{0:T(128)} %copy-done.37, ...), custom_call_target="tpu_custom_call", output_to_operand_aliasing={{4}: (5, {}), {5}: (6, {}), {6}: (7, {})} | custom-call | bytes 41512500 | tf_op jit(solution)/shard_map/mlp/pallas_call | solution.py:800
  217.5 19.2 %mlp_grad.1 = bf16[2048,3072]{1,0:T(8,128)(2,1)} custom-call(bf16[1024,2048]{1,0:T(8,128)(2,1)} %get-tuple-element.163.x, bf16[1024,2048]{1,0:T(8,128)(2,1)} %get-tuple-element.174.gate_up_back, bf16[1024,2048]{1,0:T(8,128)(2,1)} %bitcast.59, bf16[1024,1024]{1,0:T(8,128)(2,1)} %get-tuple-element.175.hidden), custom_call_target="tpu_custom_call" | custom-call | bytes 40590000 | tf_op jit(solution)/shard_map/mlp_grad/pallas_call | solution.py:857
  238.3 3.7 fusion.8
  243.8 16.4 %collective-permute-start.25 = (bf16[64,2048]{1,0:T(8,128)(2,1)S(1)}, bf16[64,2048]{1,0:T(8,128)(2,1)S(1)}, u32[]{:S(2)}, u32[]{:S(2)}) collective-permute-start(bf16[64,2048]{1,0:T(8,128)(2,1)S(1)} %get-tuple-element.278), channel_id=1, source_target_pairs={{0,2},{1,3},{2,0},{3,1},{4,6},{5,7},{6,4},{7,5},{8,10},{9,11},{10,... | collective-permute-start | bytes 786440 | tf_op jit(solution)/shard_map/ppermute | solution.py:564
  262.7 2.3 collective-permute-start.33
  267.0 6.2 %collective-permute-done.26.refs_6_ = bf16[64,2048]{1,0:T(8,128)(2,1)} collective-permute-done((bf16[64,2048]{1,0:T(8,128)(2,1)S(1)}, bf16[64,2048]{1,0:T(8,128)(2,1)}, u32[]{:S(2)}, u32[]{:S(2)}) %collective-permute-start.26) | collective-permute-done | bytes 262176 | tf_op jit(solution)/shard_map/ppermute | solution.py:564
  273.2 5.0 second_norm_back.1
  279.9 2.9 add_convert_fusion.2
  282.8 5.9 %collective-permute-done.28.other = bf16[128,2048]{1,0:T(8,128)(2,1)S(1)} collective-permute-done((bf16[128,2048]{1,0:T(8,128)(2,1)}, bf16[128,2048]{1,0:T(8,128)(2,1)S(1)}, u32[]{:S(2)}, u32[]{:S(2)}) %collective-permute-start.28) | collective-permute-done | bytes 524320 | tf_op jit(solution)/shard_map/ppermute | solution.py:564
  291.2 9.4 %all-to-all-start.1 = ((bf16[4,64,2048]{2,1,0:T(8,128)(2,1)}), bf16[4,64,2048]{2,1,0:T(8,128)(2,1)}, u32[]{:S(2)}, u32[]{:S(2)}) async-start(bf16[4,64,2048]{2,1,0:T(8,128)(2,1)} %add_convert_fusion.2), calls=%async_computation.1 | async-start | bytes 2097152 | tf_op jit(solution)/shard_map/all_to_all | solution.py:897
  305.1 3.4 attention_out_back.1
  309.6 2.5 collective-permute-start.30
  314.5 2.9 collective-permute-done.30.grad1
  321.5 2.7 add_convert_fusion.1
  324.3 4.3 all-to-all-start.2
  333.3 11.5 %attend_back.1 = (bf16[1024,256]{1,0:T(8,128)(2,1)S(1)}, bf16[256,256]{1,0:T(8,128)(2,1)S(1)}, bf16[256,256]{1,0:T(8,128)(2,1)S(1)}, bf16[256,256]{1,0:T(8,128)(...) custom-call(s32[9]{0:T(128)S(1)} %copy-done.39, bf16[1024,256]{1,0:T(8,128)(2,1)S(1)} %copy-done.15, ...), custom_call_target="tpu_custom_call" | custom-call | bytes 42435000 | tf_op jit(solution)/shard_map/attend_back/pallas_call | solution.py:921
  346.4 9.0 %collective-permute-start.36 = (bf16[1024,128]{1,0:T(8,128)(2,1)S(1)}, bf16[1024,128]{1,0:T(8,128)(2,1)S(1)}, u32[]{:S(2)}, u32[]{:S(2)}) collective-permute-start(bf16[1024,128]{1,0:T(8,128)(2,1)S(1)} %get-tuple-element.286), channel_id=1, source_target_pairs={{0,8},{8,0},{1,9},{9,1},{2,10},{10,2},{3,11},{11,3},{4,12},{12,4},... | collective-permute-start | bytes 786440 | tf_op jit(solution)/shard_map/ppermute | solution.py:570
  357.1 2.4 collective-permute-start.38
  359.7 2.7 collective-permute-done.37.q1
  362.4 7.6 %collective-permute-done.38.q2 = bf16[256,256]{1,0:T(8,128)(2,1)S(1)} collective-permute-done((bf16[256,256]{1,0:T(8,128)(2,1)S(1)}, bf16[256,256]{1,0:T(8,128)(2,1)S(1)}, u32[]{:S(2)}, u32[]{:S(2)}) %collective-permute-start.38) | collective-permute-done | bytes 131104 | tf_op jit(solution)/shard_map/ppermute | solution.py:564
  370.7 3.1 kv_back.1
  373.9 3.0 block_out.1
  377.0 2.2 collective-permute-start.40
  382.1 4.2 collective-permute-done.41.k2
  386.3 5.3 %attention_in_back.1 = (f32[128,2048]{1,0:T(8,128)S(1)}, bf16[128,2048]{1,0:T(8,128)(2,1)S(1)}) custom-call(s32[9]{0:T(128)S(1)} %copy-done.40, bf16[256,256]{1,0:T(8,128)(2,1)S(1)} %get-tuple-element.198.q0, bf16[256,256]{1,0:T(8,128)(2,1)S(1)} %collective-permute-done.37.q1, bf16[256,256]{1,0:T(8,128)(2,1)S(1)} %collective-permute-done.38.q2, ...), custom_call_target="tpu_custom_call" | custom-call | bytes 10701000 | tf_op jit(solution)/shard_map/attention_in_back/pallas_call | solution.py:982
  394.1 5.8 %weight_grad.3 = (bf16[1024,1024]{1,0:T(8,128)(2,1)}, bf16[1024,1024]{1,0:T(8,128)(2,1)}) custom-call(bf16[256,2048]{1,0:T(8,128)(2,1)} %copy-done.24, bf16[256,1024]{1,0:T(8,128)(2,1)} %pad_maximum_fusion.6.b), custom_call_target="tpu_custom_call" | custom-call | bytes 3022848 | tf_op jit(solution)/shard_map/weight_grad/pallas_call | solution.py:598
  400.9 6.1 %weight_grad.2 = (bf16[1024,384]{1,0:T(8,128)(2,1)}, bf16[1024,384]{1,0:T(8,128)(2,1)}) custom-call(bf16[1024,2048]{1,0:T(8,128)(2,1)} %get-tuple-element.217.a, bf16[1024,384]{1,0:T(8,128)(2,1)} %pad_maximum_fusion.3.b), custom_call_target="tpu_custom_call" | custom-call | bytes 4534272 | tf_op jit(solution)/shard_map/weight_grad/pallas_call | solution.py:598
  407.8 4.1 first_norm_back.1
  414.6 2.5 pair_sum.2
  424.4 10.2 %collective-permute-done.44.own = bf16[128,2048]{1,0:T(8,128)(2,1)S(1)} collective-permute-done((bf16[128,2048]{1,0:T(8,128)(2,1)}, bf16[128,2048]{1,0:T(8,128)(2,1)S(1)}, u32[]{:S(2)}, u32[]{:S(2)}) %collective-permute-start.44) | collective-permute-done | bytes 524320 | tf_op jit(solution)/shard_map/ppermute | solution.py:564
  436.1 13.2 %adam.5 = (f32[512,2,1024]{2,1,0:T(2,128)}, f32[512,2,1024]{2,1,0:T(2,128)}, f32[512,2,1024]{2,1,0:T(2,128)}) custom-call(f32[512,2,1024]{2,1,0:T(2,128)} %weight.5, f32[512,2,1024]{2,1,0:T(2,128)} %one.5, f32[512,2,1024]{2,1,0:T(2,128)} %two.5, bf16[512,3072]{1,0:T(8,128)(2,1)} %reduce-scatter.2.cloned.1.call-done.refs_0_), custom_call_target="tpu_custom_call" | custom-call | bytes 25794968 | tf_op jit(solution)/shard_map/adam/pallas_call | solution.py:1036
  449.3 6.7 %adam.6 = (f32[512,1024]{1,0:T(8,128)}, f32[512,1024]{1,0:T(8,128)}, f32[512,1024]{1,0:T(8,128)}) custom-call(f32[512,1024]{1,0:T(8,128)} %weight.6, f32[512,1024]{1,0:T(8,128)} %one.6, f32[512,1024]{1,0:T(8,128)} %two.6, bf16[512,3072]{1,0:T(8,128)(2,1)} %reduce-scatter.2.cloned.1.call-done.refs_0_), custom_call_target="tpu_custom_call" | custom-call | bytes 12897484 | tf_op jit(solution)/shard_map/adam/pallas_call | solution.py:1036
  455.9 14.2 %all-gather.14.cloned.1.call-done = bf16[512,2048]{1,0:T(8,128)(2,1)} async-done(((bf16[128,2048]{1,0:T(8,128)(2,1)}), bf16[512,2048]{1,0:T(8,128)(2,1)}) %all-gather.14.cloned.1.call-update) | async-done | bytes 2097168 | tf_op jit(solution)/shard_map/all_gather | solution.py:1023
  475.9 2.2 add_convert_fusion
  485.4 3.0 block_out_rows.1
  488.4 3.3 adam.9
  491.7 3.9 adam.7
  495.6 10.2 %collective-permute-done.58 = f32[2,512]{1,0:T(2,128)S(1)} collective-permute-done((f32[2,512]{1,0:T(2,128)S(1)}, f32[2,512]{1,0:T(2,128)S(1)}, u32[]{:S(2)}, u32[]{:S(2)}) %collective-permute-start.58) | collective-permute-done | bytes 4128 | tf_op jit(solution)/shard_map/ppermute | solution.py:564
  507.4 3.9 adam.8
  511.3 3.7 collective-permute-done.52.far
  514.9 4.2 tokens_grad.1
  (316 shorter events, 104.2 us)
Async XLA Ops:
  7.2 35.5 %all-gather.10.cloned.1.call-start = ((), (), s32[]{:S(2)}) async-start(), calls=%async_computation.6 | async-start | bytes 1310720 | tf_op jit(solution)/shard_map/all_gather | solution.py:661
  10.4 15.0 %collective-permute-start = (bf16[512,512]{1,0:T(8,128)(2,1)S(1)}, bf16[512,512]{1,0:T(8,128)(2,1)S(1)}, u32[]{:S(2)}, u32[]{:S(2)}) collective-permute-start(bf16[512,512]{1,0:T(8,128)(2,1)S(1)} %fusion.1.w0), channel_id=1, source_target_pairs={{0,16},{16,0},{1,17},{17,1},{2,18},{18,2},{3,19},{19,3},{4,20},{20... | collective-permute-start | bytes 1572872 | tf_op jit(solution)/shard_map/ppermute | solution.py:567
  13.4 12.0 %collective-permute-start.1 = (bf16[512,512]{1,0:T(8,128)(2,1)S(1)}, bf16[512,512]{1,0:T(8,128)(2,1)S(1)}, u32[]{:S(2)}, u32[]{:S(2)}) collective-permute-start(bf16[512,512]{1,0:T(8,128)(2,1)S(1)} %fusion.1.w0), channel_id=1, source_target_pairs={{0,8},{8,0},{1,9},{9,1},{2,10},{10,2},{3,11},{11,3},{4,12},{12,4},... | collective-permute-start | bytes 1572872 | tf_op jit(solution)/shard_map/ppermute | solution.py:570
  14.2 142.2 %all-gather.8.cloned.1.call-start = ((), (), s32[]{:S(2)}) async-start(), calls=%async_computation.4 | async-start | bytes 15728640 | tf_op jit(solution)/shard_map/all_gather | solution.py:584
  39.9 4.3 collective-permute-start.3
  42.7 37.0 %collective-permute-start.4 = (bf16[4,512,256]{2,1,0:T(8,128)(2,1)}, bf16[4,512,256]{2,1,0:T(8,128)(2,1)}, u32[]{:S(2)}, u32[]{:S(2)}) collective-permute-start(bf16[4,512,256]{2,1,0:T(8,128)(2,1)} %bitcast.53), channel_id=1, source_target_pairs={{0,16},{16,0},{1,17},{17,1},{2,18},{18,2},{3,19},{19,3},{4,20},{20... | collective-permute-start | bytes 3145736 | tf_op jit(solution)/shard_map/ppermute | solution.py:567
  53.9 13.8 %all-to-all-start = ((bf16[4,256,256]{2,1,0:T(8,128)(2,1)}), bf16[4,256,256]{2,1,0:T(8,128)(2,1)S(1)}, u32[]{:S(2)}, u32[]{:S(2)}) async-start(bf16[4,256,256]{2,1,0:T(8,128)(2,1)} %bitcast.10), calls=%async_computation | async-start | bytes 1048576 | tf_op jit(solution)/shard_map/all_to_all | solution.py:754
  57.4 328.9 %reduce-scatter.2.cloned.1.call-start = ((), (), s32[]{:S(2)}) async-start(), calls=%async_computation.5 | async-start | bytes 15728640 | tf_op jit(solution)/shard_map/reduce_scatter | solution.py:587
  67.7 12.1 %collective-permute-start.5 = (bf16[4,512,256]{2,1,0:T(8,128)(2,1)S(1)}, bf16[4,512,256]{2,1,0:T(8,128)(2,1)S(1)}, u32[]{:S(2)}, u32[]{:S(2)}) collective-permute-start(bf16[4,512,256]{2,1,0:T(8,128)(2,1)S(1)} %bitcast.54), channel_id=1, source_target_pairs={{0,8},{8,0},{1,9},{9,1},{2,10},{10,2},{3,11},{11,3},{4,12},{12,4},... | collective-permute-start | bytes 3145736 | tf_op jit(solution)/shard_map/ppermute | solution.py:570
  88.0 14.0 %collective-permute-start.7 = (bf16[128,2048]{1,0:T(8,128)(2,1)S(1)}, bf16[128,2048]{1,0:T(8,128)(2,1)S(1)}, u32[]{:S(2)}, u32[]{:S(2)}) collective-permute-start(bf16[128,2048]{1,0:T(8,128)(2,1)S(1)} %get-tuple-element.149), channel_id=1, source_target_pairs={{0,1},{1,0},{2,3},{3,2},{4,5},{5,4},{6,7},{7,6},{8,9},{9,8},{10,11... | collective-permute-start | bytes 1572872 | tf_op jit(solution)/shard_map/ppermute | solution.py:564
  106.3 12.1 %collective-permute-start.8 = (bf16[64,2048]{1,0:T(8,128)(2,1)}, bf16[64,2048]{1,0:T(8,128)(2,1)S(1)}, u32[]{:S(2)}, u32[]{:S(2)}) collective-permute-start(bf16[64,2048]{1,0:T(8,128)(2,1)} %get-tuple-element.151), channel_id=1, source_target_pairs={{0,2},{1,3},{2,0},{3,1},{4,6},{5,7},{6,4},{7,5},{8,10},{9,11},{10,... | collective-permute-start | bytes 786440 | tf_op jit(solution)/shard_map/ppermute | solution.py:564
  107.4 21.6 %collective-permute-start.9 = (bf16[64,2048]{1,0:T(8,128)(2,1)}, bf16[64,2048]{1,0:T(8,128)(2,1)S(1)}, u32[]{:S(2)}, u32[]{:S(2)}) collective-permute-start(bf16[64,2048]{1,0:T(8,128)(2,1)} %get-tuple-element.151), channel_id=1, source_target_pairs={{0,4},{1,5},{2,6},{3,7},{4,0},{5,1},{6,2},{7,3},{8,12},{9,13},{10,... | collective-permute-start | bytes 786440 | tf_op jit(solution)/shard_map/ppermute | solution.py:564
  108.7 20.4 %collective-permute-start.10 = (bf16[64,2048]{1,0:T(8,128)(2,1)}, bf16[64,2048]{1,0:T(8,128)(2,1)S(1)}, u32[]{:S(2)}, u32[]{:S(2)}) collective-permute-start(bf16[64,2048]{1,0:T(8,128)(2,1)} %get-tuple-element.151), channel_id=1, source_target_pairs={{0,6},{1,7},{2,4},{3,5},{4,2},{5,3},{6,0},{7,1},{8,14},{9,15},{10,... | collective-permute-start | bytes 786440 | tf_op jit(solution)/shard_map/ppermute | solution.py:564
  129.1 27.3 %collective-permute-start.11 = (bf16[256,2048]{1,0:T(8,128)(2,1)S(1)}, bf16[256,2048]{1,0:T(8,128)(2,1)}, u32[]{:S(2)}, u32[]{:S(2)}) collective-permute-start(bf16[256,2048]{1,0:T(8,128)(2,1)S(1)} %constant_dynamic-update-slice_fusion.refs_0_), channel_id=1, source_target_pairs={{0,1},{1,0},{2,3},{3,2},{4,5},{5,4},{6,7},{7,6},{8,9},{9,8},{10,11... | collective-permute-start | bytes 3145736 | tf_op jit(solution)/shard_map/ppermute | solution.py:564
  130.6 12.6 %collective-permute-start.12 = (bf16[64,2048]{1,0:T(8,128)(2,1)S(1)}, bf16[64,2048]{1,0:T(8,128)(2,1)S(1)}, u32[]{:S(2)}, u32[]{:S(2)}) collective-permute-start(bf16[64,2048]{1,0:T(8,128)(2,1)S(1)} %copy-done.67), channel_id=1, source_target_pairs={{0,2},{1,3},{2,0},{3,1},{4,6},{5,7},{6,4},{7,5},{8,10},{9,11},{10,... | collective-permute-start | bytes 786440 | tf_op jit(solution)/shard_map/ppermute | solution.py:564
  134.9 20.8 %collective-permute-start.13 = (bf16[64,2048]{1,0:T(8,128)(2,1)S(1)}, bf16[64,2048]{1,0:T(8,128)(2,1)S(1)}, u32[]{:S(2)}, u32[]{:S(2)}) collective-permute-start(bf16[64,2048]{1,0:T(8,128)(2,1)S(1)} %copy-done.67), channel_id=1, source_target_pairs={{0,4},{1,5},{2,6},{3,7},{4,0},{5,1},{6,2},{7,3},{8,12},{9,13},{10,... | collective-permute-start | bytes 786440 | tf_op jit(solution)/shard_map/ppermute | solution.py:564
  135.2 20.4 %collective-permute-start.14 = (bf16[64,2048]{1,0:T(8,128)(2,1)S(1)}, bf16[64,2048]{1,0:T(8,128)(2,1)S(1)}, u32[]{:S(2)}, u32[]{:S(2)}) collective-permute-start(bf16[64,2048]{1,0:T(8,128)(2,1)S(1)} %copy-done.67), channel_id=1, source_target_pairs={{0,6},{1,7},{2,4},{3,5},{4,2},{5,3},{6,0},{7,1},{8,14},{9,15},{10,... | collective-permute-start | bytes 786440 | tf_op jit(solution)/shard_map/ppermute | solution.py:564
  155.8 31.2 %collective-permute-start.15 = (bf16[256,2048]{1,0:T(8,128)(2,1)S(1)}, bf16[256,2048]{1,0:T(8,128)(2,1)}, u32[]{:S(2)}, u32[]{:S(2)}) collective-permute-start(bf16[256,2048]{1,0:T(8,128)(2,1)S(1)} %constant_dynamic-update-slice_fusion.4.refs_0_), channel_id=1, source_target_pairs={{0,1},{1,0},{2,3},{3,2},{4,5},{5,4},{6,7},{7,6},{8,9},{9,8},{10,11... | collective-permute-start | bytes 3145736 | tf_op jit(solution)/shard_map/ppermute | solution.py:564
  179.2 31.4 %collective-permute-start.17 = (bf16[256,2048]{1,0:T(8,128)(2,1)}, bf16[256,2048]{1,0:T(8,128)(2,1)S(1)}, u32[]{:S(2)}, u32[]{:S(2)}) collective-permute-start(bf16[256,2048]{1,0:T(8,128)(2,1)} %get-tuple-element.167), channel_id=1, source_target_pairs={{0,1},{1,0},{2,3},{3,2},{4,5},{5,4},{6,7},{7,6},{8,9},{9,8},{10,11... | collective-permute-start | bytes 3145736 | tf_op jit(solution)/shard_map/ppermute | solution.py:564
  180.8 32.3 %collective-permute-start.18 = (bf16[512,384]{1,0:T(8,128)(2,1)S(1)}, bf16[512,384]{1,0:T(8,128)(2,1)S(1)}, u32[]{:S(2)}, u32[]{:S(2)}) collective-permute-start(bf16[512,384]{1,0:T(8,128)(2,1)S(1)} %pad_maximum_fusion.7), channel_id=1, source_target_pairs={{0,2},{1,3},{2,0},{3,1},{4,6},{5,7},{6,4},{7,5},{8,10},{9,11},{10,... | collective-permute-start | bytes 1179656 | tf_op jit(solution)/shard_map/ppermute | solution.py:564
  184.5 29.9 %collective-permute-start.19 = (bf16[512,384]{1,0:T(8,128)(2,1)S(1)}, bf16[512,384]{1,0:T(8,128)(2,1)S(1)}, u32[]{:S(2)}, u32[]{:S(2)}) collective-permute-start(bf16[512,384]{1,0:T(8,128)(2,1)S(1)} %pad_maximum_fusion.7), channel_id=1, source_target_pairs={{0,4},{1,5},{2,6},{3,7},{4,0},{5,1},{6,2},{7,3},{8,12},{9,13},{10,... | collective-permute-start | bytes 1179656 | tf_op jit(solution)/shard_map/ppermute | solution.py:564
  184.9 31.5 %collective-permute-start.20 = (bf16[512,384]{1,0:T(8,128)(2,1)S(1)}, bf16[512,384]{1,0:T(8,128)(2,1)S(1)}, u32[]{:S(2)}, u32[]{:S(2)}) collective-permute-start(bf16[512,384]{1,0:T(8,128)(2,1)S(1)} %pad_maximum_fusion.7), channel_id=1, source_target_pairs={{0,6},{1,7},{2,4},{3,5},{4,2},{5,3},{6,0},{7,1},{8,14},{9,15},{10,... | collective-permute-start | bytes 1179656 | tf_op jit(solution)/shard_map/ppermute | solution.py:564
  210.0 26.7 %collective-permute-start.16 = (bf16[256,2048]{1,0:T(8,128)(2,1)}, bf16[256,2048]{1,0:T(8,128)(2,1)}, u32[]{:S(2)}, u32[]{:S(2)}) collective-permute-start(bf16[256,2048]{1,0:T(8,128)(2,1)} %get-tuple-element.162), channel_id=1, source_target_pairs={{0,1},{1,0},{2,3},{3,2},{4,5},{5,4},{6,7},{7,6},{8,9},{9,8},{10,11... | collective-permute-start | bytes 3145736 | tf_op jit(solution)/shard_map/ppermute | solution.py:564
  212.0 24.7 %collective-permute-start.21 = (bf16[64,2048]{1,0:T(8,128)(2,1)}, bf16[64,2048]{1,0:T(8,128)(2,1)S(1)}, u32[]{:S(2)}, u32[]{:S(2)}) collective-permute-start(bf16[64,2048]{1,0:T(8,128)(2,1)} %get-tuple-element.281), channel_id=1, source_target_pairs={{0,2},{1,3},{2,0},{3,1},{4,6},{5,7},{6,4},{7,5},{8,10},{9,11},{10,... | collective-permute-start | bytes 786440 | tf_op jit(solution)/shard_map/ppermute | solution.py:564
  213.1 25.2 %collective-permute-start.22 = (bf16[64,2048]{1,0:T(8,128)(2,1)}, bf16[64,2048]{1,0:T(8,128)(2,1)}, u32[]{:S(2)}, u32[]{:S(2)}) collective-permute-start(bf16[64,2048]{1,0:T(8,128)(2,1)} %get-tuple-element.280), channel_id=1, source_target_pairs={{0,4},{1,5},{2,6},{3,7},{4,0},{5,1},{6,2},{7,3},{8,12},{9,13},{10,... | collective-permute-start | bytes 786440 | tf_op jit(solution)/shard_map/ppermute | solution.py:564
  214.4 23.9 %collective-permute-start.23 = (bf16[64,2048]{1,0:T(8,128)(2,1)}, bf16[64,2048]{1,0:T(8,128)(2,1)}, u32[]{:S(2)}, u32[]{:S(2)}) collective-permute-start(bf16[64,2048]{1,0:T(8,128)(2,1)} %get-tuple-element.279), channel_id=1, source_target_pairs={{0,6},{1,7},{2,4},{3,5},{4,2},{5,3},{6,0},{7,1},{8,14},{9,15},{10,... | collective-permute-start | bytes 786440 | tf_op jit(solution)/shard_map/ppermute | solution.py:564
  242.0 37.9 %collective-permute-start.24 = (bf16[4,64,2048]{2,1,0:T(8,128)(2,1)}, bf16[4,64,2048]{2,1,0:T(8,128)(2,1)}, u32[]{:S(2)}, u32[]{:S(2)}) collective-permute-start(bf16[4,64,2048]{2,1,0:T(8,128)(2,1)} %get-tuple-element.177), channel_id=1, source_target_pairs={{0,1},{1,0},{2,3},{3,2},{4,5},{5,4},{6,7},{7,6},{8,9},{9,8},{10,11... | collective-permute-start | bytes 3145736 | tf_op jit(solution)/shard_map/ppermute | solution.py:564
  243.8 23.2 %collective-permute-start.25 = (bf16[64,2048]{1,0:T(8,128)(2,1)S(1)}, bf16[64,2048]{1,0:T(8,128)(2,1)S(1)}, u32[]{:S(2)}, u32[]{:S(2)}) collective-permute-start(bf16[64,2048]{1,0:T(8,128)(2,1)S(1)} %get-tuple-element.278), channel_id=1, source_target_pairs={{0,2},{1,3},{2,0},{3,1},{4,6},{5,7},{6,4},{7,5},{8,10},{9,11},{10,... | collective-permute-start | bytes 786440 | tf_op jit(solution)/shard_map/ppermute | solution.py:564
  260.2 13.0 %collective-permute-start.26 = (bf16[64,2048]{1,0:T(8,128)(2,1)S(1)}, bf16[64,2048]{1,0:T(8,128)(2,1)}, u32[]{:S(2)}, u32[]{:S(2)}) collective-permute-start(bf16[64,2048]{1,0:T(8,128)(2,1)S(1)} %get-tuple-element.277), channel_id=1, source_target_pairs={{0,4},{1,5},{2,6},{3,7},{4,0},{5,1},{6,2},{7,3},{8,12},{9,13},{10,... | collective-permute-start | bytes 786440 | tf_op jit(solution)/shard_map/ppermute | solution.py:564
  260.8 12.4 %collective-permute-start.27 = (bf16[64,2048]{1,0:T(8,128)(2,1)S(1)}, bf16[64,2048]{1,0:T(8,128)(2,1)}, u32[]{:S(2)}, u32[]{:S(2)}) collective-permute-start(bf16[64,2048]{1,0:T(8,128)(2,1)S(1)} %get-tuple-element.276), channel_id=1, source_target_pairs={{0,6},{1,7},{2,4},{3,5},{4,2},{5,3},{6,0},{7,1},{8,14},{9,15},{10,... | collective-permute-start | bytes 786440 | tf_op jit(solution)/shard_map/ppermute | solution.py:564
  262.7 51.8 %collective-permute-start.33 = (bf16[4,512,384]{2,1,0:T(8,128)(2,1)S(1)}, bf16[4,512,384]{2,1,0:T(8,128)(2,1)}, u32[]{:S(2)}, u32[]{:S(2)}) collective-permute-start(bf16[4,512,384]{2,1,0:T(8,128)(2,1)S(1)} %pad_maximum_fusion.1.w0), channel_id=1, source_target_pairs={{0,16},{16,0},{1,17},{17,1},{2,18},{18,2},{3,19},{19,3},{4,20},{20... | collective-permute-start | bytes 4718600 | tf_op jit(solution)/shard_map/ppermute | solution.py:567
  278.2 10.4 %collective-permute-start.28 = (bf16[128,2048]{1,0:T(8,128)(2,1)}, bf16[128,2048]{1,0:T(8,128)(2,1)S(1)}, u32[]{:S(2)}, u32[]{:S(2)}) collective-permute-start(bf16[128,2048]{1,0:T(8,128)(2,1)} %get-tuple-element.179.own), channel_id=1, source_target_pairs={{0,1},{1,0},{2,3},{3,2},{4,5},{5,4},{6,7},{7,6},{8,9},{9,8},{10,11... | collective-permute-start | bytes 1572872 | tf_op jit(solution)/shard_map/ppermute | solution.py:564
  289.5 32.1 %collective-permute-start.29 = (bf16[4,64,2048]{2,1,0:T(8,128)(2,1)}, bf16[4,64,2048]{2,1,0:T(8,128)(2,1)}, u32[]{:S(2)}, u32[]{:S(2)}) collective-permute-start(bf16[4,64,2048]{2,1,0:T(8,128)(2,1)} %get-tuple-element.184), channel_id=1, source_target_pairs={{0,1},{1,0},{2,3},{3,2},{4,5},{5,4},{6,7},{7,6},{8,9},{9,8},{10,11... | collective-permute-start | bytes 3145736 | tf_op jit(solution)/shard_map/ppermute | solution.py:564
  291.2 33.1 %all-to-all-start.1 = ((bf16[4,64,2048]{2,1,0:T(8,128)(2,1)}), bf16[4,64,2048]{2,1,0:T(8,128)(2,1)}, u32[]{:S(2)}, u32[]{:S(2)}) async-start(bf16[4,64,2048]{2,1,0:T(8,128)(2,1)} %add_convert_fusion.2), calls=%async_computation.1 | async-start | bytes 2097152 | tf_op jit(solution)/shard_map/all_to_all | solution.py:897
  309.6 7.8 %collective-permute-start.30 = (bf16[256,256]{1,0:T(8,128)(2,1)S(1)}, bf16[256,256]{1,0:T(8,128)(2,1)S(1)}, u32[]{:S(2)}, u32[]{:S(2)}) collective-permute-start(bf16[256,256]{1,0:T(8,128)(2,1)S(1)} %get-tuple-element.186), channel_id=1, source_target_pairs={{0,2},{1,3},{2,0},{3,1},{4,6},{5,7},{6,4},{7,5},{8,10},{9,11},{10,... | collective-permute-start | bytes 393224 | tf_op jit(solution)/shard_map/ppermute | solution.py:564
  312.1 7.3 %collective-permute-start.31 = (bf16[256,256]{1,0:T(8,128)(2,1)S(1)}, bf16[256,256]{1,0:T(8,128)(2,1)S(1)}, u32[]{:S(2)}, u32[]{:S(2)}) collective-permute-start(bf16[256,256]{1,0:T(8,128)(2,1)S(1)} %get-tuple-element.187), channel_id=1, source_target_pairs={{0,4},{1,5},{2,6},{3,7},{4,0},{5,1},{6,2},{7,3},{8,12},{9,13},{10,... | collective-permute-start | bytes 393224 | tf_op jit(solution)/shard_map/ppermute | solution.py:564
  314.0 6.9 %collective-permute-start.32 = (bf16[256,256]{1,0:T(8,128)(2,1)S(1)}, bf16[256,256]{1,0:T(8,128)(2,1)S(1)}, u32[]{:S(2)}, u32[]{:S(2)}) collective-permute-start(bf16[256,256]{1,0:T(8,128)(2,1)S(1)} %get-tuple-element.188), channel_id=1, source_target_pairs={{0,6},{1,7},{2,4},{3,5},{4,2},{5,3},{6,0},{7,1},{8,14},{9,15},{10,... | collective-permute-start | bytes 393224 | tf_op jit(solution)/shard_map/ppermute | solution.py:564
  314.5 14.2 %collective-permute-start.34 = (bf16[4,512,384]{2,1,0:T(8,128)(2,1)S(1)}, bf16[4,512,384]{2,1,0:T(8,128)(2,1)}, u32[]{:S(2)}, u32[]{:S(2)}) collective-permute-start(bf16[4,512,384]{2,1,0:T(8,128)(2,1)S(1)} %pad_maximum_fusion.1.w0), channel_id=1, source_target_pairs={{0,8},{8,0},{1,9},{9,1},{2,10},{10,2},{3,11},{11,3},{4,12},{12,4},... | collective-permute-start | bytes 4718600 | tf_op jit(solution)/shard_map/ppermute | solution.py:570
  317.4 11.3 %collective-permute-start.35 = (bf16[4,512,384]{2,1,0:T(8,128)(2,1)}, bf16[4,512,384]{2,1,0:T(8,128)(2,1)}, u32[]{:S(2)}, u32[]{:S(2)}) collective-permute-start(bf16[4,512,384]{2,1,0:T(8,128)(2,1)} %collective-permute-done.33.w1), channel_id=1, source_target_pairs={{0,8},{8,0},{1,9},{9,1},{2,10},{10,2},{3,11},{11,3},{4,12},{12,4},... | collective-permute-start | bytes 4718600 | tf_op jit(solution)/shard_map/ppermute | solution.py:570
  324.3 49.5 %all-to-all-start.2 = ((bf16[4,64,2048]{2,1,0:T(8,128)(2,1)}), bf16[4,64,2048]{2,1,0:T(8,128)(2,1)}, u32[]{:S(2)}, u32[]{:S(2)}) async-start(bf16[4,64,2048]{2,1,0:T(8,128)(2,1)} %add_convert_fusion.1), calls=%async_computation.2 | async-start | bytes 2097152 | tf_op jit(solution)/shard_map/all_to_all | solution.py:916
  328.6 95.8 %all-gather.12.cloned.1.call-start = ((), (), s32[]{:S(2)}) async-start(), calls=%async_computation.7 | async-start | bytes 2621440 | tf_op jit(solution)/shard_map/all_gather | solution.py:1005
  346.4 23.6 %collective-permute-start.36 = (bf16[1024,128]{1,0:T(8,128)(2,1)S(1)}, bf16[1024,128]{1,0:T(8,128)(2,1)S(1)}, u32[]{:S(2)}, u32[]{:S(2)}) collective-permute-start(bf16[1024,128]{1,0:T(8,128)(2,1)S(1)} %get-tuple-element.286), channel_id=1, source_target_pairs={{0,8},{8,0},{1,9},{9,1},{2,10},{10,2},{3,11},{11,3},{4,12},{12,4},... | collective-permute-start | bytes 786440 | tf_op jit(solution)/shard_map/ppermute | solution.py:570
  355.3 7.1 %collective-permute-start.37 = (bf16[256,256]{1,0:T(8,128)(2,1)S(1)}, bf16[256,256]{1,0:T(8,128)(2,1)S(1)}, u32[]{:S(2)}, u32[]{:S(2)}) collective-permute-start(bf16[256,256]{1,0:T(8,128)(2,1)S(1)} %get-tuple-element.199), channel_id=1, source_target_pairs={{0,2},{1,3},{2,0},{3,1},{4,6},{5,7},{6,4},{7,5},{8,10},{9,11},{10,... | collective-permute-start | bytes 393224 | tf_op jit(solution)/shard_map/ppermute | solution.py:564
  357.1 12.9 %collective-permute-start.38 = (bf16[256,256]{1,0:T(8,128)(2,1)S(1)}, bf16[256,256]{1,0:T(8,128)(2,1)S(1)}, u32[]{:S(2)}, u32[]{:S(2)}) collective-permute-start(bf16[256,256]{1,0:T(8,128)(2,1)S(1)} %get-tuple-element.200), channel_id=1, source_target_pairs={{0,4},{1,5},{2,6},{3,7},{4,0},{5,1},{6,2},{7,3},{8,12},{9,13},{10,... | collective-permute-start | bytes 393224 | tf_op jit(solution)/shard_map/ppermute | solution.py:564
  359.4 10.6 %collective-permute-start.39 = (bf16[256,256]{1,0:T(8,128)(2,1)S(1)}, bf16[256,256]{1,0:T(8,128)(2,1)S(1)}, u32[]{:S(2)}, u32[]{:S(2)}) collective-permute-start(bf16[256,256]{1,0:T(8,128)(2,1)S(1)} %get-tuple-element.201), channel_id=1, source_target_pairs={{0,6},{1,7},{2,4},{3,5},{4,2},{5,3},{6,0},{7,1},{8,14},{9,15},{10,... | collective-permute-start | bytes 393224 | tf_op jit(solution)/shard_map/ppermute | solution.py:564
  376.9 93.2 %all-gather.14.cloned.1.call-start = ((), (), s32[]{:S(2)}) async-start(), calls=%async_computation.8 | async-start | bytes 2621440 | tf_op jit(solution)/shard_map/all_gather | solution.py:1023
  377.0 5.1 collective-permute-start.40
  379.2 7.1 %collective-permute-start.41 = (bf16[256,128]{1,0:T(8,128)(2,1)S(1)}, bf16[256,128]{1,0:T(8,128)(2,1)S(1)}, u32[]{:S(2)}, u32[]{:S(2)}) collective-permute-start(bf16[256,128]{1,0:T(8,128)(2,1)S(1)} %copy-done.75), channel_id=1, source_target_pairs={{0,4},{1,5},{2,6},{3,7},{4,0},{5,1},{6,2},{7,3},{8,12},{9,13},{10,... | collective-permute-start | bytes 196616 | tf_op jit(solution)/shard_map/ppermute | solution.py:564
  380.2 6.1 %collective-permute-start.42 = (bf16[256,128]{1,0:T(8,128)(2,1)S(1)}, bf16[256,128]{1,0:T(8,128)(2,1)S(1)}, u32[]{:S(2)}, u32[]{:S(2)}) collective-permute-start(bf16[256,128]{1,0:T(8,128)(2,1)S(1)} %copy-done.74), channel_id=1, source_target_pairs={{0,6},{1,7},{2,4},{3,5},{4,2},{5,3},{6,0},{7,1},{8,14},{9,15},{10,... | collective-permute-start | bytes 196616 | tf_op jit(solution)/shard_map/ppermute | solution.py:564
  392.6 14.4 %collective-permute-start.43 = (bf16[128,2048]{1,0:T(8,128)(2,1)S(1)}, bf16[128,2048]{1,0:T(8,128)(2,1)S(1)}, u32[]{:S(2)}, u32[]{:S(2)}) collective-permute-start(bf16[128,2048]{1,0:T(8,128)(2,1)S(1)} %get-tuple-element.216), channel_id=1, source_target_pairs={{0,1},{1,0},{2,3},{3,2},{4,5},{5,4},{6,7},{7,6},{8,9},{9,8},{10,11... | collective-permute-start | bytes 1572872 | tf_op jit(solution)/shard_map/ppermute | solution.py:564
  399.9 13.1 %collective-permute-start.48 = (bf16[1024,1024]{1,0:T(8,128)(2,1)}, bf16[1024,1024]{1,0:T(8,128)(2,1)}, u32[]{:S(2)}, u32[]{:S(2)}) collective-permute-start(bf16[1024,1024]{1,0:T(8,128)(2,1)} %get-tuple-element.225), channel_id=1, source_target_pairs={{0,8},{8,0},{1,9},{9,1},{2,10},{10,2},{3,11},{11,3},{4,12},{12,4},... | collective-permute-start | bytes 6291464 | tf_op jit(solution)/shard_map/ppermute | solution.py:570
  412.4 10.2 %collective-permute-start.50 = (bf16[1024,384]{1,0:T(8,128)(2,1)}, bf16[1024,384]{1,0:T(8,128)(2,1)S(1)}, u32[]{:S(2)}, u32[]{:S(2)}) collective-permute-start(bf16[1024,384]{1,0:T(8,128)(2,1)} %get-tuple-element.221), channel_id=1, source_target_pairs={{0,8},{8,0},{1,9},{9,1},{2,10},{10,2},{3,11},{11,3},{4,12},{12,4},... | collective-permute-start | bytes 2359304 | tf_op jit(solution)/shard_map/ppermute | solution.py:570
  417.1 38.8 %collective-permute-start.49 = (bf16[512,1024]{1,0:T(8,128)(2,1)}, bf16[512,1024]{1,0:T(8,128)(2,1)}, u32[]{:S(2)}, u32[]{:S(2)}) collective-permute-start(bf16[512,1024]{1,0:T(8,128)(2,1)} %pair_sum.2), channel_id=1, source_target_pairs={{0,16},{16,0},{1,17},{17,1},{2,18},{18,2},{3,19},{19,3},{4,20},{20... | collective-permute-start | bytes 3145736 | tf_op jit(solution)/shard_map/ppermute | solution.py:567
  420.6 14.0 %collective-permute-start.44 = (bf16[128,2048]{1,0:T(8,128)(2,1)}, bf16[128,2048]{1,0:T(8,128)(2,1)S(1)}, u32[]{:S(2)}, u32[]{:S(2)}) collective-permute-start(bf16[128,2048]{1,0:T(8,128)(2,1)} %first_norm_back.1), channel_id=1, source_target_pairs={{0,1},{1,0},{2,3},{3,2},{4,5},{5,4},{6,7},{7,6},{8,9},{9,8},{10,11... | collective-permute-start | bytes 1572872 | tf_op jit(solution)/shard_map/ppermute | solution.py:564
  423.6 32.3 %collective-permute-start.51 = (bf16[512,384]{1,0:T(8,128)(2,1)}, bf16[512,384]{1,0:T(8,128)(2,1)}, u32[]{:S(2)}, u32[]{:S(2)}) collective-permute-start(bf16[512,384]{1,0:T(8,128)(2,1)} %pair_sum.3), channel_id=1, source_target_pairs={{0,16},{16,0},{1,17},{17,1},{2,18},{18,2},{3,19},{19,3},{4,20},{20... | collective-permute-start | bytes 1179656 | tf_op jit(solution)/shard_map/ppermute | solution.py:567
  423.8 12.3 %collective-permute-start.47 = (f32[2,1024]{1,0:T(2,128)S(1)}, f32[2,1024]{1,0:T(2,128)S(1)}, u32[]{:S(2)}, u32[]{:S(2)}) collective-permute-start(f32[2,1024]{1,0:T(2,128)S(1)} %fusion.4), channel_id=1, source_target_pairs={{0,1},{1,0},{2,3},{3,2},{4,5},{5,4},{6,7},{7,6},{8,9},{9,8},{10,11... | collective-permute-start | bytes 24584 | tf_op jit(solution)/shard_map/ppermute | solution.py:564
  434.6 48.8 %collective-permute-start.45 = (bf16[4,128,2048]{2,1,0:T(8,128)(2,1)}, bf16[4,128,2048]{2,1,0:T(8,128)(2,1)S(1)}, u32[]{:S(2)}, u32[]{:S(2)}) collective-permute-start(bf16[4,128,2048]{2,1,0:T(8,128)(2,1)} %bitcast.57), channel_id=1, source_target_pairs={{0,1},{1,0},{2,3},{3,2},{4,5},{5,4},{6,7},{7,6},{8,9},{9,8},{10,11... | collective-permute-start | bytes 6291464 | tf_op jit(solution)/shard_map/ppermute | solution.py:564
  472.9 42.0 %collective-permute-start.52 = (bf16[3,128,2048]{2,1,0:T(8,128)(2,1)}, bf16[3,128,2048]{2,1,0:T(8,128)(2,1)S(1)}, u32[]{:S(2)}, u32[]{:S(2)}) collective-permute-start(bf16[3,128,2048]{2,1,0:T(8,128)(2,1)} %pad_maximum_fusion.2), channel_id=1, source_target_pairs={{0,1},{1,0},{2,3},{3,2},{4,5},{5,4},{6,7},{7,6},{8,9},{9,8},{10,11... | collective-permute-start | bytes 4718600 | tf_op jit(solution)/shard_map/ppermute | solution.py:564
  474.4 3.7 collective-permute-start.56
  478.1 3.9 collective-permute-start.57
  478.9 27.5 %collective-permute-start.53 = (bf16[512,256]{1,0:T(8,128)(2,1)S(1)}, bf16[512,256]{1,0:T(8,128)(2,1)S(1)}, u32[]{:S(2)}, u32[]{:S(2)}) collective-permute-start(bf16[512,256]{1,0:T(8,128)(2,1)S(1)} %get-tuple-element.274), channel_id=1, source_target_pairs={{0,2},{1,3},{2,0},{3,1},{4,6},{5,7},{6,4},{7,5},{8,10},{9,11},{10,... | collective-permute-start | bytes 786440 | tf_op jit(solution)/shard_map/ppermute | solution.py:564
  480.9 25.5 %collective-permute-start.54 = (bf16[512,256]{1,0:T(8,128)(2,1)S(1)}, bf16[512,256]{1,0:T(8,128)(2,1)S(1)}, u32[]{:S(2)}, u32[]{:S(2)}) collective-permute-start(bf16[512,256]{1,0:T(8,128)(2,1)S(1)} %get-tuple-element.273), channel_id=1, source_target_pairs={{0,4},{1,5},{2,6},{3,7},{4,0},{5,1},{6,2},{7,3},{8,12},{9,13},{10,... | collective-permute-start | bytes 786440 | tf_op jit(solution)/shard_map/ppermute | solution.py:564
  482.0 24.5 %collective-permute-start.55 = (bf16[512,256]{1,0:T(8,128)(2,1)S(1)}, bf16[512,256]{1,0:T(8,128)(2,1)S(1)}, u32[]{:S(2)}, u32[]{:S(2)}) collective-permute-start(bf16[512,256]{1,0:T(8,128)(2,1)S(1)} %get-tuple-element.272), channel_id=1, source_target_pairs={{0,6},{1,7},{2,4},{3,5},{4,2},{5,3},{6,0},{7,1},{8,14},{9,15},{10,... | collective-permute-start | bytes 786440 | tf_op jit(solution)/shard_map/ppermute | solution.py:564
  483.4 22.5 %collective-permute-start.58 = (f32[2,512]{1,0:T(2,128)S(1)}, f32[2,512]{1,0:T(2,128)S(1)}, u32[]{:S(2)}, u32[]{:S(2)}) collective-permute-start(f32[2,512]{1,0:T(2,128)S(1)} %add.120), channel_id=1, source_target_pairs={{0,4},{1,5},{2,6},{3,7},{4,0},{5,1},{6,2},{7,3},{8,12},{9,13},{10,... | collective-permute-start | bytes 12296 | tf_op jit(solution)/shard_map/ppermute | solution.py:564
  (80 other events, 1342.0 us)
Sparse Core Ops, SparseCore 0:
  14.3 28.3 all-gather.9
  44.9 92.1 all-gather.7
  242.1 113.5 reduce-scatter.1
  377.0 46.3 all-gather.11
  425.4 44.6 all-gather.13

commit v5 on v4

--- a/solution.py
+++ b/solution.py
@@ -424,7 +424,7 @@
     out[pl.ds(pl.multiple_of(size - at, size), size), :] = far[0].astype(out.dtype)
 
 
-def place_own_kernel(info, near, own, far, out):
+def place_own_kernel(info, near, own, out):
     size = near.shape[1]
     at = info[AT_LOW] * size
     out[pl.ds(pl.multiple_of(at, size), size), :] = near[0].astype(out.dtype)
@@ -434,9 +434,9 @@
     def _():
         out[other, :] = own[...].astype(out.dtype)
 
-    @pl.when(pl.program_id(0) > 0)
-    def _():
-        out[other, :] = far[0].astype(out.dtype)
+
+def place_far_kernel(info, placed, far, out):
+    out[...] = far[0].astype(out.dtype)
 
 
 def weight_grad_kernel(a, b, *outs):
@@ -1149,7 +1149,6 @@
                         (1, block, D), lambda i, info: (lax.bitwise_xor(info[AT_HIGH], i), 0, 0)
                     ),
                     whole((block, D)),
-                    pl.BlockSpec((1, block, D), lambda i, info: (jnp.maximum(i - 1, 0), 0, 0)),
                 ],
                 out_specs=pl.BlockSpec(
                     (rows, D), lambda i, info: (lax.bitwise_xor(info[AT_HIGH], i), 0)
@@ -1159,9 +1158,31 @@
             compiler_params=vmem(48),
             cost_estimate=cost(5),
             name=name,
-        )(info, *parts).reshape(tokens.shape)
-
-    tokens_grad = place_own((tokens_near, tokens_own, tokens_far), F32, "tokens_grad")
+        )(info, *parts)
+
+    placed = place_own((tokens_near, tokens_own), F32, "tokens_grad_near")
+    tokens_grad = pl.pallas_call(
+        place_far_kernel,
+        grid_spec=pltpu.PrefetchScalarGridSpec(
+            num_scalar_prefetch=1,
+            grid=(3,),
+            in_specs=[
+                pl.BlockSpec(memory_space=pl.ANY),
+                pl.BlockSpec((1, block, D), lambda i, info: (i, 0, 0)),
+            ],
+            out_specs=pl.BlockSpec(
+                (block, D),
+                lambda i, info: (
+                    lax.bitwise_xor(info[AT_HIGH], i + 1) * 2 + 1 - info[AT_LOW],
+                    0,
+                ),
+            ),
+        ),
+        out_shape=jax.ShapeDtypeStruct((span, D), F32),
+        input_output_aliases={1: 0},
+        compiler_params=vmem(48),
+        name="tokens_grad_far",
+    )(info, placed, tokens_far).reshape(tokens.shape)
     block_out = place((block_near, block_far), BF16, "block_out_rows")
 
     results = (query_new, output_new, kv_new, gate_up_new, down_new, gains_new)

time: 535 us -> 546 us (1.021)
  local copies, waits for them, and re-layouts: 34.8 us -> 46 us
  waiting for transfers between devices: 145 us -> 137 us
    unnamed x161 -> x189, local copies, waits for them, and re-layouts: 25.4 us -> 36.6 us
    all_gather x1, waiting for transfers between devices: 14.2 us -> 5.99 us  [body(): lax.all_gather(tokens_low, 'tensor', axis=0, axis_index_groups=HIGH_GROUPS)]
  transfers between devices with their start and end apart: 67 -> 67, of which waited for: 26 -> 24; matrix products, arithmetic and copies ran while one was open for 6% -> 6% of each run, Pallas kernels for 34% -> 35%
where the time goes in v5:
time: 546 us; the launch traced here: 537 us
  Pallas kernels  188 us (34%)
  waiting for transfers between devices  137 us (25%)
  starting transfers between devices  122 us (22%)
  local copies, waits for them, and re-layouts  46 us (8%)
  other arithmetic  27.6 us (5%)
  between operations  15.2 us (3%)
    ppermute x42, waiting for transfers between devices, swap_tensor(): return lax.ppermute(value, 'tensor', [(i, i ^ mask) for i in range(8)])  111 us
    ppermute x42, starting transfers between devices, swap_tensor(): return lax.ppermute(value, 'tensor', [(i, i ^ mask) for i in range(8)])  76.1 us
    pallas_call x2, Pallas kernels, mlp(): pl.pallas_call(functools.partial(mlp_kernel, len(nears)), grid_spec=pltpu...  45.9 us
    unnamed x189, local copies, waits for them, and re-layouts  36.6 us
    pallas_call x5, Pallas kernels, adam(): pl.pallas_call(functools.partial(adam_kernel, rate, decay), grid=(4,), in...  31.1 us
    pallas_call x1, Pallas kernels, body(): pl.pallas_call(mlp_grad_kernel, grid=(4,), in_specs=[narrow, whole((span,...  19.2 us
    ppermute x11, starting transfers between devices, swap_seq(): return lax.ppermute(value, 'seq', [(0, 1), (1, 0)])  16.5 us
    ppermute x6, waiting for transfers between devices, swap_dp(): return lax.ppermute(value, 'dp', [(0, 1), (1, 0)])  13.6 us
  transfers between devices with their start and end apart: 67, of which 24 were waited for; matrix products, arithmetic and copies ran while one was open for 6% of the time, Pallas kernels for 35%

profile of v5, /device:TPU:0, one launch (start us, length us, event | category | flops | bytes accessed | tf_op | source)
XLA Modules:
  0.0 536.7 jit_solution(15446776703340609605)
XLA Ops:
  11.0 3.0 collective-permute-start
  17.6 8.3 %collective-permute-done.w1 = bf16[512,512]{1,0:T(8,128)(2,1)S(1)} collective-permute-done((bf16[512,512]{1,0:T(8,128)(2,1)S(1)}, bf16[512,512]{1,0:T(8,128)(2,1)S(1)}, u32[]{:S(2)}, u32[]{:S(2)}) %collective-permute-start) | collective-permute-done | bytes 524320 | tf_op jit(solution)/shard_map/ppermute | solution.py:567
  32.8 7.4 %project.1 = (bf16[1024,2048]{1,0:T(8,128)(2,1)}, bf16[1024,256]{1,0:T(8,128)(2,1)S(1)}, bf16[1024,128]{1,0:T(8,128)(2,1)S(1)}, f32[8,2048]{1,0:T(8,128)S(1)}) custom-call(s32[9]{0:T(128)S(1)} %stack.69.info, bf16[1024,2048]{1,0:T(8,128)(2,1)} %bitcast.60, bf16[512,512]{1,0:T(8,128)(2,1)S(1)} %copy-done.27, bf16[512,512]{1,0:T(8,128)(2,1)S(1)} %copy-done.18, ...), custom_call_target="tpu_custom_call" | custom-call | bytes 12915000 | tf_op jit(solution)/shard_map/project/pallas_call | solution.py:681
  46.3 8.1 %attend.1 = (bf16[1024,256]{1,0:T(8,128)(2,1)}, f32[4,1,1024]{2,1,0:T(1,128)S(1)}) custom-call(s32[9]{0:T(128)S(1)} %stack.69.info, bf16[1024,256]{1,0:T(8,128)(2,1)S(1)} %copy-done.15, bf16[2048,128]{1,0:T(8,128)(2,1)S(1)} %maximum_select_fusion.kv), custom_call_target="tpu_custom_call" | custom-call | bytes 33210000 | tf_op jit(solution)/shard_map/attend/pallas_call | solution.py:725
  55.8 4.9 all-to-all-start
  61.2 7.4 %reorder.1.refs_2_.refs_9_ = bf16[2,512,2048]{2,1,0:T(8,128)(2,1)} custom-call(s32[9]{0:T(128)} %copy-done.39, bf16[1024,2048]{1,0:T(8,128)(2,1)} %bitcast.64), custom_call_target="tpu_custom_call" | custom-call | bytes 13837500 | tf_op jit(solution)/shard_map/reorder/pallas_call | solution.py:668
  68.6 2.4 all-to-all-done.att
  71.0 6.5 %collective-permute-start.5 = (bf16[4,512,256]{2,1,0:T(8,128)(2,1)S(1)}, bf16[4,512,256]{2,1,0:T(8,128)(2,1)S(1)}, u32[]{:S(2)}, u32[]{:S(2)}) collective-permute-start(bf16[4,512,256]{2,1,0:T(8,128)(2,1)S(1)} %bitcast.54), channel_id=1, source_target_pairs={{0,8},{8,0},{1,9},{9,1},{2,10},{10,2},{3,11},{11,3},{4,12},{12,4},... | collective-permute-start | bytes 3145736 | tf_op jit(solution)/shard_map/ppermute | solution.py:570
  77.5 5.3 collective-permute-done.4.w1
  82.8 2.9 collective-permute-done.6.w3
  86.6 3.6 attention_out.1
  92.4 12.7 %collective-permute-done.7.got = bf16[128,2048]{1,0:T(8,128)(2,1)S(1)} collective-permute-done((bf16[128,2048]{1,0:T(8,128)(2,1)S(1)}, bf16[128,2048]{1,0:T(8,128)(2,1)S(1)}, u32[]{:S(2)}, u32[]{:S(2)}) %collective-permute-start.7) | collective-permute-done | bytes 524320 | tf_op jit(solution)/shard_map/ppermute | solution.py:564
  105.9 3.5 second_norm.1
  110.9 2.8 collective-permute-start.9
  114.9 7.1 %collective-permute-done.8 = bf16[64,2048]{1,0:T(8,128)(2,1)S(1)} collective-permute-done((bf16[64,2048]{1,0:T(8,128)(2,1)}, bf16[64,2048]{1,0:T(8,128)(2,1)S(1)}, u32[]{:S(2)}, u32[]{:S(2)}) %collective-permute-start.8) | collective-permute-done | bytes 262176 | tf_op jit(solution)/shard_map/ppermute | solution.py:564
  122.0 10.5 %collective-permute-done.9 = bf16[64,2048]{1,0:T(8,128)(2,1)S(1)} collective-permute-done((bf16[64,2048]{1,0:T(8,128)(2,1)}, bf16[64,2048]{1,0:T(8,128)(2,1)S(1)}, u32[]{:S(2)}, u32[]{:S(2)}) %collective-permute-start.9) | collective-permute-done | bytes 262176 | tf_op jit(solution)/shard_map/ppermute | solution.py:564
  134.2 4.5 collective-permute-start.12
  141.1 6.0 %collective-permute-done.12 = bf16[64,2048]{1,0:T(8,128)(2,1)S(1)} collective-permute-done((bf16[64,2048]{1,0:T(8,128)(2,1)S(1)}, bf16[64,2048]{1,0:T(8,128)(2,1)S(1)}, u32[]{:S(2)}, u32[]{:S(2)}) %collective-permute-start.12) | collective-permute-done | bytes 262176 | tf_op jit(solution)/shard_map/ppermute | solution.py:564
  147.2 12.5 %collective-permute-done.13 = bf16[64,2048]{1,0:T(8,128)(2,1)S(1)} collective-permute-done((bf16[64,2048]{1,0:T(8,128)(2,1)S(1)}, bf16[64,2048]{1,0:T(8,128)(2,1)S(1)}, u32[]{:S(2)}, u32[]{:S(2)}) %collective-permute-start.13) | collective-permute-done | bytes 262176 | tf_op jit(solution)/shard_map/ppermute | solution.py:564
  160.3 22.8 %mlp.2 = (bf16[4,64,2048]{2,1,0:T(8,128)(2,1)}, bf16[4,64,2048]{2,1,0:T(8,128)(2,1)}, bf16[256,2048]{1,0:T(8,128)(2,1)}, bf16[256,2048]{1,0:T(8,128)(2,1)}, bf16...) custom-call(s32[9]{0:T(128)} %copy-done.39, bf16[256,2048]{1,0:T(8,128)(2,1)} %copy-done.68, ...), custom_call_target="tpu_custom_call" | custom-call | bytes 41512500 | tf_op jit(solution)/shard_map/mlp/pallas_call | solution.py:800
  184.8 3.6 collective-permute-start.18
  190.8 23.1 %mlp.3 = (bf16[4,64,2048]{2,1,0:T(8,128)(2,1)}, bf16[4,64,2048]{2,1,0:T(8,128)(2,1)}, bf16[256,2048]{1,0:T(8,128)(2,1)}, bf16[256,2048]{1,0:T(8,128)(2,1)}, bf16...) custom-call(s32[9]{0:T(128)} %copy-done.39, ...), custom_call_target="tpu_custom_call", output_to_operand_aliasing={{4}: (5, {}), {5}: (6, {}), {6}: (7, {})} | custom-call | bytes 41512500 | tf_op jit(solution)/shard_map/mlp/pallas_call | solution.py:800
  221.3 19.2 %mlp_grad.1 = bf16[2048,3072]{1,0:T(8,128)(2,1)} custom-call(bf16[1024,2048]{1,0:T(8,128)(2,1)} %get-tuple-element.163.x, bf16[1024,2048]{1,0:T(8,128)(2,1)} %get-tuple-element.174.gate_up_back, bf16[1024,2048]{1,0:T(8,128)(2,1)} %bitcast.59, bf16[1024,1024]{1,0:T(8,128)(2,1)} %get-tuple-element.175.hidden), custom_call_target="tpu_custom_call" | custom-call | bytes 40590000 | tf_op jit(solution)/shard_map/mlp_grad/pallas_call | solution.py:857
  242.1 3.7 fusion.8
  247.6 16.8 %collective-permute-start.25 = (bf16[64,2048]{1,0:T(8,128)(2,1)S(1)}, bf16[64,2048]{1,0:T(8,128)(2,1)S(1)}, u32[]{:S(2)}, u32[]{:S(2)}) collective-permute-start(bf16[64,2048]{1,0:T(8,128)(2,1)S(1)} %get-tuple-element.278), channel_id=1, source_target_pairs={{0,2},{1,3},{2,0},{3,1},{4,6},{5,7},{6,4},{7,5},{8,10},{9,11},{10,... | collective-permute-start | bytes 786440 | tf_op jit(solution)/shard_map/ppermute | solution.py:564
  266.8 2.3 collective-permute-start.33
  271.2 6.2 %collective-permute-done.26.refs_6_ = bf16[64,2048]{1,0:T(8,128)(2,1)} collective-permute-done((bf16[64,2048]{1,0:T(8,128)(2,1)S(1)}, bf16[64,2048]{1,0:T(8,128)(2,1)}, u32[]{:S(2)}, u32[]{:S(2)}) %collective-permute-start.26) | collective-permute-done | bytes 262176 | tf_op jit(solution)/shard_map/ppermute | solution.py:564
  277.4 4.9 second_norm_back.1
  283.8 2.9 add_convert_fusion.2
  286.8 6.3 %collective-permute-done.28.other = bf16[128,2048]{1,0:T(8,128)(2,1)S(1)} collective-permute-done((bf16[128,2048]{1,0:T(8,128)(2,1)}, bf16[128,2048]{1,0:T(8,128)(2,1)S(1)}, u32[]{:S(2)}, u32[]{:S(2)}) %collective-permute-start.28) | collective-permute-done | bytes 524320 | tf_op jit(solution)/shard_map/ppermute | solution.py:564
  295.6 9.1 %all-to-all-start.1 = ((bf16[4,64,2048]{2,1,0:T(8,128)(2,1)}), bf16[4,64,2048]{2,1,0:T(8,128)(2,1)}, u32[]{:S(2)}, u32[]{:S(2)}) async-start(bf16[4,64,2048]{2,1,0:T(8,128)(2,1)} %add_convert_fusion.2), calls=%async_computation.1 | async-start | bytes 2097152 | tf_op jit(solution)/shard_map/all_to_all | solution.py:897
  309.3 3.4 attention_out_back.1
  313.7 2.6 collective-permute-start.30
  318.7 2.7 collective-permute-done.30.grad1
  321.4 3.6 collective-permute-done.31.grad2
  325.7 2.7 add_convert_fusion.1
  328.4 4.2 all-to-all-start.2
  337.4 11.5 %attend_back.1 = (bf16[1024,256]{1,0:T(8,128)(2,1)S(1)}, bf16[256,256]{1,0:T(8,128)(2,1)S(1)}, bf16[256,256]{1,0:T(8,128)(2,1)S(1)}, bf16[256,256]{1,0:T(8,128)(...) custom-call(s32[9]{0:T(128)S(1)} %copy-done.41, bf16[1024,256]{1,0:T(8,128)(2,1)S(1)} %copy-done.16, ...), custom_call_target="tpu_custom_call" | custom-call | bytes 42435000 | tf_op jit(solution)/shard_map/attend_back/pallas_call | solution.py:921
  350.4 9.0 %collective-permute-start.36 = (bf16[1024,128]{1,0:T(8,128)(2,1)S(1)}, bf16[1024,128]{1,0:T(8,128)(2,1)S(1)}, u32[]{:S(2)}, u32[]{:S(2)}) collective-permute-start(bf16[1024,128]{1,0:T(8,128)(2,1)S(1)} %get-tuple-element.286), channel_id=1, source_target_pairs={{0,8},{8,0},{1,9},{9,1},{2,10},{10,2},{3,11},{11,3},{4,12},{12,4},... | collective-permute-start | bytes 786440 | tf_op jit(solution)/shard_map/ppermute | solution.py:570
  361.1 2.4 collective-permute-start.38
  363.8 2.7 collective-permute-done.37.q1
  366.6 7.5 %collective-permute-done.38.q2 = bf16[256,256]{1,0:T(8,128)(2,1)S(1)} collective-permute-done((bf16[256,256]{1,0:T(8,128)(2,1)S(1)}, bf16[256,256]{1,0:T(8,128)(2,1)S(1)}, u32[]{:S(2)}, u32[]{:S(2)}) %collective-permute-start.38) | collective-permute-done | bytes 131104 | tf_op jit(solution)/shard_map/ppermute | solution.py:564
  374.8 3.1 kv_back.1
  378.0 3.0 block_out.1
  381.0 2.2 collective-permute-start.40
  386.8 3.6 collective-permute-done.41.k2
  395.9 6.2 %attention_in_back.1 = (f32[128,2048]{1,0:T(8,128)S(1)}, bf16[128,2048]{1,0:T(8,128)(2,1)}) custom-call(s32[9]{0:T(128)S(1)} %copy-done.42, bf16[256,256]{1,0:T(8,128)(2,1)S(1)} %get-tuple-element.198.q0, bf16[256,256]{1,0:T(8,128)(2,1)S(1)} %collective-permute-done.37.q1, bf16[256,256]{1,0:T(8,128)(2,1)S(1)} %collective-permute-done.38.q2, ...), custom_call_target="tpu_custom_call" | custom-call | bytes 10701000 | tf_op jit(solution)/shard_map/attention_in_back/pallas_call | solution.py:982
  403.4 5.8 %weight_grad.3 = (bf16[1024,1024]{1,0:T(8,128)(2,1)}, bf16[1024,1024]{1,0:T(8,128)(2,1)}) custom-call(bf16[256,2048]{1,0:T(8,128)(2,1)} %copy-done.28, bf16[256,1024]{1,0:T(8,128)(2,1)} %pad_maximum_fusion.6.b), custom_call_target="tpu_custom_call" | custom-call | bytes 3022848 | tf_op jit(solution)/shard_map/weight_grad/pallas_call | solution.py:598
  410.2 6.1 %weight_grad.2 = (bf16[1024,384]{1,0:T(8,128)(2,1)}, bf16[1024,384]{1,0:T(8,128)(2,1)}) custom-call(bf16[1024,2048]{1,0:T(8,128)(2,1)} %get-tuple-element.217.a, bf16[1024,384]{1,0:T(8,128)(2,1)} %pad_maximum_fusion.3.b), custom_call_target="tpu_custom_call" | custom-call | bytes 4534272 | tf_op jit(solution)/shard_map/weight_grad/pallas_call | solution.py:598
  417.1 4.1 first_norm_back.1
  426.6 2.6 pair_sum.2
  429.2 2.2 collective-permute-start.49
  436.6 10.2 %collective-permute-done.44.own = bf16[128,2048]{1,0:T(8,128)(2,1)S(1)} collective-permute-done((bf16[128,2048]{1,0:T(8,128)(2,1)}, bf16[128,2048]{1,0:T(8,128)(2,1)S(1)}, u32[]{:S(2)}, u32[]{:S(2)}) %collective-permute-start.44) | collective-permute-done | bytes 524320 | tf_op jit(solution)/shard_map/ppermute | solution.py:564
  448.4 13.2 %adam.5 = (f32[512,2,1024]{2,1,0:T(2,128)}, f32[512,2,1024]{2,1,0:T(2,128)}, f32[512,2,1024]{2,1,0:T(2,128)}) custom-call(f32[512,2,1024]{2,1,0:T(2,128)} %weight.5, f32[512,2,1024]{2,1,0:T(2,128)} %one.5, f32[512,2,1024]{2,1,0:T(2,128)} %two.5, bf16[512,3072]{1,0:T(8,128)(2,1)} %reduce-scatter.2.cloned.1.call-done.refs_0_), custom_call_target="tpu_custom_call" | custom-call | bytes 25794968 | tf_op jit(solution)/shard_map/adam/pallas_call | solution.py:1036
  461.6 6.7 %adam.6 = (f32[512,1024]{1,0:T(8,128)}, f32[512,1024]{1,0:T(8,128)}, f32[512,1024]{1,0:T(8,128)}) custom-call(f32[512,1024]{1,0:T(8,128)} %weight.6, f32[512,1024]{1,0:T(8,128)} %one.6, f32[512,1024]{1,0:T(8,128)} %two.6, bf16[512,3072]{1,0:T(8,128)(2,1)} %reduce-scatter.2.cloned.1.call-done.refs_0_), custom_call_target="tpu_custom_call" | custom-call | bytes 12897484 | tf_op jit(solution)/shard_map/adam/pallas_call | solution.py:1036
  468.3 6.0 %all-gather.14.cloned.1.call-done = bf16[512,2048]{1,0:T(8,128)(2,1)} async-done(((bf16[128,2048]{1,0:T(8,128)(2,1)}), bf16[512,2048]{1,0:T(8,128)(2,1)}) %all-gather.14.cloned.1.call-update) | async-done | bytes 2097168 | tf_op jit(solution)/shard_map/all_gather | solution.py:1023
  486.4 9.2 %collective-permute-done.45.far = bf16[4,128,2048]{2,1,0:T(8,128)(2,1)} collective-permute-done((bf16[4,128,2048]{2,1,0:T(8,128)(2,1)}, bf16[4,128,2048]{2,1,0:T(8,128)(2,1)}, u32[]{:S(2)}, u32[]{:S(2)}) %collective-permute-start.45) | collective-permute-done | bytes 2097184 | tf_op jit(solution)/shard_map/ppermute | solution.py:564
  497.1 4.7 block_out_rows.1
  501.8 3.3 adam.9
  505.2 4.0 adam.7
  509.2 4.1 tokens_grad_near.1.placed
  514.9 3.9 adam.8
  518.8 8.4 %collective-permute-done.52.far = bf16[3,128,2048]{2,1,0:T(8,128)(2,1)S(1)} collective-permute-done((bf16[3,128,2048]{2,1,0:T(8,128)(2,1)S(1)}, bf16[3,128,2048]{2,1,0:T(8,128)(2,1)S(1)}, u32[]{:S(2)}, u32[]{:S(2)}) %collective-permute-start.52) | collective-permute-done | bytes 1572896 | tf_op jit(solution)/shard_map/ppermute | solution.py:564
  527.1 2.6 tokens_grad_far.1
  (345 shorter events, 113.9 us)
Async XLA Ops:
  7.2 37.3 %all-gather.10.cloned.1.call-start = ((), (), s32[]{:S(2)}) async-start(), calls=%async_computation.6 | async-start | bytes 1310720 | tf_op jit(solution)/shard_map/all_gather | solution.py:661
  11.0 14.9 %collective-permute-start = (bf16[512,512]{1,0:T(8,128)(2,1)S(1)}, bf16[512,512]{1,0:T(8,128)(2,1)S(1)}, u32[]{:S(2)}, u32[]{:S(2)}) collective-permute-start(bf16[512,512]{1,0:T(8,128)(2,1)S(1)} %fusion.1.w0), channel_id=1, source_target_pairs={{0,16},{16,0},{1,17},{17,1},{2,18},{18,2},{3,19},{19,3},{4,20},{20... | collective-permute-start | bytes 1572872 | tf_op jit(solution)/shard_map/ppermute | solution.py:567
  14.0 12.8 %collective-permute-start.1 = (bf16[512,512]{1,0:T(8,128)(2,1)S(1)}, bf16[512,512]{1,0:T(8,128)(2,1)S(1)}, u32[]{:S(2)}, u32[]{:S(2)}) collective-permute-start(bf16[512,512]{1,0:T(8,128)(2,1)S(1)} %fusion.1.w0), channel_id=1, source_target_pairs={{0,8},{8,0},{1,9},{9,1},{2,10},{10,2},{3,11},{11,3},{4,12},{12,4},... | collective-permute-start | bytes 1572872 | tf_op jit(solution)/shard_map/ppermute | solution.py:570
  14.7 145.6 %all-gather.8.cloned.1.call-start = ((), (), s32[]{:S(2)}) async-start(), calls=%async_computation.4 | async-start | bytes 15728640 | tf_op jit(solution)/shard_map/all_gather | solution.py:584
  44.5 38.3 %collective-permute-start.4 = (bf16[4,512,256]{2,1,0:T(8,128)(2,1)}, bf16[4,512,256]{2,1,0:T(8,128)(2,1)}, u32[]{:S(2)}, u32[]{:S(2)}) collective-permute-start(bf16[4,512,256]{2,1,0:T(8,128)(2,1)} %bitcast.53), channel_id=1, source_target_pairs={{0,16},{16,0},{1,17},{17,1},{2,18},{18,2},{3,19},{19,3},{4,20},{20... | collective-permute-start | bytes 3145736 | tf_op jit(solution)/shard_map/ppermute | solution.py:567
  55.8 15.2 %all-to-all-start = ((bf16[4,256,256]{2,1,0:T(8,128)(2,1)}), bf16[4,256,256]{2,1,0:T(8,128)(2,1)S(1)}, u32[]{:S(2)}, u32[]{:S(2)}) async-start(bf16[4,256,256]{2,1,0:T(8,128)(2,1)} %bitcast.10), calls=%async_computation | async-start | bytes 1048576 | tf_op jit(solution)/shard_map/all_to_all | solution.py:754
  60.7 330.9 %reduce-scatter.2.cloned.1.call-start = ((), (), s32[]{:S(2)}) async-start(), calls=%async_computation.5 | async-start | bytes 15728640 | tf_op jit(solution)/shard_map/reduce_scatter | solution.py:587
  71.0 11.8 %collective-permute-start.5 = (bf16[4,512,256]{2,1,0:T(8,128)(2,1)S(1)}, bf16[4,512,256]{2,1,0:T(8,128)(2,1)S(1)}, u32[]{:S(2)}, u32[]{:S(2)}) collective-permute-start(bf16[4,512,256]{2,1,0:T(8,128)(2,1)S(1)} %bitcast.54), channel_id=1, source_target_pairs={{0,8},{8,0},{1,9},{9,1},{2,10},{10,2},{3,11},{11,3},{4,12},{12,4},... | collective-permute-start | bytes 3145736 | tf_op jit(solution)/shard_map/ppermute | solution.py:570
  82.8 2.9 collective-permute-start.6
  91.2 13.9 %collective-permute-start.7 = (bf16[128,2048]{1,0:T(8,128)(2,1)S(1)}, bf16[128,2048]{1,0:T(8,128)(2,1)S(1)}, u32[]{:S(2)}, u32[]{:S(2)}) collective-permute-start(bf16[128,2048]{1,0:T(8,128)(2,1)S(1)} %get-tuple-element.149), channel_id=1, source_target_pairs={{0,1},{1,0},{2,3},{3,2},{4,5},{5,4},{6,7},{7,6},{8,9},{9,8},{10,11... | collective-permute-start | bytes 1572872 | tf_op jit(solution)/shard_map/ppermute | solution.py:564
  109.5 12.5 %collective-permute-start.8 = (bf16[64,2048]{1,0:T(8,128)(2,1)}, bf16[64,2048]{1,0:T(8,128)(2,1)S(1)}, u32[]{:S(2)}, u32[]{:S(2)}) collective-permute-start(bf16[64,2048]{1,0:T(8,128)(2,1)} %get-tuple-element.151), channel_id=1, source_target_pairs={{0,2},{1,3},{2,0},{3,1},{4,6},{5,7},{6,4},{7,5},{8,10},{9,11},{10,... | collective-permute-start | bytes 786440 | tf_op jit(solution)/shard_map/ppermute | solution.py:564
  110.9 21.6 %collective-permute-start.9 = (bf16[64,2048]{1,0:T(8,128)(2,1)}, bf16[64,2048]{1,0:T(8,128)(2,1)S(1)}, u32[]{:S(2)}, u32[]{:S(2)}) collective-permute-start(bf16[64,2048]{1,0:T(8,128)(2,1)} %get-tuple-element.151), channel_id=1, source_target_pairs={{0,4},{1,5},{2,6},{3,7},{4,0},{5,1},{6,2},{7,3},{8,12},{9,13},{10,... | collective-permute-start | bytes 786440 | tf_op jit(solution)/shard_map/ppermute | solution.py:564
  114.7 17.8 %collective-permute-start.10 = (bf16[64,2048]{1,0:T(8,128)(2,1)}, bf16[64,2048]{1,0:T(8,128)(2,1)S(1)}, u32[]{:S(2)}, u32[]{:S(2)}) collective-permute-start(bf16[64,2048]{1,0:T(8,128)(2,1)} %get-tuple-element.151), channel_id=1, source_target_pairs={{0,6},{1,7},{2,4},{3,5},{4,2},{5,3},{6,0},{7,1},{8,14},{9,15},{10,... | collective-permute-start | bytes 786440 | tf_op jit(solution)/shard_map/ppermute | solution.py:564
  132.6 27.8 %collective-permute-start.11 = (bf16[256,2048]{1,0:T(8,128)(2,1)S(1)}, bf16[256,2048]{1,0:T(8,128)(2,1)}, u32[]{:S(2)}, u32[]{:S(2)}) collective-permute-start(bf16[256,2048]{1,0:T(8,128)(2,1)S(1)} %constant_dynamic-update-slice_fusion.refs_0_), channel_id=1, source_target_pairs={{0,1},{1,0},{2,3},{3,2},{4,5},{5,4},{6,7},{7,6},{8,9},{9,8},{10,11... | collective-permute-start | bytes 3145736 | tf_op jit(solution)/shard_map/ppermute | solution.py:564
  134.2 13.0 %collective-permute-start.12 = (bf16[64,2048]{1,0:T(8,128)(2,1)S(1)}, bf16[64,2048]{1,0:T(8,128)(2,1)S(1)}, u32[]{:S(2)}, u32[]{:S(2)}) collective-permute-start(bf16[64,2048]{1,0:T(8,128)(2,1)S(1)} %copy-done.81), channel_id=1, source_target_pairs={{0,2},{1,3},{2,0},{3,1},{4,6},{5,7},{6,4},{7,5},{8,10},{9,11},{10,... | collective-permute-start | bytes 786440 | tf_op jit(solution)/shard_map/ppermute | solution.py:564
  138.6 21.0 %collective-permute-start.13 = (bf16[64,2048]{1,0:T(8,128)(2,1)S(1)}, bf16[64,2048]{1,0:T(8,128)(2,1)S(1)}, u32[]{:S(2)}, u32[]{:S(2)}) collective-permute-start(bf16[64,2048]{1,0:T(8,128)(2,1)S(1)} %copy-done.81), channel_id=1, source_target_pairs={{0,4},{1,5},{2,6},{3,7},{4,0},{5,1},{6,2},{7,3},{8,12},{9,13},{10,... | collective-permute-start | bytes 786440 | tf_op jit(solution)/shard_map/ppermute | solution.py:564
  139.6 20.1 %collective-permute-start.14 = (bf16[64,2048]{1,0:T(8,128)(2,1)S(1)}, bf16[64,2048]{1,0:T(8,128)(2,1)S(1)}, u32[]{:S(2)}, u32[]{:S(2)}) collective-permute-start(bf16[64,2048]{1,0:T(8,128)(2,1)S(1)} %copy-done.81), channel_id=1, source_target_pairs={{0,6},{1,7},{2,4},{3,5},{4,2},{5,3},{6,0},{7,1},{8,14},{9,15},{10,... | collective-permute-start | bytes 786440 | tf_op jit(solution)/shard_map/ppermute | solution.py:564
  159.7 31.1 %collective-permute-start.15 = (bf16[256,2048]{1,0:T(8,128)(2,1)S(1)}, bf16[256,2048]{1,0:T(8,128)(2,1)}, u32[]{:S(2)}, u32[]{:S(2)}) collective-permute-start(bf16[256,2048]{1,0:T(8,128)(2,1)S(1)} %constant_dynamic-update-slice_fusion.4.refs_0_), channel_id=1, source_target_pairs={{0,1},{1,0},{2,3},{3,2},{4,5},{5,4},{6,7},{7,6},{8,9},{9,8},{10,11... | collective-permute-start | bytes 3145736 | tf_op jit(solution)/shard_map/ppermute | solution.py:564
  183.2 31.3 %collective-permute-start.17 = (bf16[256,2048]{1,0:T(8,128)(2,1)}, bf16[256,2048]{1,0:T(8,128)(2,1)S(1)}, u32[]{:S(2)}, u32[]{:S(2)}) collective-permute-start(bf16[256,2048]{1,0:T(8,128)(2,1)} %get-tuple-element.167), channel_id=1, source_target_pairs={{0,1},{1,0},{2,3},{3,2},{4,5},{5,4},{6,7},{7,6},{8,9},{9,8},{10,11... | collective-permute-start | bytes 3145736 | tf_op jit(solution)/shard_map/ppermute | solution.py:564
  184.8 32.1 %collective-permute-start.18 = (bf16[512,384]{1,0:T(8,128)(2,1)S(1)}, bf16[512,384]{1,0:T(8,128)(2,1)S(1)}, u32[]{:S(2)}, u32[]{:S(2)}) collective-permute-start(bf16[512,384]{1,0:T(8,128)(2,1)S(1)} %pad_maximum_fusion.7), channel_id=1, source_target_pairs={{0,2},{1,3},{2,0},{3,1},{4,6},{5,7},{6,4},{7,5},{8,10},{9,11},{10,... | collective-permute-start | bytes 1179656 | tf_op jit(solution)/shard_map/ppermute | solution.py:564
  188.4 30.3 %collective-permute-start.19 = (bf16[512,384]{1,0:T(8,128)(2,1)S(1)}, bf16[512,384]{1,0:T(8,128)(2,1)S(1)}, u32[]{:S(2)}, u32[]{:S(2)}) collective-permute-start(bf16[512,384]{1,0:T(8,128)(2,1)S(1)} %pad_maximum_fusion.7), channel_id=1, source_target_pairs={{0,4},{1,5},{2,6},{3,7},{4,0},{5,1},{6,2},{7,3},{8,12},{9,13},{10,... | collective-permute-start | bytes 1179656 | tf_op jit(solution)/shard_map/ppermute | solution.py:564
  189.2 31.0 %collective-permute-start.20 = (bf16[512,384]{1,0:T(8,128)(2,1)S(1)}, bf16[512,384]{1,0:T(8,128)(2,1)S(1)}, u32[]{:S(2)}, u32[]{:S(2)}) collective-permute-start(bf16[512,384]{1,0:T(8,128)(2,1)S(1)} %pad_maximum_fusion.7), channel_id=1, source_target_pairs={{0,6},{1,7},{2,4},{3,5},{4,2},{5,3},{6,0},{7,1},{8,14},{9,15},{10,... | collective-permute-start | bytes 1179656 | tf_op jit(solution)/shard_map/ppermute | solution.py:564
  213.9 26.7 %collective-permute-start.16 = (bf16[256,2048]{1,0:T(8,128)(2,1)}, bf16[256,2048]{1,0:T(8,128)(2,1)}, u32[]{:S(2)}, u32[]{:S(2)}) collective-permute-start(bf16[256,2048]{1,0:T(8,128)(2,1)} %get-tuple-element.162), channel_id=1, source_target_pairs={{0,1},{1,0},{2,3},{3,2},{4,5},{5,4},{6,7},{7,6},{8,9},{9,8},{10,11... | collective-permute-start | bytes 3145736 | tf_op jit(solution)/shard_map/ppermute | solution.py:564
  215.9 24.7 %collective-permute-start.21 = (bf16[64,2048]{1,0:T(8,128)(2,1)}, bf16[64,2048]{1,0:T(8,128)(2,1)S(1)}, u32[]{:S(2)}, u32[]{:S(2)}) collective-permute-start(bf16[64,2048]{1,0:T(8,128)(2,1)} %get-tuple-element.281), channel_id=1, source_target_pairs={{0,2},{1,3},{2,0},{3,1},{4,6},{5,7},{6,4},{7,5},{8,10},{9,11},{10,... | collective-permute-start | bytes 786440 | tf_op jit(solution)/shard_map/ppermute | solution.py:564
  216.9 25.2 %collective-permute-start.22 = (bf16[64,2048]{1,0:T(8,128)(2,1)}, bf16[64,2048]{1,0:T(8,128)(2,1)}, u32[]{:S(2)}, u32[]{:S(2)}) collective-permute-start(bf16[64,2048]{1,0:T(8,128)(2,1)} %get-tuple-element.280), channel_id=1, source_target_pairs={{0,4},{1,5},{2,6},{3,7},{4,0},{5,1},{6,2},{7,3},{8,12},{9,13},{10,... | collective-permute-start | bytes 786440 | tf_op jit(solution)/shard_map/ppermute | solution.py:564
  218.7 23.5 %collective-permute-start.23 = (bf16[64,2048]{1,0:T(8,128)(2,1)}, bf16[64,2048]{1,0:T(8,128)(2,1)}, u32[]{:S(2)}, u32[]{:S(2)}) collective-permute-start(bf16[64,2048]{1,0:T(8,128)(2,1)} %get-tuple-element.279), channel_id=1, source_target_pairs={{0,6},{1,7},{2,4},{3,5},{4,2},{5,3},{6,0},{7,1},{8,14},{9,15},{10,... | collective-permute-start | bytes 786440 | tf_op jit(solution)/shard_map/ppermute | solution.py:564
  245.8 38.0 %collective-permute-start.24 = (bf16[4,64,2048]{2,1,0:T(8,128)(2,1)}, bf16[4,64,2048]{2,1,0:T(8,128)(2,1)}, u32[]{:S(2)}, u32[]{:S(2)}) collective-permute-start(bf16[4,64,2048]{2,1,0:T(8,128)(2,1)} %get-tuple-element.177), channel_id=1, source_target_pairs={{0,1},{1,0},{2,3},{3,2},{4,5},{5,4},{6,7},{7,6},{8,9},{9,8},{10,11... | collective-permute-start | bytes 3145736 | tf_op jit(solution)/shard_map/ppermute | solution.py:564
  247.6 23.6 %collective-permute-start.25 = (bf16[64,2048]{1,0:T(8,128)(2,1)S(1)}, bf16[64,2048]{1,0:T(8,128)(2,1)S(1)}, u32[]{:S(2)}, u32[]{:S(2)}) collective-permute-start(bf16[64,2048]{1,0:T(8,128)(2,1)S(1)} %get-tuple-element.278), channel_id=1, source_target_pairs={{0,2},{1,3},{2,0},{3,1},{4,6},{5,7},{6,4},{7,5},{8,10},{9,11},{10,... | collective-permute-start | bytes 786440 | tf_op jit(solution)/shard_map/ppermute | solution.py:564
  264.4 13.0 %collective-permute-start.26 = (bf16[64,2048]{1,0:T(8,128)(2,1)S(1)}, bf16[64,2048]{1,0:T(8,128)(2,1)}, u32[]{:S(2)}, u32[]{:S(2)}) collective-permute-start(bf16[64,2048]{1,0:T(8,128)(2,1)S(1)} %get-tuple-element.277), channel_id=1, source_target_pairs={{0,4},{1,5},{2,6},{3,7},{4,0},{5,1},{6,2},{7,3},{8,12},{9,13},{10,... | collective-permute-start | bytes 786440 | tf_op jit(solution)/shard_map/ppermute | solution.py:564
  264.8 12.6 %collective-permute-start.27 = (bf16[64,2048]{1,0:T(8,128)(2,1)S(1)}, bf16[64,2048]{1,0:T(8,128)(2,1)}, u32[]{:S(2)}, u32[]{:S(2)}) collective-permute-start(bf16[64,2048]{1,0:T(8,128)(2,1)S(1)} %get-tuple-element.276), channel_id=1, source_target_pairs={{0,6},{1,7},{2,4},{3,5},{4,2},{5,3},{6,0},{7,1},{8,14},{9,15},{10,... | collective-permute-start | bytes 786440 | tf_op jit(solution)/shard_map/ppermute | solution.py:564
  266.8 51.9 %collective-permute-start.33 = (bf16[4,512,384]{2,1,0:T(8,128)(2,1)S(1)}, bf16[4,512,384]{2,1,0:T(8,128)(2,1)}, u32[]{:S(2)}, u32[]{:S(2)}) collective-permute-start(bf16[4,512,384]{2,1,0:T(8,128)(2,1)S(1)} %pad_maximum_fusion.1.w0), channel_id=1, source_target_pairs={{0,16},{16,0},{1,17},{17,1},{2,18},{18,2},{3,19},{19,3},{4,20},{20... | collective-permute-start | bytes 4718600 | tf_op jit(solution)/shard_map/ppermute | solution.py:567
  282.3 10.8 %collective-permute-start.28 = (bf16[128,2048]{1,0:T(8,128)(2,1)}, bf16[128,2048]{1,0:T(8,128)(2,1)S(1)}, u32[]{:S(2)}, u32[]{:S(2)}) collective-permute-start(bf16[128,2048]{1,0:T(8,128)(2,1)} %get-tuple-element.179.own), channel_id=1, source_target_pairs={{0,1},{1,0},{2,3},{3,2},{4,5},{5,4},{6,7},{7,6},{8,9},{9,8},{10,11... | collective-permute-start | bytes 1572872 | tf_op jit(solution)/shard_map/ppermute | solution.py:564
  293.9 31.8 %collective-permute-start.29 = (bf16[4,64,2048]{2,1,0:T(8,128)(2,1)}, bf16[4,64,2048]{2,1,0:T(8,128)(2,1)}, u32[]{:S(2)}, u32[]{:S(2)}) collective-permute-start(bf16[4,64,2048]{2,1,0:T(8,128)(2,1)} %get-tuple-element.184), channel_id=1, source_target_pairs={{0,1},{1,0},{2,3},{3,2},{4,5},{5,4},{6,7},{7,6},{8,9},{9,8},{10,11... | collective-permute-start | bytes 3145736 | tf_op jit(solution)/shard_map/ppermute | solution.py:564
  295.6 32.8 %all-to-all-start.1 = ((bf16[4,64,2048]{2,1,0:T(8,128)(2,1)}), bf16[4,64,2048]{2,1,0:T(8,128)(2,1)}, u32[]{:S(2)}, u32[]{:S(2)}) async-start(bf16[4,64,2048]{2,1,0:T(8,128)(2,1)} %add_convert_fusion.2), calls=%async_computation.1 | async-start | bytes 2097152 | tf_op jit(solution)/shard_map/all_to_all | solution.py:897
  313.7 7.7 %collective-permute-start.30 = (bf16[256,256]{1,0:T(8,128)(2,1)S(1)}, bf16[256,256]{1,0:T(8,128)(2,1)S(1)}, u32[]{:S(2)}, u32[]{:S(2)}) collective-permute-start(bf16[256,256]{1,0:T(8,128)(2,1)S(1)} %get-tuple-element.186), channel_id=1, source_target_pairs={{0,2},{1,3},{2,0},{3,1},{4,6},{5,7},{6,4},{7,5},{8,10},{9,11},{10,... | collective-permute-start | bytes 393224 | tf_op jit(solution)/shard_map/ppermute | solution.py:564
  316.3 8.7 %collective-permute-start.31 = (bf16[256,256]{1,0:T(8,128)(2,1)S(1)}, bf16[256,256]{1,0:T(8,128)(2,1)S(1)}, u32[]{:S(2)}, u32[]{:S(2)}) collective-permute-start(bf16[256,256]{1,0:T(8,128)(2,1)S(1)} %get-tuple-element.187), channel_id=1, source_target_pairs={{0,4},{1,5},{2,6},{3,7},{4,0},{5,1},{6,2},{7,3},{8,12},{9,13},{10,... | collective-permute-start | bytes 393224 | tf_op jit(solution)/shard_map/ppermute | solution.py:564
  318.1 6.9 %collective-permute-start.32 = (bf16[256,256]{1,0:T(8,128)(2,1)S(1)}, bf16[256,256]{1,0:T(8,128)(2,1)S(1)}, u32[]{:S(2)}, u32[]{:S(2)}) collective-permute-start(bf16[256,256]{1,0:T(8,128)(2,1)S(1)} %get-tuple-element.188), channel_id=1, source_target_pairs={{0,6},{1,7},{2,4},{3,5},{4,2},{5,3},{6,0},{7,1},{8,14},{9,15},{10,... | collective-permute-start | bytes 393224 | tf_op jit(solution)/shard_map/ppermute | solution.py:564
  318.7 14.0 %collective-permute-start.34 = (bf16[4,512,384]{2,1,0:T(8,128)(2,1)S(1)}, bf16[4,512,384]{2,1,0:T(8,128)(2,1)}, u32[]{:S(2)}, u32[]{:S(2)}) collective-permute-start(bf16[4,512,384]{2,1,0:T(8,128)(2,1)S(1)} %pad_maximum_fusion.1.w0), channel_id=1, source_target_pairs={{0,8},{8,0},{1,9},{9,1},{2,10},{10,2},{3,11},{11,3},{4,12},{12,4},... | collective-permute-start | bytes 4718600 | tf_op jit(solution)/shard_map/ppermute | solution.py:570
  321.4 11.3 %collective-permute-start.35 = (bf16[4,512,384]{2,1,0:T(8,128)(2,1)}, bf16[4,512,384]{2,1,0:T(8,128)(2,1)}, u32[]{:S(2)}, u32[]{:S(2)}) collective-permute-start(bf16[4,512,384]{2,1,0:T(8,128)(2,1)} %collective-permute-done.33.w1), channel_id=1, source_target_pairs={{0,8},{8,0},{1,9},{9,1},{2,10},{10,2},{3,11},{11,3},{4,12},{12,4},... | collective-permute-start | bytes 4718600 | tf_op jit(solution)/shard_map/ppermute | solution.py:570
  328.4 49.5 %all-to-all-start.2 = ((bf16[4,64,2048]{2,1,0:T(8,128)(2,1)}), bf16[4,64,2048]{2,1,0:T(8,128)(2,1)}, u32[]{:S(2)}, u32[]{:S(2)}) async-start(bf16[4,64,2048]{2,1,0:T(8,128)(2,1)} %add_convert_fusion.1), calls=%async_computation.2 | async-start | bytes 2097152 | tf_op jit(solution)/shard_map/all_to_all | solution.py:916
  332.6 104.0 %all-gather.12.cloned.1.call-start = ((), (), s32[]{:S(2)}) async-start(), calls=%async_computation.7 | async-start | bytes 2621440 | tf_op jit(solution)/shard_map/all_gather | solution.py:1005
  350.4 23.6 %collective-permute-start.36 = (bf16[1024,128]{1,0:T(8,128)(2,1)S(1)}, bf16[1024,128]{1,0:T(8,128)(2,1)S(1)}, u32[]{:S(2)}, u32[]{:S(2)}) collective-permute-start(bf16[1024,128]{1,0:T(8,128)(2,1)S(1)} %get-tuple-element.286), channel_id=1, source_target_pairs={{0,8},{8,0},{1,9},{9,1},{2,10},{10,2},{3,11},{11,3},{4,12},{12,4},... | collective-permute-start | bytes 786440 | tf_op jit(solution)/shard_map/ppermute | solution.py:570
  359.4 7.1 %collective-permute-start.37 = (bf16[256,256]{1,0:T(8,128)(2,1)S(1)}, bf16[256,256]{1,0:T(8,128)(2,1)S(1)}, u32[]{:S(2)}, u32[]{:S(2)}) collective-permute-start(bf16[256,256]{1,0:T(8,128)(2,1)S(1)} %get-tuple-element.199), channel_id=1, source_target_pairs={{0,2},{1,3},{2,0},{3,1},{4,6},{5,7},{6,4},{7,5},{8,10},{9,11},{10,... | collective-permute-start | bytes 393224 | tf_op jit(solution)/shard_map/ppermute | solution.py:564
  361.1 12.9 %collective-permute-start.38 = (bf16[256,256]{1,0:T(8,128)(2,1)S(1)}, bf16[256,256]{1,0:T(8,128)(2,1)S(1)}, u32[]{:S(2)}, u32[]{:S(2)}) collective-permute-start(bf16[256,256]{1,0:T(8,128)(2,1)S(1)} %get-tuple-element.200), channel_id=1, source_target_pairs={{0,4},{1,5},{2,6},{3,7},{4,0},{5,1},{6,2},{7,3},{8,12},{9,13},{10,... | collective-permute-start | bytes 393224 | tf_op jit(solution)/shard_map/ppermute | solution.py:564
  363.5 10.5 %collective-permute-start.39 = (bf16[256,256]{1,0:T(8,128)(2,1)S(1)}, bf16[256,256]{1,0:T(8,128)(2,1)S(1)}, u32[]{:S(2)}, u32[]{:S(2)}) collective-permute-start(bf16[256,256]{1,0:T(8,128)(2,1)S(1)} %get-tuple-element.201), channel_id=1, source_target_pairs={{0,6},{1,7},{2,4},{3,5},{4,2},{5,3},{6,0},{7,1},{8,14},{9,15},{10,... | collective-permute-start | bytes 393224 | tf_op jit(solution)/shard_map/ppermute | solution.py:564
  381.0 93.3 %all-gather.14.cloned.1.call-start = ((), (), s32[]{:S(2)}) async-start(), calls=%async_computation.8 | async-start | bytes 2621440 | tf_op jit(solution)/shard_map/all_gather | solution.py:1023
  381.0 5.1 collective-permute-start.40
  383.2 7.1 %collective-permute-start.41 = (bf16[256,128]{1,0:T(8,128)(2,1)S(1)}, bf16[256,128]{1,0:T(8,128)(2,1)S(1)}, u32[]{:S(2)}, u32[]{:S(2)}) collective-permute-start(bf16[256,128]{1,0:T(8,128)(2,1)S(1)} %copy-done.89), channel_id=1, source_target_pairs={{0,4},{1,5},{2,6},{3,7},{4,0},{5,1},{6,2},{7,3},{8,12},{9,13},{10,... | collective-permute-start | bytes 196616 | tf_op jit(solution)/shard_map/ppermute | solution.py:564
  384.3 6.7 %collective-permute-start.42 = (bf16[256,128]{1,0:T(8,128)(2,1)S(1)}, bf16[256,128]{1,0:T(8,128)(2,1)S(1)}, u32[]{:S(2)}, u32[]{:S(2)}) collective-permute-start(bf16[256,128]{1,0:T(8,128)(2,1)S(1)} %copy-done.88), channel_id=1, source_target_pairs={{0,6},{1,7},{2,4},{3,5},{4,2},{5,3},{6,0},{7,1},{8,14},{9,15},{10,... | collective-permute-start | bytes 196616 | tf_op jit(solution)/shard_map/ppermute | solution.py:564
  402.1 14.2 %collective-permute-start.43 = (bf16[128,2048]{1,0:T(8,128)(2,1)}, bf16[128,2048]{1,0:T(8,128)(2,1)S(1)}, u32[]{:S(2)}, u32[]{:S(2)}) collective-permute-start(bf16[128,2048]{1,0:T(8,128)(2,1)} %get-tuple-element.216), channel_id=1, source_target_pairs={{0,1},{1,0},{2,3},{3,2},{4,5},{5,4},{6,7},{7,6},{8,9},{9,8},{10,11... | collective-permute-start | bytes 1572872 | tf_op jit(solution)/shard_map/ppermute | solution.py:564
  409.2 15.8 %collective-permute-start.48 = (bf16[1024,1024]{1,0:T(8,128)(2,1)}, bf16[1024,1024]{1,0:T(8,128)(2,1)}, u32[]{:S(2)}, u32[]{:S(2)}) collective-permute-start(bf16[1024,1024]{1,0:T(8,128)(2,1)} %get-tuple-element.225), channel_id=1, source_target_pairs={{0,8},{8,0},{1,9},{9,1},{2,10},{10,2},{3,11},{11,3},{4,12},{12,4},... | collective-permute-start | bytes 6291464 | tf_op jit(solution)/shard_map/ppermute | solution.py:570
  424.3 10.6 %collective-permute-start.50 = (bf16[1024,384]{1,0:T(8,128)(2,1)}, bf16[1024,384]{1,0:T(8,128)(2,1)S(1)}, u32[]{:S(2)}, u32[]{:S(2)}) collective-permute-start(bf16[1024,384]{1,0:T(8,128)(2,1)} %get-tuple-element.221), channel_id=1, source_target_pairs={{0,8},{8,0},{1,9},{9,1},{2,10},{10,2},{3,11},{11,3},{4,12},{12,4},... | collective-permute-start | bytes 2359304 | tf_op jit(solution)/shard_map/ppermute | solution.py:570
  429.2 39.1 %collective-permute-start.49 = (bf16[512,1024]{1,0:T(8,128)(2,1)}, bf16[512,1024]{1,0:T(8,128)(2,1)}, u32[]{:S(2)}, u32[]{:S(2)}) collective-permute-start(bf16[512,1024]{1,0:T(8,128)(2,1)} %pair_sum.2), channel_id=1, source_target_pairs={{0,16},{16,0},{1,17},{17,1},{2,18},{18,2},{3,19},{19,3},{4,20},{20... | collective-permute-start | bytes 3145736 | tf_op jit(solution)/shard_map/ppermute | solution.py:567
  432.8 14.0 %collective-permute-start.44 = (bf16[128,2048]{1,0:T(8,128)(2,1)}, bf16[128,2048]{1,0:T(8,128)(2,1)S(1)}, u32[]{:S(2)}, u32[]{:S(2)}) collective-permute-start(bf16[128,2048]{1,0:T(8,128)(2,1)} %first_norm_back.1), channel_id=1, source_target_pairs={{0,1},{1,0},{2,3},{3,2},{4,5},{5,4},{6,7},{7,6},{8,9},{9,8},{10,11... | collective-permute-start | bytes 1572872 | tf_op jit(solution)/shard_map/ppermute | solution.py:564
  435.1 33.2 %collective-permute-start.51 = (bf16[512,384]{1,0:T(8,128)(2,1)S(1)}, bf16[512,384]{1,0:T(8,128)(2,1)S(1)}, u32[]{:S(2)}, u32[]{:S(2)}) collective-permute-start(bf16[512,384]{1,0:T(8,128)(2,1)S(1)} %pair_sum.3), channel_id=1, source_target_pairs={{0,16},{16,0},{1,17},{17,1},{2,18},{18,2},{3,19},{19,3},{4,20},{20... | collective-permute-start | bytes 1179656 | tf_op jit(solution)/shard_map/ppermute | solution.py:567
  436.1 12.3 %collective-permute-start.47 = (f32[2,1024]{1,0:T(2,128)S(1)}, f32[2,1024]{1,0:T(2,128)S(1)}, u32[]{:S(2)}, u32[]{:S(2)}) collective-permute-start(f32[2,1024]{1,0:T(2,128)S(1)} %fusion.4), channel_id=1, source_target_pairs={{0,1},{1,0},{2,3},{3,2},{4,5},{5,4},{6,7},{7,6},{8,9},{9,8},{10,11... | collective-permute-start | bytes 24584 | tf_op jit(solution)/shard_map/ppermute | solution.py:564
  446.8 48.9 %collective-permute-start.45 = (bf16[4,128,2048]{2,1,0:T(8,128)(2,1)}, bf16[4,128,2048]{2,1,0:T(8,128)(2,1)}, u32[]{:S(2)}, u32[]{:S(2)}) collective-permute-start(bf16[4,128,2048]{2,1,0:T(8,128)(2,1)} %bitcast.57), channel_id=1, source_target_pairs={{0,1},{1,0},{2,3},{3,2},{4,5},{5,4},{6,7},{7,6},{8,9},{9,8},{10,11... | collective-permute-start | bytes 6291464 | tf_op jit(solution)/shard_map/ppermute | solution.py:564
  476.0 51.2 %collective-permute-start.52 = (bf16[3,128,2048]{2,1,0:T(8,128)(2,1)S(1)}, bf16[3,128,2048]{2,1,0:T(8,128)(2,1)S(1)}, u32[]{:S(2)}, u32[]{:S(2)}) collective-permute-start(bf16[3,128,2048]{2,1,0:T(8,128)(2,1)S(1)} %pad_maximum_fusion.2), channel_id=1, source_target_pairs={{0,1},{1,0},{2,3},{3,2},{4,5},{5,4},{6,7},{7,6},{8,9},{9,8},{10,11... | collective-permute-start | bytes 4718600 | tf_op jit(solution)/shard_map/ppermute | solution.py:564
  477.5 3.6 collective-permute-start.56
  481.2 4.0 collective-permute-start.57
  482.1 31.9 %collective-permute-start.53 = (bf16[512,256]{1,0:T(8,128)(2,1)S(1)}, bf16[512,256]{1,0:T(8,128)(2,1)S(1)}, u32[]{:S(2)}, u32[]{:S(2)}) collective-permute-start(bf16[512,256]{1,0:T(8,128)(2,1)S(1)} %get-tuple-element.274), channel_id=1, source_target_pairs={{0,2},{1,3},{2,0},{3,1},{4,6},{5,7},{6,4},{7,5},{8,10},{9,11},{10,... | collective-permute-start | bytes 786440 | tf_op jit(solution)/shard_map/ppermute | solution.py:564
  484.1 29.9 %collective-permute-start.54 = (bf16[512,256]{1,0:T(8,128)(2,1)S(1)}, bf16[512,256]{1,0:T(8,128)(2,1)S(1)}, u32[]{:S(2)}, u32[]{:S(2)}) collective-permute-start(bf16[512,256]{1,0:T(8,128)(2,1)S(1)} %get-tuple-element.273), channel_id=1, source_target_pairs={{0,4},{1,5},{2,6},{3,7},{4,0},{5,1},{6,2},{7,3},{8,12},{9,13},{10,... | collective-permute-start | bytes 786440 | tf_op jit(solution)/shard_map/ppermute | solution.py:564
  485.1 28.9 %collective-permute-start.55 = (bf16[512,256]{1,0:T(8,128)(2,1)S(1)}, bf16[512,256]{1,0:T(8,128)(2,1)S(1)}, u32[]{:S(2)}, u32[]{:S(2)}) collective-permute-start(bf16[512,256]{1,0:T(8,128)(2,1)S(1)} %get-tuple-element.272), channel_id=1, source_target_pairs={{0,6},{1,7},{2,4},{3,5},{4,2},{5,3},{6,0},{7,1},{8,14},{9,15},{10,... | collective-permute-start | bytes 786440 | tf_op jit(solution)/shard_map/ppermute | solution.py:564
  495.7 17.7 %collective-permute-start.58 = (f32[2,512]{1,0:T(2,128)S(1)}, f32[2,512]{1,0:T(2,128)S(1)}, u32[]{:S(2)}, u32[]{:S(2)}) collective-permute-start(f32[2,512]{1,0:T(2,128)S(1)} %add.120), channel_id=1, source_target_pairs={{0,4},{1,5},{2,6},{3,7},{4,0},{5,1},{6,2},{7,3},{8,12},{9,13},{10,... | collective-permute-start | bytes 12296 | tf_op jit(solution)/shard_map/ppermute | solution.py:564
  (94 other events, 1469.4 us)
Sparse Core Ops, SparseCore 0:
  14.8 28.3 all-gather.9
  45.4 93.9 all-gather.7
  245.9 113.5 reduce-scatter.1
  381.1 46.4 all-gather.11
  429.6 44.6 all-gather.13
